TPU v7x, 32 devices: a whole 2x2x4 slice. The times are simulated.
32 devices in a mesh: gx: 8 (over y, x, core), gy: 4 (over z).
Axes of the slice: x: 2, y: 2, z: 4, core: 2. Of those that a mesh axis runs over, the one named last changes fastest.
Arguments:
- state: float32 [4, 256, 1024], P(None, 'gx', 'gy'), as said below
Outputs:
- advanced: float32 [4, 256, 1024], P(None, 'gx', 'gy')
Inputs may be any that keep to these rules, and one draw needn't show every extreme that they name: `state`: density lies between 0.5 and 1.5 and pressure between 0.3 and 1.5 in every cell, and each velocity component is under 0.35 in size.
All inputs are finite; a program needn't handle non-finite values.
Results may differ from a plain program's by a relative error of at most 0.0003.
Values sent between devices are 32-bit elements; how exact they have to be, the bound alone decides.
No kernel may reach another device: no remote copies, remote signals or barrier semaphores. Data moves between devices by JAX's collectives and lax.ppermute only.
A program may use at most 64 MiB of HBM per device.

v0:
```python
import functools

import jax
import jax.numpy as jnp
from jax import lax
from jax.experimental import pallas as pl
from jax.experimental.pallas import tpu as pltpu
from jax.sharding import PartitionSpec as P

STEPS = 4
HALO = 4 * STEPS
GROUP = 2
LANES = 128
GAMMA = 1.4
COURANT = 0.35
TINY = 1e-30

VMEM = pl.BlockSpec(memory_space=pltpu.VMEM)


def params(limit):
    return pltpu.CompilerParams(vmem_limit_bytes=limit << 20)


def speed_kernel(state_ref, top_ref):
    density, mom_x, mom_y, energy = (state_ref[comp] for comp in range(4))
    inv = 1.0 / density
    pressure = (GAMMA - 1.0) * (energy - 0.5 * (mom_x * mom_x + mom_y * mom_y) * inv)
    speed = jnp.maximum(jnp.abs(mom_x * inv), jnp.abs(mom_y * inv)) + jnp.sqrt(GAMMA * pressure * inv)
    top_ref[...] = jnp.full(top_ref.shape, jnp.max(speed))


def lane_of(shape):
    return lax.broadcasted_iota(jnp.int32, shape, len(shape) - 1)


def pack_kernel(state_ref, up_ref, down_ref, left_ref, right_ref):
    rows = state_ref.shape[1]
    cols = state_ref.shape[2]
    half = rows // 2 + HALO

    def edge(low, at):
        total = jnp.zeros((half, LANES), jnp.float32)
        lane = lane_of((half, LANES))
        for side in range(2):
            for comp in range(4):
                if side == 0:
                    cells = jnp.concatenate(
                        [up_ref[comp, :, low : low + LANES], state_ref[comp, 0 : rows // 2, low : low + LANES]], axis=0
                    )
                else:
                    cells = jnp.concatenate(
                        [state_ref[comp, rows // 2 : rows, low : low + LANES], down_ref[comp, :, low : low + LANES]], axis=0
                    )
                goal = side * (LANES // 2) + comp * HALO
                moved = pltpu.roll(cells, (goal - at) % LANES, axis=1)
                total = jnp.where((lane >= goal) & (lane < goal + HALO), moved, total)
        return total

    left_ref[...] = edge(0, 0)
    right_ref[...] = edge(cols - LANES, LANES - HALO)


def minmod(first, second):
    low = jnp.minimum(first, second)
    high = jnp.maximum(first, second)
    return jnp.maximum(low, jnp.minimum(high, 0.0))


def fluxes(state):
    density, normal, tangent, energy = state
    inv = pl.reciprocal(density, approx=True)
    vel = normal * inv
    carried = normal * vel
    pressure = (GAMMA - 1.0) * energy - (0.5 * (GAMMA - 1.0)) * (carried + tangent * tangent * inv)
    square = GAMMA * pressure * inv
    sound = square * lax.rsqrt(jnp.maximum(square, TINY))
    return (normal, carried + pressure, tangent * vel, (energy + pressure) * vel), jnp.abs(vel) + sound


def face(left, left_flux, left_speed, right, right_flux, right_speed):
    top = jnp.maximum(left_speed, right_speed)
    return [
        (left_flux[comp] + right_flux[comp]) - top * (right[comp] - left[comp]) for comp in range(4)
    ]


def swapped(parts):
    return [parts[0], parts[2], parts[1], parts[3]]


def steps_kernel(rows, cols, state_ref, up_ref, down_ref, before_ref, after_ref, top_ref, out_ref, field, mid, diff):
    tall = rows + 2 * HALO
    tiles = cols // LANES
    wide = (tiles + 1) * LANES
    half = tall // 2
    factor = -0.5 * COURANT / jnp.max(top_ref[...].reshape(-1, LANES))

    for comp in range(4):
        for tile in range(tiles):
            lanes = slice(tile * LANES, (tile + 1) * LANES)
            field[comp, tile, 0:HALO, :] = up_ref[comp, :, lanes]
            field[comp, tile, HALO : HALO + rows, :] = state_ref[comp, :, lanes]
            field[comp, tile, HALO + rows : tall, :] = down_ref[comp, :, lanes]
    lane = lane_of((half, LANES))
    from_before = before_ref[...]
    from_after = after_ref[...]
    for side in range(2):
        for comp in range(4):
            at = side * (LANES // 2) + comp * HALO
            left = pltpu.roll(from_before, (LANES - HALO - at) % LANES, axis=1)
            right = pltpu.roll(from_after, (-at) % LANES, axis=1)
            field[comp, tiles, side * half : (side + 1) * half, :] = jnp.where(lane < LANES // 2, right, left)

    def rolled(tree, by):
        return jax.tree.map(lambda value: pltpu.roll(value, by % 8, axis=0), tree)

    def jump_of(first, second):
        return [0.5 * (second[comp] - first[comp]) for comp in range(4)]

    def cell(here, before_jump, after_jump):
        half_slope = [minmod(before_jump[comp], after_jump[comp]) for comp in range(4)]
        low = [here[comp] - half_slope[comp] for comp in range(4)]
        high = [here[comp] + half_slope[comp] for comp in range(4)]
        return (low, *fluxes(low)), (high, *fluxes(high))

    def x_pass(src, start, step):
        def one_tile(tile, none):
            values = [
                [src[comp, tile, pl.ds(start + at, 8, stride=step), :] for comp in range(4)] for at in range(step)
            ]
            jumps = [jump_of(values[at], values[at + 1]) for at in range(step - 1)]
            jumps.append(jump_of(values[step - 1], rolled(values[0], -1)))
            lows, highs, faces = {}, {}, {}
            for at in range(step):
                jump_before = jumps[at - 1] if at else rolled(jumps[step - 1], 1)
                lows[at], highs[at] = cell(values[at], jump_before, jumps[at])
                if at:
                    faces[at - 1] = face(*highs[at - 1], *lows[at])
                if at > 1:
                    for comp in range(4):
                        diff[comp, tile, at - 1] = faces[at - 1][comp] - faces[at - 2][comp]
            faces[step - 1] = face(*highs[step - 1], *rolled(lows[0], -1))
            first = rolled(faces[step - 1], 1)
            for comp in range(4):
                diff[comp, tile, step - 1] = faces[step - 1][comp] - faces[step - 2][comp]
                diff[comp, tile, 0] = faces[0][comp] - first[comp]
            return none

        lax.fori_loop(0, tiles + 1, one_tile, None)

    def load_wide(src, start, step, at, comp):
        return jnp.concatenate(
            [src[comp, tile, pl.ds(start + at, 8, stride=step), :] for tile in range(tiles + 1)], axis=1
        )

    def shifted(parts, by):
        return [pltpu.roll(part, by % wide, axis=1) for part in parts]

    def y_change(src, start, step, at):
        here = [load_wide(src, start, step, at, comp) for comp in (0, 2, 1, 3)]
        ahead = shifted(here, -1)
        jumps = jump_of(here, ahead)
        behind = shifted(jumps, 1)
        half_slope = [minmod(behind[comp], jumps[comp]) for comp in range(4)]
        low = shifted([here[comp] - half_slope[comp] for comp in range(4)], -1)
        high = [here[comp] + half_slope[comp] for comp in range(4)]
        faces = face(high, *fluxes(high), low, *fluxes(low))
        lower = shifted(faces, 1)
        change = swapped([faces[comp] - lower[comp] for comp in range(4)])
        return swapped(here), [
            change[comp] + jnp.concatenate([diff[comp, tile, at] for tile in range(tiles + 1)], axis=1)
            for comp in range(4)
        ]

    def store(dst, start, step, at, comp, value):
        for tile in range(tiles + 1):
            dst[comp, tile, pl.ds(start + at, 8, stride=step), :] = value[:, tile * LANES : (tile + 1) * LANES]

    def two_steps(start, step):
        def first_rows(group, none):
            for inner in range(GROUP):
                at = group * GROUP + inner
                here, change = y_change(field, start, step, at)
                for comp in range(4):
                    store(mid, start, step, at, comp, here[comp] + factor * change[comp])
            return none

        def second_rows(group, none):
            for inner in range(GROUP):
                at = group * GROUP + inner
                here, change = y_change(mid, start, step, at)
                for comp in range(4):
                    old = load_wide(field, start, step, at, comp)
                    store(field, start, step, at, comp, 0.5 * (old + here[comp]) + (0.5 * factor) * change[comp])
            return none

        def one_step(index, none):
            x_pass(field, start, step)
            lax.fori_loop(0, step // GROUP, first_rows, None)
            x_pass(mid, start, step)
            lax.fori_loop(0, step // GROUP, second_rows, None)
            return none

        lax.fori_loop(0, 2, one_step, None)

    for index in range(0, STEPS, 2):
        two_steps(4 * index, (tall - 8 * index) // 8)
    for comp in range(4):
        for tile in range(tiles):
            out_ref[comp, :, tile * LANES : (tile + 1) * LANES] = field[comp, tile, HALO : HALO + rows, :]


def local(state):
    parts, rows, cols = state.shape
    count_x, count_y = lax.axis_size("gx"), lax.axis_size("gy")
    tall = rows + 2 * HALO
    tiles = cols // LANES

    def ahead(count):
        return [(i, (i + 1) % count) for i in range(count)]

    def back(count):
        return [((i + 1) % count, i) for i in range(count)]

    up = lax.ppermute(state[:, rows - HALO :, :], "gx", ahead(count_x))
    down = lax.ppermute(state[:, :HALO, :], "gx", back(count_x))
    top = pl.pallas_call(
        speed_kernel,
        out_shape=jax.ShapeDtypeStruct((8, LANES), jnp.float32),
        in_specs=[VMEM],
        out_specs=VMEM,
        compiler_params=params(4),
        name="speed",
    )(state)
    top = lax.all_gather(top, ("gx", "gy"))
    edge_type = jax.ShapeDtypeStruct((tall // 2, LANES), jnp.float32)
    left, right = pl.pallas_call(
        pack_kernel,
        out_shape=(edge_type, edge_type),
        in_specs=[VMEM] * 3,
        out_specs=(VMEM, VMEM),
        compiler_params=params(4),
        name="pack",
    )(state, up, down)
    before = lax.ppermute(right, "gy", ahead(count_y))
    after = lax.ppermute(left, "gy", back(count_y))
    return pl.pallas_call(
        functools.partial(steps_kernel, rows, cols),
        out_shape=jax.ShapeDtypeStruct(state.shape, jnp.float32),
        in_specs=[VMEM] * 6,
        out_specs=VMEM,
        scratch_shapes=[
            pltpu.VMEM((parts, tiles + 1, tall, LANES), jnp.float32),
            pltpu.VMEM((parts, tiles + 1, tall, LANES), jnp.float32),
            pltpu.VMEM((parts, tiles + 1, tall // 8, 8, LANES), jnp.float32),
        ],
        compiler_params=params(16),
        name="steps",
    )(state, up, down, before, after, top)


def solution(mesh):
    in_specs = (P(None, "gx", "gy"),)
    out_specs = P(None, "gx", "gy")
    return jax.shard_map(local, mesh=mesh, in_specs=in_specs, out_specs=out_specs, check_vma=False)
```

profile of v0, /device:TPU:0, one launch (start us, length us, event | category | flops | bytes accessed | tf_op | source)
XLA Modules:
  0.0 91.3 jit_solution(6132138248913933701)
XLA Ops:
  0.0 0.0 copy-start
  0.0 0.9 %fusion = (f32[4,16,256]{2,1,0:T(8,128)S(1)}, f32[4,16,256]{2,1,0:T(8,128)S(1)}) fusion(f32[4,32,256]{2,1,0:T(8,128)} %state_ref.5), kind=kLoop, calls=%fused_computation | loop fusion | bytes 262144 | tf_op jit(solution)/shard_map/slice | solution.py:227
  0.9 3.4 %collective-permute-start.1 = (f32[4,16,256]{2,1,0:T(8,128)S(1)}, f32[4,16,256]{2,1,0:T(8,128)S(1)}, u32[]{:S(2)}, u32[]{:S(2)}) collective-permute-start(f32[4,16,256]{2,1,0:T(8,128)S(1)} %get-tuple-element.9), channel_id=1, source_target_pairs={{4,0},{8,4},{12,8},{16,12},{20,16},{24,20},{28,24},{0,28},{5,1},{9... | collective-permute-start | bytes 196616 | tf_op jit(solution)/shard_map/ppermute | solution.py:227
  4.3 0.0 collective-permute-start
  4.3 0.0 copy-done
  4.3 0.1 speed.1
  4.5 1.7 %collective-permute-done.1.down_ref = f32[4,16,256]{2,1,0:T(8,128)S(1)} collective-permute-done((f32[4,16,256]{2,1,0:T(8,128)S(1)}, f32[4,16,256]{2,1,0:T(8,128)S(1)}, u32[]{:S(2)}, u32[]{:S(2)}) %collective-permute-start.1) | collective-permute-done | bytes 65568 | tf_op jit(solution)/shard_map/ppermute | solution.py:227
  6.2 2.7 %collective-permute-done.up_ref = f32[4,16,256]{2,1,0:T(8,128)S(1)} collective-permute-done((f32[4,16,256]{2,1,0:T(8,128)S(1)}, f32[4,16,256]{2,1,0:T(8,128)S(1)}, u32[]{:S(2)}, u32[]{:S(2)}) %collective-permute-start) | collective-permute-done | bytes 65568 | tf_op jit(solution)/shard_map/ppermute | solution.py:226
  8.9 0.1 pack.1
  9.0 1.6 %collective-permute-start.2 = (f32[32,128]{1,0:T(8,128)S(1)}, f32[32,128]{1,0:T(8,128)S(1)}, u32[]{:S(2)}, u32[]{:S(2)}) collective-permute-start(f32[32,128]{1,0:T(8,128)S(1)} %get-tuple-element.7), channel_id=1, source_target_pairs={{0,1},{1,2},{2,3},{3,0},{4,5},{5,6},{6,7},{7,4},{8,9},{9,10},{10,1... | collective-permute-start | bytes 49160 | tf_op jit(solution)/shard_map/ppermute | solution.py:246
  10.7 2.2 %collective-permute-start.3 = (f32[32,128]{1,0:T(8,128)S(1)}, f32[32,128]{1,0:T(8,128)S(1)}, u32[]{:S(2)}, u32[]{:S(2)}) collective-permute-start(f32[32,128]{1,0:T(8,128)S(1)} %get-tuple-element.8), channel_id=1, source_target_pairs={{1,0},{2,1},{3,2},{0,3},{5,4},{6,5},{7,6},{4,7},{9,8},{10,9},{11,1... | collective-permute-start | bytes 49160 | tf_op jit(solution)/shard_map/ppermute | solution.py:247
  12.9 65.0 %all-gather = f32[256,128]{1,0:T(8,128)S(1)} all-gather(f32[8,128]{1,0:T(8,128)S(1)} %speed.1), channel_id=2, replica_groups=mesh['gx'=8,'gy'=4] {'gx','gy'}, dimensions={0}, use_global_device_ids=true | all-gather | bytes 135168 | tf_op jit(solution)/shard_map/all_gather | solution.py:236
  77.9 0.0 collective-permute-done.2.before_ref
  77.9 0.0 collective-permute-done.3.after_ref
  77.9 13.4 %steps.1 = f32[4,32,256]{2,1,0:T(8,128)} custom-call(f32[4,32,256]{2,1,0:T(8,128)S(1)} %copy-done, f32[4,16,256]{2,1,0:T(8,128)S(1)} %collective-permute-done.up_ref, f32[4,16,256]{2,1,0:T(8,128)S(1)} %collective-permute-done.1.down_ref, f32[32,128]{1,0:T(8,128)S(1)} %collective-permute-done.2.before_ref, f32[32,128]{1,0:T(8,128)S(1)} %collective-permute-done.3.after_ref, ...), custom_call_target="tpu_custom_call" | custom-call | tf_op jit(solution)/shard_map/steps/pallas_call | solution.py:248
Async XLA Ops:
  0.0 4.3 %copy-start = (f32[4,32,256]{2,1,0:T(8,128)S(1)}, f32[4,32,256]{2,1,0:T(8,128)}, u32[]{:S(2)}) copy-start(f32[4,32,256]{2,1,0:T(8,128)} %state_ref.5) | copy-start | bytes 393220
  0.9 5.3 %collective-permute-start.1 = (f32[4,16,256]{2,1,0:T(8,128)S(1)}, f32[4,16,256]{2,1,0:T(8,128)S(1)}, u32[]{:S(2)}, u32[]{:S(2)}) collective-permute-start(f32[4,16,256]{2,1,0:T(8,128)S(1)} %get-tuple-element.9), channel_id=1, source_target_pairs={{4,0},{8,4},{12,8},{16,12},{20,16},{24,20},{28,24},{0,28},{5,1},{9... | collective-permute-start | bytes 196616 | tf_op jit(solution)/shard_map/ppermute | solution.py:227
  4.3 4.6 %collective-permute-start = (f32[4,16,256]{2,1,0:T(8,128)S(1)}, f32[4,16,256]{2,1,0:T(8,128)S(1)}, u32[]{:S(2)}, u32[]{:S(2)}) collective-permute-start(f32[4,16,256]{2,1,0:T(8,128)S(1)} %get-tuple-element.10), channel_id=1, source_target_pairs={{0,4},{4,8},{8,12},{12,16},{16,20},{20,24},{24,28},{28,0},{1,5},{5... | collective-permute-start | bytes 196616 | tf_op jit(solution)/shard_map/ppermute | solution.py:226
  9.0 68.9 %collective-permute-start.2 = (f32[32,128]{1,0:T(8,128)S(1)}, f32[32,128]{1,0:T(8,128)S(1)}, u32[]{:S(2)}, u32[]{:S(2)}) collective-permute-start(f32[32,128]{1,0:T(8,128)S(1)} %get-tuple-element.7), channel_id=1, source_target_pairs={{0,1},{1,2},{2,3},{3,0},{4,5},{5,6},{6,7},{7,4},{8,9},{9,10},{10,1... | collective-permute-start | bytes 49160 | tf_op jit(solution)/shard_map/ppermute | solution.py:246
  10.7 67.2 %collective-permute-start.3 = (f32[32,128]{1,0:T(8,128)S(1)}, f32[32,128]{1,0:T(8,128)S(1)}, u32[]{:S(2)}, u32[]{:S(2)}) collective-permute-start(f32[32,128]{1,0:T(8,128)S(1)} %get-tuple-element.8), channel_id=1, source_target_pairs={{1,0},{2,1},{3,2},{0,3},{5,4},{6,5},{7,6},{4,7},{9,8},{10,9},{11,1... | collective-permute-start | bytes 49160 | tf_op jit(solution)/shard_map/ppermute | solution.py:247
where the time goes:
time: 91.4 us; the launch traced here: 91.3 us
  blocking collectives  65 us (71%)
  Pallas kernels  13.7 us (15%)
  starting transfers between devices  7.26 us (8%)
  waiting for transfers between devices  4.43 us (5%)
  local copies, waits for them, and re-layouts  0.93 us (1%)
    all_gather x1, blocking collectives, local(): top = lax.all_gather(top, ('gx', 'gy'))  65 us
    pallas_call x1, Pallas kernels, local(): pl.pallas_call(functools.partial(steps_kernel, rows, cols), out_shape=jax...  13.4 us
    ppermute x1, starting transfers between devices, local(): down = lax.ppermute(state[:, :HALO, :], 'gx', back(count_x))  3.39 us
    ppermute x1, waiting for transfers between devices, local(): up = lax.ppermute(state[:, rows - HALO:, :], 'gx', ahead(count_x))  2.68 us
    ppermute x1, starting transfers between devices, local(): after = lax.ppermute(left, 'gy', back(count_y))  2.25 us
  transfers between devices with their start and end apart: 4, of which 2 were waited for; matrix products, arithmetic and copies ran while one was open for 0% of the time, Pallas kernels for 0%

commit v1 on v0

v1 whole, which is shorter than its diff:
```python
import functools

import jax
import jax.numpy as jnp
from jax import lax
from jax.experimental import pallas as pl
from jax.experimental.pallas import tpu as pltpu
from jax.sharding import PartitionSpec as P

STEPS = 4
HALO = 4 * STEPS
LANES = 128
GAMMA = 1.4
COURANT = 0.35
TINY = 1e-30

VMEM = pl.BlockSpec(memory_space=pltpu.VMEM)


def params(limit):
    return pltpu.CompilerParams(vmem_limit_bytes=limit << 20)


def array(*shape):
    return jax.ShapeDtypeStruct(shape, jnp.float32)


def iota(shape, dim):
    return lax.broadcasted_iota(jnp.int32, shape, dim)


def edge_kernel(state_ref, head_ref, tail_ref, top_ref):
    rows = state_ref.shape[1]
    density, mom_x, mom_y, energy = (state_ref[comp] for comp in range(4))
    inv = 1.0 / density
    pressure = (GAMMA - 1.0) * (energy - 0.5 * (mom_x * mom_x + mom_y * mom_y) * inv)
    speed = jnp.maximum(jnp.abs(mom_x * inv), jnp.abs(mom_y * inv)) + jnp.sqrt(GAMMA * pressure * inv)
    top = jnp.max(speed)
    for comp in range(4):
        head_ref[comp * HALO : (comp + 1) * HALO, :] = state_ref[comp, 0:HALO, :]
        tail_ref[comp * HALO : (comp + 1) * HALO, :] = state_ref[comp, rows - HALO : rows, :]
    head_ref[4 * HALO :, :] = jnp.full((8, head_ref.shape[1]), top)
    tail_ref[4 * HALO :, :] = jnp.full((8, tail_ref.shape[1]), top)
    top_ref[...] = jnp.full(top_ref.shape, top)


def pack_kernel(state_ref, up_ref, down_ref, own_ref, far_ref, left_ref, right_ref, top_ref):
    rows = state_ref.shape[1]
    cols = state_ref.shape[2]
    half = rows // 2 + HALO
    lane = iota((half, LANES), 1)
    top = jnp.maximum(jnp.maximum(own_ref[...], far_ref[...]),
                      jnp.maximum(up_ref[4 * HALO :, 0:LANES], down_ref[4 * HALO :, 0:LANES]))

    def edge(low, at):
        lanes = slice(low, low + LANES)
        total = jnp.zeros((half, LANES), jnp.float32)
        for side in range(2):
            for comp in range(4):
                span = slice(comp * HALO, (comp + 1) * HALO)
                if side == 0:
                    cells = jnp.concatenate([up_ref[span, lanes], state_ref[comp, 0 : rows // 2, lanes]], axis=0)
                else:
                    cells = jnp.concatenate([state_ref[comp, rows // 2 : rows, lanes], down_ref[span, lanes]], axis=0)
                goal = side * (LANES // 2) + comp * HALO
                moved = pltpu.roll(cells, (goal - at) % LANES, axis=1)
                total = jnp.where((lane >= goal) & (lane < goal + HALO), moved, total)
        return total

    left_ref[0:half, :] = edge(0, 0)
    right_ref[0:half, :] = edge(cols - LANES, LANES - HALO)
    left_ref[half:, :] = top
    right_ref[half:, :] = top
    top_ref[...] = top


def selected(values, select):
    total = None
    for _ in range(3):
        part = values.astype(jnp.bfloat16)
        values = values - part.astype(jnp.float32)
        term = jnp.dot(part, select, preferred_element_type=jnp.float32)
        total = term if total is None else total + term
    return total


def minmod(first, second):
    low = jnp.minimum(first, second)
    high = jnp.maximum(first, second)
    return jnp.maximum(low, jnp.minimum(high, 0.0))


def fluxes(state):
    density, normal, tangent, energy = state
    inv = pl.reciprocal(density, approx=True)
    vel = normal * inv
    carried = normal * vel
    pressure = (GAMMA - 1.0) * energy - (0.5 * (GAMMA - 1.0)) * (carried + tangent * tangent * inv)
    square = GAMMA * pressure * inv
    sound = square * lax.rsqrt(jnp.maximum(square, TINY))
    return (normal, carried + pressure, tangent * vel, (energy + pressure) * vel), jnp.abs(vel) + sound


def face(left, right):
    (left_state, left_flux, left_speed), (right_state, right_flux, right_speed) = left, right
    top = jnp.maximum(left_speed, right_speed)
    return [
        (left_flux[comp] + right_flux[comp]) - top * (right_state[comp] - left_state[comp]) for comp in range(4)
    ]


def minus(first, second):
    return [first[comp] - second[comp] for comp in range(4)]


def sweep(load, store, count, axis):
    def rolled(tree, by):
        return jax.tree.map(lambda value: pltpu.roll(value, by % value.shape[axis], axis=axis), tree)

    def half(parts):
        return [0.5 * part for part in parts]

    here = load(0)
    end_jump = half(minus(rolled(here, -1), load(count - 1)))
    jump = rolled(end_jump, 1)
    for at in range(count):
        after = load(at + 1) if at + 1 < count else None
        next_jump = half(minus(after, here)) if at + 1 < count else end_jump
        slope = [minmod(jump[comp], next_jump[comp]) for comp in range(4)]
        low_state = minus(here, slope)
        high_state = [here[comp] + slope[comp] for comp in range(4)]
        low = (low_state, *fluxes(low_state))
        if at == 0:
            first_low = low
        else:
            flux = face(high, low)
            if at == 1:
                first_flux = flux
            else:
                store(at - 1, minus(flux, last_flux))
            last_flux = flux
        high = (high_state, *fluxes(high_state))
        here, jump = after, next_jump
    flux = face(high, rolled(first_low, -1))
    store(count - 1, minus(flux, last_flux))
    store(0, minus(first_flux, rolled(flux, 1)))


X_ORDER = (0, 1, 2, 3)
Y_ORDER = (0, 2, 1, 3)


def changes(src, diff, rows, cols, store):
    for col in range(cols):
        def keep(row, parts, col=col):
            for comp in range(4):
                diff[comp, row, col] = parts[comp]

        sweep(lambda row, col=col: [src[comp, row, col] for comp in X_ORDER], keep, rows, 0)
    for row in range(rows):
        def add(col, parts, row=row):
            store(row, col, [parts[Y_ORDER[comp]] + diff[comp, row, col] for comp in range(4)])

        sweep(lambda col, row=row: [src[comp, row, col] for comp in Y_ORDER], add, cols, 1)


def first_kernel(state_ref, up_ref, down_ref, before_ref, after_ref, field_ref, change_ref, plain, dealt, diff):
    rows, cols = state_ref.shape[1:]
    tall = rows + 2 * HALO
    half = tall // 2
    wide = plain.shape[1]
    groups = wide // LANES
    for comp in range(4):
        span = slice(comp * HALO, (comp + 1) * HALO)
        low = comp * tall
        plain[low : low + HALO, 0:cols] = up_ref[span, :]
        plain[low + HALO : low + HALO + rows, 0:cols] = state_ref[comp]
        plain[low + HALO + rows : low + tall, 0:cols] = down_ref[span, :]
    lane = iota((half, LANES), 1)
    from_before = before_ref[0:half, :]
    from_after = after_ref[0:half, :]
    for side in range(2):
        for comp in range(4):
            at = side * (LANES // 2) + comp * HALO
            left = pltpu.roll(from_before, (LANES - HALO - at) % LANES, axis=1)
            right = pltpu.roll(from_after, (-at) % LANES, axis=1)
            low = comp * tall + side * half
            plain[low : low + half, cols:] = jnp.where(lane < LANES // 2, right, left)
    source = iota((wide, wide), 0)
    goal = iota((wide, wide), 1)
    place = groups * (goal % LANES) + goal // LANES
    place = jnp.where(place < cols + 2 * HALO, (place + wide - HALO) % wide, 0)
    select = jnp.where(source == place, 1.0, 0.0).astype(jnp.bfloat16)
    found = selected(plain[...], select)
    for comp in range(4):
        for group in range(groups):
            dealt[comp, group] = found[comp * tall : (comp + 1) * tall, group * LANES : (group + 1) * LANES]
    count = tall // 8
    for comp in range(4):
        for row in range(count):
            for group in range(groups):
                field_ref[comp, row, group] = dealt[comp, group, pl.ds(row, 8, stride=count), :]

    def store(row, col, parts):
        for comp in range(4):
            change_ref[comp, row, col] = parts[comp]

    changes(field_ref, diff, count, groups, store)


def steps_kernel(field_ref, change_ref, own_ref, far_ref, out_ref, field, mid, diff, dealt):
    rows, cols = out_ref.shape[1:]
    tall = rows + 2 * HALO
    groups = field_ref.shape[2]
    factor = -0.5 * COURANT / jnp.maximum(own_ref[...], far_ref[...])
    half_factor = 0.5 * factor

    for index in range(STEPS):
        start = 4 * index
        count = (tall - 8 * index) // 8
        old = field_ref if index == 0 else field

        def to_mid(row, col, parts):
            for comp in range(4):
                mid[comp, row, col] = old[comp, row, col] + factor * parts[comp]

        def to_field(row, col, parts):
            for comp in range(4):
                mean = 0.5 * (old[comp, row, col] + mid[comp, row, col])
                dealt[comp, col, pl.ds(start + row, 8, stride=count), :] = mean + half_factor * parts[comp]

        if index == 0:
            for row in range(count):
                for col in range(groups):
                    to_mid(row, col, [change_ref[comp, row, col] for comp in range(4)])
        else:
            for comp in range(4):
                for row in range(count):
                    for col in range(groups):
                        field[comp, row, col] = dealt[comp, col, pl.ds(start + row, 8, stride=count), :]
            changes(field, diff, count, groups, to_mid)
        changes(mid, diff, count, groups, to_field)

    wide = groups * LANES
    source = iota((wide, cols), 0)
    goal = iota((wide, cols), 1)
    select = jnp.where(groups * (source % LANES) + source // LANES == goal + HALO, 1.0, 0.0).astype(jnp.bfloat16)
    lane = iota((rows, LANES), 1)
    parts = []
    for comp in range(4):
        line = []
        for group in range(groups):
            place = groups * lane + group
            inside = (place >= HALO) & (place < HALO + cols)
            line.append(jnp.where(inside, dealt[comp, group, HALO : HALO + rows, :], 0.0))
        parts.append(jnp.concatenate(line, axis=1))
    found = selected(jnp.concatenate(parts, axis=0), select)
    for comp in range(4):
        out_ref[comp] = found[comp * rows : (comp + 1) * rows, :]


def local(state):
    parts, rows, cols = state.shape
    tall = rows + 2 * HALO
    groups = -(-(cols + 2 * HALO) // LANES)

    def sent(value, axis, by):
        count = lax.axis_size(axis)
        return lax.ppermute(value, axis, [(i, (i + by) % count) for i in range(count)])

    edge_type = array(parts * HALO + 8, cols)
    head, tail, top = pl.pallas_call(
        edge_kernel,
        out_shape=(edge_type, edge_type, array(8, LANES)),
        in_specs=[VMEM],
        out_specs=(VMEM,) * 3,
        compiler_params=params(4),
        name="edge",
    )(state)
    up = sent(tail, "gx", 1)
    down = sent(head, "gx", -1)
    far = sent(top, "gx", 2)
    side_type = array(tall // 2 + 8, LANES)
    left, right, top = pl.pallas_call(
        pack_kernel,
        out_shape=(side_type, side_type, array(8, LANES)),
        in_specs=[VMEM] * 5,
        out_specs=(VMEM,) * 3,
        compiler_params=params(4),
        name="pack",
    )(state, up, down, top, far)
    before = sent(right, "gy", 1)
    after = sent(left, "gy", -1)
    far = sent(top, "gy", 2)
    top = jnp.maximum(jnp.maximum(top, far), jnp.maximum(before[tall // 2 :], after[tall // 2 :]))
    for axis in ("gy", "gx"):
        covered = 4
        while covered < lax.axis_size(axis):
            far = sent(top, axis, covered)
            covered *= 2
            last = axis == "gx" and covered >= lax.axis_size(axis)
            if not last:
                top = jnp.maximum(top, far)
    dealt_type = array(parts, tall // 8, groups, 8, LANES)
    dealt = pltpu.VMEM(dealt_type.shape, jnp.float32)
    plain = pltpu.VMEM((parts, groups, tall, LANES), jnp.float32)
    field, change = pl.pallas_call(
        first_kernel,
        out_shape=(dealt_type, dealt_type),
        in_specs=[VMEM] * 5,
        out_specs=(VMEM,) * 2,
        scratch_shapes=[pltpu.VMEM((parts * tall, groups * LANES), jnp.float32), plain, dealt],
        compiler_params=params(16),
        cost_estimate=pl.CostEstimate(flops=20_000_000, bytes_accessed=2_000_000, transcendentals=400_000),
        name="first",
    )(state, up, down, before, after)
    return pl.pallas_call(
        steps_kernel,
        out_shape=array(parts, rows, cols),
        in_specs=[VMEM] * 4,
        out_specs=VMEM,
        scratch_shapes=[dealt, dealt, dealt, plain],
        compiler_params=params(16),
        name="steps",
    )(field, change, top, far)


def solution(mesh):
    in_specs = (P(None, "gx", "gy"),)
    out_specs = P(None, "gx", "gy")
    return jax.shard_map(local, mesh=mesh, in_specs=in_specs, out_specs=out_specs, check_vma=False)
```

time: 91.4 us -> 27.2 us (0.30)
  blocking collectives: 65 us -> 0 us
  Pallas kernels: 13.7 us -> 6.83 us
  starting transfers between devices: 7.26 us -> 11.7 us
  waiting for transfers between devices: 4.43 us -> 7.54 us
    all_gather x1 -> x0, blocking collectives: 65 us -> none  [local(): top = lax.all_gather(top, ('gx', 'gy'))]
    pallas_call x3 -> x4, Pallas kernels: 13.7 us -> 6.83 us  [the longest x1 5.28 us: local(): pl.pallas_call(steps_kernel, out_shape=array(parts, rows, cols), in_specs...]
    ppermute x4 -> x7, starting transfers between devices: 7.26 us -> 11.7 us  [sent(): lax.ppermute(value, axis, [(i, (i + by) % count) for i in range(count)])]
    ppermute x4 -> x7, waiting for transfers between devices: 4.43 us -> 7.54 us  [sent(): lax.ppermute(value, axis, [(i, (i + by) % count) for i in range(count)])]
    slice x1 -> x0, local copies, waits for them, and re-layouts: 0.92 us -> none  [local(): down = lax.ppermute(state[:, :HALO, :], 'gx', back(count_x))]
  transfers between devices with their start and end apart: 4 -> 7, of which waited for: 2 -> 3; matrix products, arithmetic and copies ran while one was open for 0% -> 0% of each run, Pallas kernels for 0% -> 5%
where the time goes in v1:
time: 27.2 us; the launch traced here: 27 us
  starting transfers between devices  11.7 us (43%)
  waiting for transfers between devices  7.54 us (28%)
  Pallas kernels  6.83 us (25%)
  local copies, waits for them, and re-layouts  0.91 us (3%)
    ppermute x7, starting transfers between devices, sent(): lax.ppermute(value, axis, [(i, (i + by) % count) for i in range(count)])  11.7 us
    ppermute x7, waiting for transfers between devices, sent(): lax.ppermute(value, axis, [(i, (i + by) % count) for i in range(count)])  7.54 us
    pallas_call x1, Pallas kernels, local(): pl.pallas_call(steps_kernel, out_shape=array(parts, rows, cols), in_specs...  5.28 us
    pallas_call x1, Pallas kernels, local(): pl.pallas_call(first_kernel, out_shape=(dealt_type, dealt_type), in_specs...  1.28 us
    unnamed x4, local copies, waits for them, and re-layouts  0.91 us
  transfers between devices with their start and end apart: 7, of which 3 were waited for; matrix products, arithmetic and copies ran while one was open for 0% of the time, Pallas kernels for 5%

profile of v1, /device:TPU:0, one launch (start us, length us, event | category | flops | bytes accessed | tf_op | source)
XLA Modules:
  0.0 27.0 jit_solution(12099860087419914685)
XLA Ops:
  0.0 0.0 copy-start
  0.0 0.9 %copy-done = f32[4,32,256]{2,1,0:T(8,128)S(1)} copy-done((f32[4,32,256]{2,1,0:T(8,128)S(1)}, f32[4,32,256]{2,1,0:T(8,128)}, u32[]{:S(2)}) %copy-start) | copy-done | bytes 131096
  0.9 0.1 edge.1
  1.1 0.5 %collective-permute-start = (f32[72,256]{1,0:T(8,128)S(1)}, f32[72,256]{1,0:T(8,128)S(1)}, u32[]{:S(2)}, u32[]{:S(2)}) collective-permute-start(f32[72,256]{1,0:T(8,128)S(1)} %get-tuple-element.13), channel_id=1, source_target_pairs={{0,4},{4,8},{8,12},{12,16},{16,20},{20,24},{24,28},{28,0},{1,5},{5... | collective-permute-start | bytes 221192 | tf_op jit(solution)/shard_map/ppermute | solution.py:269
  1.6 2.9 %collective-permute-start.1 = (f32[72,256]{1,0:T(8,128)S(1)}, f32[72,256]{1,0:T(8,128)S(1)}, u32[]{:S(2)}, u32[]{:S(2)}) collective-permute-start(f32[72,256]{1,0:T(8,128)S(1)} %get-tuple-element.14), channel_id=1, source_target_pairs={{0,28},{4,0},{8,4},{12,8},{16,12},{20,16},{24,20},{28,24},{1,29},{... | collective-permute-start | bytes 221192 | tf_op jit(solution)/shard_map/ppermute | solution.py:269
  4.5 0.0 copy-start.1
  4.5 1.3 %collective-permute-start.2 = (f32[8,128]{1,0:T(8,128)S(1)}, f32[8,128]{1,0:T(8,128)S(1)}, u32[]{:S(2)}, u32[]{:S(2)}) collective-permute-start(f32[8,128]{1,0:T(8,128)S(1)} %get-tuple-element.15.own_ref), channel_id=1, source_target_pairs={{0,8},{4,12},{8,16},{12,20},{16,24},{20,28},{24,0},{28,4},{1,9},{5... | collective-permute-start | bytes 12296 | tf_op jit(solution)/shard_map/ppermute | solution.py:269
  5.8 3.3 %collective-permute-done.2.far_ref = f32[8,128]{1,0:T(8,128)S(1)} collective-permute-done((f32[8,128]{1,0:T(8,128)S(1)}, f32[8,128]{1,0:T(8,128)S(1)}, u32[]{:S(2)}, u32[]{:S(2)}) %collective-permute-start.2) | collective-permute-done | bytes 4128 | tf_op jit(solution)/shard_map/ppermute | solution.py:269
  9.1 0.0 collective-permute-done.up_ref
  9.1 0.0 collective-permute-done.1.down_ref
  9.1 0.1 pack.1
  9.3 2.2 %collective-permute-start.3 = (f32[40,128]{1,0:T(8,128)S(1)}, f32[40,128]{1,0:T(8,128)S(1)}, u32[]{:S(2)}, u32[]{:S(2)}) collective-permute-start(f32[40,128]{1,0:T(8,128)S(1)} %get-tuple-element.16), channel_id=1, source_target_pairs={{0,1},{1,2},{2,3},{3,0},{4,5},{5,6},{6,7},{7,4},{8,9},{9,10},{10,1... | collective-permute-start | bytes 61448 | tf_op jit(solution)/shard_map/ppermute | solution.py:269
  11.5 2.1 %collective-permute-start.4 = (f32[40,128]{1,0:T(8,128)S(1)}, f32[40,128]{1,0:T(8,128)S(1)}, u32[]{:S(2)}, u32[]{:S(2)}) collective-permute-start(f32[40,128]{1,0:T(8,128)S(1)} %get-tuple-element.17), channel_id=1, source_target_pairs={{0,3},{1,0},{2,1},{3,2},{4,7},{5,4},{6,5},{7,6},{8,11},{9,8},{10,9... | collective-permute-start | bytes 61448 | tf_op jit(solution)/shard_map/ppermute | solution.py:269
  13.6 0.9 %collective-permute-start.5 = (f32[8,128]{1,0:T(8,128)S(1)}, f32[8,128]{1,0:T(8,128)S(1)}, u32[]{:S(2)}, u32[]{:S(2)}) collective-permute-start(f32[8,128]{1,0:T(8,128)S(1)} %get-tuple-element.20), channel_id=1, source_target_pairs={{0,2},{1,3},{2,0},{3,1},{4,6},{5,7},{6,4},{7,5},{8,10},{9,11},{10,... | collective-permute-start | bytes 12296 | tf_op jit(solution)/shard_map/ppermute | solution.py:269
  14.5 3.6 %collective-permute-done.5 = f32[8,128]{1,0:T(8,128)S(1)} collective-permute-done((f32[8,128]{1,0:T(8,128)S(1)}, f32[8,128]{1,0:T(8,128)S(1)}, u32[]{:S(2)}, u32[]{:S(2)}) %collective-permute-start.5) | collective-permute-done | bytes 4128 | tf_op jit(solution)/shard_map/ppermute | solution.py:269
  18.1 0.0 collective-permute-done.3.before_ref
  18.1 0.0 collective-permute-done.4.after_ref
  18.1 1.7 %collective-permute-start.6 = (f32[8,128]{1,0:T(8,128)S(1)}, f32[8,128]{1,0:T(8,128)S(1)}, u32[]{:S(2)}, u32[]{:S(2)}) collective-permute-start(f32[8,128]{1,0:T(8,128)S(1)} %fusion.own_ref), channel_id=1, source_target_pairs={{0,16},{4,20},{8,24},{12,28},{16,0},{20,4},{24,8},{28,12},{1,17},{... | collective-permute-start | bytes 12296 | tf_op jit(solution)/shard_map/ppermute | solution.py:269
  19.8 0.0 copy-done.1
  19.8 1.3 %first.1 = (f32[4,8,3,8,128]{4,3,2,1,0:T(8,128)S(1)}, f32[4,8,3,8,128]{4,3,2,1,0:T(8,128)S(1)}) custom-call(f32[4,32,256]{2,1,0:T(8,128)S(1)} %copy-done.1, f32[72,256]{1,0:T(8,128)S(1)} %collective-permute-done.up_ref, f32[72,256]{1,0:T(8,128)S(1)} %collective-permute-done.1.down_ref, f32[40,128]{1,0:T(8,128)S(1)} %collective-permute-done.3.before_ref, ...), custom_call_target="tpu_custom_call" | custom-call | flops 20000000 | bytes 2000000 | tf_op jit(solution)/shard_map/first/pallas_call | solution.py:307
  21.1 0.6 %collective-permute-done.6.far_ref = f32[8,128]{1,0:T(8,128)S(1)} collective-permute-done((f32[8,128]{1,0:T(8,128)S(1)}, f32[8,128]{1,0:T(8,128)S(1)}, u32[]{:S(2)}, u32[]{:S(2)}) %collective-permute-start.6) | collective-permute-done | bytes 4128 | tf_op jit(solution)/shard_map/ppermute | solution.py:269
  21.8 5.3 %steps.1 = f32[4,32,256]{2,1,0:T(8,128)} custom-call(f32[4,8,3,8,128]{4,3,2,1,0:T(8,128)S(1)} %get-tuple-element.18.field_ref, f32[4,8,3,8,128]{4,3,2,1,0:T(8,128)S(1)} %get-tuple-element.19.change_ref, f32[8,128]{1,0:T(8,128)S(1)} %fusion.own_ref, f32[8,128]{1,0:T(8,128)S(1)} %collective-permute-done.6.far_ref), custom_call_target="tpu_custom_call" | custom-call | tf_op jit(solution)/shard_map/steps/pallas_call | solution.py:317
  (1 shorter events, 0.0 us)
Async XLA Ops:
  0.0 0.9 %copy-start = (f32[4,32,256]{2,1,0:T(8,128)S(1)}, f32[4,32,256]{2,1,0:T(8,128)}, u32[]{:S(2)}) copy-start(f32[4,32,256]{2,1,0:T(8,128)} %state_ref.5) | copy-start | bytes 393220
  1.1 8.1 %collective-permute-start = (f32[72,256]{1,0:T(8,128)S(1)}, f32[72,256]{1,0:T(8,128)S(1)}, u32[]{:S(2)}, u32[]{:S(2)}) collective-permute-start(f32[72,256]{1,0:T(8,128)S(1)} %get-tuple-element.13), channel_id=1, source_target_pairs={{0,4},{4,8},{8,12},{12,16},{16,20},{20,24},{24,28},{28,0},{1,5},{5... | collective-permute-start | bytes 221192 | tf_op jit(solution)/shard_map/ppermute | solution.py:269
  1.6 7.6 %collective-permute-start.1 = (f32[72,256]{1,0:T(8,128)S(1)}, f32[72,256]{1,0:T(8,128)S(1)}, u32[]{:S(2)}, u32[]{:S(2)}) collective-permute-start(f32[72,256]{1,0:T(8,128)S(1)} %get-tuple-element.14), channel_id=1, source_target_pairs={{0,28},{4,0},{8,4},{12,8},{16,12},{20,16},{24,20},{28,24},{1,29},{... | collective-permute-start | bytes 221192 | tf_op jit(solution)/shard_map/ppermute | solution.py:269
  4.5 15.3 %copy-start.1 = (f32[4,32,256]{2,1,0:T(8,128)S(1)}, f32[4,32,256]{2,1,0:T(8,128)}, u32[]{:S(2)}) copy-start(f32[4,32,256]{2,1,0:T(8,128)} %state_ref.5) | copy-start | bytes 393220
  4.5 4.6 %collective-permute-start.2 = (f32[8,128]{1,0:T(8,128)S(1)}, f32[8,128]{1,0:T(8,128)S(1)}, u32[]{:S(2)}, u32[]{:S(2)}) collective-permute-start(f32[8,128]{1,0:T(8,128)S(1)} %get-tuple-element.15.own_ref), channel_id=1, source_target_pairs={{0,8},{4,12},{8,16},{12,20},{16,24},{20,28},{24,0},{28,4},{1,9},{5... | collective-permute-start | bytes 12296 | tf_op jit(solution)/shard_map/ppermute | solution.py:269
  9.3 8.8 %collective-permute-start.3 = (f32[40,128]{1,0:T(8,128)S(1)}, f32[40,128]{1,0:T(8,128)S(1)}, u32[]{:S(2)}, u32[]{:S(2)}) collective-permute-start(f32[40,128]{1,0:T(8,128)S(1)} %get-tuple-element.16), channel_id=1, source_target_pairs={{0,1},{1,2},{2,3},{3,0},{4,5},{5,6},{6,7},{7,4},{8,9},{9,10},{10,1... | collective-permute-start | bytes 61448 | tf_op jit(solution)/shard_map/ppermute | solution.py:269
  11.5 6.6 %collective-permute-start.4 = (f32[40,128]{1,0:T(8,128)S(1)}, f32[40,128]{1,0:T(8,128)S(1)}, u32[]{:S(2)}, u32[]{:S(2)}) collective-permute-start(f32[40,128]{1,0:T(8,128)S(1)} %get-tuple-element.17), channel_id=1, source_target_pairs={{0,3},{1,0},{2,1},{3,2},{4,7},{5,4},{6,5},{7,6},{8,11},{9,8},{10,9... | collective-permute-start | bytes 61448 | tf_op jit(solution)/shard_map/ppermute | solution.py:269
  13.6 4.5 %collective-permute-start.5 = (f32[8,128]{1,0:T(8,128)S(1)}, f32[8,128]{1,0:T(8,128)S(1)}, u32[]{:S(2)}, u32[]{:S(2)}) collective-permute-start(f32[8,128]{1,0:T(8,128)S(1)} %get-tuple-element.20), channel_id=1, source_target_pairs={{0,2},{1,3},{2,0},{3,1},{4,6},{5,7},{6,4},{7,5},{8,10},{9,11},{10,... | collective-permute-start | bytes 12296 | tf_op jit(solution)/shard_map/ppermute | solution.py:269
  18.1 3.7 %collective-permute-start.6 = (f32[8,128]{1,0:T(8,128)S(1)}, f32[8,128]{1,0:T(8,128)S(1)}, u32[]{:S(2)}, u32[]{:S(2)}) collective-permute-start(f32[8,128]{1,0:T(8,128)S(1)} %fusion.own_ref), channel_id=1, source_target_pairs={{0,16},{4,20},{8,24},{12,28},{16,0},{20,4},{24,8},{28,12},{1,17},{... | collective-permute-start | bytes 12296 | tf_op jit(solution)/shard_map/ppermute | solution.py:269

commit v2 on v1

--- a/solution.py
+++ b/solution.py
@@ -29,26 +29,48 @@
     return lax.broadcasted_iota(jnp.int32, shape, dim)
 
 
-def edge_kernel(state_ref, head_ref, tail_ref, top_ref):
+def odd(axis):
+    return lax.rem(lax.axis_index(axis), 2) == 1
+
+
+def edge_kernel(state_ref, block_ref, first_ref, second_ref, top_ref, sems):
     rows = state_ref.shape[1]
-    density, mom_x, mom_y, energy = (state_ref[comp] for comp in range(4))
+    copies = [
+        pltpu.make_async_copy(
+            state_ref.at[comp, pl.ds(low, rows // 2)], block_ref.at[comp, pl.ds(low, rows // 2)], sems.at[comp, side]
+        )
+        for comp in range(4)
+        for side, low in enumerate((0, rows // 2))
+    ]
+    for copy in copies:
+        copy.start()
+    for copy in copies:
+        copy.wait()
+    density, mom_x, mom_y, energy = (block_ref[comp] for comp in range(4))
     inv = 1.0 / density
     pressure = (GAMMA - 1.0) * (energy - 0.5 * (mom_x * mom_x + mom_y * mom_y) * inv)
     speed = jnp.maximum(jnp.abs(mom_x * inv), jnp.abs(mom_y * inv)) + jnp.sqrt(GAMMA * pressure * inv)
     top = jnp.max(speed)
-    for comp in range(4):
-        head_ref[comp * HALO : (comp + 1) * HALO, :] = state_ref[comp, 0:HALO, :]
-        tail_ref[comp * HALO : (comp + 1) * HALO, :] = state_ref[comp, rows - HALO : rows, :]
-    head_ref[4 * HALO :, :] = jnp.full((8, head_ref.shape[1]), top)
-    tail_ref[4 * HALO :, :] = jnp.full((8, tail_ref.shape[1]), top)
+    is_odd = odd("gx")
+    for comp in range(4):
+        span = slice(comp * HALO, (comp + 1) * HALO)
+        head = block_ref[comp, 0:HALO, :]
+        tail = block_ref[comp, rows - HALO : rows, :]
+        first_ref[span, :] = jnp.where(is_odd, head, tail)
+        second_ref[span, :] = jnp.where(is_odd, tail, head)
+    first_ref[4 * HALO :, :] = jnp.full((8, first_ref.shape[1]), top)
+    second_ref[4 * HALO :, :] = jnp.full((8, second_ref.shape[1]), top)
     top_ref[...] = jnp.full(top_ref.shape, top)
 
 
-def pack_kernel(state_ref, up_ref, down_ref, own_ref, far_ref, left_ref, right_ref, top_ref):
+def pack_kernel(state_ref, swap_ref, next_ref, own_ref, far_ref, up_ref, down_ref, first_ref, second_ref, top_ref):
     rows = state_ref.shape[1]
     cols = state_ref.shape[2]
     half = rows // 2 + HALO
     lane = iota((half, LANES), 1)
+    is_odd = odd("gx")
+    up_ref[...] = jnp.where(is_odd, swap_ref[...], next_ref[...])
+    down_ref[...] = jnp.where(is_odd, next_ref[...], swap_ref[...])
     top = jnp.maximum(jnp.maximum(own_ref[...], far_ref[...]),
                       jnp.maximum(up_ref[4 * HALO :, 0:LANES], down_ref[4 * HALO :, 0:LANES]))
 
@@ -67,10 +89,13 @@
                 total = jnp.where((lane >= goal) & (lane < goal + HALO), moved, total)
         return total
 
-    left_ref[0:half, :] = edge(0, 0)
-    right_ref[0:half, :] = edge(cols - LANES, LANES - HALO)
-    left_ref[half:, :] = top
-    right_ref[half:, :] = top
+    left = edge(0, 0)
+    right = edge(cols - LANES, LANES - HALO)
+    is_odd = odd("gy")
+    first_ref[0:half, :] = jnp.where(is_odd, left, right)
+    second_ref[0:half, :] = jnp.where(is_odd, right, left)
+    first_ref[half:, :] = top
+    second_ref[half:, :] = top
     top_ref[...] = top
 
 
@@ -164,7 +189,7 @@
         sweep(lambda col, row=row: [src[comp, row, col] for comp in Y_ORDER], add, cols, 1)
 
 
-def first_kernel(state_ref, up_ref, down_ref, before_ref, after_ref, field_ref, change_ref, plain, dealt, diff):
+def first_kernel(state_ref, up_ref, down_ref, swap_ref, next_ref, field_ref, change_ref, plain, dealt, diff):
     rows, cols = state_ref.shape[1:]
     tall = rows + 2 * HALO
     half = tall // 2
@@ -177,8 +202,11 @@
         plain[low + HALO : low + HALO + rows, 0:cols] = state_ref[comp]
         plain[low + HALO + rows : low + tall, 0:cols] = down_ref[span, :]
     lane = iota((half, LANES), 1)
-    from_before = before_ref[0:half, :]
-    from_after = after_ref[0:half, :]
+    is_odd = odd("gy")
+    from_swap = swap_ref[0:half, :]
+    from_next = next_ref[0:half, :]
+    from_before = jnp.where(is_odd, from_swap, from_next)
+    from_after = jnp.where(is_odd, from_next, from_swap)
     for side in range(2):
         for comp in range(4):
             at = side * (LANES // 2) + comp * HALO
@@ -212,7 +240,7 @@
     rows, cols = out_ref.shape[1:]
     tall = rows + 2 * HALO
     groups = field_ref.shape[2]
-    factor = -0.5 * COURANT / jnp.maximum(own_ref[...], far_ref[...])
+    factor = -0.5 * COURANT / jnp.where(odd("gx"), own_ref[...], far_ref[...])
     half_factor = 0.5 * factor
 
     for index in range(STEPS):
@@ -264,43 +292,58 @@
     tall = rows + 2 * HALO
     groups = -(-(cols + 2 * HALO) // LANES)
 
-    def sent(value, axis, by):
+    def sent(value, axis, by, odd_x=False):
         count = lax.axis_size(axis)
-        return lax.ppermute(value, axis, [(i, (i + by) % count) for i in range(count)])
+        if not odd_x:
+            return lax.ppermute(value, axis, [(i, (i + by) % count) for i in range(count)])
+        count_x, count_y = lax.axis_size("gx"), lax.axis_size("gy")
+        pairs = []
+        for x in range(1, count_x, 2):
+            for y in range(count_y):
+                goal = ((x + by) % count_x, y) if axis == "gx" else (x, (y + by) % count_y)
+                pairs.append((x * count_y + y, goal[0] * count_y + goal[1]))
+        return lax.ppermute(value, ("gx", "gy"), pairs)
+
+    def swapped_pairs(value, axis, first):
+        count = lax.axis_size(axis)
+        pairs = []
+        for low in range(first, count, 2):
+            high = (low + 1) % count
+            pairs += [(low, high), (high, low)]
+        return lax.ppermute(value, axis, pairs)
 
     edge_type = array(parts * HALO + 8, cols)
-    head, tail, top = pl.pallas_call(
+    block, first, second, top = pl.pallas_call(
         edge_kernel,
-        out_shape=(edge_type, edge_type, array(8, LANES)),
-        in_specs=[VMEM],
-        out_specs=(VMEM,) * 3,
+        out_shape=(array(parts, rows, cols), edge_type, edge_type, array(8, LANES)),
+        in_specs=[pl.BlockSpec(memory_space=pltpu.HBM)],
+        out_specs=(VMEM,) * 4,
+        scratch_shapes=[pltpu.SemaphoreType.DMA((4, 2))],
         compiler_params=params(4),
         name="edge",
     )(state)
-    up = sent(tail, "gx", 1)
-    down = sent(head, "gx", -1)
-    far = sent(top, "gx", 2)
+    first = swapped_pairs(first, "gx", 0)
+    second = swapped_pairs(second, "gx", 1)
+    far = sent(top, "gx", 2, odd_x=True)
     side_type = array(tall // 2 + 8, LANES)
-    left, right, top = pl.pallas_call(
+    up, down, first, second, top = pl.pallas_call(
         pack_kernel,
-        out_shape=(side_type, side_type, array(8, LANES)),
+        out_shape=(edge_type, edge_type, side_type, side_type, array(8, LANES)),
         in_specs=[VMEM] * 5,
-        out_specs=(VMEM,) * 3,
+        out_specs=(VMEM,) * 5,
         compiler_params=params(4),
         name="pack",
-    )(state, up, down, top, far)
-    before = sent(right, "gy", 1)
-    after = sent(left, "gy", -1)
-    far = sent(top, "gy", 2)
-    top = jnp.maximum(jnp.maximum(top, far), jnp.maximum(before[tall // 2 :], after[tall // 2 :]))
+    )(block, first, second, top, far)
+    first = swapped_pairs(first, "gy", 0)
+    second = swapped_pairs(second, "gy", 1)
+    far = sent(top, "gy", 2, odd_x=True)
+    top = jnp.maximum(jnp.maximum(top, far), jnp.maximum(first[tall // 2 :], second[tall // 2 :]))
     for axis in ("gy", "gx"):
         covered = 4
         while covered < lax.axis_size(axis):
-            far = sent(top, axis, covered)
+            top = jnp.maximum(top, sent(top, axis, covered, odd_x=True))
             covered *= 2
-            last = axis == "gx" and covered >= lax.axis_size(axis)
-            if not last:
-                top = jnp.maximum(top, far)
+    far = lax.ppermute(top, "gx", [(i, i - 1) for i in range(1, lax.axis_size("gx"), 2)])
     dealt_type = array(parts, tall // 8, groups, 8, LANES)
     dealt = pltpu.VMEM(dealt_type.shape, jnp.float32)
     plain = pltpu.VMEM((parts, groups, tall, LANES), jnp.float32)
@@ -313,7 +356,7 @@
         compiler_params=params(16),
         cost_estimate=pl.CostEstimate(flops=20_000_000, bytes_accessed=2_000_000, transcendentals=400_000),
         name="first",
-    )(state, up, down, before, after)
+    )(block, up, down, first, second)
     return pl.pallas_call(
         steps_kernel,
         out_shape=array(parts, rows, cols),

time: 27.2 us -> 30.6 us (1.12)
  waiting for transfers between devices: 7.54 us -> 10.4 us
    ppermute x7 -> x8, waiting for transfers between devices: 7.54 us -> 10.4 us  [the longest x1 6.6 us: local(): lax.ppermute(top, 'gx', [(i, i - 1) for i in range(1, lax.axis_size('gx')...]
    ppermute x7 -> x8, starting transfers between devices: 11.7 us -> 11.8 us  [the longest x4 8.52 us: swapped_pairs(): return lax.ppermute(value, axis, pairs)]
    unnamed x4 -> x2, local copies, waits for them, and re-layouts: 0.91 us -> 0.9 us
  transfers between devices with their start and end apart: 7 -> 8, of which waited for: 3 -> 3; matrix products, arithmetic and copies ran while one was open for 0% -> 0% of each run, Pallas kernels for 5% -> 4%
where the time goes in v2:
time: 30.6 us; the launch traced here: 30.2 us
  starting transfers between devices  11.8 us (39%)
  waiting for transfers between devices  10.4 us (34%)
  Pallas kernels  7.04 us (23%)
  local copies, waits for them, and re-layouts  0.9 us (3%)
    ppermute x4, starting transfers between devices, swapped_pairs(): return lax.ppermute(value, axis, pairs)  8.52 us
    ppermute x1, waiting for transfers between devices, local(): lax.ppermute(top, 'gx', [(i, i - 1) for i in range(1, lax.axis_size('gx')...  6.6 us
    pallas_call x1, Pallas kernels, local(): pl.pallas_call(steps_kernel, out_shape=array(parts, rows, cols), in_specs...  5.27 us
    ppermute x4, waiting for transfers between devices, swapped_pairs(): return lax.ppermute(value, axis, pairs)  3.81 us
    ppermute x3, starting transfers between devices, sent(): return lax.ppermute(value, ('gx', 'gy'), pairs)  1.95 us
    ppermute x1, starting transfers between devices, local(): lax.ppermute(top, 'gx', [(i, i - 1) for i in range(1, lax.axis_size('gx')...  1.29 us
    pallas_call x1, Pallas kernels, local(): pl.pallas_call(first_kernel, out_shape=(dealt_type, dealt_type), in_specs...  1.26 us
    unnamed x2, local copies, waits for them, and re-layouts  0.9 us
  transfers between devices with their start and end apart: 8, of which 3 were waited for; matrix products, arithmetic and copies ran while one was open for 0% of the time, Pallas kernels for 4%

profile of v2, /device:TPU:0, one launch (start us, length us, event | category | flops | bytes accessed | tf_op | source)
XLA Modules:
  0.0 30.2 jit_solution(10312036174359273030)
XLA Ops:
  0.0 0.0 copy-start
  0.0 0.9 %copy-done = f32[4,32,256]{2,1,0:T(8,128)S(1)} copy-done((f32[4,32,256]{2,1,0:T(8,128)S(1)}, f32[4,32,256]{2,1,0:T(8,128)}, u32[]{:S(2)}) %copy-start) | copy-done | bytes 131096
  0.9 0.4 %edge.1 = (f32[4,32,256]{2,1,0:T(8,128)S(1)}, f32[72,256]{1,0:T(8,128)S(1)}, f32[72,256]{1,0:T(8,128)S(1)}, f32[8,128]{1,0:T(8,128)S(1)}) custom-call(f32[4,32,256]{2,1,0:T(8,128)S(1)} %copy-done), custom_call_target="tpu_custom_call" | custom-call | tf_op jit(solution)/shard_map/edge/pallas_call | solution.py:316
  1.3 0.5 %collective-permute-start = (f32[72,256]{1,0:T(8,128)S(1)}, f32[72,256]{1,0:T(8,128)S(1)}, u32[]{:S(2)}, u32[]{:S(2)}) collective-permute-start(f32[72,256]{1,0:T(8,128)S(1)} %get-tuple-element.17), channel_id=1, source_target_pairs={{0,4},{4,0},{8,12},{12,8},{16,20},{20,16},{24,28},{28,24},{1,5},{5... | collective-permute-start | bytes 221192 | tf_op jit(solution)/shard_map/ppermute | solution.py:313
  1.8 3.6 %collective-permute-start.1 = (f32[72,256]{1,0:T(8,128)S(1)}, f32[72,256]{1,0:T(8,128)S(1)}, u32[]{:S(2)}, u32[]{:S(2)}) collective-permute-start(f32[72,256]{1,0:T(8,128)S(1)} %get-tuple-element.18), channel_id=1, source_target_pairs={{4,8},{8,4},{12,16},{16,12},{20,24},{24,20},{28,0},{0,28},{5,9},{9... | collective-permute-start | bytes 221192 | tf_op jit(solution)/shard_map/ppermute | solution.py:313
  5.4 0.6 %collective-permute-start.2 = (f32[8,128]{1,0:T(8,128)S(1)}, f32[8,128]{1,0:T(8,128)S(1)}, u32[]{:S(2)}, u32[]{:S(2)}) collective-permute-start(f32[8,128]{1,0:T(8,128)S(1)} %get-tuple-element.19.own_ref), channel_id=1, source_target_pairs={{4,12},{5,13},{6,14},{7,15},{12,20},{13,21},{14,22},{15,23},{20,28... | collective-permute-start | bytes 12296 | tf_op jit(solution)/shard_map/ppermute | solution.py:305
  6.0 0.0 collective-permute-done.2.far_ref
  6.0 0.0 collective-permute-done.swap_ref
  6.0 1.4 %collective-permute-done.1.next_ref = f32[72,256]{1,0:T(8,128)S(1)} collective-permute-done((f32[72,256]{1,0:T(8,128)S(1)}, f32[72,256]{1,0:T(8,128)S(1)}, u32[]{:S(2)}, u32[]{:S(2)}) %collective-permute-start.1) | collective-permute-done | bytes 73760 | tf_op jit(solution)/shard_map/ppermute | solution.py:313
  7.4 0.1 pack.1
  7.5 2.0 %collective-permute-start.3 = (f32[40,128]{1,0:T(8,128)S(1)}, f32[40,128]{1,0:T(8,128)S(1)}, u32[]{:S(2)}, u32[]{:S(2)}) collective-permute-start(f32[40,128]{1,0:T(8,128)S(1)} %get-tuple-element.22), channel_id=1, source_target_pairs={{0,1},{1,0},{2,3},{3,2},{4,5},{5,4},{6,7},{7,6},{8,9},{9,8},{10,11... | collective-permute-start | bytes 61448 | tf_op jit(solution)/shard_map/ppermute | solution.py:313
  9.5 2.5 %collective-permute-start.4 = (f32[40,128]{1,0:T(8,128)S(1)}, f32[40,128]{1,0:T(8,128)S(1)}, u32[]{:S(2)}, u32[]{:S(2)}) collective-permute-start(f32[40,128]{1,0:T(8,128)S(1)} %get-tuple-element.23), channel_id=1, source_target_pairs={{1,2},{2,1},{3,0},{0,3},{5,6},{6,5},{7,4},{4,7},{9,10},{10,9},{11,... | collective-permute-start | bytes 61448 | tf_op jit(solution)/shard_map/ppermute | solution.py:313
  12.0 0.6 %collective-permute-start.5 = (f32[8,128]{1,0:T(8,128)S(1)}, f32[8,128]{1,0:T(8,128)S(1)}, u32[]{:S(2)}, u32[]{:S(2)}) collective-permute-start(f32[8,128]{1,0:T(8,128)S(1)} %get-tuple-element.26), channel_id=1, source_target_pairs={{4,6},{5,7},{6,4},{7,5},{12,14},{13,15},{14,12},{15,13},{20,22},{2... | collective-permute-start | bytes 12296 | tf_op jit(solution)/shard_map/ppermute | solution.py:305
  12.6 0.0 collective-permute-done.5
  12.7 0.0 collective-permute-done.3.swap_ref
  12.7 2.5 %collective-permute-done.4.next_ref = f32[40,128]{1,0:T(8,128)S(1)} collective-permute-done((f32[40,128]{1,0:T(8,128)S(1)}, f32[40,128]{1,0:T(8,128)S(1)}, u32[]{:S(2)}, u32[]{:S(2)}) %collective-permute-start.4) | collective-permute-done | bytes 20512 | tf_op jit(solution)/shard_map/ppermute | solution.py:313
  15.1 0.7 %collective-permute-start.6 = (f32[8,128]{1,0:T(8,128)S(1)}, f32[8,128]{1,0:T(8,128)S(1)}, u32[]{:S(2)}, u32[]{:S(2)}) collective-permute-start(f32[8,128]{1,0:T(8,128)S(1)} %fusion), channel_id=1, source_target_pairs={{4,20},{5,21},{6,22},{7,23},{12,28},{13,29},{14,30},{15,31},{20,4}... | collective-permute-start | bytes 12296 | tf_op jit(solution)/shard_map/ppermute | solution.py:305
  15.8 0.0 collective-permute-done.6
  15.8 1.3 %collective-permute-start.7 = (f32[8,128]{1,0:T(8,128)S(1)}, f32[8,128]{1,0:T(8,128)S(1)}, u32[]{:S(2)}, u32[]{:S(2)}) collective-permute-start(f32[8,128]{1,0:T(8,128)S(1)} %max.15.own_ref), channel_id=1, source_target_pairs={{4,0},{12,8},{20,16},{28,24},{5,1},{13,9},{21,17},{29,25},{6,2},{1... | collective-permute-start | bytes 12296 | tf_op jit(solution)/shard_map/ppermute | solution.py:346
  17.1 1.3 %first.1 = (f32[4,8,3,8,128]{4,3,2,1,0:T(8,128)S(1)}, f32[4,8,3,8,128]{4,3,2,1,0:T(8,128)S(1)}) custom-call(f32[4,32,256]{2,1,0:T(8,128)S(1)} %get-tuple-element.16.state_ref, f32[72,256]{1,0:T(8,128)S(1)} %get-tuple-element.20.up_ref, f32[72,256]{1,0:T(8,128)S(1)} %get-tuple-element.21.down_ref, f32[40,128]{1,0:T(8,128)S(1)} %collective-permute-done.3.swap_ref, ...), custom_call_target="tpu_custom_call" | custom-call | flops 20000000 | bytes 2000000 | tf_op jit(solution)/shard_map/first/pallas_call | solution.py:350
  18.4 6.6 %collective-permute-done.7.far_ref = f32[8,128]{1,0:T(8,128)S(1)} collective-permute-done((f32[8,128]{1,0:T(8,128)S(1)}, f32[8,128]{1,0:T(8,128)S(1)}, u32[]{:S(2)}, u32[]{:S(2)}) %collective-permute-start.7) | collective-permute-done | bytes 4128 | tf_op jit(solution)/shard_map/ppermute | solution.py:346
  25.0 5.3 %steps.1 = f32[4,32,256]{2,1,0:T(8,128)} custom-call(f32[4,8,3,8,128]{4,3,2,1,0:T(8,128)S(1)} %get-tuple-element.24.field_ref, f32[4,8,3,8,128]{4,3,2,1,0:T(8,128)S(1)} %get-tuple-element.25.change_ref, f32[8,128]{1,0:T(8,128)S(1)} %max.15.own_ref, f32[8,128]{1,0:T(8,128)S(1)} %collective-permute-done.7.far_ref), custom_call_target="tpu_custom_call" | custom-call | tf_op jit(solution)/shard_map/steps/pallas_call | solution.py:360
  (2 shorter events, 0.0 us)
Async XLA Ops:
  0.0 0.9 %copy-start = (f32[4,32,256]{2,1,0:T(8,128)S(1)}, f32[4,32,256]{2,1,0:T(8,128)}, u32[]{:S(2)}) copy-start(f32[4,32,256]{2,1,0:T(8,128)} %state_ref.1) | copy-start | bytes 393220
  1.3 4.7 %collective-permute-start = (f32[72,256]{1,0:T(8,128)S(1)}, f32[72,256]{1,0:T(8,128)S(1)}, u32[]{:S(2)}, u32[]{:S(2)}) collective-permute-start(f32[72,256]{1,0:T(8,128)S(1)} %get-tuple-element.17), channel_id=1, source_target_pairs={{0,4},{4,0},{8,12},{12,8},{16,20},{20,16},{24,28},{28,24},{1,5},{5... | collective-permute-start | bytes 221192 | tf_op jit(solution)/shard_map/ppermute | solution.py:313
  1.8 5.6 %collective-permute-start.1 = (f32[72,256]{1,0:T(8,128)S(1)}, f32[72,256]{1,0:T(8,128)S(1)}, u32[]{:S(2)}, u32[]{:S(2)}) collective-permute-start(f32[72,256]{1,0:T(8,128)S(1)} %get-tuple-element.18), channel_id=1, source_target_pairs={{4,8},{8,4},{12,16},{16,12},{20,24},{24,20},{28,0},{0,28},{5,9},{9... | collective-permute-start | bytes 221192 | tf_op jit(solution)/shard_map/ppermute | solution.py:313
  5.4 0.7 %collective-permute-start.2 = (f32[8,128]{1,0:T(8,128)S(1)}, f32[8,128]{1,0:T(8,128)S(1)}, u32[]{:S(2)}, u32[]{:S(2)}) collective-permute-start(f32[8,128]{1,0:T(8,128)S(1)} %get-tuple-element.19.own_ref), channel_id=1, source_target_pairs={{4,12},{5,13},{6,14},{7,15},{12,20},{13,21},{14,22},{15,23},{20,28... | collective-permute-start | bytes 12296 | tf_op jit(solution)/shard_map/ppermute | solution.py:305
  7.5 5.1 %collective-permute-start.3 = (f32[40,128]{1,0:T(8,128)S(1)}, f32[40,128]{1,0:T(8,128)S(1)}, u32[]{:S(2)}, u32[]{:S(2)}) collective-permute-start(f32[40,128]{1,0:T(8,128)S(1)} %get-tuple-element.22), channel_id=1, source_target_pairs={{0,1},{1,0},{2,3},{3,2},{4,5},{5,4},{6,7},{7,6},{8,9},{9,8},{10,11... | collective-permute-start | bytes 61448 | tf_op jit(solution)/shard_map/ppermute | solution.py:313
  9.5 5.6 %collective-permute-start.4 = (f32[40,128]{1,0:T(8,128)S(1)}, f32[40,128]{1,0:T(8,128)S(1)}, u32[]{:S(2)}, u32[]{:S(2)}) collective-permute-start(f32[40,128]{1,0:T(8,128)S(1)} %get-tuple-element.23), channel_id=1, source_target_pairs={{1,2},{2,1},{3,0},{0,3},{5,6},{6,5},{7,4},{4,7},{9,10},{10,9},{11,... | collective-permute-start | bytes 61448 | tf_op jit(solution)/shard_map/ppermute | solution.py:313
  12.0 0.7 %collective-permute-start.5 = (f32[8,128]{1,0:T(8,128)S(1)}, f32[8,128]{1,0:T(8,128)S(1)}, u32[]{:S(2)}, u32[]{:S(2)}) collective-permute-start(f32[8,128]{1,0:T(8,128)S(1)} %get-tuple-element.26), channel_id=1, source_target_pairs={{4,6},{5,7},{6,4},{7,5},{12,14},{13,15},{14,12},{15,13},{20,22},{2... | collective-permute-start | bytes 12296 | tf_op jit(solution)/shard_map/ppermute | solution.py:305
  15.1 0.7 %collective-permute-start.6 = (f32[8,128]{1,0:T(8,128)S(1)}, f32[8,128]{1,0:T(8,128)S(1)}, u32[]{:S(2)}, u32[]{:S(2)}) collective-permute-start(f32[8,128]{1,0:T(8,128)S(1)} %fusion), channel_id=1, source_target_pairs={{4,20},{5,21},{6,22},{7,23},{12,28},{13,29},{14,30},{15,31},{20,4}... | collective-permute-start | bytes 12296 | tf_op jit(solution)/shard_map/ppermute | solution.py:305
  15.8 9.2 %collective-permute-start.7 = (f32[8,128]{1,0:T(8,128)S(1)}, f32[8,128]{1,0:T(8,128)S(1)}, u32[]{:S(2)}, u32[]{:S(2)}) collective-permute-start(f32[8,128]{1,0:T(8,128)S(1)} %max.15.own_ref), channel_id=1, source_target_pairs={{4,0},{12,8},{20,16},{28,24},{5,1},{13,9},{21,17},{29,25},{6,2},{1... | collective-permute-start | bytes 12296 | tf_op jit(solution)/shard_map/ppermute | solution.py:346

commit v3 on v2

--- a/solution.py
+++ b/solution.py
@@ -33,19 +33,8 @@
     return lax.rem(lax.axis_index(axis), 2) == 1
 
 
-def edge_kernel(state_ref, block_ref, first_ref, second_ref, top_ref, sems):
-    rows = state_ref.shape[1]
-    copies = [
-        pltpu.make_async_copy(
-            state_ref.at[comp, pl.ds(low, rows // 2)], block_ref.at[comp, pl.ds(low, rows // 2)], sems.at[comp, side]
-        )
-        for comp in range(4)
-        for side, low in enumerate((0, rows // 2))
-    ]
-    for copy in copies:
-        copy.start()
-    for copy in copies:
-        copy.wait()
+def edge_kernel(block_ref, first_ref, second_ref, top_ref):
+    rows = block_ref.shape[1]
     density, mom_x, mom_y, energy = (block_ref[comp] for comp in range(4))
     inv = 1.0 / density
     pressure = (GAMMA - 1.0) * (energy - 0.5 * (mom_x * mom_x + mom_y * mom_y) * inv)
@@ -240,7 +229,7 @@
     rows, cols = out_ref.shape[1:]
     tall = rows + 2 * HALO
     groups = field_ref.shape[2]
-    factor = -0.5 * COURANT / jnp.where(odd("gx"), own_ref[...], far_ref[...])
+    factor = -0.5 * COURANT / jnp.maximum(own_ref[...], far_ref[...])
     half_factor = 0.5 * factor
 
     for index in range(STEPS):
@@ -292,17 +281,13 @@
     tall = rows + 2 * HALO
     groups = -(-(cols + 2 * HALO) // LANES)
 
-    def sent(value, axis, by, odd_x=False):
+    def sent(value, axis, by):
         count = lax.axis_size(axis)
-        if not odd_x:
-            return lax.ppermute(value, axis, [(i, (i + by) % count) for i in range(count)])
-        count_x, count_y = lax.axis_size("gx"), lax.axis_size("gy")
-        pairs = []
-        for x in range(1, count_x, 2):
-            for y in range(count_y):
-                goal = ((x + by) % count_x, y) if axis == "gx" else (x, (y + by) % count_y)
-                pairs.append((x * count_y + y, goal[0] * count_y + goal[1]))
-        return lax.ppermute(value, ("gx", "gy"), pairs)
+        return lax.ppermute(value, axis, [(i, (i + by) % count) for i in range(count)])
+
+    def swapped_twos(value, axis):
+        count = lax.axis_size(axis)
+        return lax.ppermute(value, axis, [(i, i ^ 2) for i in range(count)])
 
     def swapped_pairs(value, axis, first):
         count = lax.axis_size(axis)
@@ -313,18 +298,17 @@
         return lax.ppermute(value, axis, pairs)
 
     edge_type = array(parts * HALO + 8, cols)
-    block, first, second, top = pl.pallas_call(
+    first, second, top = pl.pallas_call(
         edge_kernel,
-        out_shape=(array(parts, rows, cols), edge_type, edge_type, array(8, LANES)),
-        in_specs=[pl.BlockSpec(memory_space=pltpu.HBM)],
-        out_specs=(VMEM,) * 4,
-        scratch_shapes=[pltpu.SemaphoreType.DMA((4, 2))],
+        out_shape=(edge_type, edge_type, array(8, LANES)),
+        in_specs=[VMEM],
+        out_specs=(VMEM,) * 3,
         compiler_params=params(4),
         name="edge",
     )(state)
+    second = swapped_pairs(second, "gx", 1)
     first = swapped_pairs(first, "gx", 0)
-    second = swapped_pairs(second, "gx", 1)
-    far = sent(top, "gx", 2, odd_x=True)
+    far = swapped_twos(top, "gx")
     side_type = array(tall // 2 + 8, LANES)
     up, down, first, second, top = pl.pallas_call(
         pack_kernel,
@@ -333,17 +317,18 @@
         out_specs=(VMEM,) * 5,
         compiler_params=params(4),
         name="pack",
-    )(block, first, second, top, far)
+    )(state, first, second, top, far)
+    second = swapped_pairs(second, "gy", 1)
     first = swapped_pairs(first, "gy", 0)
-    second = swapped_pairs(second, "gy", 1)
-    far = sent(top, "gy", 2, odd_x=True)
+    far = swapped_twos(top, "gy")
     top = jnp.maximum(jnp.maximum(top, far), jnp.maximum(first[tall // 2 :], second[tall // 2 :]))
     for axis in ("gy", "gx"):
         covered = 4
         while covered < lax.axis_size(axis):
-            top = jnp.maximum(top, sent(top, axis, covered, odd_x=True))
+            far = sent(top, axis, covered)
             covered *= 2
-    far = lax.ppermute(top, "gx", [(i, i - 1) for i in range(1, lax.axis_size("gx"), 2)])
+            if axis == "gy" or covered < lax.axis_size(axis):
+                top = jnp.maximum(top, far)
     dealt_type = array(parts, tall // 8, groups, 8, LANES)
     dealt = pltpu.VMEM(dealt_type.shape, jnp.float32)
     plain = pltpu.VMEM((parts, groups, tall, LANES), jnp.float32)
@@ -356,7 +341,7 @@
         compiler_params=params(16),
         cost_estimate=pl.CostEstimate(flops=20_000_000, bytes_accessed=2_000_000, transcendentals=400_000),
         name="first",
-    )(block, up, down, first, second)
+    )(state, up, down, first, second)
     return pl.pallas_call(
         steps_kernel,
         out_shape=array(parts, rows, cols),

time: 30.6 us -> 26.6 us (0.87)
  starting transfers between devices: 11.8 us -> 8.92 us
  waiting for transfers between devices: 10.4 us -> 9.81 us
    ppermute x4, waiting for transfers between devices: 3.81 us -> 0.01 us  [swapped_pairs(): return lax.ppermute(value, axis, pairs)]
    ppermute x4 -> x3, waiting for transfers between devices: 6.61 us -> 9.8 us  [the longest x2 7.99 us: swapped_twos(): return lax.ppermute(value, axis, [(i, i ^ 2) for i in range(count)])]
    ppermute x4 -> x3, starting transfers between devices: 3.24 us -> 0.72 us  [the longest x1 0.61 us: sent(): lax.ppermute(value, axis, [(i, (i + by) % count) for i in range(count)])]
    ppermute x4, starting transfers between devices: 8.52 us -> 8.19 us  [swapped_pairs(): return lax.ppermute(value, axis, pairs)]
    unnamed x2 -> x4, local copies, waits for them, and re-layouts: 0.9 us -> 0.91 us
  transfers between devices with their start and end apart: 8 -> 7, of which waited for: 3 -> 3; matrix products, arithmetic and copies ran while one was open for 0% -> 0% of each run, Pallas kernels for 4% -> 5%
where the time goes in v3:
time: 26.6 us; the launch traced here: 26.5 us
  waiting for transfers between devices  9.81 us (37%)
  starting transfers between devices  8.92 us (34%)
  Pallas kernels  6.81 us (26%)
  local copies, waits for them, and re-layouts  0.91 us (3%)
    ppermute x4, starting transfers between devices, swapped_pairs(): return lax.ppermute(value, axis, pairs)  8.19 us
    ppermute x2, waiting for transfers between devices, swapped_twos(): return lax.ppermute(value, axis, [(i, i ^ 2) for i in range(count)])  7.99 us
    pallas_call x1, Pallas kernels, local(): pl.pallas_call(steps_kernel, out_shape=array(parts, rows, cols), in_specs...  5.27 us
    ppermute x1, waiting for transfers between devices, sent(): lax.ppermute(value, axis, [(i, (i + by) % count) for i in range(count)])  1.81 us
    pallas_call x1, Pallas kernels, local(): pl.pallas_call(first_kernel, out_shape=(dealt_type, dealt_type), in_specs...  1.25 us
    unnamed x4, local copies, waits for them, and re-layouts  0.91 us
    ppermute x1, starting transfers between devices, sent(): lax.ppermute(value, axis, [(i, (i + by) % count) for i in range(count)])  0.61 us
  transfers between devices with their start and end apart: 7, of which 3 were waited for; matrix products, arithmetic and copies ran while one was open for 0% of the time, Pallas kernels for 5%

profile of v3, /device:TPU:0, one launch (start us, length us, event | category | flops | bytes accessed | tf_op | source)
XLA Modules:
  0.0 26.5 jit_solution(8594466912069368648)
XLA Ops:
  0.0 0.0 copy-start
  0.0 0.9 %copy-done = f32[4,32,256]{2,1,0:T(8,128)S(1)} copy-done((f32[4,32,256]{2,1,0:T(8,128)S(1)}, f32[4,32,256]{2,1,0:T(8,128)}, u32[]{:S(2)}) %copy-start) | copy-done | bytes 131096
  0.9 0.2 edge.1
  1.1 0.5 %collective-permute-start = (f32[72,256]{1,0:T(8,128)S(1)}, f32[72,256]{1,0:T(8,128)S(1)}, u32[]{:S(2)}, u32[]{:S(2)}) collective-permute-start(f32[72,256]{1,0:T(8,128)S(1)} %get-tuple-element.15), channel_id=1, source_target_pairs={{0,4},{4,0},{8,12},{12,8},{16,20},{20,16},{24,28},{28,24},{1,5},{5... | collective-permute-start | bytes 221192 | tf_op jit(solution)/shard_map/ppermute | solution.py:298
  1.6 3.6 %collective-permute-start.1 = (f32[72,256]{1,0:T(8,128)S(1)}, f32[72,256]{1,0:T(8,128)S(1)}, u32[]{:S(2)}, u32[]{:S(2)}) collective-permute-start(f32[72,256]{1,0:T(8,128)S(1)} %get-tuple-element.16), channel_id=1, source_target_pairs={{4,8},{8,4},{12,16},{16,12},{20,24},{24,20},{28,0},{0,28},{5,9},{9... | collective-permute-start | bytes 221192 | tf_op jit(solution)/shard_map/ppermute | solution.py:298
  5.1 0.0 copy-start.1
  5.1 0.0 collective-permute-start.2
  5.1 3.6 %collective-permute-done.2.far_ref = f32[8,128]{1,0:T(8,128)S(1)} collective-permute-done((f32[8,128]{1,0:T(8,128)S(1)}, f32[8,128]{1,0:T(8,128)S(1)}, u32[]{:S(2)}, u32[]{:S(2)}) %collective-permute-start.2) | collective-permute-done | bytes 4128 | tf_op jit(solution)/shard_map/ppermute | solution.py:290
  8.8 0.0 collective-permute-done.swap_ref
  8.8 0.0 collective-permute-done.1.next_ref
  8.8 0.1 pack.1
  8.9 1.6 %collective-permute-start.3 = (f32[40,128]{1,0:T(8,128)S(1)}, f32[40,128]{1,0:T(8,128)S(1)}, u32[]{:S(2)}, u32[]{:S(2)}) collective-permute-start(f32[40,128]{1,0:T(8,128)S(1)} %get-tuple-element.20), channel_id=1, source_target_pairs={{0,1},{1,0},{2,3},{3,2},{4,5},{5,4},{6,7},{7,6},{8,9},{9,8},{10,11... | collective-permute-start | bytes 61448 | tf_op jit(solution)/shard_map/ppermute | solution.py:298
  10.5 2.5 %collective-permute-start.4 = (f32[40,128]{1,0:T(8,128)S(1)}, f32[40,128]{1,0:T(8,128)S(1)}, u32[]{:S(2)}, u32[]{:S(2)}) collective-permute-start(f32[40,128]{1,0:T(8,128)S(1)} %get-tuple-element.21), channel_id=1, source_target_pairs={{1,2},{2,1},{3,0},{0,3},{5,6},{6,5},{7,4},{4,7},{9,10},{10,9},{11,... | collective-permute-start | bytes 61448 | tf_op jit(solution)/shard_map/ppermute | solution.py:298
  13.0 0.1 collective-permute-start.5
  13.1 4.4 %collective-permute-done.5 = f32[8,128]{1,0:T(8,128)S(1)} collective-permute-done((f32[8,128]{1,0:T(8,128)S(1)}, f32[8,128]{1,0:T(8,128)S(1)}, u32[]{:S(2)}, u32[]{:S(2)}) %collective-permute-start.5) | collective-permute-done | bytes 4128 | tf_op jit(solution)/shard_map/ppermute | solution.py:290
  17.5 0.0 collective-permute-done.3.swap_ref
  17.5 0.0 collective-permute-done.4.next_ref
  17.5 0.6 %collective-permute-start.6 = (f32[8,128]{1,0:T(8,128)S(1)}, f32[8,128]{1,0:T(8,128)S(1)}, u32[]{:S(2)}, u32[]{:S(2)}) collective-permute-start(f32[8,128]{1,0:T(8,128)S(1)} %fusion.own_ref), channel_id=1, source_target_pairs={{0,16},{4,20},{8,24},{12,28},{16,0},{20,4},{24,8},{28,12},{1,17},{... | collective-permute-start | bytes 12296 | tf_op jit(solution)/shard_map/ppermute | solution.py:286
  18.1 0.0 copy-done.1
  18.1 1.3 %first.1 = (f32[4,8,3,8,128]{4,3,2,1,0:T(8,128)S(1)}, f32[4,8,3,8,128]{4,3,2,1,0:T(8,128)S(1)}) custom-call(f32[4,32,256]{2,1,0:T(8,128)S(1)} %copy-done.1, f32[72,256]{1,0:T(8,128)S(1)} %get-tuple-element.18.up_ref, f32[72,256]{1,0:T(8,128)S(1)} %get-tuple-element.19.down_ref, f32[40,128]{1,0:T(8,128)S(1)} %collective-permute-done.3.swap_ref, ...), custom_call_target="tpu_custom_call" | custom-call | flops 20000000 | bytes 2000000 | tf_op jit(solution)/shard_map/first/pallas_call | solution.py:335
  19.4 1.8 %collective-permute-done.6.far_ref = f32[8,128]{1,0:T(8,128)S(1)} collective-permute-done((f32[8,128]{1,0:T(8,128)S(1)}, f32[8,128]{1,0:T(8,128)S(1)}, u32[]{:S(2)}, u32[]{:S(2)}) %collective-permute-start.6) | collective-permute-done | bytes 4128 | tf_op jit(solution)/shard_map/ppermute | solution.py:286
  21.2 5.3 %steps.1 = f32[4,32,256]{2,1,0:T(8,128)} custom-call(f32[4,8,3,8,128]{4,3,2,1,0:T(8,128)S(1)} %get-tuple-element.22.field_ref, f32[4,8,3,8,128]{4,3,2,1,0:T(8,128)S(1)} %get-tuple-element.23.change_ref, f32[8,128]{1,0:T(8,128)S(1)} %fusion.own_ref, f32[8,128]{1,0:T(8,128)S(1)} %collective-permute-done.6.far_ref), custom_call_target="tpu_custom_call" | custom-call | tf_op jit(solution)/shard_map/steps/pallas_call | solution.py:345
  (1 shorter events, 0.0 us)
Async XLA Ops:
  0.0 0.9 %copy-start = (f32[4,32,256]{2,1,0:T(8,128)S(1)}, f32[4,32,256]{2,1,0:T(8,128)}, u32[]{:S(2)}) copy-start(f32[4,32,256]{2,1,0:T(8,128)} %state_ref.3) | copy-start | bytes 393220
  1.1 7.7 %collective-permute-start = (f32[72,256]{1,0:T(8,128)S(1)}, f32[72,256]{1,0:T(8,128)S(1)}, u32[]{:S(2)}, u32[]{:S(2)}) collective-permute-start(f32[72,256]{1,0:T(8,128)S(1)} %get-tuple-element.15), channel_id=1, source_target_pairs={{0,4},{4,0},{8,12},{12,8},{16,20},{20,16},{24,28},{28,24},{1,5},{5... | collective-permute-start | bytes 221192 | tf_op jit(solution)/shard_map/ppermute | solution.py:298
  1.6 7.2 %collective-permute-start.1 = (f32[72,256]{1,0:T(8,128)S(1)}, f32[72,256]{1,0:T(8,128)S(1)}, u32[]{:S(2)}, u32[]{:S(2)}) collective-permute-start(f32[72,256]{1,0:T(8,128)S(1)} %get-tuple-element.16), channel_id=1, source_target_pairs={{4,8},{8,4},{12,16},{16,12},{20,24},{24,20},{28,0},{0,28},{5,9},{9... | collective-permute-start | bytes 221192 | tf_op jit(solution)/shard_map/ppermute | solution.py:298
  5.1 13.0 %copy-start.1 = (f32[4,32,256]{2,1,0:T(8,128)S(1)}, f32[4,32,256]{2,1,0:T(8,128)}, u32[]{:S(2)}) copy-start(f32[4,32,256]{2,1,0:T(8,128)} %state_ref.3) | copy-start | bytes 393220
  5.1 3.6 %collective-permute-start.2 = (f32[8,128]{1,0:T(8,128)S(1)}, f32[8,128]{1,0:T(8,128)S(1)}, u32[]{:S(2)}, u32[]{:S(2)}) collective-permute-start(f32[8,128]{1,0:T(8,128)S(1)} %get-tuple-element.17.own_ref), channel_id=1, source_target_pairs={{0,8},{4,12},{8,0},{12,4},{16,24},{20,28},{24,16},{28,20},{1,9},{5... | collective-permute-start | bytes 12296 | tf_op jit(solution)/shard_map/ppermute | solution.py:290
  8.9 8.6 %collective-permute-start.3 = (f32[40,128]{1,0:T(8,128)S(1)}, f32[40,128]{1,0:T(8,128)S(1)}, u32[]{:S(2)}, u32[]{:S(2)}) collective-permute-start(f32[40,128]{1,0:T(8,128)S(1)} %get-tuple-element.20), channel_id=1, source_target_pairs={{0,1},{1,0},{2,3},{3,2},{4,5},{5,4},{6,7},{7,6},{8,9},{9,8},{10,11... | collective-permute-start | bytes 61448 | tf_op jit(solution)/shard_map/ppermute | solution.py:298
  10.5 7.0 %collective-permute-start.4 = (f32[40,128]{1,0:T(8,128)S(1)}, f32[40,128]{1,0:T(8,128)S(1)}, u32[]{:S(2)}, u32[]{:S(2)}) collective-permute-start(f32[40,128]{1,0:T(8,128)S(1)} %get-tuple-element.21), channel_id=1, source_target_pairs={{1,2},{2,1},{3,0},{0,3},{5,6},{6,5},{7,4},{4,7},{9,10},{10,9},{11,... | collective-permute-start | bytes 61448 | tf_op jit(solution)/shard_map/ppermute | solution.py:298
  13.0 4.5 %collective-permute-start.5 = (f32[8,128]{1,0:T(8,128)S(1)}, f32[8,128]{1,0:T(8,128)S(1)}, u32[]{:S(2)}, u32[]{:S(2)}) collective-permute-start(f32[8,128]{1,0:T(8,128)S(1)} %get-tuple-element.24), channel_id=1, source_target_pairs={{0,2},{1,3},{2,0},{3,1},{4,6},{5,7},{6,4},{7,5},{8,10},{9,11},{10,... | collective-permute-start | bytes 12296 | tf_op jit(solution)/shard_map/ppermute | solution.py:290
  17.5 3.7 %collective-permute-start.6 = (f32[8,128]{1,0:T(8,128)S(1)}, f32[8,128]{1,0:T(8,128)S(1)}, u32[]{:S(2)}, u32[]{:S(2)}) collective-permute-start(f32[8,128]{1,0:T(8,128)S(1)} %fusion.own_ref), channel_id=1, source_target_pairs={{0,16},{4,20},{8,24},{12,28},{16,0},{20,4},{24,8},{28,12},{1,17},{... | collective-permute-start | bytes 12296 | tf_op jit(solution)/shard_map/ppermute | solution.py:286

commit v4 on v3

--- a/solution.py
+++ b/solution.py
@@ -306,9 +306,9 @@
         compiler_params=params(4),
         name="edge",
     )(state)
+    far = swapped_twos(top, "gx")
+    first = swapped_pairs(first, "gx", 0)
     second = swapped_pairs(second, "gx", 1)
-    first = swapped_pairs(first, "gx", 0)
-    far = swapped_twos(top, "gx")
     side_type = array(tall // 2 + 8, LANES)
     up, down, first, second, top = pl.pallas_call(
         pack_kernel,
@@ -318,9 +318,9 @@
         compiler_params=params(4),
         name="pack",
     )(state, first, second, top, far)
+    far = swapped_twos(top, "gy")
+    first = swapped_pairs(first, "gy", 0)
     second = swapped_pairs(second, "gy", 1)
-    first = swapped_pairs(first, "gy", 0)
-    far = swapped_twos(top, "gy")
     top = jnp.maximum(jnp.maximum(top, far), jnp.maximum(first[tall // 2 :], second[tall // 2 :]))
     for axis in ("gy", "gx"):
         covered = 4

time: 26.6 us -> 26.6 us (level)
  no operation moved by 1% of the time
where the time goes in v4:
time: 26.6 us; the launch traced here: 26.5 us
  waiting for transfers between devices  9.81 us (37%)
  starting transfers between devices  8.92 us (34%)
  Pallas kernels  6.81 us (26%)
  local copies, waits for them, and re-layouts  0.91 us (3%)
    ppermute x4, starting transfers between devices, swapped_pairs(): return lax.ppermute(value, axis, pairs)  8.19 us
    ppermute x2, waiting for transfers between devices, swapped_twos(): return lax.ppermute(value, axis, [(i, i ^ 2) for i in range(count)])  7.99 us
    pallas_call x1, Pallas kernels, local(): pl.pallas_call(steps_kernel, out_shape=array(parts, rows, cols), in_specs...  5.27 us
    ppermute x1, waiting for transfers between devices, sent(): lax.ppermute(value, axis, [(i, (i + by) % count) for i in range(count)])  1.81 us
    pallas_call x1, Pallas kernels, local(): pl.pallas_call(first_kernel, out_shape=(dealt_type, dealt_type), in_specs...  1.25 us
    unnamed x4, local copies, waits for them, and re-layouts  0.91 us
    ppermute x1, starting transfers between devices, sent(): lax.ppermute(value, axis, [(i, (i + by) % count) for i in range(count)])  0.61 us
  transfers between devices with their start and end apart: 7, of which 3 were waited for; matrix products, arithmetic and copies ran while one was open for 0% of the time, Pallas kernels for 5%

profile of v4, /device:TPU:0, one launch (start us, length us, event | category | flops | bytes accessed | tf_op | source)
XLA Modules:
  0.0 26.5 jit_solution(8594466912069368648)
XLA Ops:
  0.0 0.0 copy-start
  0.0 0.9 %copy-done = f32[4,32,256]{2,1,0:T(8,128)S(1)} copy-done((f32[4,32,256]{2,1,0:T(8,128)S(1)}, f32[4,32,256]{2,1,0:T(8,128)}, u32[]{:S(2)}) %copy-start) | copy-done | bytes 131096
  0.9 0.2 edge.1
  1.1 0.5 %collective-permute-start = (f32[72,256]{1,0:T(8,128)S(1)}, f32[72,256]{1,0:T(8,128)S(1)}, u32[]{:S(2)}, u32[]{:S(2)}) collective-permute-start(f32[72,256]{1,0:T(8,128)S(1)} %get-tuple-element.15), channel_id=1, source_target_pairs={{0,4},{4,0},{8,12},{12,8},{16,20},{20,16},{24,28},{28,24},{1,5},{5... | collective-permute-start | bytes 221192 | tf_op jit(solution)/shard_map/ppermute | solution.py:298
  1.6 3.6 %collective-permute-start.1 = (f32[72,256]{1,0:T(8,128)S(1)}, f32[72,256]{1,0:T(8,128)S(1)}, u32[]{:S(2)}, u32[]{:S(2)}) collective-permute-start(f32[72,256]{1,0:T(8,128)S(1)} %get-tuple-element.16), channel_id=1, source_target_pairs={{4,8},{8,4},{12,16},{16,12},{20,24},{24,20},{28,0},{0,28},{5,9},{9... | collective-permute-start | bytes 221192 | tf_op jit(solution)/shard_map/ppermute | solution.py:298
  5.1 0.0 copy-start.1
  5.1 0.0 collective-permute-start.2
  5.1 3.6 %collective-permute-done.2.far_ref = f32[8,128]{1,0:T(8,128)S(1)} collective-permute-done((f32[8,128]{1,0:T(8,128)S(1)}, f32[8,128]{1,0:T(8,128)S(1)}, u32[]{:S(2)}, u32[]{:S(2)}) %collective-permute-start.2) | collective-permute-done | bytes 4128 | tf_op jit(solution)/shard_map/ppermute | solution.py:290
  8.8 0.0 collective-permute-done.swap_ref
  8.8 0.0 collective-permute-done.1.next_ref
  8.8 0.1 pack.1
  8.9 1.6 %collective-permute-start.3 = (f32[40,128]{1,0:T(8,128)S(1)}, f32[40,128]{1,0:T(8,128)S(1)}, u32[]{:S(2)}, u32[]{:S(2)}) collective-permute-start(f32[40,128]{1,0:T(8,128)S(1)} %get-tuple-element.20), channel_id=1, source_target_pairs={{0,1},{1,0},{2,3},{3,2},{4,5},{5,4},{6,7},{7,6},{8,9},{9,8},{10,11... | collective-permute-start | bytes 61448 | tf_op jit(solution)/shard_map/ppermute | solution.py:298
  10.5 2.5 %collective-permute-start.4 = (f32[40,128]{1,0:T(8,128)S(1)}, f32[40,128]{1,0:T(8,128)S(1)}, u32[]{:S(2)}, u32[]{:S(2)}) collective-permute-start(f32[40,128]{1,0:T(8,128)S(1)} %get-tuple-element.21), channel_id=1, source_target_pairs={{1,2},{2,1},{3,0},{0,3},{5,6},{6,5},{7,4},{4,7},{9,10},{10,9},{11,... | collective-permute-start | bytes 61448 | tf_op jit(solution)/shard_map/ppermute | solution.py:298
  13.0 0.1 collective-permute-start.5
  13.1 4.4 %collective-permute-done.5 = f32[8,128]{1,0:T(8,128)S(1)} collective-permute-done((f32[8,128]{1,0:T(8,128)S(1)}, f32[8,128]{1,0:T(8,128)S(1)}, u32[]{:S(2)}, u32[]{:S(2)}) %collective-permute-start.5) | collective-permute-done | bytes 4128 | tf_op jit(solution)/shard_map/ppermute | solution.py:290
  17.5 0.0 collective-permute-done.3.swap_ref
  17.5 0.0 collective-permute-done.4.next_ref
  17.5 0.6 %collective-permute-start.6 = (f32[8,128]{1,0:T(8,128)S(1)}, f32[8,128]{1,0:T(8,128)S(1)}, u32[]{:S(2)}, u32[]{:S(2)}) collective-permute-start(f32[8,128]{1,0:T(8,128)S(1)} %fusion.own_ref), channel_id=1, source_target_pairs={{0,16},{4,20},{8,24},{12,28},{16,0},{20,4},{24,8},{28,12},{1,17},{... | collective-permute-start | bytes 12296 | tf_op jit(solution)/shard_map/ppermute | solution.py:286
  18.1 0.0 copy-done.1
  18.1 1.3 %first.1 = (f32[4,8,3,8,128]{4,3,2,1,0:T(8,128)S(1)}, f32[4,8,3,8,128]{4,3,2,1,0:T(8,128)S(1)}) custom-call(f32[4,32,256]{2,1,0:T(8,128)S(1)} %copy-done.1, f32[72,256]{1,0:T(8,128)S(1)} %get-tuple-element.18.up_ref, f32[72,256]{1,0:T(8,128)S(1)} %get-tuple-element.19.down_ref, f32[40,128]{1,0:T(8,128)S(1)} %collective-permute-done.3.swap_ref, ...), custom_call_target="tpu_custom_call" | custom-call | flops 20000000 | bytes 2000000 | tf_op jit(solution)/shard_map/first/pallas_call | solution.py:335
  19.4 1.8 %collective-permute-done.6.far_ref = f32[8,128]{1,0:T(8,128)S(1)} collective-permute-done((f32[8,128]{1,0:T(8,128)S(1)}, f32[8,128]{1,0:T(8,128)S(1)}, u32[]{:S(2)}, u32[]{:S(2)}) %collective-permute-start.6) | collective-permute-done | bytes 4128 | tf_op jit(solution)/shard_map/ppermute | solution.py:286
  21.2 5.3 %steps.1 = f32[4,32,256]{2,1,0:T(8,128)} custom-call(f32[4,8,3,8,128]{4,3,2,1,0:T(8,128)S(1)} %get-tuple-element.22.field_ref, f32[4,8,3,8,128]{4,3,2,1,0:T(8,128)S(1)} %get-tuple-element.23.change_ref, f32[8,128]{1,0:T(8,128)S(1)} %fusion.own_ref, f32[8,128]{1,0:T(8,128)S(1)} %collective-permute-done.6.far_ref), custom_call_target="tpu_custom_call" | custom-call | tf_op jit(solution)/shard_map/steps/pallas_call | solution.py:345
  (1 shorter events, 0.0 us)
Async XLA Ops:
  0.0 0.9 %copy-start = (f32[4,32,256]{2,1,0:T(8,128)S(1)}, f32[4,32,256]{2,1,0:T(8,128)}, u32[]{:S(2)}) copy-start(f32[4,32,256]{2,1,0:T(8,128)} %state_ref.3) | copy-start | bytes 393220
  1.1 7.7 %collective-permute-start = (f32[72,256]{1,0:T(8,128)S(1)}, f32[72,256]{1,0:T(8,128)S(1)}, u32[]{:S(2)}, u32[]{:S(2)}) collective-permute-start(f32[72,256]{1,0:T(8,128)S(1)} %get-tuple-element.15), channel_id=1, source_target_pairs={{0,4},{4,0},{8,12},{12,8},{16,20},{20,16},{24,28},{28,24},{1,5},{5... | collective-permute-start | bytes 221192 | tf_op jit(solution)/shard_map/ppermute | solution.py:298
  1.6 7.2 %collective-permute-start.1 = (f32[72,256]{1,0:T(8,128)S(1)}, f32[72,256]{1,0:T(8,128)S(1)}, u32[]{:S(2)}, u32[]{:S(2)}) collective-permute-start(f32[72,256]{1,0:T(8,128)S(1)} %get-tuple-element.16), channel_id=1, source_target_pairs={{4,8},{8,4},{12,16},{16,12},{20,24},{24,20},{28,0},{0,28},{5,9},{9... | collective-permute-start | bytes 221192 | tf_op jit(solution)/shard_map/ppermute | solution.py:298
  5.1 13.0 %copy-start.1 = (f32[4,32,256]{2,1,0:T(8,128)S(1)}, f32[4,32,256]{2,1,0:T(8,128)}, u32[]{:S(2)}) copy-start(f32[4,32,256]{2,1,0:T(8,128)} %state_ref.3) | copy-start | bytes 393220
  5.1 3.6 %collective-permute-start.2 = (f32[8,128]{1,0:T(8,128)S(1)}, f32[8,128]{1,0:T(8,128)S(1)}, u32[]{:S(2)}, u32[]{:S(2)}) collective-permute-start(f32[8,128]{1,0:T(8,128)S(1)} %get-tuple-element.17.own_ref), channel_id=1, source_target_pairs={{0,8},{4,12},{8,0},{12,4},{16,24},{20,28},{24,16},{28,20},{1,9},{5... | collective-permute-start | bytes 12296 | tf_op jit(solution)/shard_map/ppermute | solution.py:290
  8.9 8.6 %collective-permute-start.3 = (f32[40,128]{1,0:T(8,128)S(1)}, f32[40,128]{1,0:T(8,128)S(1)}, u32[]{:S(2)}, u32[]{:S(2)}) collective-permute-start(f32[40,128]{1,0:T(8,128)S(1)} %get-tuple-element.20), channel_id=1, source_target_pairs={{0,1},{1,0},{2,3},{3,2},{4,5},{5,4},{6,7},{7,6},{8,9},{9,8},{10,11... | collective-permute-start | bytes 61448 | tf_op jit(solution)/shard_map/ppermute | solution.py:298
  10.5 7.0 %collective-permute-start.4 = (f32[40,128]{1,0:T(8,128)S(1)}, f32[40,128]{1,0:T(8,128)S(1)}, u32[]{:S(2)}, u32[]{:S(2)}) collective-permute-start(f32[40,128]{1,0:T(8,128)S(1)} %get-tuple-element.21), channel_id=1, source_target_pairs={{1,2},{2,1},{3,0},{0,3},{5,6},{6,5},{7,4},{4,7},{9,10},{10,9},{11,... | collective-permute-start | bytes 61448 | tf_op jit(solution)/shard_map/ppermute | solution.py:298
  13.0 4.5 %collective-permute-start.5 = (f32[8,128]{1,0:T(8,128)S(1)}, f32[8,128]{1,0:T(8,128)S(1)}, u32[]{:S(2)}, u32[]{:S(2)}) collective-permute-start(f32[8,128]{1,0:T(8,128)S(1)} %get-tuple-element.24), channel_id=1, source_target_pairs={{0,2},{1,3},{2,0},{3,1},{4,6},{5,7},{6,4},{7,5},{8,10},{9,11},{10,... | collective-permute-start | bytes 12296 | tf_op jit(solution)/shard_map/ppermute | solution.py:290
  17.5 3.7 %collective-permute-start.6 = (f32[8,128]{1,0:T(8,128)S(1)}, f32[8,128]{1,0:T(8,128)S(1)}, u32[]{:S(2)}, u32[]{:S(2)}) collective-permute-start(f32[8,128]{1,0:T(8,128)S(1)} %fusion.own_ref), channel_id=1, source_target_pairs={{0,16},{4,20},{8,24},{12,28},{16,0},{20,4},{24,8},{28,12},{1,17},{... | collective-permute-start | bytes 12296 | tf_op jit(solution)/shard_map/ppermute | solution.py:286

commit v5 on v3

--- a/solution.py
+++ b/solution.py
@@ -52,7 +52,7 @@
     top_ref[...] = jnp.full(top_ref.shape, top)
 
 
-def pack_kernel(state_ref, swap_ref, next_ref, own_ref, far_ref, up_ref, down_ref, first_ref, second_ref, top_ref):
+def pack_kernel(state_ref, swap_ref, next_ref, own_ref, three_ref, four_ref, up_ref, down_ref, first_ref, second_ref, top_ref):
     rows = state_ref.shape[1]
     cols = state_ref.shape[2]
     half = rows // 2 + HALO
@@ -60,7 +60,7 @@
     is_odd = odd("gx")
     up_ref[...] = jnp.where(is_odd, swap_ref[...], next_ref[...])
     down_ref[...] = jnp.where(is_odd, next_ref[...], swap_ref[...])
-    top = jnp.maximum(jnp.maximum(own_ref[...], far_ref[...]),
+    top = jnp.maximum(jnp.maximum(own_ref[...], jnp.maximum(three_ref[...], four_ref[...])),
                       jnp.maximum(up_ref[4 * HALO :, 0:LANES], down_ref[4 * HALO :, 0:LANES]))
 
     def edge(low, at):
@@ -109,10 +109,12 @@
     inv = pl.reciprocal(density, approx=True)
     vel = normal * inv
     carried = normal * vel
-    pressure = (GAMMA - 1.0) * energy - (0.5 * (GAMMA - 1.0)) * (carried + tangent * tangent * inv)
-    square = GAMMA * pressure * inv
-    sound = square * lax.rsqrt(jnp.maximum(square, TINY))
-    return (normal, carried + pressure, tangent * vel, (energy + pressure) * vel), jnp.abs(vel) + sound
+    kinetic = (0.5 * (GAMMA - 1.0)) * (carried + tangent * tangent * inv)
+    pressure = energy - kinetic
+    scaled = GAMMA * pressure
+    square = jnp.maximum(scaled * inv, TINY)
+    sound = square * lax.rsqrt(square)
+    return (normal, carried + pressure, tangent * vel, (scaled + kinetic) * vel), jnp.abs(vel) + sound
 
 
 def face(left, right):
@@ -211,7 +213,8 @@
     found = selected(plain[...], select)
     for comp in range(4):
         for group in range(groups):
-            dealt[comp, group] = found[comp * tall : (comp + 1) * tall, group * LANES : (group + 1) * LANES]
+            cells = found[comp * tall : (comp + 1) * tall, group * LANES : (group + 1) * LANES]
+            dealt[comp, group] = (GAMMA - 1.0) * cells if comp == 3 else cells
     count = tall // 8
     for comp in range(4):
         for row in range(count):
@@ -225,12 +228,11 @@
     changes(field_ref, diff, count, groups, store)
 
 
-def steps_kernel(field_ref, change_ref, own_ref, far_ref, out_ref, field, mid, diff, dealt):
+def steps_kernel(field_ref, change_ref, own_ref, far_ref, out_ref, field, base, mid, diff, dealt):
     rows, cols = out_ref.shape[1:]
     tall = rows + 2 * HALO
     groups = field_ref.shape[2]
-    factor = -0.5 * COURANT / jnp.maximum(own_ref[...], far_ref[...])
-    half_factor = 0.5 * factor
+    half_factor = -0.25 * COURANT / jnp.maximum(own_ref[...], far_ref[...])
 
     for index in range(STEPS):
         start = 4 * index
@@ -239,12 +241,15 @@
 
         def to_mid(row, col, parts):
             for comp in range(4):
-                mid[comp, row, col] = old[comp, row, col] + factor * parts[comp]
+                move = half_factor * parts[comp]
+                moved = old[comp, row, col] + move
+                base[comp, row, col] = moved
+                mid[comp, row, col] = moved + move
 
         def to_field(row, col, parts):
             for comp in range(4):
-                mean = 0.5 * (old[comp, row, col] + mid[comp, row, col])
-                dealt[comp, col, pl.ds(start + row, 8, stride=count), :] = mean + half_factor * parts[comp]
+                new = base[comp, row, col] + half_factor * parts[comp]
+                dealt[comp, col, pl.ds(start + row, 8, stride=count), :] = new
 
         if index == 0:
             for row in range(count):
@@ -273,7 +278,8 @@
         parts.append(jnp.concatenate(line, axis=1))
     found = selected(jnp.concatenate(parts, axis=0), select)
     for comp in range(4):
-        out_ref[comp] = found[comp * rows : (comp + 1) * rows, :]
+        cells = found[comp * rows : (comp + 1) * rows, :]
+        out_ref[comp] = cells / (GAMMA - 1.0) if comp == 3 else cells
 
 
 def local(state):
@@ -285,9 +291,8 @@
         count = lax.axis_size(axis)
         return lax.ppermute(value, axis, [(i, (i + by) % count) for i in range(count)])
 
-    def swapped_twos(value, axis):
-        count = lax.axis_size(axis)
-        return lax.ppermute(value, axis, [(i, i ^ 2) for i in range(count)])
+    def swapped_bit(value, axis, by):
+        return lax.ppermute(value, axis, [(i, i ^ by) for i in range(lax.axis_size(axis))])
 
     def swapped_pairs(value, axis, first):
         count = lax.axis_size(axis)
@@ -296,6 +301,10 @@
             high = (low + 1) % count
             pairs += [(low, high), (high, low)]
         return lax.ppermute(value, axis, pairs)
+
+    def swapped_threes(value, axis):
+        count = lax.axis_size(axis)
+        return lax.ppermute(value, axis, [(i, (i + 3 - 6 * (i % 2)) % count) for i in range(count)])
 
     edge_type = array(parts * HALO + 8, cols)
     first, second, top = pl.pallas_call(
@@ -308,27 +317,25 @@
     )(state)
     second = swapped_pairs(second, "gx", 1)
     first = swapped_pairs(first, "gx", 0)
-    far = swapped_twos(top, "gx")
+    far = swapped_threes(top, "gx"), swapped_bit(top, "gx", 4)
     side_type = array(tall // 2 + 8, LANES)
     up, down, first, second, top = pl.pallas_call(
         pack_kernel,
         out_shape=(edge_type, edge_type, side_type, side_type, array(8, LANES)),
-        in_specs=[VMEM] * 5,
+        in_specs=[VMEM] * 6,
         out_specs=(VMEM,) * 5,
         compiler_params=params(4),
         name="pack",
-    )(state, first, second, top, far)
+    )(state, first, second, top, *far)
     second = swapped_pairs(second, "gy", 1)
     first = swapped_pairs(first, "gy", 0)
-    far = swapped_twos(top, "gy")
+    far = swapped_bit(top, "gy", 2)
     top = jnp.maximum(jnp.maximum(top, far), jnp.maximum(first[tall // 2 :], second[tall // 2 :]))
-    for axis in ("gy", "gx"):
-        covered = 4
+    for axis, covered in (("gy", 4), ("gx", 8)):
         while covered < lax.axis_size(axis):
-            far = sent(top, axis, covered)
+            top = jnp.maximum(top, sent(top, axis, covered))
             covered *= 2
-            if axis == "gy" or covered < lax.axis_size(axis):
-                top = jnp.maximum(top, far)
+    far = swapped_bit(top, "gx", 1)
     dealt_type = array(parts, tall // 8, groups, 8, LANES)
     dealt = pltpu.VMEM(dealt_type.shape, jnp.float32)
     plain = pltpu.VMEM((parts, groups, tall, LANES), jnp.float32)
@@ -347,7 +354,7 @@
         out_shape=array(parts, rows, cols),
         in_specs=[VMEM] * 4,
         out_specs=VMEM,
-        scratch_shapes=[dealt, dealt, dealt, plain],
+        scratch_shapes=[dealt] * 4 + [plain],
         compiler_params=params(16),
         name="steps",
     )(field, change, top, far)

time: 26.6 us -> 24.7 us (0.929)
  waiting for transfers between devices: 9.81 us -> 7.66 us
    ppermute x3 -> x4, waiting for transfers between devices: 9.8 us -> 7.65 us  [the longest x3 5.19 us: swapped_bit(): lax.ppermute(value, axis, [(i, i ^ by) for i in range(lax.axis_size(axis))])]
    ppermute x3 -> x4, starting transfers between devices: 0.72 us -> 0.75 us  [the longest x3 0.54 us: swapped_bit(): lax.ppermute(value, axis, [(i, i ^ by) for i in range(lax.axis_size(axis))])]
  transfers between devices with their start and end apart: 7 -> 8, of which waited for: 3 -> 3; matrix products, arithmetic and copies ran while one was open for 0% -> 0% of each run, Pallas kernels for 5% -> 5%
where the time goes in v5:
time: 24.7 us; the launch traced here: 24.5 us
  starting transfers between devices  8.94 us (36%)
  waiting for transfers between devices  7.66 us (31%)
  Pallas kernels  6.9 us (28%)
  local copies, waits for them, and re-layouts  0.91 us (4%)
    ppermute x4, starting transfers between devices, swapped_pairs(): return lax.ppermute(value, axis, pairs)  8.19 us
    pallas_call x1, Pallas kernels, local(): pl.pallas_call(steps_kernel, out_shape=array(parts, rows, cols), in_specs...  5.33 us
    ppermute x3, waiting for transfers between devices, swapped_bit(): lax.ppermute(value, axis, [(i, i ^ by) for i in range(lax.axis_size(axis))])  5.19 us
    ppermute x1, waiting for transfers between devices, swapped_threes(): lax.ppermute(value, axis, [(i, (i + 3 - 6 * (i % 2)) % count) for i in ra...  2.47 us
    pallas_call x1, Pallas kernels, local(): pl.pallas_call(first_kernel, out_shape=(dealt_type, dealt_type), in_specs...  1.28 us
    unnamed x4, local copies, waits for them, and re-layouts  0.91 us
    ppermute x3, starting transfers between devices, swapped_bit(): lax.ppermute(value, axis, [(i, i ^ by) for i in range(lax.axis_size(axis))])  0.54 us
  transfers between devices with their start and end apart: 8, of which 3 were waited for; matrix products, arithmetic and copies ran while one was open for 0% of the time, Pallas kernels for 5%

profile of v5, /device:TPU:0, one launch (start us, length us, event | category | flops | bytes accessed | tf_op | source)
XLA Modules:
  0.0 24.5 jit_solution(1380777202795573960)
XLA Ops:
  0.0 0.0 copy-start
  0.0 0.9 %copy-done = f32[4,32,256]{2,1,0:T(8,128)S(1)} copy-done((f32[4,32,256]{2,1,0:T(8,128)S(1)}, f32[4,32,256]{2,1,0:T(8,128)}, u32[]{:S(2)}) %copy-start) | copy-done | bytes 131096
  0.9 0.2 edge.1
  1.1 0.5 %collective-permute-start = (f32[72,256]{1,0:T(8,128)S(1)}, f32[72,256]{1,0:T(8,128)S(1)}, u32[]{:S(2)}, u32[]{:S(2)}) collective-permute-start(f32[72,256]{1,0:T(8,128)S(1)} %get-tuple-element.15), channel_id=1, source_target_pairs={{0,4},{4,0},{8,12},{12,8},{16,20},{20,16},{24,28},{28,24},{1,5},{5... | collective-permute-start | bytes 221192 | tf_op jit(solution)/shard_map/ppermute | solution.py:303
  1.6 3.6 %collective-permute-start.1 = (f32[72,256]{1,0:T(8,128)S(1)}, f32[72,256]{1,0:T(8,128)S(1)}, u32[]{:S(2)}, u32[]{:S(2)}) collective-permute-start(f32[72,256]{1,0:T(8,128)S(1)} %get-tuple-element.16), channel_id=1, source_target_pairs={{4,8},{8,4},{12,16},{16,12},{20,24},{24,20},{28,0},{0,28},{5,9},{9... | collective-permute-start | bytes 221192 | tf_op jit(solution)/shard_map/ppermute | solution.py:303
  5.1 0.0 copy-start.1
  5.1 0.2 collective-permute-start.2
  5.4 0.3 %collective-permute-start.3 = (f32[8,128]{1,0:T(8,128)S(1)}, f32[8,128]{1,0:T(8,128)S(1)}, u32[]{:S(2)}, u32[]{:S(2)}) collective-permute-start(f32[8,128]{1,0:T(8,128)S(1)} %get-tuple-element.17.own_ref), channel_id=1, source_target_pairs={{0,16},{4,20},{8,24},{12,28},{16,0},{20,4},{24,8},{28,12},{1,17},{... | collective-permute-start | bytes 12296 | tf_op jit(solution)/shard_map/ppermute | solution.py:295
  5.7 2.5 %collective-permute-done.2.three_ref = f32[8,128]{1,0:T(8,128)S(1)} collective-permute-done((f32[8,128]{1,0:T(8,128)S(1)}, f32[8,128]{1,0:T(8,128)S(1)}, u32[]{:S(2)}, u32[]{:S(2)}) %collective-permute-start.2) | collective-permute-done | bytes 4128 | tf_op jit(solution)/shard_map/ppermute | solution.py:307
  8.2 0.8 %collective-permute-done.3.four_ref = f32[8,128]{1,0:T(8,128)S(1)} collective-permute-done((f32[8,128]{1,0:T(8,128)S(1)}, f32[8,128]{1,0:T(8,128)S(1)}, u32[]{:S(2)}, u32[]{:S(2)}) %collective-permute-start.3) | collective-permute-done | bytes 4128 | tf_op jit(solution)/shard_map/ppermute | solution.py:295
  9.0 0.0 collective-permute-done.swap_ref
  9.0 0.0 collective-permute-done.1.next_ref
  9.0 0.1 pack.1
  9.1 1.6 %collective-permute-start.4 = (f32[40,128]{1,0:T(8,128)S(1)}, f32[40,128]{1,0:T(8,128)S(1)}, u32[]{:S(2)}, u32[]{:S(2)}) collective-permute-start(f32[40,128]{1,0:T(8,128)S(1)} %get-tuple-element.20), channel_id=1, source_target_pairs={{0,1},{1,0},{2,3},{3,2},{4,5},{5,4},{6,7},{7,6},{8,9},{9,8},{10,11... | collective-permute-start | bytes 61448 | tf_op jit(solution)/shard_map/ppermute | solution.py:303
  10.8 2.5 %collective-permute-start.5 = (f32[40,128]{1,0:T(8,128)S(1)}, f32[40,128]{1,0:T(8,128)S(1)}, u32[]{:S(2)}, u32[]{:S(2)}) collective-permute-start(f32[40,128]{1,0:T(8,128)S(1)} %get-tuple-element.21), channel_id=1, source_target_pairs={{1,2},{2,1},{3,0},{0,3},{5,6},{6,5},{7,4},{4,7},{9,10},{10,9},{11,... | collective-permute-start | bytes 61448 | tf_op jit(solution)/shard_map/ppermute | solution.py:303
  13.2 0.1 collective-permute-start.6
  13.4 4.4 %collective-permute-done.6 = f32[8,128]{1,0:T(8,128)S(1)} collective-permute-done((f32[8,128]{1,0:T(8,128)S(1)}, f32[8,128]{1,0:T(8,128)S(1)}, u32[]{:S(2)}, u32[]{:S(2)}) %collective-permute-start.6) | collective-permute-done | bytes 4128 | tf_op jit(solution)/shard_map/ppermute | solution.py:295
  17.7 0.0 collective-permute-done.4.swap_ref
  17.7 0.0 collective-permute-done.5.next_ref
  17.8 0.1 collective-permute-start.7
  17.8 0.0 copy-done.1
  17.8 1.3 %first.1 = (f32[4,8,3,8,128]{4,3,2,1,0:T(8,128)S(1)}, f32[4,8,3,8,128]{4,3,2,1,0:T(8,128)S(1)}) custom-call(f32[4,32,256]{2,1,0:T(8,128)S(1)} %copy-done.1, f32[72,256]{1,0:T(8,128)S(1)} %get-tuple-element.18.up_ref, f32[72,256]{1,0:T(8,128)S(1)} %get-tuple-element.19.down_ref, f32[40,128]{1,0:T(8,128)S(1)} %collective-permute-done.4.swap_ref, ...), custom_call_target="tpu_custom_call" | custom-call | flops 20000000 | bytes 2000000 | tf_op jit(solution)/shard_map/first/pallas_call | solution.py:342
  19.1 0.0 collective-permute-done.7.far_ref
  19.1 5.3 %steps.1 = f32[4,32,256]{2,1,0:T(8,128)} custom-call(f32[4,8,3,8,128]{4,3,2,1,0:T(8,128)S(1)} %get-tuple-element.22.field_ref, f32[4,8,3,8,128]{4,3,2,1,0:T(8,128)S(1)} %get-tuple-element.23.change_ref, f32[8,128]{1,0:T(8,128)S(1)} %fusion.own_ref, f32[8,128]{1,0:T(8,128)S(1)} %collective-permute-done.7.far_ref), custom_call_target="tpu_custom_call" | custom-call | tf_op jit(solution)/shard_map/steps/pallas_call | solution.py:352
  (1 shorter events, 0.0 us)
Async XLA Ops:
  0.0 0.9 %copy-start = (f32[4,32,256]{2,1,0:T(8,128)S(1)}, f32[4,32,256]{2,1,0:T(8,128)}, u32[]{:S(2)}) copy-start(f32[4,32,256]{2,1,0:T(8,128)} %state_ref.3) | copy-start | bytes 393220
  1.1 7.9 %collective-permute-start = (f32[72,256]{1,0:T(8,128)S(1)}, f32[72,256]{1,0:T(8,128)S(1)}, u32[]{:S(2)}, u32[]{:S(2)}) collective-permute-start(f32[72,256]{1,0:T(8,128)S(1)} %get-tuple-element.15), channel_id=1, source_target_pairs={{0,4},{4,0},{8,12},{12,8},{16,20},{20,16},{24,28},{28,24},{1,5},{5... | collective-permute-start | bytes 221192 | tf_op jit(solution)/shard_map/ppermute | solution.py:303
  1.6 7.4 %collective-permute-start.1 = (f32[72,256]{1,0:T(8,128)S(1)}, f32[72,256]{1,0:T(8,128)S(1)}, u32[]{:S(2)}, u32[]{:S(2)}) collective-permute-start(f32[72,256]{1,0:T(8,128)S(1)} %get-tuple-element.16), channel_id=1, source_target_pairs={{4,8},{8,4},{12,16},{16,12},{20,24},{24,20},{28,0},{0,28},{5,9},{9... | collective-permute-start | bytes 221192 | tf_op jit(solution)/shard_map/ppermute | solution.py:303
  5.1 12.7 %copy-start.1 = (f32[4,32,256]{2,1,0:T(8,128)S(1)}, f32[4,32,256]{2,1,0:T(8,128)}, u32[]{:S(2)}) copy-start(f32[4,32,256]{2,1,0:T(8,128)} %state_ref.3) | copy-start | bytes 393220
  5.1 3.0 %collective-permute-start.2 = (f32[8,128]{1,0:T(8,128)S(1)}, f32[8,128]{1,0:T(8,128)S(1)}, u32[]{:S(2)}, u32[]{:S(2)}) collective-permute-start(f32[8,128]{1,0:T(8,128)S(1)} %get-tuple-element.17.own_ref), channel_id=1, source_target_pairs={{0,12},{4,24},{8,20},{12,0},{16,28},{20,8},{24,4},{28,16},{1,13},{... | collective-permute-start | bytes 12296 | tf_op jit(solution)/shard_map/ppermute | solution.py:307
  5.4 3.6 %collective-permute-start.3 = (f32[8,128]{1,0:T(8,128)S(1)}, f32[8,128]{1,0:T(8,128)S(1)}, u32[]{:S(2)}, u32[]{:S(2)}) collective-permute-start(f32[8,128]{1,0:T(8,128)S(1)} %get-tuple-element.17.own_ref), channel_id=1, source_target_pairs={{0,16},{4,20},{8,24},{12,28},{16,0},{20,4},{24,8},{28,12},{1,17},{... | collective-permute-start | bytes 12296 | tf_op jit(solution)/shard_map/ppermute | solution.py:295
  9.1 8.6 %collective-permute-start.4 = (f32[40,128]{1,0:T(8,128)S(1)}, f32[40,128]{1,0:T(8,128)S(1)}, u32[]{:S(2)}, u32[]{:S(2)}) collective-permute-start(f32[40,128]{1,0:T(8,128)S(1)} %get-tuple-element.20), channel_id=1, source_target_pairs={{0,1},{1,0},{2,3},{3,2},{4,5},{5,4},{6,7},{7,6},{8,9},{9,8},{10,11... | collective-permute-start | bytes 61448 | tf_op jit(solution)/shard_map/ppermute | solution.py:303
  10.8 7.0 %collective-permute-start.5 = (f32[40,128]{1,0:T(8,128)S(1)}, f32[40,128]{1,0:T(8,128)S(1)}, u32[]{:S(2)}, u32[]{:S(2)}) collective-permute-start(f32[40,128]{1,0:T(8,128)S(1)} %get-tuple-element.21), channel_id=1, source_target_pairs={{1,2},{2,1},{3,0},{0,3},{5,6},{6,5},{7,4},{4,7},{9,10},{10,9},{11,... | collective-permute-start | bytes 61448 | tf_op jit(solution)/shard_map/ppermute | solution.py:303
  13.2 4.5 %collective-permute-start.6 = (f32[8,128]{1,0:T(8,128)S(1)}, f32[8,128]{1,0:T(8,128)S(1)}, u32[]{:S(2)}, u32[]{:S(2)}) collective-permute-start(f32[8,128]{1,0:T(8,128)S(1)} %get-tuple-element.24), channel_id=1, source_target_pairs={{0,2},{1,3},{2,0},{3,1},{4,6},{5,7},{6,4},{7,5},{8,10},{9,11},{10,... | collective-permute-start | bytes 12296 | tf_op jit(solution)/shard_map/ppermute | solution.py:295
  17.8 1.4 %collective-permute-start.7 = (f32[8,128]{1,0:T(8,128)S(1)}, f32[8,128]{1,0:T(8,128)S(1)}, u32[]{:S(2)}, u32[]{:S(2)}) collective-permute-start(f32[8,128]{1,0:T(8,128)S(1)} %fusion.own_ref), channel_id=1, source_target_pairs={{0,4},{4,0},{8,12},{12,8},{16,20},{20,16},{24,28},{28,24},{1,5},{5... | collective-permute-start | bytes 12296 | tf_op jit(solution)/shard_map/ppermute | solution.py:295

commit v6 on v5

--- a/solution.py
+++ b/solution.py
@@ -104,9 +104,8 @@
     return jnp.maximum(low, jnp.minimum(high, 0.0))
 
 
-def fluxes(state):
-    density, normal, tangent, energy = state
-    inv = pl.reciprocal(density, approx=True)
+def known(state, inv):
+    _, normal, tangent, energy = state
     vel = normal * inv
     carried = normal * vel
     kinetic = (0.5 * (GAMMA - 1.0)) * (carried + tangent * tangent * inv)
@@ -114,7 +113,7 @@
     scaled = GAMMA * pressure
     square = jnp.maximum(scaled * inv, TINY)
     sound = square * lax.rsqrt(square)
-    return (normal, carried + pressure, tangent * vel, (scaled + kinetic) * vel), jnp.abs(vel) + sound
+    return state, (normal, carried + pressure, tangent * vel, (scaled + kinetic) * vel), jnp.abs(vel) + sound
 
 
 def face(left, right):
@@ -145,7 +144,8 @@
         slope = [minmod(jump[comp], next_jump[comp]) for comp in range(4)]
         low_state = minus(here, slope)
         high_state = [here[comp] + slope[comp] for comp in range(4)]
-        low = (low_state, *fluxes(low_state))
+        both = pl.reciprocal(low_state[0] * high_state[0], approx=True)
+        low = known(low_state, high_state[0] * both)
         if at == 0:
             first_low = low
         else:
@@ -155,7 +155,7 @@
             else:
                 store(at - 1, minus(flux, last_flux))
             last_flux = flux
-        high = (high_state, *fluxes(high_state))
+        high = known(high_state, low_state[0] * both)
         here, jump = after, next_jump
     flux = face(high, rolled(first_low, -1))
     store(count - 1, minus(flux, last_flux))

time: 24.7 us -> 24.7 us (level)
  no operation moved by 1% of the time
where the time goes in v6:
time: 24.7 us; the launch traced here: 24.5 us
  starting transfers between devices  8.94 us (36%)
  waiting for transfers between devices  7.66 us (31%)
  Pallas kernels  6.92 us (28%)
  local copies, waits for them, and re-layouts  0.91 us (4%)
    ppermute x4, starting transfers between devices, swapped_pairs(): return lax.ppermute(value, axis, pairs)  8.19 us
    pallas_call x1, Pallas kernels, local(): pl.pallas_call(steps_kernel, out_shape=array(parts, rows, cols), in_specs...  5.35 us
    ppermute x3, waiting for transfers between devices, swapped_bit(): lax.ppermute(value, axis, [(i, i ^ by) for i in range(lax.axis_size(axis))])  5.19 us
    ppermute x1, waiting for transfers between devices, swapped_threes(): lax.ppermute(value, axis, [(i, (i + 3 - 6 * (i % 2)) % count) for i in ra...  2.47 us
    pallas_call x1, Pallas kernels, local(): pl.pallas_call(first_kernel, out_shape=(dealt_type, dealt_type), in_specs...  1.29 us
    unnamed x4, local copies, waits for them, and re-layouts  0.91 us
    ppermute x3, starting transfers between devices, swapped_bit(): lax.ppermute(value, axis, [(i, i ^ by) for i in range(lax.axis_size(axis))])  0.54 us
  transfers between devices with their start and end apart: 8, of which 3 were waited for; matrix products, arithmetic and copies ran while one was open for 0% of the time, Pallas kernels for 5%

profile of v6, /device:TPU:0, one launch (start us, length us, event | category | flops | bytes accessed | tf_op | source)
XLA Modules:
  0.0 24.5 jit_solution(15834151799736803891)
XLA Ops:
  0.0 0.0 copy-start
  0.0 0.9 %copy-done = f32[4,32,256]{2,1,0:T(8,128)S(1)} copy-done((f32[4,32,256]{2,1,0:T(8,128)S(1)}, f32[4,32,256]{2,1,0:T(8,128)}, u32[]{:S(2)}) %copy-start) | copy-done | bytes 131096
  0.9 0.2 edge.1
  1.1 0.5 %collective-permute-start = (f32[72,256]{1,0:T(8,128)S(1)}, f32[72,256]{1,0:T(8,128)S(1)}, u32[]{:S(2)}, u32[]{:S(2)}) collective-permute-start(f32[72,256]{1,0:T(8,128)S(1)} %get-tuple-element.15), channel_id=1, source_target_pairs={{0,4},{4,0},{8,12},{12,8},{16,20},{20,16},{24,28},{28,24},{1,5},{5... | collective-permute-start | bytes 221192 | tf_op jit(solution)/shard_map/ppermute | solution.py:303
  1.6 3.6 %collective-permute-start.1 = (f32[72,256]{1,0:T(8,128)S(1)}, f32[72,256]{1,0:T(8,128)S(1)}, u32[]{:S(2)}, u32[]{:S(2)}) collective-permute-start(f32[72,256]{1,0:T(8,128)S(1)} %get-tuple-element.16), channel_id=1, source_target_pairs={{4,8},{8,4},{12,16},{16,12},{20,24},{24,20},{28,0},{0,28},{5,9},{9... | collective-permute-start | bytes 221192 | tf_op jit(solution)/shard_map/ppermute | solution.py:303
  5.1 0.0 copy-start.1
  5.1 0.2 collective-permute-start.2
  5.4 0.3 %collective-permute-start.3 = (f32[8,128]{1,0:T(8,128)S(1)}, f32[8,128]{1,0:T(8,128)S(1)}, u32[]{:S(2)}, u32[]{:S(2)}) collective-permute-start(f32[8,128]{1,0:T(8,128)S(1)} %get-tuple-element.17.own_ref), channel_id=1, source_target_pairs={{0,16},{4,20},{8,24},{12,28},{16,0},{20,4},{24,8},{28,12},{1,17},{... | collective-permute-start | bytes 12296 | tf_op jit(solution)/shard_map/ppermute | solution.py:295
  5.7 2.5 %collective-permute-done.2.three_ref = f32[8,128]{1,0:T(8,128)S(1)} collective-permute-done((f32[8,128]{1,0:T(8,128)S(1)}, f32[8,128]{1,0:T(8,128)S(1)}, u32[]{:S(2)}, u32[]{:S(2)}) %collective-permute-start.2) | collective-permute-done | bytes 4128 | tf_op jit(solution)/shard_map/ppermute | solution.py:307
  8.2 0.8 %collective-permute-done.3.four_ref = f32[8,128]{1,0:T(8,128)S(1)} collective-permute-done((f32[8,128]{1,0:T(8,128)S(1)}, f32[8,128]{1,0:T(8,128)S(1)}, u32[]{:S(2)}, u32[]{:S(2)}) %collective-permute-start.3) | collective-permute-done | bytes 4128 | tf_op jit(solution)/shard_map/ppermute | solution.py:295
  9.0 0.0 collective-permute-done.swap_ref
  9.0 0.0 collective-permute-done.1.next_ref
  9.0 0.1 pack.1
  9.1 1.6 %collective-permute-start.4 = (f32[40,128]{1,0:T(8,128)S(1)}, f32[40,128]{1,0:T(8,128)S(1)}, u32[]{:S(2)}, u32[]{:S(2)}) collective-permute-start(f32[40,128]{1,0:T(8,128)S(1)} %get-tuple-element.20), channel_id=1, source_target_pairs={{0,1},{1,0},{2,3},{3,2},{4,5},{5,4},{6,7},{7,6},{8,9},{9,8},{10,11... | collective-permute-start | bytes 61448 | tf_op jit(solution)/shard_map/ppermute | solution.py:303
  10.8 2.5 %collective-permute-start.5 = (f32[40,128]{1,0:T(8,128)S(1)}, f32[40,128]{1,0:T(8,128)S(1)}, u32[]{:S(2)}, u32[]{:S(2)}) collective-permute-start(f32[40,128]{1,0:T(8,128)S(1)} %get-tuple-element.21), channel_id=1, source_target_pairs={{1,2},{2,1},{3,0},{0,3},{5,6},{6,5},{7,4},{4,7},{9,10},{10,9},{11,... | collective-permute-start | bytes 61448 | tf_op jit(solution)/shard_map/ppermute | solution.py:303
  13.2 0.1 collective-permute-start.6
  13.4 4.4 %collective-permute-done.6 = f32[8,128]{1,0:T(8,128)S(1)} collective-permute-done((f32[8,128]{1,0:T(8,128)S(1)}, f32[8,128]{1,0:T(8,128)S(1)}, u32[]{:S(2)}, u32[]{:S(2)}) %collective-permute-start.6) | collective-permute-done | bytes 4128 | tf_op jit(solution)/shard_map/ppermute | solution.py:295
  17.7 0.0 collective-permute-done.4.swap_ref
  17.7 0.0 collective-permute-done.5.next_ref
  17.8 0.1 collective-permute-start.7
  17.8 0.0 copy-done.1
  17.8 1.3 %first.1 = (f32[4,8,3,8,128]{4,3,2,1,0:T(8,128)S(1)}, f32[4,8,3,8,128]{4,3,2,1,0:T(8,128)S(1)}) custom-call(f32[4,32,256]{2,1,0:T(8,128)S(1)} %copy-done.1, f32[72,256]{1,0:T(8,128)S(1)} %get-tuple-element.18.up_ref, f32[72,256]{1,0:T(8,128)S(1)} %get-tuple-element.19.down_ref, f32[40,128]{1,0:T(8,128)S(1)} %collective-permute-done.4.swap_ref, ...), custom_call_target="tpu_custom_call" | custom-call | flops 20000000 | bytes 2000000 | tf_op jit(solution)/shard_map/first/pallas_call | solution.py:342
  19.1 0.0 collective-permute-done.7.far_ref
  19.2 5.3 %steps.1 = f32[4,32,256]{2,1,0:T(8,128)} custom-call(f32[4,8,3,8,128]{4,3,2,1,0:T(8,128)S(1)} %get-tuple-element.22.field_ref, f32[4,8,3,8,128]{4,3,2,1,0:T(8,128)S(1)} %get-tuple-element.23.change_ref, f32[8,128]{1,0:T(8,128)S(1)} %fusion.own_ref, f32[8,128]{1,0:T(8,128)S(1)} %collective-permute-done.7.far_ref), custom_call_target="tpu_custom_call" | custom-call | tf_op jit(solution)/shard_map/steps/pallas_call | solution.py:352
  (1 shorter events, 0.0 us)
Async XLA Ops:
  0.0 0.9 %copy-start = (f32[4,32,256]{2,1,0:T(8,128)S(1)}, f32[4,32,256]{2,1,0:T(8,128)}, u32[]{:S(2)}) copy-start(f32[4,32,256]{2,1,0:T(8,128)} %state_ref.3) | copy-start | bytes 393220
  1.1 7.9 %collective-permute-start = (f32[72,256]{1,0:T(8,128)S(1)}, f32[72,256]{1,0:T(8,128)S(1)}, u32[]{:S(2)}, u32[]{:S(2)}) collective-permute-start(f32[72,256]{1,0:T(8,128)S(1)} %get-tuple-element.15), channel_id=1, source_target_pairs={{0,4},{4,0},{8,12},{12,8},{16,20},{20,16},{24,28},{28,24},{1,5},{5... | collective-permute-start | bytes 221192 | tf_op jit(solution)/shard_map/ppermute | solution.py:303
  1.6 7.4 %collective-permute-start.1 = (f32[72,256]{1,0:T(8,128)S(1)}, f32[72,256]{1,0:T(8,128)S(1)}, u32[]{:S(2)}, u32[]{:S(2)}) collective-permute-start(f32[72,256]{1,0:T(8,128)S(1)} %get-tuple-element.16), channel_id=1, source_target_pairs={{4,8},{8,4},{12,16},{16,12},{20,24},{24,20},{28,0},{0,28},{5,9},{9... | collective-permute-start | bytes 221192 | tf_op jit(solution)/shard_map/ppermute | solution.py:303
  5.1 12.7 %copy-start.1 = (f32[4,32,256]{2,1,0:T(8,128)S(1)}, f32[4,32,256]{2,1,0:T(8,128)}, u32[]{:S(2)}) copy-start(f32[4,32,256]{2,1,0:T(8,128)} %state_ref.3) | copy-start | bytes 393220
  5.1 3.0 %collective-permute-start.2 = (f32[8,128]{1,0:T(8,128)S(1)}, f32[8,128]{1,0:T(8,128)S(1)}, u32[]{:S(2)}, u32[]{:S(2)}) collective-permute-start(f32[8,128]{1,0:T(8,128)S(1)} %get-tuple-element.17.own_ref), channel_id=1, source_target_pairs={{0,12},{4,24},{8,20},{12,0},{16,28},{20,8},{24,4},{28,16},{1,13},{... | collective-permute-start | bytes 12296 | tf_op jit(solution)/shard_map/ppermute | solution.py:307
  5.4 3.6 %collective-permute-start.3 = (f32[8,128]{1,0:T(8,128)S(1)}, f32[8,128]{1,0:T(8,128)S(1)}, u32[]{:S(2)}, u32[]{:S(2)}) collective-permute-start(f32[8,128]{1,0:T(8,128)S(1)} %get-tuple-element.17.own_ref), channel_id=1, source_target_pairs={{0,16},{4,20},{8,24},{12,28},{16,0},{20,4},{24,8},{28,12},{1,17},{... | collective-permute-start | bytes 12296 | tf_op jit(solution)/shard_map/ppermute | solution.py:295
  9.1 8.6 %collective-permute-start.4 = (f32[40,128]{1,0:T(8,128)S(1)}, f32[40,128]{1,0:T(8,128)S(1)}, u32[]{:S(2)}, u32[]{:S(2)}) collective-permute-start(f32[40,128]{1,0:T(8,128)S(1)} %get-tuple-element.20), channel_id=1, source_target_pairs={{0,1},{1,0},{2,3},{3,2},{4,5},{5,4},{6,7},{7,6},{8,9},{9,8},{10,11... | collective-permute-start | bytes 61448 | tf_op jit(solution)/shard_map/ppermute | solution.py:303
  10.8 7.0 %collective-permute-start.5 = (f32[40,128]{1,0:T(8,128)S(1)}, f32[40,128]{1,0:T(8,128)S(1)}, u32[]{:S(2)}, u32[]{:S(2)}) collective-permute-start(f32[40,128]{1,0:T(8,128)S(1)} %get-tuple-element.21), channel_id=1, source_target_pairs={{1,2},{2,1},{3,0},{0,3},{5,6},{6,5},{7,4},{4,7},{9,10},{10,9},{11,... | collective-permute-start | bytes 61448 | tf_op jit(solution)/shard_map/ppermute | solution.py:303
  13.2 4.5 %collective-permute-start.6 = (f32[8,128]{1,0:T(8,128)S(1)}, f32[8,128]{1,0:T(8,128)S(1)}, u32[]{:S(2)}, u32[]{:S(2)}) collective-permute-start(f32[8,128]{1,0:T(8,128)S(1)} %get-tuple-element.24), channel_id=1, source_target_pairs={{0,2},{1,3},{2,0},{3,1},{4,6},{5,7},{6,4},{7,5},{8,10},{9,11},{10,... | collective-permute-start | bytes 12296 | tf_op jit(solution)/shard_map/ppermute | solution.py:295
  17.8 1.4 %collective-permute-start.7 = (f32[8,128]{1,0:T(8,128)S(1)}, f32[8,128]{1,0:T(8,128)S(1)}, u32[]{:S(2)}, u32[]{:S(2)}) collective-permute-start(f32[8,128]{1,0:T(8,128)S(1)} %fusion.own_ref), channel_id=1, source_target_pairs={{0,4},{4,0},{8,12},{12,8},{16,20},{20,16},{24,28},{28,24},{1,5},{5... | collective-permute-start | bytes 12296 | tf_op jit(solution)/shard_map/ppermute | solution.py:295

commit v7 on v5

--- a/solution.py
+++ b/solution.py
@@ -129,58 +129,93 @@
     return [first[comp] - second[comp] for comp in range(4)]
 
 
-def sweep(load, store, count, axis):
-    def rolled(tree, by):
-        return jax.tree.map(lambda value: pltpu.roll(value, by % value.shape[axis], axis=axis), tree)
-
-    def half(parts):
-        return [0.5 * part for part in parts]
-
-    here = load(0)
-    end_jump = half(minus(rolled(here, -1), load(count - 1)))
-    jump = rolled(end_jump, 1)
+def half(parts):
+    return [0.5 * part for part in parts]
+
+
+def rolled(tree, by, axis):
+    return jax.tree.map(lambda value: pltpu.roll(value, by % value.shape[axis], axis=axis), tree)
+
+
+def cell(here, jump_before, jump_after):
+    slope = [minmod(jump_before[comp], jump_after[comp]) for comp in range(4)]
+    low = minus(here, slope)
+    high = [here[comp] + slope[comp] for comp in range(4)]
+    return (low, *fluxes(low)), (high, *fluxes(high))
+
+
+def row_changes(values):
+    count = len(values)
+    end_jump = half(minus(rolled(values[0], -1, 1), values[-1]))
+    jumps = [half(minus(values[at + 1], values[at])) for at in range(count - 1)] + [end_jump]
+    faces, first_low, high = [], None, None
     for at in range(count):
-        after = load(at + 1) if at + 1 < count else None
-        next_jump = half(minus(after, here)) if at + 1 < count else end_jump
-        slope = [minmod(jump[comp], next_jump[comp]) for comp in range(4)]
-        low_state = minus(here, slope)
-        high_state = [here[comp] + slope[comp] for comp in range(4)]
-        low = (low_state, *fluxes(low_state))
-        if at == 0:
+        low, next_high = cell(values[at], jumps[at - 1] if at else rolled(end_jump, 1, 1), jumps[at])
+        if at:
+            faces.append(face(high, low))
+        else:
             first_low = low
+        high = next_high
+    faces.append(face(high, rolled(first_low, -1, 1)))
+    return [minus(faces[at], faces[at - 1] if at else rolled(faces[-1], 1, 1)) for at in range(count)]
+
+
+class Column:
+    def __init__(self, count, begin, here, after):
+        self.count, self.begin = count, begin
+        self.jump = self.first_jump = half(minus(after, here))
+        self.first_low = self.first_flux = self.last_flux = self.high = None
+
+    def feed(self, row, here, after):
+        next_row = (row + 1) % self.count
+        if after is None:
+            next_jump = self.first_jump
         else:
-            flux = face(high, low)
-            if at == 1:
-                first_flux = flux
+            next_jump = half(minus(rolled(after, -1, 0) if next_row == 0 else after, here))
+        jump = rolled(self.jump, 1, 0) if row == 0 else self.jump
+        low, high = cell(here, jump, next_jump)
+        done = []
+        if self.first_low is None:
+            self.first_low = low
+        else:
+            flux = face(rolled(self.high, 1, 0) if row == 0 else self.high, low)
+            if self.last_flux is None:
+                self.first_flux = flux
             else:
-                store(at - 1, minus(flux, last_flux))
-            last_flux = flux
-        high = (high_state, *fluxes(high_state))
-        here, jump = after, next_jump
-    flux = face(high, rolled(first_low, -1))
-    store(count - 1, minus(flux, last_flux))
-    store(0, minus(first_flux, rolled(flux, 1)))
-
-
-X_ORDER = (0, 1, 2, 3)
+                seen = rolled(flux, -1, 0) if row == 0 else flux
+                done.append(((row - 1) % self.count, minus(seen, self.last_flux)))
+            self.last_flux = flux
+        self.high, self.jump = high, next_jump
+        if after is None:
+            flux = face(high, self.first_low)
+            done.append((row, minus(flux, self.last_flux)))
+            done.append(((row + 1) % self.count, minus(self.first_flux, flux)))
+        return done
+
+
 Y_ORDER = (0, 2, 1, 3)
 
 
-def changes(src, diff, rows, cols, store):
-    for col in range(cols):
-        def keep(row, parts, col=col):
-            for comp in range(4):
-                diff[comp, row, col] = parts[comp]
-
-        sweep(lambda row, col=col: [src[comp, row, col] for comp in X_ORDER], keep, rows, 0)
-    for row in range(rows):
-        def add(col, parts, row=row):
-            store(row, col, [parts[Y_ORDER[comp]] + diff[comp, row, col] for comp in range(4)])
-
-        sweep(lambda col, row=row: [src[comp, row, col] for comp in Y_ORDER], add, cols, 1)
-
-
-def first_kernel(state_ref, up_ref, down_ref, swap_ref, next_ref, field_ref, change_ref, plain, dealt, diff):
+def changes(load, rows, cols, begin, store):
+    along_y = {}
+    values = {at: [load((begin + at) % rows, col) for col in range(cols)] for at in range(2)}
+    columns = [Column(rows, begin, values[0][col], values[1][col]) for col in range(cols)]
+    for at in range(1, rows + 1):
+        row = (begin + at) % rows
+        here = values.pop(at)
+        if at < rows:
+            values[at + 1] = [load((row + 1) % rows, col) for col in range(cols)]
+        ready = []
+        for col in range(cols):
+            after = values[at + 1][col] if at < rows else None
+            ready += [(col, *item) for item in columns[col].feed(row, here[col], after)]
+        along_y[row] = row_changes([[part[comp] for comp in Y_ORDER] for part in here])
+        for col, done, parts in ready:
+            other = along_y[done][col]
+            store(done, col, [parts[comp] + other[Y_ORDER[comp]] for comp in range(4)])
+
+
+def first_kernel(state_ref, up_ref, down_ref, swap_ref, next_ref, field_ref, change_ref, plain, dealt):
     rows, cols = state_ref.shape[1:]
     tall = rows + 2 * HALO
     half = tall // 2
@@ -225,10 +260,13 @@
         for comp in range(4):
             change_ref[comp, row, col] = parts[comp]
 
-    changes(field_ref, diff, count, groups, store)
-
-
-def steps_kernel(field_ref, change_ref, own_ref, far_ref, out_ref, field, base, mid, diff, dealt):
+    def load(row, col):
+        return [field_ref[comp, row, col] for comp in range(4)]
+
+    changes(load, count, groups, 0, store)
+
+
+def steps_kernel(field_ref, change_ref, own_ref, far_ref, out_ref, field, base, mid, dealt):
     rows, cols = out_ref.shape[1:]
     tall = rows + 2 * HALO
     groups = field_ref.shape[2]
@@ -260,8 +298,8 @@
                 for row in range(count):
                     for col in range(groups):
                         field[comp, row, col] = dealt[comp, col, pl.ds(start + row, 8, stride=count), :]
-            changes(field, diff, count, groups, to_mid)
-        changes(mid, diff, count, groups, to_field)
+            changes(lambda row, col: [field[comp, row, col] for comp in range(4)], count, groups, 0, to_mid)
+        changes(lambda row, col: [mid[comp, row, col] for comp in range(4)], count, groups, count // 2, to_field)
 
     wide = groups * LANES
     source = iota((wide, cols), 0)
@@ -344,7 +382,7 @@
         out_shape=(dealt_type, dealt_type),
         in_specs=[VMEM] * 5,
         out_specs=(VMEM,) * 2,
-        scratch_shapes=[pltpu.VMEM((parts * tall, groups * LANES), jnp.float32), plain, dealt],
+        scratch_shapes=[pltpu.VMEM((parts * tall, groups * LANES), jnp.float32), plain],
         compiler_params=params(16),
         cost_estimate=pl.CostEstimate(flops=20_000_000, bytes_accessed=2_000_000, transcendentals=400_000),
         name="first",
@@ -354,7 +392,7 @@
         out_shape=array(parts, rows, cols),
         in_specs=[VMEM] * 4,
         out_specs=VMEM,
-        scratch_shapes=[dealt] * 4 + [plain],
+        scratch_shapes=[dealt] * 3 + [plain],
         compiler_params=params(16),
         name="steps",
     )(field, change, top, far)

time: 24.7 us -> 24.7 us (level)
  no operation moved by 1% of the time
where the time goes in v7:
time: 24.7 us; the launch traced here: 24.5 us
  starting transfers between devices  8.94 us (36%)
  waiting for transfers between devices  7.66 us (31%)
  Pallas kernels  6.9 us (28%)
  local copies, waits for them, and re-layouts  0.91 us (4%)
    ppermute x4, starting transfers between devices, swapped_pairs(): return lax.ppermute(value, axis, pairs)  8.19 us
    pallas_call x1, Pallas kernels, local(): pl.pallas_call(steps_kernel, out_shape=array(parts, rows, cols), in_specs...  5.33 us
    ppermute x3, waiting for transfers between devices, swapped_bit(): lax.ppermute(value, axis, [(i, i ^ by) for i in range(lax.axis_size(axis))])  5.19 us
    ppermute x1, waiting for transfers between devices, swapped_threes(): lax.ppermute(value, axis, [(i, (i + 3 - 6 * (i % 2)) % count) for i in ra...  2.47 us
    pallas_call x1, Pallas kernels, local(): pl.pallas_call(first_kernel, out_shape=(dealt_type, dealt_type), in_specs...  1.28 us
    unnamed x4, local copies, waits for them, and re-layouts  0.91 us
    ppermute x3, starting transfers between devices, swapped_bit(): lax.ppermute(value, axis, [(i, i ^ by) for i in range(lax.axis_size(axis))])  0.54 us
  transfers between devices with their start and end apart: 8, of which 3 were waited for; matrix products, arithmetic and copies ran while one was open for 0% of the time, Pallas kernels for 5%

profile of v7, /device:TPU:0, one launch (start us, length us, event | category | flops | bytes accessed | tf_op | source)
XLA Modules:
  0.0 24.5 jit_solution(12315964439730315364)
XLA Ops:
  0.0 0.0 copy-start
  0.0 0.9 %copy-done = f32[4,32,256]{2,1,0:T(8,128)S(1)} copy-done((f32[4,32,256]{2,1,0:T(8,128)S(1)}, f32[4,32,256]{2,1,0:T(8,128)}, u32[]{:S(2)}) %copy-start) | copy-done | bytes 131096
  0.9 0.2 edge.1
  1.1 0.5 %collective-permute-start = (f32[72,256]{1,0:T(8,128)S(1)}, f32[72,256]{1,0:T(8,128)S(1)}, u32[]{:S(2)}, u32[]{:S(2)}) collective-permute-start(f32[72,256]{1,0:T(8,128)S(1)} %get-tuple-element.15), channel_id=1, source_target_pairs={{0,4},{4,0},{8,12},{12,8},{16,20},{20,16},{24,28},{28,24},{1,5},{5... | collective-permute-start | bytes 221192 | tf_op jit(solution)/shard_map/ppermute | solution.py:341
  1.6 3.6 %collective-permute-start.1 = (f32[72,256]{1,0:T(8,128)S(1)}, f32[72,256]{1,0:T(8,128)S(1)}, u32[]{:S(2)}, u32[]{:S(2)}) collective-permute-start(f32[72,256]{1,0:T(8,128)S(1)} %get-tuple-element.16), channel_id=1, source_target_pairs={{4,8},{8,4},{12,16},{16,12},{20,24},{24,20},{28,0},{0,28},{5,9},{9... | collective-permute-start | bytes 221192 | tf_op jit(solution)/shard_map/ppermute | solution.py:341
  5.1 0.0 copy-start.1
  5.1 0.2 collective-permute-start.2
  5.4 0.3 %collective-permute-start.3 = (f32[8,128]{1,0:T(8,128)S(1)}, f32[8,128]{1,0:T(8,128)S(1)}, u32[]{:S(2)}, u32[]{:S(2)}) collective-permute-start(f32[8,128]{1,0:T(8,128)S(1)} %get-tuple-element.17.own_ref), channel_id=1, source_target_pairs={{0,16},{4,20},{8,24},{12,28},{16,0},{20,4},{24,8},{28,12},{1,17},{... | collective-permute-start | bytes 12296 | tf_op jit(solution)/shard_map/ppermute | solution.py:333
  5.7 2.5 %collective-permute-done.2.three_ref = f32[8,128]{1,0:T(8,128)S(1)} collective-permute-done((f32[8,128]{1,0:T(8,128)S(1)}, f32[8,128]{1,0:T(8,128)S(1)}, u32[]{:S(2)}, u32[]{:S(2)}) %collective-permute-start.2) | collective-permute-done | bytes 4128 | tf_op jit(solution)/shard_map/ppermute | solution.py:345
  8.2 0.8 %collective-permute-done.3.four_ref = f32[8,128]{1,0:T(8,128)S(1)} collective-permute-done((f32[8,128]{1,0:T(8,128)S(1)}, f32[8,128]{1,0:T(8,128)S(1)}, u32[]{:S(2)}, u32[]{:S(2)}) %collective-permute-start.3) | collective-permute-done | bytes 4128 | tf_op jit(solution)/shard_map/ppermute | solution.py:333
  9.0 0.0 collective-permute-done.swap_ref
  9.0 0.0 collective-permute-done.1.next_ref
  9.0 0.1 pack.1
  9.1 1.6 %collective-permute-start.4 = (f32[40,128]{1,0:T(8,128)S(1)}, f32[40,128]{1,0:T(8,128)S(1)}, u32[]{:S(2)}, u32[]{:S(2)}) collective-permute-start(f32[40,128]{1,0:T(8,128)S(1)} %get-tuple-element.20), channel_id=1, source_target_pairs={{0,1},{1,0},{2,3},{3,2},{4,5},{5,4},{6,7},{7,6},{8,9},{9,8},{10,11... | collective-permute-start | bytes 61448 | tf_op jit(solution)/shard_map/ppermute | solution.py:341
  10.8 2.5 %collective-permute-start.5 = (f32[40,128]{1,0:T(8,128)S(1)}, f32[40,128]{1,0:T(8,128)S(1)}, u32[]{:S(2)}, u32[]{:S(2)}) collective-permute-start(f32[40,128]{1,0:T(8,128)S(1)} %get-tuple-element.21), channel_id=1, source_target_pairs={{1,2},{2,1},{3,0},{0,3},{5,6},{6,5},{7,4},{4,7},{9,10},{10,9},{11,... | collective-permute-start | bytes 61448 | tf_op jit(solution)/shard_map/ppermute | solution.py:341
  13.2 0.1 collective-permute-start.6
  13.4 4.4 %collective-permute-done.6 = f32[8,128]{1,0:T(8,128)S(1)} collective-permute-done((f32[8,128]{1,0:T(8,128)S(1)}, f32[8,128]{1,0:T(8,128)S(1)}, u32[]{:S(2)}, u32[]{:S(2)}) %collective-permute-start.6) | collective-permute-done | bytes 4128 | tf_op jit(solution)/shard_map/ppermute | solution.py:333
  17.7 0.0 collective-permute-done.4.swap_ref
  17.7 0.0 collective-permute-done.5.next_ref
  17.8 0.1 collective-permute-start.7
  17.8 0.0 copy-done.1
  17.8 1.3 %first.1 = (f32[4,8,3,8,128]{4,3,2,1,0:T(8,128)S(1)}, f32[4,8,3,8,128]{4,3,2,1,0:T(8,128)S(1)}) custom-call(f32[4,32,256]{2,1,0:T(8,128)S(1)} %copy-done.1, f32[72,256]{1,0:T(8,128)S(1)} %get-tuple-element.18.up_ref, f32[72,256]{1,0:T(8,128)S(1)} %get-tuple-element.19.down_ref, f32[40,128]{1,0:T(8,128)S(1)} %collective-permute-done.4.swap_ref, ...), custom_call_target="tpu_custom_call" | custom-call | flops 20000000 | bytes 2000000 | tf_op jit(solution)/shard_map/first/pallas_call | solution.py:380
  19.1 0.0 collective-permute-done.7.far_ref
  19.1 5.3 %steps.1 = f32[4,32,256]{2,1,0:T(8,128)} custom-call(f32[4,8,3,8,128]{4,3,2,1,0:T(8,128)S(1)} %get-tuple-element.22.field_ref, f32[4,8,3,8,128]{4,3,2,1,0:T(8,128)S(1)} %get-tuple-element.23.change_ref, f32[8,128]{1,0:T(8,128)S(1)} %fusion.own_ref, f32[8,128]{1,0:T(8,128)S(1)} %collective-permute-done.7.far_ref), custom_call_target="tpu_custom_call" | custom-call | tf_op jit(solution)/shard_map/steps/pallas_call | solution.py:390
  (1 shorter events, 0.0 us)
Async XLA Ops:
  0.0 0.9 %copy-start = (f32[4,32,256]{2,1,0:T(8,128)S(1)}, f32[4,32,256]{2,1,0:T(8,128)}, u32[]{:S(2)}) copy-start(f32[4,32,256]{2,1,0:T(8,128)} %state_ref.3) | copy-start | bytes 393220
  1.1 7.9 %collective-permute-start = (f32[72,256]{1,0:T(8,128)S(1)}, f32[72,256]{1,0:T(8,128)S(1)}, u32[]{:S(2)}, u32[]{:S(2)}) collective-permute-start(f32[72,256]{1,0:T(8,128)S(1)} %get-tuple-element.15), channel_id=1, source_target_pairs={{0,4},{4,0},{8,12},{12,8},{16,20},{20,16},{24,28},{28,24},{1,5},{5... | collective-permute-start | bytes 221192 | tf_op jit(solution)/shard_map/ppermute | solution.py:341
  1.6 7.4 %collective-permute-start.1 = (f32[72,256]{1,0:T(8,128)S(1)}, f32[72,256]{1,0:T(8,128)S(1)}, u32[]{:S(2)}, u32[]{:S(2)}) collective-permute-start(f32[72,256]{1,0:T(8,128)S(1)} %get-tuple-element.16), channel_id=1, source_target_pairs={{4,8},{8,4},{12,16},{16,12},{20,24},{24,20},{28,0},{0,28},{5,9},{9... | collective-permute-start | bytes 221192 | tf_op jit(solution)/shard_map/ppermute | solution.py:341
  5.1 12.7 %copy-start.1 = (f32[4,32,256]{2,1,0:T(8,128)S(1)}, f32[4,32,256]{2,1,0:T(8,128)}, u32[]{:S(2)}) copy-start(f32[4,32,256]{2,1,0:T(8,128)} %state_ref.3) | copy-start | bytes 393220
  5.1 3.0 %collective-permute-start.2 = (f32[8,128]{1,0:T(8,128)S(1)}, f32[8,128]{1,0:T(8,128)S(1)}, u32[]{:S(2)}, u32[]{:S(2)}) collective-permute-start(f32[8,128]{1,0:T(8,128)S(1)} %get-tuple-element.17.own_ref), channel_id=1, source_target_pairs={{0,12},{4,24},{8,20},{12,0},{16,28},{20,8},{24,4},{28,16},{1,13},{... | collective-permute-start | bytes 12296 | tf_op jit(solution)/shard_map/ppermute | solution.py:345
  5.4 3.6 %collective-permute-start.3 = (f32[8,128]{1,0:T(8,128)S(1)}, f32[8,128]{1,0:T(8,128)S(1)}, u32[]{:S(2)}, u32[]{:S(2)}) collective-permute-start(f32[8,128]{1,0:T(8,128)S(1)} %get-tuple-element.17.own_ref), channel_id=1, source_target_pairs={{0,16},{4,20},{8,24},{12,28},{16,0},{20,4},{24,8},{28,12},{1,17},{... | collective-permute-start | bytes 12296 | tf_op jit(solution)/shard_map/ppermute | solution.py:333
  9.1 8.6 %collective-permute-start.4 = (f32[40,128]{1,0:T(8,128)S(1)}, f32[40,128]{1,0:T(8,128)S(1)}, u32[]{:S(2)}, u32[]{:S(2)}) collective-permute-start(f32[40,128]{1,0:T(8,128)S(1)} %get-tuple-element.20), channel_id=1, source_target_pairs={{0,1},{1,0},{2,3},{3,2},{4,5},{5,4},{6,7},{7,6},{8,9},{9,8},{10,11... | collective-permute-start | bytes 61448 | tf_op jit(solution)/shard_map/ppermute | solution.py:341
  10.8 7.0 %collective-permute-start.5 = (f32[40,128]{1,0:T(8,128)S(1)}, f32[40,128]{1,0:T(8,128)S(1)}, u32[]{:S(2)}, u32[]{:S(2)}) collective-permute-start(f32[40,128]{1,0:T(8,128)S(1)} %get-tuple-element.21), channel_id=1, source_target_pairs={{1,2},{2,1},{3,0},{0,3},{5,6},{6,5},{7,4},{4,7},{9,10},{10,9},{11,... | collective-permute-start | bytes 61448 | tf_op jit(solution)/shard_map/ppermute | solution.py:341
  13.2 4.5 %collective-permute-start.6 = (f32[8,128]{1,0:T(8,128)S(1)}, f32[8,128]{1,0:T(8,128)S(1)}, u32[]{:S(2)}, u32[]{:S(2)}) collective-permute-start(f32[8,128]{1,0:T(8,128)S(1)} %get-tuple-element.24), channel_id=1, source_target_pairs={{0,2},{1,3},{2,0},{3,1},{4,6},{5,7},{6,4},{7,5},{8,10},{9,11},{10,... | collective-permute-start | bytes 12296 | tf_op jit(solution)/shard_map/ppermute | solution.py:333
  17.8 1.4 %collective-permute-start.7 = (f32[8,128]{1,0:T(8,128)S(1)}, f32[8,128]{1,0:T(8,128)S(1)}, u32[]{:S(2)}, u32[]{:S(2)}) collective-permute-start(f32[8,128]{1,0:T(8,128)S(1)} %fusion.own_ref), channel_id=1, source_target_pairs={{0,4},{4,0},{8,12},{12,8},{16,20},{20,16},{24,28},{28,24},{1,5},{5... | collective-permute-start | bytes 12296 | tf_op jit(solution)/shard_map/ppermute | solution.py:333

commit v8 on v7

--- a/solution.py
+++ b/solution.py
@@ -52,7 +52,7 @@
     top_ref[...] = jnp.full(top_ref.shape, top)
 
 
-def pack_kernel(state_ref, swap_ref, next_ref, own_ref, three_ref, four_ref, up_ref, down_ref, first_ref, second_ref, top_ref):
+def pack_kernel(state_ref, next_ref, three_ref, four_ref, swap_ref, own_ref, up_ref, down_ref, first_ref, second_ref, top_ref):
     rows = state_ref.shape[1]
     cols = state_ref.shape[2]
     half = rows // 2 + HALO
@@ -215,7 +215,7 @@
             store(done, col, [parts[comp] + other[Y_ORDER[comp]] for comp in range(4)])
 
 
-def first_kernel(state_ref, up_ref, down_ref, swap_ref, next_ref, field_ref, change_ref, plain, dealt):
+def first_kernel(state_ref, up_ref, down_ref, next_ref, far_ref, swap_ref, own_ref, field_ref, change_ref, top_ref, plain, dealt):
     rows, cols = state_ref.shape[1:]
     tall = rows + 2 * HALO
     half = tall // 2
@@ -229,6 +229,7 @@
         plain[low + HALO + rows : low + tall, 0:cols] = down_ref[span, :]
     lane = iota((half, LANES), 1)
     is_odd = odd("gy")
+    top_ref[...] = jnp.maximum(jnp.maximum(own_ref[...], far_ref[...]), jnp.maximum(next_ref[half:, :], swap_ref[half:, :]))
     from_swap = swap_ref[0:half, :]
     from_next = next_ref[0:half, :]
     from_before = jnp.where(is_odd, from_swap, from_next)
@@ -266,17 +267,13 @@
     changes(load, count, groups, 0, store)
 
 
-def steps_kernel(field_ref, change_ref, own_ref, far_ref, out_ref, field, base, mid, dealt):
+def steps_kernel(field_ref, change_ref, own_ref, mate_ref, wide_ref, out_ref, field, base, mid, dealt):
     rows, cols = out_ref.shape[1:]
     tall = rows + 2 * HALO
     groups = field_ref.shape[2]
-    half_factor = -0.25 * COURANT / jnp.maximum(own_ref[...], far_ref[...])
-
-    for index in range(STEPS):
-        start = 4 * index
-        count = (tall - 8 * index) // 8
-        old = field_ref if index == 0 else field
-
+    half_factor = -0.25 * COURANT / jnp.maximum(own_ref[...], jnp.maximum(mate_ref[...], wide_ref[...]))
+
+    def one_step(start, count, old, first_changes):
         def to_mid(row, col, parts):
             for comp in range(4):
                 move = half_factor * parts[comp]
@@ -289,17 +286,28 @@
                 new = base[comp, row, col] + half_factor * parts[comp]
                 dealt[comp, col, pl.ds(start + row, 8, stride=count), :] = new
 
-        if index == 0:
+        def load_from(ref):
+            return lambda row, col: [ref[comp, row, col] for comp in range(4)]
+
+        if first_changes is not None:
             for row in range(count):
                 for col in range(groups):
-                    to_mid(row, col, [change_ref[comp, row, col] for comp in range(4)])
+                    to_mid(row, col, [first_changes[comp, row, col] for comp in range(4)])
         else:
             for comp in range(4):
                 for row in range(count):
                     for col in range(groups):
-                        field[comp, row, col] = dealt[comp, col, pl.ds(start + row, 8, stride=count), :]
-            changes(lambda row, col: [field[comp, row, col] for comp in range(4)], count, groups, 0, to_mid)
-        changes(lambda row, col: [mid[comp, row, col] for comp in range(4)], count, groups, count // 2, to_field)
+                        old[comp, row, col] = dealt[comp, col, pl.ds(start + row, 8, stride=count), :]
+            changes(load_from(old), count, groups, 0, to_mid)
+        changes(load_from(mid), count, groups, count // 2, to_field)
+
+    def looped(_, none):
+        one_step(8, (tall - 16) // 8, field, None)
+        return none
+
+    one_step(0, tall // 8, field_ref, change_ref)
+    one_step(4, (tall - 8) // 8, field, None)
+    lax.fori_loop(2, STEPS, looped, None)
 
     wide = groups * LANES
     source = iota((wide, cols), 0)
@@ -364,38 +372,39 @@
         out_specs=(VMEM,) * 5,
         compiler_params=params(4),
         name="pack",
-    )(state, first, second, top, *far)
+    )(state, second, *far, first, top)
     second = swapped_pairs(second, "gy", 1)
     first = swapped_pairs(first, "gy", 0)
     far = swapped_bit(top, "gy", 2)
-    top = jnp.maximum(jnp.maximum(top, far), jnp.maximum(first[tall // 2 :], second[tall // 2 :]))
+    own = top
+    top = jnp.maximum(jnp.maximum(own, far), jnp.maximum(first[tall // 2 :], second[tall // 2 :]))
     for axis, covered in (("gy", 4), ("gx", 8)):
         while covered < lax.axis_size(axis):
             top = jnp.maximum(top, sent(top, axis, covered))
             covered *= 2
-    far = swapped_bit(top, "gx", 1)
+    top = swapped_bit(top, "gx", 1), top
     dealt_type = array(parts, tall // 8, groups, 8, LANES)
     dealt = pltpu.VMEM(dealt_type.shape, jnp.float32)
     plain = pltpu.VMEM((parts, groups, tall, LANES), jnp.float32)
-    field, change = pl.pallas_call(
+    field, change, own = pl.pallas_call(
         first_kernel,
-        out_shape=(dealt_type, dealt_type),
-        in_specs=[VMEM] * 5,
-        out_specs=(VMEM,) * 2,
+        out_shape=(dealt_type, dealt_type, array(8, LANES)),
+        in_specs=[VMEM] * 7,
+        out_specs=(VMEM,) * 3,
         scratch_shapes=[pltpu.VMEM((parts * tall, groups * LANES), jnp.float32), plain],
         compiler_params=params(16),
         cost_estimate=pl.CostEstimate(flops=20_000_000, bytes_accessed=2_000_000, transcendentals=400_000),
         name="first",
-    )(state, up, down, first, second)
+    )(state, up, down, second, far, first, own)
     return pl.pallas_call(
         steps_kernel,
         out_shape=array(parts, rows, cols),
-        in_specs=[VMEM] * 4,
+        in_specs=[VMEM] * 5,
         out_specs=VMEM,
         scratch_shapes=[dealt] * 3 + [plain],
         compiler_params=params(16),
         name="steps",
-    )(field, change, top, far)
+    )(field, change, own, *top)
 
 
 def solution(mesh):

time: 24.7 us -> 24.3 us (0.984)
  waiting for transfers between devices: 7.66 us -> 6.84 us
  starting transfers between devices: 8.94 us -> 9.24 us
    ppermute x4, starting transfers between devices: 8.19 us -> 7.07 us  [swapped_pairs(): return lax.ppermute(value, axis, pairs)]
    ppermute x3, starting transfers between devices: 0.54 us -> 1.35 us  [swapped_bit(): lax.ppermute(value, axis, [(i, i ^ by) for i in range(lax.axis_size(axis))])]
    ppermute x1, waiting for transfers between devices: 2.47 us -> 1.72 us  [swapped_threes(): lax.ppermute(value, axis, [(i, (i + 3 - 6 * (i % 2)) % count) for i in ra...]
    ppermute x1, starting transfers between devices: 0.22 us -> 0.82 us  [swapped_threes(): lax.ppermute(value, axis, [(i, (i + 3 - 6 * (i % 2)) % count) for i in ra...]
where the time goes in v8:
time: 24.3 us; the launch traced here: 24.1 us
  starting transfers between devices  9.24 us (38%)
  Pallas kernels  7.07 us (29%)
  waiting for transfers between devices  6.84 us (28%)
  local copies, waits for them, and re-layouts  0.91 us (4%)
    ppermute x4, starting transfers between devices, swapped_pairs(): return lax.ppermute(value, axis, pairs)  7.07 us
    pallas_call x1, Pallas kernels, local(): pl.pallas_call(steps_kernel, out_shape=array(parts, rows, cols), in_specs...  5.5 us
    ppermute x3, waiting for transfers between devices, swapped_bit(): lax.ppermute(value, axis, [(i, i ^ by) for i in range(lax.axis_size(axis))])  5.12 us
    ppermute x1, waiting for transfers between devices, swapped_threes(): lax.ppermute(value, axis, [(i, (i + 3 - 6 * (i % 2)) % count) for i in ra...  1.72 us
    ppermute x3, starting transfers between devices, swapped_bit(): lax.ppermute(value, axis, [(i, i ^ by) for i in range(lax.axis_size(axis))])  1.35 us
    pallas_call x1, Pallas kernels, local(): pl.pallas_call(first_kernel, out_shape=(dealt_type, dealt_type, array(8,...  1.28 us
    unnamed x4, local copies, waits for them, and re-layouts  0.91 us
    ppermute x1, starting transfers between devices, swapped_threes(): lax.ppermute(value, axis, [(i, (i + 3 - 6 * (i % 2)) % count) for i in ra...  0.82 us
  transfers between devices with their start and end apart: 8, of which 3 were waited for; matrix products, arithmetic and copies ran while one was open for 0% of the time, Pallas kernels for 5%

profile of v8, /device:TPU:0, one launch (start us, length us, event | category | flops | bytes accessed | tf_op | source)
XLA Modules:
  0.0 24.1 jit_solution(7121626234004357841)
XLA Ops:
  0.0 0.0 copy-start
  0.0 0.9 %copy-done = f32[4,32,256]{2,1,0:T(8,128)S(1)} copy-done((f32[4,32,256]{2,1,0:T(8,128)S(1)}, f32[4,32,256]{2,1,0:T(8,128)}, u32[]{:S(2)}) %copy-start) | copy-done | bytes 131096
  0.9 0.2 edge.1
  1.1 3.4 %collective-permute-start = (f32[72,256]{1,0:T(8,128)S(1)}, f32[72,256]{1,0:T(8,128)S(1)}, u32[]{:S(2)}, u32[]{:S(2)}) collective-permute-start(f32[72,256]{1,0:T(8,128)S(1)} %get-tuple-element.16), channel_id=1, source_target_pairs={{4,8},{8,4},{12,16},{16,12},{20,24},{24,20},{28,0},{0,28},{5,9},{9... | collective-permute-start | bytes 221192 | tf_op jit(solution)/shard_map/ppermute | solution.py:349
  4.5 0.0 collective-permute-start.3
  4.5 0.0 copy-start.1
  4.5 0.8 %collective-permute-start.1 = (f32[8,128]{1,0:T(8,128)S(1)}, f32[8,128]{1,0:T(8,128)S(1)}, u32[]{:S(2)}, u32[]{:S(2)}) collective-permute-start(f32[8,128]{1,0:T(8,128)S(1)} %get-tuple-element.17.own_ref), channel_id=1, source_target_pairs={{0,12},{4,24},{8,20},{12,0},{16,28},{20,8},{24,4},{28,16},{1,13},{... | collective-permute-start | bytes 12296 | tf_op jit(solution)/shard_map/ppermute | solution.py:353
  5.3 0.5 %collective-permute-start.2 = (f32[8,128]{1,0:T(8,128)S(1)}, f32[8,128]{1,0:T(8,128)S(1)}, u32[]{:S(2)}, u32[]{:S(2)}) collective-permute-start(f32[8,128]{1,0:T(8,128)S(1)} %get-tuple-element.17.own_ref), channel_id=1, source_target_pairs={{0,16},{4,20},{8,24},{12,28},{16,0},{20,4},{24,8},{28,12},{1,17},{... | collective-permute-start | bytes 12296 | tf_op jit(solution)/shard_map/ppermute | solution.py:341
  5.8 1.7 %collective-permute-done.1.three_ref = f32[8,128]{1,0:T(8,128)S(1)} collective-permute-done((f32[8,128]{1,0:T(8,128)S(1)}, f32[8,128]{1,0:T(8,128)S(1)}, u32[]{:S(2)}, u32[]{:S(2)}) %collective-permute-start.1) | collective-permute-done | bytes 4128 | tf_op jit(solution)/shard_map/ppermute | solution.py:353
  7.5 1.4 %collective-permute-done.2.four_ref = f32[8,128]{1,0:T(8,128)S(1)} collective-permute-done((f32[8,128]{1,0:T(8,128)S(1)}, f32[8,128]{1,0:T(8,128)S(1)}, u32[]{:S(2)}, u32[]{:S(2)}) %collective-permute-start.2) | collective-permute-done | bytes 4128 | tf_op jit(solution)/shard_map/ppermute | solution.py:341
  8.9 0.0 collective-permute-done.next_ref
  8.9 0.0 collective-permute-done.3.swap_ref
  8.9 0.1 pack.1
  9.0 3.7 %collective-permute-start.4 = (f32[40,128]{1,0:T(8,128)S(1)}, f32[40,128]{1,0:T(8,128)S(1)}, u32[]{:S(2)}, u32[]{:S(2)}) collective-permute-start(f32[40,128]{1,0:T(8,128)S(1)} %get-tuple-element.21), channel_id=1, source_target_pairs={{1,2},{2,1},{3,0},{0,3},{5,6},{6,5},{7,4},{4,7},{9,10},{10,9},{11,... | collective-permute-start | bytes 61448 | tf_op jit(solution)/shard_map/ppermute | solution.py:349
  12.7 0.0 collective-permute-start.6
  12.7 0.8 %collective-permute-start.5 = (f32[8,128]{1,0:T(8,128)S(1)}, f32[8,128]{1,0:T(8,128)S(1)}, u32[]{:S(2)}, u32[]{:S(2)}) collective-permute-start(f32[8,128]{1,0:T(8,128)S(1)} %get-tuple-element.22.own_ref), channel_id=1, source_target_pairs={{0,2},{1,3},{2,0},{3,1},{4,6},{5,7},{6,4},{7,5},{8,10},{9,11},{10,... | collective-permute-start | bytes 12296 | tf_op jit(solution)/shard_map/ppermute | solution.py:341
  13.5 3.7 %collective-permute-done.5.far_ref = f32[8,128]{1,0:T(8,128)S(1)} collective-permute-done((f32[8,128]{1,0:T(8,128)S(1)}, f32[8,128]{1,0:T(8,128)S(1)}, u32[]{:S(2)}, u32[]{:S(2)}) %collective-permute-start.5) | collective-permute-done | bytes 4128 | tf_op jit(solution)/shard_map/ppermute | solution.py:341
  17.2 0.0 collective-permute-done.4.next_ref
  17.2 0.0 collective-permute-done.6.swap_ref
  17.2 0.1 collective-permute-start.7
  17.3 0.0 copy-done.1
  17.3 1.3 %first.1 = (f32[4,8,3,8,128]{4,3,2,1,0:T(8,128)S(1)}, f32[4,8,3,8,128]{4,3,2,1,0:T(8,128)S(1)}, f32[8,128]{1,0:T(8,128)S(1)}) custom-call(f32[4,32,256]{2,1,0:T(8,128)S(1)} %copy-done.1, f32[72,256]{1,0:T(8,128)S(1)} %get-tuple-element.19.up_ref, f32[72,256]{1,0:T(8,128)S(1)} %get-tuple-element.20.down_ref, f32[40,128]{1,0:T(8,128)S(1)} %collective-permute-done.4.next_ref, ...), custom_call_target="tpu_custom_call" | custom-call | flops 20000000 | bytes 2000000 | tf_op jit(solution)/shard_map/first/pallas_call | solution.py:389
  18.6 0.0 collective-permute-done.7.mate_ref
  18.6 5.5 %steps.1 = f32[4,32,256]{2,1,0:T(8,128)} custom-call(f32[4,8,3,8,128]{4,3,2,1,0:T(8,128)S(1)} %get-tuple-element.24.field_ref, f32[4,8,3,8,128]{4,3,2,1,0:T(8,128)S(1)} %get-tuple-element.25.change_ref, f32[8,128]{1,0:T(8,128)S(1)} %get-tuple-element.26.own_ref, f32[8,128]{1,0:T(8,128)S(1)} %collective-permute-done.7.mate_ref, f32[8,128]{1,0:T(8,128)S(1)} %fusion.wide_ref), custom_call_target="tpu_custom_call" | custom-call | tf_op jit(solution)/shard_map/steps/pallas_call | solution.py:399
  (1 shorter events, 0.0 us)
Async XLA Ops:
  0.0 0.9 %copy-start = (f32[4,32,256]{2,1,0:T(8,128)S(1)}, f32[4,32,256]{2,1,0:T(8,128)}, u32[]{:S(2)}) copy-start(f32[4,32,256]{2,1,0:T(8,128)} %state_ref.3) | copy-start | bytes 393220
  1.1 7.8 %collective-permute-start = (f32[72,256]{1,0:T(8,128)S(1)}, f32[72,256]{1,0:T(8,128)S(1)}, u32[]{:S(2)}, u32[]{:S(2)}) collective-permute-start(f32[72,256]{1,0:T(8,128)S(1)} %get-tuple-element.16), channel_id=1, source_target_pairs={{4,8},{8,4},{12,16},{16,12},{20,24},{24,20},{28,0},{0,28},{5,9},{9... | collective-permute-start | bytes 221192 | tf_op jit(solution)/shard_map/ppermute | solution.py:349
  4.5 4.4 %collective-permute-start.3 = (f32[72,256]{1,0:T(8,128)S(1)}, f32[72,256]{1,0:T(8,128)S(1)}, u32[]{:S(2)}, u32[]{:S(2)}) collective-permute-start(f32[72,256]{1,0:T(8,128)S(1)} %get-tuple-element.18), channel_id=1, source_target_pairs={{0,4},{4,0},{8,12},{12,8},{16,20},{20,16},{24,28},{28,24},{1,5},{5... | collective-permute-start | bytes 221192 | tf_op jit(solution)/shard_map/ppermute | solution.py:349
  4.5 12.8 %copy-start.1 = (f32[4,32,256]{2,1,0:T(8,128)S(1)}, f32[4,32,256]{2,1,0:T(8,128)}, u32[]{:S(2)}) copy-start(f32[4,32,256]{2,1,0:T(8,128)} %state_ref.3) | copy-start | bytes 393220
  4.5 3.0 %collective-permute-start.1 = (f32[8,128]{1,0:T(8,128)S(1)}, f32[8,128]{1,0:T(8,128)S(1)}, u32[]{:S(2)}, u32[]{:S(2)}) collective-permute-start(f32[8,128]{1,0:T(8,128)S(1)} %get-tuple-element.17.own_ref), channel_id=1, source_target_pairs={{0,12},{4,24},{8,20},{12,0},{16,28},{20,8},{24,4},{28,16},{1,13},{... | collective-permute-start | bytes 12296 | tf_op jit(solution)/shard_map/ppermute | solution.py:353
  5.3 3.6 %collective-permute-start.2 = (f32[8,128]{1,0:T(8,128)S(1)}, f32[8,128]{1,0:T(8,128)S(1)}, u32[]{:S(2)}, u32[]{:S(2)}) collective-permute-start(f32[8,128]{1,0:T(8,128)S(1)} %get-tuple-element.17.own_ref), channel_id=1, source_target_pairs={{0,16},{4,20},{8,24},{12,28},{16,0},{20,4},{24,8},{28,12},{1,17},{... | collective-permute-start | bytes 12296 | tf_op jit(solution)/shard_map/ppermute | solution.py:341
  9.0 8.2 %collective-permute-start.4 = (f32[40,128]{1,0:T(8,128)S(1)}, f32[40,128]{1,0:T(8,128)S(1)}, u32[]{:S(2)}, u32[]{:S(2)}) collective-permute-start(f32[40,128]{1,0:T(8,128)S(1)} %get-tuple-element.21), channel_id=1, source_target_pairs={{1,2},{2,1},{3,0},{0,3},{5,6},{6,5},{7,4},{4,7},{9,10},{10,9},{11,... | collective-permute-start | bytes 61448 | tf_op jit(solution)/shard_map/ppermute | solution.py:349
  12.7 4.5 %collective-permute-start.6 = (f32[40,128]{1,0:T(8,128)S(1)}, f32[40,128]{1,0:T(8,128)S(1)}, u32[]{:S(2)}, u32[]{:S(2)}) collective-permute-start(f32[40,128]{1,0:T(8,128)S(1)} %get-tuple-element.23), channel_id=1, source_target_pairs={{0,1},{1,0},{2,3},{3,2},{4,5},{5,4},{6,7},{7,6},{8,9},{9,8},{10,11... | collective-permute-start | bytes 61448 | tf_op jit(solution)/shard_map/ppermute | solution.py:349
  12.7 4.5 %collective-permute-start.5 = (f32[8,128]{1,0:T(8,128)S(1)}, f32[8,128]{1,0:T(8,128)S(1)}, u32[]{:S(2)}, u32[]{:S(2)}) collective-permute-start(f32[8,128]{1,0:T(8,128)S(1)} %get-tuple-element.22.own_ref), channel_id=1, source_target_pairs={{0,2},{1,3},{2,0},{3,1},{4,6},{5,7},{6,4},{7,5},{8,10},{9,11},{10,... | collective-permute-start | bytes 12296 | tf_op jit(solution)/shard_map/ppermute | solution.py:341
  17.2 1.4 %collective-permute-start.7 = (f32[8,128]{1,0:T(8,128)S(1)}, f32[8,128]{1,0:T(8,128)S(1)}, u32[]{:S(2)}, u32[]{:S(2)}) collective-permute-start(f32[8,128]{1,0:T(8,128)S(1)} %fusion.wide_ref), channel_id=1, source_target_pairs={{0,4},{4,0},{8,12},{12,8},{16,20},{20,16},{24,28},{28,24},{1,5},{5... | collective-permute-start | bytes 12296 | tf_op jit(solution)/shard_map/ppermute | solution.py:341

commit v9 on v8

--- a/solution.py
+++ b/solution.py
@@ -33,59 +33,69 @@
     return lax.rem(lax.axis_index(axis), 2) == 1
 
 
+def odd(axis):
+    return lax.rem(lax.axis_index(axis), 2) == 1
+
+
+def put_rows(block_ref, out_ref, at_tail, top):
+    rows = block_ref.shape[1]
+    for comp in range(4):
+        head = block_ref[comp, 0:HALO, :]
+        tail = block_ref[comp, rows - HALO : rows, :]
+        out_ref[comp * HALO : (comp + 1) * HALO, :] = jnp.where(at_tail, tail, head)
+    out_ref[4 * HALO :, :] = jnp.concatenate([top] * (out_ref.shape[1] // LANES), axis=1)
+
+
 def edge_kernel(block_ref, first_ref, second_ref, top_ref):
-    rows = block_ref.shape[1]
     density, mom_x, mom_y, energy = (block_ref[comp] for comp in range(4))
     inv = 1.0 / density
     pressure = (GAMMA - 1.0) * (energy - 0.5 * (mom_x * mom_x + mom_y * mom_y) * inv)
     speed = jnp.maximum(jnp.abs(mom_x * inv), jnp.abs(mom_y * inv)) + jnp.sqrt(GAMMA * pressure * inv)
-    top = jnp.max(speed)
-    is_odd = odd("gx")
-    for comp in range(4):
-        span = slice(comp * HALO, (comp + 1) * HALO)
-        head = block_ref[comp, 0:HALO, :]
-        tail = block_ref[comp, rows - HALO : rows, :]
-        first_ref[span, :] = jnp.where(is_odd, head, tail)
-        second_ref[span, :] = jnp.where(is_odd, tail, head)
-    first_ref[4 * HALO :, :] = jnp.full((8, first_ref.shape[1]), top)
-    second_ref[4 * HALO :, :] = jnp.full((8, second_ref.shape[1]), top)
-    top_ref[...] = jnp.full(top_ref.shape, top)
-
-
-def pack_kernel(state_ref, next_ref, three_ref, four_ref, swap_ref, own_ref, up_ref, down_ref, first_ref, second_ref, top_ref):
+    top = jnp.full(top_ref.shape, jnp.max(speed))
+    put_rows(block_ref, first_ref, jnp.logical_not(odd("gx")), top)
+    put_rows(block_ref, second_ref, odd("gx"), top)
+    top_ref[...] = top
+
+
+def packed(state_ref, up_ref, down_ref, low, at):
     rows = state_ref.shape[1]
-    cols = state_ref.shape[2]
     half = rows // 2 + HALO
     lane = iota((half, LANES), 1)
+    lanes = slice(low, low + LANES)
+    total = jnp.zeros((half, LANES), jnp.float32)
+    for side in range(2):
+        for comp in range(4):
+            span = slice(comp * HALO, (comp + 1) * HALO)
+            if side == 0:
+                cells = jnp.concatenate([up_ref[span, lanes], state_ref[comp, 0 : rows // 2, lanes]], axis=0)
+            else:
+                cells = jnp.concatenate([state_ref[comp, rows // 2 : rows, lanes], down_ref[span, lanes]], axis=0)
+            goal = side * (LANES // 2) + comp * HALO
+            moved = pltpu.roll(cells, (goal - at) % LANES, axis=1)
+            total = jnp.where((lane >= goal) & (lane < goal + HALO), moved, total)
+    return total
+
+
+def put_columns(state_ref, up_ref, down_ref, out_ref, at_right, top):
+    cols = state_ref.shape[2]
+    left = packed(state_ref, up_ref, down_ref, 0, 0)
+    right = packed(state_ref, up_ref, down_ref, cols - LANES, LANES - HALO)
+    out_ref[0 : left.shape[0], :] = jnp.where(at_right, right, left)
+    out_ref[left.shape[0] :, :] = top
+
+
+def pack_kernel(state_ref, next_ref, three_ref, four_ref, swap_ref, own_ref, up_ref, down_ref, second_ref, top_ref):
     is_odd = odd("gx")
     up_ref[...] = jnp.where(is_odd, swap_ref[...], next_ref[...])
     down_ref[...] = jnp.where(is_odd, next_ref[...], swap_ref[...])
     top = jnp.maximum(jnp.maximum(own_ref[...], jnp.maximum(three_ref[...], four_ref[...])),
                       jnp.maximum(up_ref[4 * HALO :, 0:LANES], down_ref[4 * HALO :, 0:LANES]))
-
-    def edge(low, at):
-        lanes = slice(low, low + LANES)
-        total = jnp.zeros((half, LANES), jnp.float32)
-        for side in range(2):
-            for comp in range(4):
-                span = slice(comp * HALO, (comp + 1) * HALO)
-                if side == 0:
-                    cells = jnp.concatenate([up_ref[span, lanes], state_ref[comp, 0 : rows // 2, lanes]], axis=0)
-                else:
-                    cells = jnp.concatenate([state_ref[comp, rows // 2 : rows, lanes], down_ref[span, lanes]], axis=0)
-                goal = side * (LANES // 2) + comp * HALO
-                moved = pltpu.roll(cells, (goal - at) % LANES, axis=1)
-                total = jnp.where((lane >= goal) & (lane < goal + HALO), moved, total)
-        return total
-
-    left = edge(0, 0)
-    right = edge(cols - LANES, LANES - HALO)
-    is_odd = odd("gy")
-    first_ref[0:half, :] = jnp.where(is_odd, left, right)
-    second_ref[0:half, :] = jnp.where(is_odd, right, left)
-    first_ref[half:, :] = top
-    second_ref[half:, :] = top
-    top_ref[...] = top
+    put_columns(state_ref, up_ref, down_ref, second_ref, odd("gy"), top)
+    top_ref[...] = jnp.concatenate([top] * (top_ref.shape[0] // 8), axis=0)
+
+
+def near_kernel(state_ref, up_ref, down_ref, top_ref, first_ref):
+    put_columns(state_ref, up_ref, down_ref, first_ref, jnp.logical_not(odd("gy")), top_ref[0:8, :])
 
 
 def selected(values, select):
@@ -229,7 +239,7 @@
         plain[low + HALO + rows : low + tall, 0:cols] = down_ref[span, :]
     lane = iota((half, LANES), 1)
     is_odd = odd("gy")
-    top_ref[...] = jnp.maximum(jnp.maximum(own_ref[...], far_ref[...]), jnp.maximum(next_ref[half:, :], swap_ref[half:, :]))
+    top_ref[...] = jnp.maximum(jnp.maximum(own_ref[0:8, :], far_ref[0:8, :]), jnp.maximum(next_ref[half:, :], swap_ref[half:, :]))
     from_swap = swap_ref[0:half, :]
     from_next = next_ref[0:half, :]
     from_before = jnp.where(is_odd, from_swap, from_next)
@@ -267,7 +277,7 @@
     changes(load, count, groups, 0, store)
 
 
-def steps_kernel(field_ref, change_ref, own_ref, mate_ref, wide_ref, out_ref, field, base, mid, dealt):
+def steps_kernel(field_ref, change_ref, own_ref, mate_ref, wide_ref, out_ref, field, base, mid, dealt, result, sems):
     rows, cols = out_ref.shape[1:]
     tall = rows + 2 * HALO
     groups = field_ref.shape[2]
@@ -301,31 +311,28 @@
             changes(load_from(old), count, groups, 0, to_mid)
         changes(load_from(mid), count, groups, count // 2, to_field)
 
-    def looped(_, none):
-        one_step(8, (tall - 16) // 8, field, None)
-        return none
-
     one_step(0, tall // 8, field_ref, change_ref)
-    one_step(4, (tall - 8) // 8, field, None)
-    lax.fori_loop(2, STEPS, looped, None)
+    for index in range(1, STEPS):
+        one_step(4 * index, (tall - 8 * index) // 8, field, None)
 
     wide = groups * LANES
     source = iota((wide, cols), 0)
     goal = iota((wide, cols), 1)
     select = jnp.where(groups * (source % LANES) + source // LANES == goal + HALO, 1.0, 0.0).astype(jnp.bfloat16)
     lane = iota((rows, LANES), 1)
-    parts = []
+    copies = []
     for comp in range(4):
         line = []
         for group in range(groups):
             place = groups * lane + group
             inside = (place >= HALO) & (place < HALO + cols)
             line.append(jnp.where(inside, dealt[comp, group, HALO : HALO + rows, :], 0.0))
-        parts.append(jnp.concatenate(line, axis=1))
-    found = selected(jnp.concatenate(parts, axis=0), select)
-    for comp in range(4):
-        cells = found[comp * rows : (comp + 1) * rows, :]
-        out_ref[comp] = cells / (GAMMA - 1.0) if comp == 3 else cells
+        cells = selected(jnp.concatenate(line, axis=1), select)
+        result[comp] = cells / (GAMMA - 1.0) if comp == 3 else cells
+        copies.append(pltpu.make_async_copy(result.at[comp], out_ref.at[comp], sems.at[comp]))
+        copies[-1].start()
+    for copy in copies:
+        copy.wait()
 
 
 def local(state):
@@ -353,31 +360,30 @@
         return lax.ppermute(value, axis, [(i, (i + 3 - 6 * (i % 2)) % count) for i in range(count)])
 
     edge_type = array(parts * HALO + 8, cols)
-    first, second, top = pl.pallas_call(
-        edge_kernel,
-        out_shape=(edge_type, edge_type, array(8, LANES)),
-        in_specs=[VMEM],
-        out_specs=(VMEM,) * 3,
-        compiler_params=params(4),
-        name="edge",
-    )(state)
+    def call(kernel, out_shape, name, *operands):
+        return pl.pallas_call(
+            kernel,
+            out_shape=out_shape,
+            in_specs=[VMEM] * len(operands),
+            out_specs=jax.tree.map(lambda _: VMEM, out_shape),
+            compiler_params=params(4),
+            name=name,
+        )(*operands)
+
+    top_type = array(8, LANES)
+    first, second, top = call(edge_kernel, (edge_type, edge_type, top_type), "edge", state)
     second = swapped_pairs(second, "gx", 1)
+    far = swapped_threes(top, "gx"), swapped_bit(top, "gx", 4)
     first = swapped_pairs(first, "gx", 0)
-    far = swapped_threes(top, "gx"), swapped_bit(top, "gx", 4)
     side_type = array(tall // 2 + 8, LANES)
-    up, down, first, second, top = pl.pallas_call(
-        pack_kernel,
-        out_shape=(edge_type, edge_type, side_type, side_type, array(8, LANES)),
-        in_specs=[VMEM] * 6,
-        out_specs=(VMEM,) * 5,
-        compiler_params=params(4),
-        name="pack",
-    )(state, second, *far, first, top)
+    up, down, second, top = call(
+        pack_kernel, (edge_type, edge_type, side_type, side_type), "pack", state, second, *far, first, top
+    )
     second = swapped_pairs(second, "gy", 1)
-    first = swapped_pairs(first, "gy", 0)
     far = swapped_bit(top, "gy", 2)
+    first = swapped_pairs(call(near_kernel, side_type, "near", state, up, down, top), "gy", 0)
     own = top
-    top = jnp.maximum(jnp.maximum(own, far), jnp.maximum(first[tall // 2 :], second[tall // 2 :]))
+    top = jnp.maximum(jnp.maximum(own, far)[:8], jnp.maximum(first[tall // 2 :], second[tall // 2 :]))
     for axis, covered in (("gy", 4), ("gx", 8)):
         while covered < lax.axis_size(axis):
             top = jnp.maximum(top, sent(top, axis, covered))
@@ -400,8 +406,9 @@
         steps_kernel,
         out_shape=array(parts, rows, cols),
         in_specs=[VMEM] * 5,
-        out_specs=VMEM,
-        scratch_shapes=[dealt] * 3 + [plain],
+        out_specs=pl.BlockSpec(memory_space=pl.ANY),
+        scratch_shapes=[dealt] * 3
+        + [plain, pltpu.VMEM((parts, rows, cols), jnp.float32), pltpu.SemaphoreType.DMA((parts,))],
         compiler_params=params(16),
         name="steps",
     )(field, change, own, *top)

time: 24.3 us -> 24.5 us (level)
    ppermute x3, waiting for transfers between devices: 5.12 us -> 4.1 us  [swapped_bit(): lax.ppermute(value, axis, [(i, i ^ by) for i in range(lax.axis_size(axis))])]
    ppermute x4, waiting for transfers between devices: 0.01 us -> 1 us  [swapped_pairs(): return lax.ppermute(value, axis, pairs)]
    ppermute x4, starting transfers between devices: 7.07 us -> 7.92 us  [swapped_pairs(): return lax.ppermute(value, axis, pairs)]
    ppermute x3, starting transfers between devices: 1.35 us -> 0.57 us  [swapped_bit(): lax.ppermute(value, axis, [(i, i ^ by) for i in range(lax.axis_size(axis))])]
  transfers between devices with their start and end apart: 8 -> 8, of which waited for: 3 -> 4; matrix products, arithmetic and copies ran while one was open for 0% -> 0% of each run, Pallas kernels for 5% -> 6%
where the time goes in v9:
time: 24.5 us; the launch traced here: 24.3 us
  starting transfers between devices  9.3 us (38%)
  Pallas kernels  7.23 us (30%)
  waiting for transfers between devices  6.81 us (28%)
  local copies, waits for them, and re-layouts  0.91 us (4%)
    ppermute x4, starting transfers between devices, swapped_pairs(): return lax.ppermute(value, axis, pairs)  7.92 us
    pallas_call x1, Pallas kernels, local(): pl.pallas_call(steps_kernel, out_shape=array(parts, rows, cols), in_specs...  5.54 us
    ppermute x3, waiting for transfers between devices, swapped_bit(): lax.ppermute(value, axis, [(i, i ^ by) for i in range(lax.axis_size(axis))])  4.1 us
    ppermute x1, waiting for transfers between devices, swapped_threes(): lax.ppermute(value, axis, [(i, (i + 3 - 6 * (i % 2)) % count) for i in ra...  1.72 us
    pallas_call x1, Pallas kernels, local(): pl.pallas_call(first_kernel, out_shape=(dealt_type, dealt_type, array(8,...  1.28 us
    ppermute x4, waiting for transfers between devices, swapped_pairs(): return lax.ppermute(value, axis, pairs)  1 us
    unnamed x4, local copies, waits for them, and re-layouts  0.91 us
    ppermute x1, starting transfers between devices, swapped_threes(): lax.ppermute(value, axis, [(i, (i + 3 - 6 * (i % 2)) % count) for i in ra...  0.82 us
  transfers between devices with their start and end apart: 8, of which 4 were waited for; matrix products, arithmetic and copies ran while one was open for 0% of the time, Pallas kernels for 6%

profile of v9, /device:TPU:0, one launch (start us, length us, event | category | flops | bytes accessed | tf_op | source)
XLA Modules:
  0.0 24.3 jit_solution(8141717832733724097)
XLA Ops:
  0.0 0.0 copy-start
  0.0 0.9 %copy-done = f32[4,32,256]{2,1,0:T(8,128)S(1)} copy-done((f32[4,32,256]{2,1,0:T(8,128)S(1)}, f32[4,32,256]{2,1,0:T(8,128)}, u32[]{:S(2)}) %copy-start) | copy-done | bytes 131096
  0.9 0.2 edge.1
  1.1 3.4 %collective-permute-start = (f32[72,256]{1,0:T(8,128)S(1)}, f32[72,256]{1,0:T(8,128)S(1)}, u32[]{:S(2)}, u32[]{:S(2)}) collective-permute-start(f32[72,256]{1,0:T(8,128)S(1)} %get-tuple-element.15), channel_id=1, source_target_pairs={{4,8},{8,4},{12,16},{16,12},{20,24},{24,20},{28,0},{0,28},{5,9},{9... | collective-permute-start | bytes 221192 | tf_op jit(solution)/shard_map/ppermute | solution.py:356
  4.5 0.0 collective-permute-start.3
  4.5 0.8 %collective-permute-start.1 = (f32[8,128]{1,0:T(8,128)S(1)}, f32[8,128]{1,0:T(8,128)S(1)}, u32[]{:S(2)}, u32[]{:S(2)}) collective-permute-start(f32[8,128]{1,0:T(8,128)S(1)} %get-tuple-element.16.own_ref), channel_id=1, source_target_pairs={{0,12},{4,24},{8,20},{12,0},{16,28},{20,8},{24,4},{28,16},{1,13},{... | collective-permute-start | bytes 12296 | tf_op jit(solution)/shard_map/ppermute | solution.py:360
  5.3 0.5 %collective-permute-start.2 = (f32[8,128]{1,0:T(8,128)S(1)}, f32[8,128]{1,0:T(8,128)S(1)}, u32[]{:S(2)}, u32[]{:S(2)}) collective-permute-start(f32[8,128]{1,0:T(8,128)S(1)} %get-tuple-element.16.own_ref), channel_id=1, source_target_pairs={{0,16},{4,20},{8,24},{12,28},{16,0},{20,4},{24,8},{28,12},{1,17},{... | collective-permute-start | bytes 12296 | tf_op jit(solution)/shard_map/ppermute | solution.py:348
  5.8 1.7 %collective-permute-done.1.three_ref = f32[8,128]{1,0:T(8,128)S(1)} collective-permute-done((f32[8,128]{1,0:T(8,128)S(1)}, f32[8,128]{1,0:T(8,128)S(1)}, u32[]{:S(2)}, u32[]{:S(2)}) %collective-permute-start.1) | collective-permute-done | bytes 4128 | tf_op jit(solution)/shard_map/ppermute | solution.py:360
  7.5 1.4 %collective-permute-done.2.four_ref = f32[8,128]{1,0:T(8,128)S(1)} collective-permute-done((f32[8,128]{1,0:T(8,128)S(1)}, f32[8,128]{1,0:T(8,128)S(1)}, u32[]{:S(2)}, u32[]{:S(2)}) %collective-permute-start.2) | collective-permute-done | bytes 4128 | tf_op jit(solution)/shard_map/ppermute | solution.py:348
  8.9 0.0 collective-permute-done.next_ref
  8.9 0.0 collective-permute-done.3.swap_ref
  8.9 0.1 pack.1
  9.0 3.7 %collective-permute-start.4 = (f32[40,128]{1,0:T(8,128)S(1)}, f32[40,128]{1,0:T(8,128)S(1)}, u32[]{:S(2)}, u32[]{:S(2)}) collective-permute-start(f32[40,128]{1,0:T(8,128)S(1)} %get-tuple-element.20), channel_id=1, source_target_pairs={{1,2},{2,1},{3,0},{0,3},{5,6},{6,5},{7,4},{4,7},{9,10},{10,9},{11,... | collective-permute-start | bytes 61448 | tf_op jit(solution)/shard_map/ppermute | solution.py:356
  12.7 0.0 collective-permute-start.5
  12.7 0.0 copy-start.1
  12.7 0.1 near.1
  12.8 0.8 %collective-permute-start.6 = (f32[40,128]{1,0:T(8,128)S(1)}, f32[40,128]{1,0:T(8,128)S(1)}, u32[]{:S(2)}, u32[]{:S(2)}) collective-permute-start(f32[40,128]{1,0:T(8,128)S(1)} %near.1), channel_id=1, source_target_pairs={{0,1},{1,0},{2,3},{3,2},{4,5},{5,4},{6,7},{7,6},{8,9},{9,8},{10,11... | collective-permute-start | bytes 61448 | tf_op jit(solution)/shard_map/ppermute | solution.py:356
  13.7 1.0 %collective-permute-done.4.next_ref = f32[40,128]{1,0:T(8,128)S(1)} collective-permute-done((f32[40,128]{1,0:T(8,128)S(1)}, f32[40,128]{1,0:T(8,128)S(1)}, u32[]{:S(2)}, u32[]{:S(2)}) %collective-permute-start.4) | collective-permute-done | bytes 20512 | tf_op jit(solution)/shard_map/ppermute | solution.py:356
  14.7 2.7 %collective-permute-done.5.far_ref = f32[40,128]{1,0:T(8,128)S(1)} collective-permute-done((f32[40,128]{1,0:T(8,128)S(1)}, f32[40,128]{1,0:T(8,128)S(1)}, u32[]{:S(2)}, u32[]{:S(2)}) %collective-permute-start.5) | collective-permute-done | bytes 20512 | tf_op jit(solution)/shard_map/ppermute | solution.py:348
  17.4 0.0 collective-permute-done.6.swap_ref
  17.4 0.1 collective-permute-start.7
  17.5 0.0 copy-done.1
  17.5 1.3 %first.1 = (f32[4,8,3,8,128]{4,3,2,1,0:T(8,128)S(1)}, f32[4,8,3,8,128]{4,3,2,1,0:T(8,128)S(1)}, f32[8,128]{1,0:T(8,128)S(1)}) custom-call(f32[4,32,256]{2,1,0:T(8,128)S(1)} %copy-done.1, f32[72,256]{1,0:T(8,128)S(1)} %get-tuple-element.18.up_ref, f32[72,256]{1,0:T(8,128)S(1)} %get-tuple-element.19.down_ref, f32[40,128]{1,0:T(8,128)S(1)} %collective-permute-done.4.next_ref, ...), custom_call_target="tpu_custom_call" | custom-call | flops 20000000 | bytes 2000000 | tf_op jit(solution)/shard_map/first/pallas_call | solution.py:395
  18.8 0.0 collective-permute-done.7.mate_ref
  18.8 5.5 %steps.1 = f32[4,32,256]{2,1,0:T(8,128)} custom-call(f32[4,8,3,8,128]{4,3,2,1,0:T(8,128)S(1)} %get-tuple-element.22.field_ref, f32[4,8,3,8,128]{4,3,2,1,0:T(8,128)S(1)} %get-tuple-element.23.change_ref, f32[8,128]{1,0:T(8,128)S(1)} %get-tuple-element.24.own_ref, f32[8,128]{1,0:T(8,128)S(1)} %collective-permute-done.7.mate_ref, f32[8,128]{1,0:T(8,128)S(1)} %fusion.wide_ref), custom_call_target="tpu_custom_call" | custom-call | tf_op jit(solution)/shard_map/steps/pallas_call | solution.py:405
  (1 shorter events, 0.0 us)
Async XLA Ops:
  0.0 0.9 %copy-start = (f32[4,32,256]{2,1,0:T(8,128)S(1)}, f32[4,32,256]{2,1,0:T(8,128)}, u32[]{:S(2)}) copy-start(f32[4,32,256]{2,1,0:T(8,128)} %state_ref.5) | copy-start | bytes 393220
  1.1 7.8 %collective-permute-start = (f32[72,256]{1,0:T(8,128)S(1)}, f32[72,256]{1,0:T(8,128)S(1)}, u32[]{:S(2)}, u32[]{:S(2)}) collective-permute-start(f32[72,256]{1,0:T(8,128)S(1)} %get-tuple-element.15), channel_id=1, source_target_pairs={{4,8},{8,4},{12,16},{16,12},{20,24},{24,20},{28,0},{0,28},{5,9},{9... | collective-permute-start | bytes 221192 | tf_op jit(solution)/shard_map/ppermute | solution.py:356
  4.5 4.4 %collective-permute-start.3 = (f32[72,256]{1,0:T(8,128)S(1)}, f32[72,256]{1,0:T(8,128)S(1)}, u32[]{:S(2)}, u32[]{:S(2)}) collective-permute-start(f32[72,256]{1,0:T(8,128)S(1)} %get-tuple-element.17), channel_id=1, source_target_pairs={{0,4},{4,0},{8,12},{12,8},{16,20},{20,16},{24,28},{28,24},{1,5},{5... | collective-permute-start | bytes 221192 | tf_op jit(solution)/shard_map/ppermute | solution.py:356
  4.5 3.0 %collective-permute-start.1 = (f32[8,128]{1,0:T(8,128)S(1)}, f32[8,128]{1,0:T(8,128)S(1)}, u32[]{:S(2)}, u32[]{:S(2)}) collective-permute-start(f32[8,128]{1,0:T(8,128)S(1)} %get-tuple-element.16.own_ref), channel_id=1, source_target_pairs={{0,12},{4,24},{8,20},{12,0},{16,28},{20,8},{24,4},{28,16},{1,13},{... | collective-permute-start | bytes 12296 | tf_op jit(solution)/shard_map/ppermute | solution.py:360
  5.3 3.6 %collective-permute-start.2 = (f32[8,128]{1,0:T(8,128)S(1)}, f32[8,128]{1,0:T(8,128)S(1)}, u32[]{:S(2)}, u32[]{:S(2)}) collective-permute-start(f32[8,128]{1,0:T(8,128)S(1)} %get-tuple-element.16.own_ref), channel_id=1, source_target_pairs={{0,16},{4,20},{8,24},{12,28},{16,0},{20,4},{24,8},{28,12},{1,17},{... | collective-permute-start | bytes 12296 | tf_op jit(solution)/shard_map/ppermute | solution.py:348
  9.0 5.6 %collective-permute-start.4 = (f32[40,128]{1,0:T(8,128)S(1)}, f32[40,128]{1,0:T(8,128)S(1)}, u32[]{:S(2)}, u32[]{:S(2)}) collective-permute-start(f32[40,128]{1,0:T(8,128)S(1)} %get-tuple-element.20), channel_id=1, source_target_pairs={{1,2},{2,1},{3,0},{0,3},{5,6},{6,5},{7,4},{4,7},{9,10},{10,9},{11,... | collective-permute-start | bytes 61448 | tf_op jit(solution)/shard_map/ppermute | solution.py:356
  12.7 4.7 %collective-permute-start.5 = (f32[40,128]{1,0:T(8,128)S(1)}, f32[40,128]{1,0:T(8,128)S(1)}, u32[]{:S(2)}, u32[]{:S(2)}) collective-permute-start(f32[40,128]{1,0:T(8,128)S(1)} %get-tuple-element.21.top_ref.own_ref), channel_id=1, source_target_pairs={{0,2},{1,3},{2,0},{3,1},{4,6},{5,7},{6,4},{7,5},{8,10},{9,11},{10,... | collective-permute-start | bytes 61448 | tf_op jit(solution)/shard_map/ppermute | solution.py:348
  12.7 4.8 %copy-start.1 = (f32[4,32,256]{2,1,0:T(8,128)S(1)}, f32[4,32,256]{2,1,0:T(8,128)}, u32[]{:S(2)}) copy-start(f32[4,32,256]{2,1,0:T(8,128)} %state_ref.5) | copy-start | bytes 393220
  12.8 4.5 %collective-permute-start.6 = (f32[40,128]{1,0:T(8,128)S(1)}, f32[40,128]{1,0:T(8,128)S(1)}, u32[]{:S(2)}, u32[]{:S(2)}) collective-permute-start(f32[40,128]{1,0:T(8,128)S(1)} %near.1), channel_id=1, source_target_pairs={{0,1},{1,0},{2,3},{3,2},{4,5},{5,4},{6,7},{7,6},{8,9},{9,8},{10,11... | collective-permute-start | bytes 61448 | tf_op jit(solution)/shard_map/ppermute | solution.py:356
  17.4 1.4 %collective-permute-start.7 = (f32[8,128]{1,0:T(8,128)S(1)}, f32[8,128]{1,0:T(8,128)S(1)}, u32[]{:S(2)}, u32[]{:S(2)}) collective-permute-start(f32[8,128]{1,0:T(8,128)S(1)} %fusion.wide_ref), channel_id=1, source_target_pairs={{0,4},{4,0},{8,12},{12,8},{16,20},{20,16},{24,28},{28,24},{1,5},{5... | collective-permute-start | bytes 12296 | tf_op jit(solution)/shard_map/ppermute | solution.py:348

commit v10 on v8

--- a/solution.py
+++ b/solution.py
@@ -1,4 +1,5 @@
 import functools
+import math
 
 import jax
 import jax.numpy as jnp
@@ -89,13 +90,13 @@
 
 
 def selected(values, select):
-    total = None
+    rows = values.shape[0]
+    parts = []
     for _ in range(3):
-        part = values.astype(jnp.bfloat16)
-        values = values - part.astype(jnp.float32)
-        term = jnp.dot(part, select, preferred_element_type=jnp.float32)
-        total = term if total is None else total + term
-    return total
+        parts.append(values.astype(jnp.bfloat16))
+        values = values - parts[-1].astype(jnp.float32)
+    found = jnp.dot(jnp.concatenate(parts, axis=0), select, preferred_element_type=jnp.float32)
+    return (found[0:rows] + found[rows : 2 * rows]) + found[2 * rows :]
 
 
 def minmod(first, second):
@@ -104,50 +105,49 @@
     return jnp.maximum(low, jnp.minimum(high, 0.0))
 
 
-def fluxes(state):
+MOMENTUM = math.sqrt(0.5 * (GAMMA - 1.0))
+SCALES = (1.0, MOMENTUM, MOMENTUM, GAMMA - 1.0)
+
+
+def known(state):
     density, normal, tangent, energy = state
     inv = pl.reciprocal(density, approx=True)
     vel = normal * inv
-    carried = normal * vel
-    kinetic = (0.5 * (GAMMA - 1.0)) * (carried + tangent * tangent * inv)
-    pressure = energy - kinetic
-    scaled = GAMMA * pressure
-    square = jnp.maximum(scaled * inv, TINY)
-    sound = square * lax.rsqrt(square)
-    return (normal, carried + pressure, tangent * vel, (scaled + kinetic) * vel), jnp.abs(vel) + sound
+    pressure = energy - (normal * normal + tangent * tangent) * inv
+    square = jnp.maximum((GAMMA * MOMENTUM * MOMENTUM) * pressure * inv, TINY)
+    return state, vel, pressure, pressure * vel, jnp.abs(vel) + square * lax.rsqrt(square)
 
 
 def face(left, right):
-    (left_state, left_flux, left_speed), (right_state, right_flux, right_speed) = left, right
+    (left_state, left_vel, left_pressure, left_work, left_speed) = left
+    (right_state, right_vel, right_pressure, right_work, right_speed) = right
     top = jnp.maximum(left_speed, right_speed)
-    return [
-        (left_flux[comp] + right_flux[comp]) - top * (right_state[comp] - left_state[comp]) for comp in range(4)
-    ]
+    left_rate = left_vel + top
+    right_rate = right_vel - top
+    flux = [left_rate * left_state[comp] + right_rate * right_state[comp] for comp in range(4)]
+    flux[1] = flux[1] + (MOMENTUM * MOMENTUM) * (left_pressure + right_pressure)
+    flux[3] = flux[3] + (GAMMA - 1.0) * (left_work + right_work)
+    return flux
 
 
 def minus(first, second):
     return [first[comp] - second[comp] for comp in range(4)]
 
 
-def half(parts):
-    return [0.5 * part for part in parts]
-
-
 def rolled(tree, by, axis):
     return jax.tree.map(lambda value: pltpu.roll(value, by % value.shape[axis], axis=axis), tree)
 
 
 def cell(here, jump_before, jump_after):
     slope = [minmod(jump_before[comp], jump_after[comp]) for comp in range(4)]
-    low = minus(here, slope)
-    high = [here[comp] + slope[comp] for comp in range(4)]
-    return (low, *fluxes(low)), (high, *fluxes(high))
+    whole = [here[comp] + here[comp] for comp in range(4)]
+    return known(minus(whole, slope)), known([whole[comp] + slope[comp] for comp in range(4)])
 
 
 def row_changes(values):
     count = len(values)
-    end_jump = half(minus(rolled(values[0], -1, 1), values[-1]))
-    jumps = [half(minus(values[at + 1], values[at])) for at in range(count - 1)] + [end_jump]
+    end_jump = minus(rolled(values[0], -1, 1), values[-1])
+    jumps = [minus(values[at + 1], values[at]) for at in range(count - 1)] + [end_jump]
     faces, first_low, high = [], None, None
     for at in range(count):
         low, next_high = cell(values[at], jumps[at - 1] if at else rolled(end_jump, 1, 1), jumps[at])
@@ -163,7 +163,7 @@
 class Column:
     def __init__(self, count, begin, here, after):
         self.count, self.begin = count, begin
-        self.jump = self.first_jump = half(minus(after, here))
+        self.jump = self.first_jump = minus(after, here)
         self.first_low = self.first_flux = self.last_flux = self.high = None
 
     def feed(self, row, here, after):
@@ -171,7 +171,7 @@
         if after is None:
             next_jump = self.first_jump
         else:
-            next_jump = half(minus(rolled(after, -1, 0) if next_row == 0 else after, here))
+            next_jump = minus(rolled(after, -1, 0) if next_row == 0 else after, here)
         jump = rolled(self.jump, 1, 0) if row == 0 else self.jump
         low, high = cell(here, jump, next_jump)
         done = []
@@ -250,7 +250,7 @@
     for comp in range(4):
         for group in range(groups):
             cells = found[comp * tall : (comp + 1) * tall, group * LANES : (group + 1) * LANES]
-            dealt[comp, group] = (GAMMA - 1.0) * cells if comp == 3 else cells
+            dealt[comp, group] = (0.5 * SCALES[comp]) * cells
     count = tall // 8
     for comp in range(4):
         for row in range(count):
@@ -267,11 +267,11 @@
     changes(load, count, groups, 0, store)
 
 
-def steps_kernel(field_ref, change_ref, own_ref, mate_ref, wide_ref, out_ref, field, base, mid, dealt):
+def steps_kernel(field_ref, change_ref, own_ref, mate_ref, wide_ref, out_ref, field, base, mid, dealt, result, sems):
     rows, cols = out_ref.shape[1:]
     tall = rows + 2 * HALO
     groups = field_ref.shape[2]
-    half_factor = -0.25 * COURANT / jnp.maximum(own_ref[...], jnp.maximum(mate_ref[...], wide_ref[...]))
+    half_factor = (-0.125 * COURANT / MOMENTUM) / jnp.maximum(own_ref[...], jnp.maximum(mate_ref[...], wide_ref[...]))
 
     def one_step(start, count, old, first_changes):
         def to_mid(row, col, parts):
@@ -301,13 +301,9 @@
             changes(load_from(old), count, groups, 0, to_mid)
         changes(load_from(mid), count, groups, count // 2, to_field)
 
-    def looped(_, none):
-        one_step(8, (tall - 16) // 8, field, None)
-        return none
-
     one_step(0, tall // 8, field_ref, change_ref)
-    one_step(4, (tall - 8) // 8, field, None)
-    lax.fori_loop(2, STEPS, looped, None)
+    for index in range(1, STEPS):
+        one_step(4 * index, (tall - 8 * index) // 8, field, None)
 
     wide = groups * LANES
     source = iota((wide, cols), 0)
@@ -323,9 +319,13 @@
             line.append(jnp.where(inside, dealt[comp, group, HALO : HALO + rows, :], 0.0))
         parts.append(jnp.concatenate(line, axis=1))
     found = selected(jnp.concatenate(parts, axis=0), select)
-    for comp in range(4):
-        cells = found[comp * rows : (comp + 1) * rows, :]
-        out_ref[comp] = cells / (GAMMA - 1.0) if comp == 3 else cells
+    copies = []
+    for comp in range(4):
+        result[comp] = (2.0 / SCALES[comp]) * found[comp * rows : (comp + 1) * rows, :]
+        copies.append(pltpu.make_async_copy(result.at[comp], out_ref.at[comp], sems.at[comp]))
+        copies[-1].start()
+    for copy in copies:
+        copy.wait()
 
 
 def local(state):
@@ -400,8 +400,9 @@
         steps_kernel,
         out_shape=array(parts, rows, cols),
         in_specs=[VMEM] * 5,
-        out_specs=VMEM,
-        scratch_shapes=[dealt] * 3 + [plain],
+        out_specs=pl.BlockSpec(memory_space=pl.ANY),
+        scratch_shapes=[dealt] * 3
+        + [plain, pltpu.VMEM((parts, rows, cols), jnp.float32), pltpu.SemaphoreType.DMA((parts,))],
         compiler_params=params(16),
         name="steps",
     )(field, change, own, *top)

time: 24.3 us -> 23.4 us (0.963)
  Pallas kernels: 7.07 us -> 6.21 us
    pallas_call x1, Pallas kernels: 5.5 us -> 4.71 us  [local(): pl.pallas_call(steps_kernel, out_shape=array(parts, rows, cols), in_specs...]
where the time goes in v10:
time: 23.4 us; the launch traced here: 23.3 us
  starting transfers between devices  9.24 us (39%)
  waiting for transfers between devices  6.84 us (29%)
  Pallas kernels  6.21 us (27%)
  local copies, waits for them, and re-layouts  0.91 us (4%)
    ppermute x4, starting transfers between devices, swapped_pairs(): return lax.ppermute(value, axis, pairs)  7.07 us
    ppermute x3, waiting for transfers between devices, swapped_bit(): lax.ppermute(value, axis, [(i, i ^ by) for i in range(lax.axis_size(axis))])  5.12 us
    pallas_call x1, Pallas kernels, local(): pl.pallas_call(steps_kernel, out_shape=array(parts, rows, cols), in_specs...  4.71 us
    ppermute x1, waiting for transfers between devices, swapped_threes(): lax.ppermute(value, axis, [(i, (i + 3 - 6 * (i % 2)) % count) for i in ra...  1.72 us
    ppermute x3, starting transfers between devices, swapped_bit(): lax.ppermute(value, axis, [(i, i ^ by) for i in range(lax.axis_size(axis))])  1.35 us
    pallas_call x1, Pallas kernels, local(): pl.pallas_call(first_kernel, out_shape=(dealt_type, dealt_type, array(8,...  1.21 us
    unnamed x4, local copies, waits for them, and re-layouts  0.91 us
    ppermute x1, starting transfers between devices, swapped_threes(): lax.ppermute(value, axis, [(i, (i + 3 - 6 * (i % 2)) % count) for i in ra...  0.82 us
  transfers between devices with their start and end apart: 8, of which 3 were waited for; matrix products, arithmetic and copies ran while one was open for 0% of the time, Pallas kernels for 5%

profile of v10, /device:TPU:0, one launch (start us, length us, event | category | flops | bytes accessed | tf_op | source)
XLA Modules:
  0.0 23.3 jit_solution(14869033789741450030)
XLA Ops:
  0.0 0.0 copy-start
  0.0 0.9 %copy-done = f32[4,32,256]{2,1,0:T(8,128)S(1)} copy-done((f32[4,32,256]{2,1,0:T(8,128)S(1)}, f32[4,32,256]{2,1,0:T(8,128)}, u32[]{:S(2)}) %copy-start) | copy-done | bytes 131096
  0.9 0.2 edge.1
  1.1 3.4 %collective-permute-start = (f32[72,256]{1,0:T(8,128)S(1)}, f32[72,256]{1,0:T(8,128)S(1)}, u32[]{:S(2)}, u32[]{:S(2)}) collective-permute-start(f32[72,256]{1,0:T(8,128)S(1)} %get-tuple-element.16), channel_id=1, source_target_pairs={{4,8},{8,4},{12,16},{16,12},{20,24},{24,20},{28,0},{0,28},{5,9},{9... | collective-permute-start | bytes 221192 | tf_op jit(solution)/shard_map/ppermute | solution.py:349
  4.5 0.0 collective-permute-start.3
  4.5 0.0 copy-start.1
  4.5 0.8 %collective-permute-start.1 = (f32[8,128]{1,0:T(8,128)S(1)}, f32[8,128]{1,0:T(8,128)S(1)}, u32[]{:S(2)}, u32[]{:S(2)}) collective-permute-start(f32[8,128]{1,0:T(8,128)S(1)} %get-tuple-element.17.own_ref), channel_id=1, source_target_pairs={{0,12},{4,24},{8,20},{12,0},{16,28},{20,8},{24,4},{28,16},{1,13},{... | collective-permute-start | bytes 12296 | tf_op jit(solution)/shard_map/ppermute | solution.py:353
  5.3 0.5 %collective-permute-start.2 = (f32[8,128]{1,0:T(8,128)S(1)}, f32[8,128]{1,0:T(8,128)S(1)}, u32[]{:S(2)}, u32[]{:S(2)}) collective-permute-start(f32[8,128]{1,0:T(8,128)S(1)} %get-tuple-element.17.own_ref), channel_id=1, source_target_pairs={{0,16},{4,20},{8,24},{12,28},{16,0},{20,4},{24,8},{28,12},{1,17},{... | collective-permute-start | bytes 12296 | tf_op jit(solution)/shard_map/ppermute | solution.py:341
  5.8 1.7 %collective-permute-done.1.three_ref = f32[8,128]{1,0:T(8,128)S(1)} collective-permute-done((f32[8,128]{1,0:T(8,128)S(1)}, f32[8,128]{1,0:T(8,128)S(1)}, u32[]{:S(2)}, u32[]{:S(2)}) %collective-permute-start.1) | collective-permute-done | bytes 4128 | tf_op jit(solution)/shard_map/ppermute | solution.py:353
  7.5 1.4 %collective-permute-done.2.four_ref = f32[8,128]{1,0:T(8,128)S(1)} collective-permute-done((f32[8,128]{1,0:T(8,128)S(1)}, f32[8,128]{1,0:T(8,128)S(1)}, u32[]{:S(2)}, u32[]{:S(2)}) %collective-permute-start.2) | collective-permute-done | bytes 4128 | tf_op jit(solution)/shard_map/ppermute | solution.py:341
  8.9 0.0 collective-permute-done.next_ref
  8.9 0.0 collective-permute-done.3.swap_ref
  8.9 0.1 pack.1
  9.0 3.7 %collective-permute-start.4 = (f32[40,128]{1,0:T(8,128)S(1)}, f32[40,128]{1,0:T(8,128)S(1)}, u32[]{:S(2)}, u32[]{:S(2)}) collective-permute-start(f32[40,128]{1,0:T(8,128)S(1)} %get-tuple-element.21), channel_id=1, source_target_pairs={{1,2},{2,1},{3,0},{0,3},{5,6},{6,5},{7,4},{4,7},{9,10},{10,9},{11,... | collective-permute-start | bytes 61448 | tf_op jit(solution)/shard_map/ppermute | solution.py:349
  12.7 0.0 collective-permute-start.6
  12.7 0.8 %collective-permute-start.5 = (f32[8,128]{1,0:T(8,128)S(1)}, f32[8,128]{1,0:T(8,128)S(1)}, u32[]{:S(2)}, u32[]{:S(2)}) collective-permute-start(f32[8,128]{1,0:T(8,128)S(1)} %get-tuple-element.22.own_ref), channel_id=1, source_target_pairs={{0,2},{1,3},{2,0},{3,1},{4,6},{5,7},{6,4},{7,5},{8,10},{9,11},{10,... | collective-permute-start | bytes 12296 | tf_op jit(solution)/shard_map/ppermute | solution.py:341
  13.5 3.7 %collective-permute-done.5.far_ref = f32[8,128]{1,0:T(8,128)S(1)} collective-permute-done((f32[8,128]{1,0:T(8,128)S(1)}, f32[8,128]{1,0:T(8,128)S(1)}, u32[]{:S(2)}, u32[]{:S(2)}) %collective-permute-start.5) | collective-permute-done | bytes 4128 | tf_op jit(solution)/shard_map/ppermute | solution.py:341
  17.2 0.0 collective-permute-done.4.next_ref
  17.2 0.0 collective-permute-done.6.swap_ref
  17.2 0.1 collective-permute-start.7
  17.3 0.0 copy-done.1
  17.3 1.2 %first.1 = (f32[4,8,3,8,128]{4,3,2,1,0:T(8,128)S(1)}, f32[4,8,3,8,128]{4,3,2,1,0:T(8,128)S(1)}, f32[8,128]{1,0:T(8,128)S(1)}) custom-call(f32[4,32,256]{2,1,0:T(8,128)S(1)} %copy-done.1, f32[72,256]{1,0:T(8,128)S(1)} %get-tuple-element.19.up_ref, f32[72,256]{1,0:T(8,128)S(1)} %get-tuple-element.20.down_ref, f32[40,128]{1,0:T(8,128)S(1)} %collective-permute-done.4.next_ref, ...), custom_call_target="tpu_custom_call" | custom-call | flops 20000000 | bytes 2000000 | tf_op jit(solution)/shard_map/first/pallas_call | solution.py:389
  18.5 0.0 collective-permute-done.7.mate_ref
  18.6 4.7 %steps.1 = f32[4,32,256]{2,1,0:T(8,128)} custom-call(f32[4,8,3,8,128]{4,3,2,1,0:T(8,128)S(1)} %get-tuple-element.24.field_ref, f32[4,8,3,8,128]{4,3,2,1,0:T(8,128)S(1)} %get-tuple-element.25.change_ref, f32[8,128]{1,0:T(8,128)S(1)} %get-tuple-element.26.own_ref, f32[8,128]{1,0:T(8,128)S(1)} %collective-permute-done.7.mate_ref, f32[8,128]{1,0:T(8,128)S(1)} %fusion.wide_ref), custom_call_target="tpu_custom_call" | custom-call | tf_op jit(solution)/shard_map/steps/pallas_call | solution.py:399
  (1 shorter events, 0.0 us)
Async XLA Ops:
  0.0 0.9 %copy-start = (f32[4,32,256]{2,1,0:T(8,128)S(1)}, f32[4,32,256]{2,1,0:T(8,128)}, u32[]{:S(2)}) copy-start(f32[4,32,256]{2,1,0:T(8,128)} %state_ref.3) | copy-start | bytes 393220
  1.1 7.8 %collective-permute-start = (f32[72,256]{1,0:T(8,128)S(1)}, f32[72,256]{1,0:T(8,128)S(1)}, u32[]{:S(2)}, u32[]{:S(2)}) collective-permute-start(f32[72,256]{1,0:T(8,128)S(1)} %get-tuple-element.16), channel_id=1, source_target_pairs={{4,8},{8,4},{12,16},{16,12},{20,24},{24,20},{28,0},{0,28},{5,9},{9... | collective-permute-start | bytes 221192 | tf_op jit(solution)/shard_map/ppermute | solution.py:349
  4.5 4.4 %collective-permute-start.3 = (f32[72,256]{1,0:T(8,128)S(1)}, f32[72,256]{1,0:T(8,128)S(1)}, u32[]{:S(2)}, u32[]{:S(2)}) collective-permute-start(f32[72,256]{1,0:T(8,128)S(1)} %get-tuple-element.18), channel_id=1, source_target_pairs={{0,4},{4,0},{8,12},{12,8},{16,20},{20,16},{24,28},{28,24},{1,5},{5... | collective-permute-start | bytes 221192 | tf_op jit(solution)/shard_map/ppermute | solution.py:349
  4.5 12.8 %copy-start.1 = (f32[4,32,256]{2,1,0:T(8,128)S(1)}, f32[4,32,256]{2,1,0:T(8,128)}, u32[]{:S(2)}) copy-start(f32[4,32,256]{2,1,0:T(8,128)} %state_ref.3) | copy-start | bytes 393220
  4.5 3.0 %collective-permute-start.1 = (f32[8,128]{1,0:T(8,128)S(1)}, f32[8,128]{1,0:T(8,128)S(1)}, u32[]{:S(2)}, u32[]{:S(2)}) collective-permute-start(f32[8,128]{1,0:T(8,128)S(1)} %get-tuple-element.17.own_ref), channel_id=1, source_target_pairs={{0,12},{4,24},{8,20},{12,0},{16,28},{20,8},{24,4},{28,16},{1,13},{... | collective-permute-start | bytes 12296 | tf_op jit(solution)/shard_map/ppermute | solution.py:353
  5.3 3.6 %collective-permute-start.2 = (f32[8,128]{1,0:T(8,128)S(1)}, f32[8,128]{1,0:T(8,128)S(1)}, u32[]{:S(2)}, u32[]{:S(2)}) collective-permute-start(f32[8,128]{1,0:T(8,128)S(1)} %get-tuple-element.17.own_ref), channel_id=1, source_target_pairs={{0,16},{4,20},{8,24},{12,28},{16,0},{20,4},{24,8},{28,12},{1,17},{... | collective-permute-start | bytes 12296 | tf_op jit(solution)/shard_map/ppermute | solution.py:341
  9.0 8.2 %collective-permute-start.4 = (f32[40,128]{1,0:T(8,128)S(1)}, f32[40,128]{1,0:T(8,128)S(1)}, u32[]{:S(2)}, u32[]{:S(2)}) collective-permute-start(f32[40,128]{1,0:T(8,128)S(1)} %get-tuple-element.21), channel_id=1, source_target_pairs={{1,2},{2,1},{3,0},{0,3},{5,6},{6,5},{7,4},{4,7},{9,10},{10,9},{11,... | collective-permute-start | bytes 61448 | tf_op jit(solution)/shard_map/ppermute | solution.py:349
  12.7 4.5 %collective-permute-start.6 = (f32[40,128]{1,0:T(8,128)S(1)}, f32[40,128]{1,0:T(8,128)S(1)}, u32[]{:S(2)}, u32[]{:S(2)}) collective-permute-start(f32[40,128]{1,0:T(8,128)S(1)} %get-tuple-element.23), channel_id=1, source_target_pairs={{0,1},{1,0},{2,3},{3,2},{4,5},{5,4},{6,7},{7,6},{8,9},{9,8},{10,11... | collective-permute-start | bytes 61448 | tf_op jit(solution)/shard_map/ppermute | solution.py:349
  12.7 4.5 %collective-permute-start.5 = (f32[8,128]{1,0:T(8,128)S(1)}, f32[8,128]{1,0:T(8,128)S(1)}, u32[]{:S(2)}, u32[]{:S(2)}) collective-permute-start(f32[8,128]{1,0:T(8,128)S(1)} %get-tuple-element.22.own_ref), channel_id=1, source_target_pairs={{0,2},{1,3},{2,0},{3,1},{4,6},{5,7},{6,4},{7,5},{8,10},{9,11},{10,... | collective-permute-start | bytes 12296 | tf_op jit(solution)/shard_map/ppermute | solution.py:341
  17.2 1.3 %collective-permute-start.7 = (f32[8,128]{1,0:T(8,128)S(1)}, f32[8,128]{1,0:T(8,128)S(1)}, u32[]{:S(2)}, u32[]{:S(2)}) collective-permute-start(f32[8,128]{1,0:T(8,128)S(1)} %fusion.wide_ref), channel_id=1, source_target_pairs={{0,4},{4,0},{8,12},{12,8},{16,20},{20,16},{24,28},{28,24},{1,5},{5... | collective-permute-start | bytes 12296 | tf_op jit(solution)/shard_map/ppermute | solution.py:341

commit v11 on v10

--- a/solution.py
+++ b/solution.py
@@ -81,11 +81,13 @@
 
     left = edge(0, 0)
     right = edge(cols - LANES, LANES - HALO)
+    free = (iota((half, LANES), 0) == 0) & (lane < LANES // 2)
+    under = jnp.concatenate([top] * (half // 8), axis=0)
+    left = jnp.where(free, under, left)
+    right = jnp.where(free, under, right)
     is_odd = odd("gy")
-    first_ref[0:half, :] = jnp.where(is_odd, left, right)
-    second_ref[0:half, :] = jnp.where(is_odd, right, left)
-    first_ref[half:, :] = top
-    second_ref[half:, :] = top
+    first_ref[...] = jnp.where(is_odd, left, right)
+    second_ref[...] = jnp.where(is_odd, right, left)
     top_ref[...] = top
 
 
@@ -138,19 +140,18 @@
     return jax.tree.map(lambda value: pltpu.roll(value, by % value.shape[axis], axis=axis), tree)
 
 
-def cell(here, jump_before, jump_after):
+def cell(whole, jump_before, jump_after):
     slope = [minmod(jump_before[comp], jump_after[comp]) for comp in range(4)]
-    whole = [here[comp] + here[comp] for comp in range(4)]
     return known(minus(whole, slope)), known([whole[comp] + slope[comp] for comp in range(4)])
 
 
-def row_changes(values):
+def row_changes(values, wholes):
     count = len(values)
     end_jump = minus(rolled(values[0], -1, 1), values[-1])
     jumps = [minus(values[at + 1], values[at]) for at in range(count - 1)] + [end_jump]
     faces, first_low, high = [], None, None
     for at in range(count):
-        low, next_high = cell(values[at], jumps[at - 1] if at else rolled(end_jump, 1, 1), jumps[at])
+        low, next_high = cell(wholes[at], jumps[at - 1] if at else rolled(end_jump, 1, 1), jumps[at])
         if at:
             faces.append(face(high, low))
         else:
@@ -166,14 +167,14 @@
         self.jump = self.first_jump = minus(after, here)
         self.first_low = self.first_flux = self.last_flux = self.high = None
 
-    def feed(self, row, here, after):
+    def feed(self, row, here, whole, after):
         next_row = (row + 1) % self.count
         if after is None:
             next_jump = self.first_jump
         else:
             next_jump = minus(rolled(after, -1, 0) if next_row == 0 else after, here)
         jump = rolled(self.jump, 1, 0) if row == 0 else self.jump
-        low, high = cell(here, jump, next_jump)
+        low, high = cell(whole, jump, next_jump)
         done = []
         if self.first_low is None:
             self.first_low = low
@@ -205,33 +206,61 @@
         here = values.pop(at)
         if at < rows:
             values[at + 1] = [load((row + 1) % rows, col) for col in range(cols)]
+        whole = [[part + part for part in value] for value in here]
         ready = []
         for col in range(cols):
             after = values[at + 1][col] if at < rows else None
-            ready += [(col, *item) for item in columns[col].feed(row, here[col], after)]
-        along_y[row] = row_changes([[part[comp] for comp in Y_ORDER] for part in here])
+            ready += [(col, *item) for item in columns[col].feed(row, here[col], whole[col], after)]
+        along_y[row] = row_changes(*([[part[comp] for comp in Y_ORDER] for part in value] for value in (here, whole)))
         for col, done, parts in ready:
             other = along_y[done][col]
             store(done, col, [parts[comp] + other[Y_ORDER[comp]] for comp in range(4)])
 
 
-def first_kernel(state_ref, up_ref, down_ref, next_ref, far_ref, swap_ref, own_ref, field_ref, change_ref, top_ref, plain, dealt):
+def place_of(lane, group, groups):
+    return groups * lane + group
+
+
+def deal_kernel(state_ref, up_ref, down_ref, own_ref, dealt_ref, halo_select_ref, back_select_ref, top_ref, plain):
+    top_ref[...] = own_ref[...]
     rows, cols = state_ref.shape[1:]
     tall = rows + 2 * HALO
-    half = tall // 2
-    wide = plain.shape[1]
+    wide = dealt_ref.shape[1]
     groups = wide // LANES
     for comp in range(4):
         span = slice(comp * HALO, (comp + 1) * HALO)
         low = comp * tall
-        plain[low : low + HALO, 0:cols] = up_ref[span, :]
-        plain[low + HALO : low + HALO + rows, 0:cols] = state_ref[comp]
-        plain[low + HALO + rows : low + tall, 0:cols] = down_ref[span, :]
+        plain[low : low + HALO, :] = up_ref[span, :]
+        plain[low + HALO : low + HALO + rows, :] = state_ref[comp]
+        plain[low + HALO + rows : low + tall, :] = down_ref[span, :]
+    source = iota((wide, wide), 0)
+    goal = iota((wide, wide), 1)
+    place = place_of(goal % LANES, goal // LANES, groups)
+    place = jnp.where(place < cols + 2 * HALO, (place + wide - HALO) % wide, 0)
+    select = jnp.where(source == place, 1.0, 0.0).astype(jnp.bfloat16)
+    dealt_ref[...] = selected(plain[...], select[0:cols])
+    halo_select_ref[...] = select[cols:]
+    source = iota((wide, cols), 0)
+    goal = iota((wide, cols), 1)
+    back = place_of(source % LANES, source // LANES, groups) == goal + HALO
+    back_select_ref[...] = jnp.where(back, 1.0, 0.0).astype(jnp.bfloat16)
+
+
+def join_kernel(next_ref, swap_ref, far_ref, own_ref, top_ref):
+    speeds = jnp.maximum(next_ref[0:8, :], swap_ref[0:8, :])
+    carried = (iota((8, LANES), 0) == 0) & (iota((8, LANES), 1) < LANES // 2)
+    known_here = jnp.maximum(own_ref[...], far_ref[...])
+    top_ref[...] = jnp.full((8, LANES), jnp.max(jnp.where(carried, speeds, known_here)))
+
+
+def first_kernel(cells_ref, select_ref, next_ref, swap_ref, field_ref, change_ref, plain, dealt):
+    half = next_ref.shape[0]
+    tall = 2 * half
+    groups = cells_ref.shape[1] // LANES
     lane = iota((half, LANES), 1)
     is_odd = odd("gy")
-    top_ref[...] = jnp.maximum(jnp.maximum(own_ref[...], far_ref[...]), jnp.maximum(next_ref[half:, :], swap_ref[half:, :]))
-    from_swap = swap_ref[0:half, :]
-    from_next = next_ref[0:half, :]
+    from_swap = swap_ref[...]
+    from_next = next_ref[...]
     from_before = jnp.where(is_odd, from_swap, from_next)
     from_after = jnp.where(is_odd, from_next, from_swap)
     for side in range(2):
@@ -240,13 +269,8 @@
             left = pltpu.roll(from_before, (LANES - HALO - at) % LANES, axis=1)
             right = pltpu.roll(from_after, (-at) % LANES, axis=1)
             low = comp * tall + side * half
-            plain[low : low + half, cols:] = jnp.where(lane < LANES // 2, right, left)
-    source = iota((wide, wide), 0)
-    goal = iota((wide, wide), 1)
-    place = groups * (goal % LANES) + goal // LANES
-    place = jnp.where(place < cols + 2 * HALO, (place + wide - HALO) % wide, 0)
-    select = jnp.where(source == place, 1.0, 0.0).astype(jnp.bfloat16)
-    found = selected(plain[...], select)
+            plain[low : low + half, :] = jnp.where(lane < LANES // 2, right, left)
+    found = cells_ref[...] + selected(plain[...], select_ref[...])
     for comp in range(4):
         for group in range(groups):
             cells = found[comp * tall : (comp + 1) * tall, group * LANES : (group + 1) * LANES]
@@ -267,23 +291,26 @@
     changes(load, count, groups, 0, store)
 
 
-def steps_kernel(field_ref, change_ref, own_ref, mate_ref, wide_ref, out_ref, field, base, mid, dealt, result, sems):
+def steps_kernel(field_ref, change_ref, select_ref, own_ref, mate_ref, out_ref, field, base, mid, dealt, result, sems):
     rows, cols = out_ref.shape[1:]
     tall = rows + 2 * HALO
     groups = field_ref.shape[2]
-    half_factor = (-0.125 * COURANT / MOMENTUM) / jnp.maximum(own_ref[...], jnp.maximum(mate_ref[...], wide_ref[...]))
+    scale = (0.125 * COURANT / MOMENTUM) / jnp.max(jnp.maximum(own_ref[...], mate_ref[...]))
+    scales = (1.0, scale, scale, scale * scale)
 
     def one_step(start, count, old, first_changes):
         def to_mid(row, col, parts):
             for comp in range(4):
-                move = half_factor * parts[comp]
-                moved = old[comp, row, col] + move
+                cells, move = old[comp, row, col], parts[comp]
+                if first_changes is not None:
+                    cells, move = scales[comp] * cells, (scales[comp] * scale) * move
+                moved = cells - move
                 base[comp, row, col] = moved
-                mid[comp, row, col] = moved + move
+                mid[comp, row, col] = moved - move
 
         def to_field(row, col, parts):
             for comp in range(4):
-                new = base[comp, row, col] + half_factor * parts[comp]
+                new = base[comp, row, col] - parts[comp]
                 dealt[comp, col, pl.ds(start + row, 8, stride=count), :] = new
 
         def load_from(ref):
@@ -306,22 +333,19 @@
         one_step(4 * index, (tall - 8 * index) // 8, field, None)
 
     wide = groups * LANES
-    source = iota((wide, cols), 0)
-    goal = iota((wide, cols), 1)
-    select = jnp.where(groups * (source % LANES) + source // LANES == goal + HALO, 1.0, 0.0).astype(jnp.bfloat16)
     lane = iota((rows, LANES), 1)
     parts = []
     for comp in range(4):
         line = []
         for group in range(groups):
-            place = groups * lane + group
+            place = place_of(lane, group, groups)
             inside = (place >= HALO) & (place < HALO + cols)
             line.append(jnp.where(inside, dealt[comp, group, HALO : HALO + rows, :], 0.0))
         parts.append(jnp.concatenate(line, axis=1))
-    found = selected(jnp.concatenate(parts, axis=0), select)
+    found = selected(jnp.concatenate(parts, axis=0), select_ref[...])
     copies = []
     for comp in range(4):
-        result[comp] = (2.0 / SCALES[comp]) * found[comp * rows : (comp + 1) * rows, :]
+        result[comp] = ((2.0 / SCALES[comp]) / scales[comp]) * found[comp * rows : (comp + 1) * rows, :]
         copies.append(pltpu.make_async_copy(result.at[comp], out_ref.at[comp], sems.at[comp]))
         copies[-1].start()
     for copy in copies:
@@ -364,7 +388,7 @@
     second = swapped_pairs(second, "gx", 1)
     first = swapped_pairs(first, "gx", 0)
     far = swapped_threes(top, "gx"), swapped_bit(top, "gx", 4)
-    side_type = array(tall // 2 + 8, LANES)
+    side_type = array(tall // 2, LANES)
     up, down, first, second, top = pl.pallas_call(
         pack_kernel,
         out_shape=(edge_type, edge_type, side_type, side_type, array(8, LANES)),
@@ -376,26 +400,48 @@
     second = swapped_pairs(second, "gy", 1)
     first = swapped_pairs(first, "gy", 0)
     far = swapped_bit(top, "gy", 2)
-    own = top
-    top = jnp.maximum(jnp.maximum(own, far), jnp.maximum(first[tall // 2 :], second[tall // 2 :]))
+    wide = groups * LANES
+    cells, halo_select, back_select, top = pl.pallas_call(
+        deal_kernel,
+        out_shape=(
+            array(parts * tall, wide),
+            jax.ShapeDtypeStruct((wide - cols, wide), jnp.bfloat16),
+            jax.ShapeDtypeStruct((wide, cols), jnp.bfloat16),
+            array(8, LANES),
+        ),
+        in_specs=[VMEM] * 4,
+        out_specs=(VMEM,) * 4,
+        scratch_shapes=[pltpu.VMEM((parts * tall, cols), jnp.float32)],
+        compiler_params=params(8),
+        cost_estimate=pl.CostEstimate(flops=300_000_000, bytes_accessed=1_500_000, transcendentals=0),
+        name="deal",
+    )(state, up, down, top)
+    top = pl.pallas_call(
+        join_kernel,
+        out_shape=array(8, LANES),
+        in_specs=[VMEM] * 4,
+        out_specs=VMEM,
+        compiler_params=params(4),
+        name="join",
+    )(second, first, far, top)
     for axis, covered in (("gy", 4), ("gx", 8)):
         while covered < lax.axis_size(axis):
             top = jnp.maximum(top, sent(top, axis, covered))
             covered *= 2
-    top = swapped_bit(top, "gx", 1), top
+    mate = swapped_bit(top, "gx", 1)
     dealt_type = array(parts, tall // 8, groups, 8, LANES)
     dealt = pltpu.VMEM(dealt_type.shape, jnp.float32)
     plain = pltpu.VMEM((parts, groups, tall, LANES), jnp.float32)
-    field, change, own = pl.pallas_call(
+    field, change = pl.pallas_call(
         first_kernel,
-        out_shape=(dealt_type, dealt_type, array(8, LANES)),
-        in_specs=[VMEM] * 7,
-        out_specs=(VMEM,) * 3,
-        scratch_shapes=[pltpu.VMEM((parts * tall, groups * LANES), jnp.float32), plain],
+        out_shape=(dealt_type, dealt_type),
+        in_specs=[VMEM] * 4,
+        out_specs=(VMEM,) * 2,
+        scratch_shapes=[pltpu.VMEM((parts * tall, LANES), jnp.float32), plain],
         compiler_params=params(16),
         cost_estimate=pl.CostEstimate(flops=20_000_000, bytes_accessed=2_000_000, transcendentals=400_000),
         name="first",
-    )(state, up, down, second, far, first, own)
+    )(cells, halo_select, second, first)
     return pl.pallas_call(
         steps_kernel,
         out_shape=array(parts, rows, cols),
@@ -405,7 +451,7 @@
         + [plain, pltpu.VMEM((parts, rows, cols), jnp.float32), pltpu.SemaphoreType.DMA((parts,))],
         compiler_params=params(16),
         name="steps",
-    )(field, change, own, *top)
+    )(field, change, back_select, top, mate)
 
 
 def solution(mesh):

time: 23.4 us -> 23.3 us (level)
  Pallas kernels: 6.21 us -> 6.58 us
  starting transfers between devices: 9.24 us -> 8.95 us
    ppermute x4, waiting for transfers between devices: 0.01 us -> 3.48 us  [swapped_pairs(): return lax.ppermute(value, axis, pairs)]
    ppermute x3, starting transfers between devices: 1.35 us -> 3.96 us  [swapped_bit(): lax.ppermute(value, axis, [(i, i ^ by) for i in range(lax.axis_size(axis))])]
    ppermute x3, waiting for transfers between devices: 5.12 us -> 2.52 us  [swapped_bit(): lax.ppermute(value, axis, [(i, i ^ by) for i in range(lax.axis_size(axis))])]
    ppermute x4, starting transfers between devices: 7.07 us -> 4.98 us  [swapped_pairs(): return lax.ppermute(value, axis, pairs)]
    ppermute x1, waiting for transfers between devices: 1.72 us -> 0.66 us  [swapped_threes(): lax.ppermute(value, axis, [(i, (i + 3 - 6 * (i % 2)) % count) for i in ra...]
    ppermute x1, starting transfers between devices: 0.82 us -> 0.01 us  [swapped_threes(): lax.ppermute(value, axis, [(i, (i + 3 - 6 * (i % 2)) % count) for i in ra...]
    pallas_call x1 -> x3, Pallas kernels: 1.21 us -> 1.59 us  [the longest x1 1 us: local(): pl.pallas_call(first_kernel, out_shape=(dealt_type, dealt_type), in_specs...]
  transfers between devices with their start and end apart: 8 -> 8, of which waited for: 3 -> 4; matrix products, arithmetic and copies ran while one was open for 0% -> 0% of each run, Pallas kernels for 5% -> 6%
where the time goes in v11:
time: 23.3 us; the launch traced here: 23.2 us
  starting transfers between devices  8.95 us (38%)
  waiting for transfers between devices  6.66 us (29%)
  Pallas kernels  6.58 us (28%)
  local copies, waits for them, and re-layouts  0.91 us (4%)
    ppermute x4, starting transfers between devices, swapped_pairs(): return lax.ppermute(value, axis, pairs)  4.98 us
    pallas_call x1, Pallas kernels, local(): pl.pallas_call(steps_kernel, out_shape=array(parts, rows, cols), in_specs...  4.71 us
    ppermute x3, starting transfers between devices, swapped_bit(): lax.ppermute(value, axis, [(i, i ^ by) for i in range(lax.axis_size(axis))])  3.96 us
    ppermute x4, waiting for transfers between devices, swapped_pairs(): return lax.ppermute(value, axis, pairs)  3.48 us
    ppermute x3, waiting for transfers between devices, swapped_bit(): lax.ppermute(value, axis, [(i, i ^ by) for i in range(lax.axis_size(axis))])  2.52 us
    pallas_call x1, Pallas kernels, local(): pl.pallas_call(first_kernel, out_shape=(dealt_type, dealt_type), in_specs...  1 us
    unnamed x4, local copies, waits for them, and re-layouts  0.91 us
    ppermute x1, waiting for transfers between devices, swapped_threes(): lax.ppermute(value, axis, [(i, (i + 3 - 6 * (i % 2)) % count) for i in ra...  0.66 us
  transfers between devices with their start and end apart: 8, of which 4 were waited for; matrix products, arithmetic and copies ran while one was open for 0% of the time, Pallas kernels for 6%

profile of v11, /device:TPU:0, one launch (start us, length us, event | category | flops | bytes accessed | tf_op | source)
XLA Modules:
  0.0 23.2 jit_solution(18381555272907205575)
XLA Ops:
  0.0 0.0 copy-start
  0.0 0.9 %copy-done = f32[4,32,256]{2,1,0:T(8,128)S(1)} copy-done((f32[4,32,256]{2,1,0:T(8,128)S(1)}, f32[4,32,256]{2,1,0:T(8,128)}, u32[]{:S(2)}) %copy-start) | copy-done | bytes 131096
  0.9 0.2 edge.1
  1.1 3.4 %collective-permute-start = (f32[72,256]{1,0:T(8,128)S(1)}, f32[72,256]{1,0:T(8,128)S(1)}, u32[]{:S(2)}, u32[]{:S(2)}) collective-permute-start(f32[72,256]{1,0:T(8,128)S(1)} %get-tuple-element.19), channel_id=1, source_target_pairs={{4,8},{8,4},{12,16},{16,12},{20,24},{24,20},{28,0},{0,28},{5,9},{9... | collective-permute-start | bytes 221192 | tf_op jit(solution)/shard_map/ppermute | solution.py:373
  4.5 0.0 collective-permute-start.3
  4.5 0.0 copy-start.1
  4.5 1.2 %collective-permute-start.2 = (f32[8,128]{1,0:T(8,128)S(1)}, f32[8,128]{1,0:T(8,128)S(1)}, u32[]{:S(2)}, u32[]{:S(2)}) collective-permute-start(f32[8,128]{1,0:T(8,128)S(1)} %get-tuple-element.20.own_ref), channel_id=1, source_target_pairs={{0,16},{4,20},{8,24},{12,28},{16,0},{20,4},{24,8},{28,12},{1,17},{... | collective-permute-start | bytes 12296 | tf_op jit(solution)/shard_map/ppermute | solution.py:365
  5.7 0.0 collective-permute-start.1
  5.7 2.4 %collective-permute-done.2.four_ref = f32[8,128]{1,0:T(8,128)S(1)} collective-permute-done((f32[8,128]{1,0:T(8,128)S(1)}, f32[8,128]{1,0:T(8,128)S(1)}, u32[]{:S(2)}, u32[]{:S(2)}) %collective-permute-start.2) | collective-permute-done | bytes 4128 | tf_op jit(solution)/shard_map/ppermute | solution.py:365
  8.1 0.7 %collective-permute-done.1.three_ref = f32[8,128]{1,0:T(8,128)S(1)} collective-permute-done((f32[8,128]{1,0:T(8,128)S(1)}, f32[8,128]{1,0:T(8,128)S(1)}, u32[]{:S(2)}, u32[]{:S(2)}) %collective-permute-start.1) | collective-permute-done | bytes 4128 | tf_op jit(solution)/shard_map/ppermute | solution.py:377
  8.7 0.0 collective-permute-done.next_ref
  8.7 0.0 collective-permute-done.3.swap_ref
  8.8 0.1 pack.1
  8.9 2.7 %collective-permute-start.6 = (f32[8,128]{1,0:T(8,128)S(1)}, f32[8,128]{1,0:T(8,128)S(1)}, u32[]{:S(2)}, u32[]{:S(2)}) collective-permute-start(f32[8,128]{1,0:T(8,128)S(1)} %get-tuple-element.24.own_ref), channel_id=1, source_target_pairs={{0,2},{1,3},{2,0},{3,1},{4,6},{5,7},{6,4},{7,5},{8,10},{9,11},{10,... | collective-permute-start | bytes 12296 | tf_op jit(solution)/shard_map/ppermute | solution.py:365
  11.5 1.4 %collective-permute-start.4 = (f32[32,128]{1,0:T(8,128)S(1)}, f32[32,128]{1,0:T(8,128)S(1)}, u32[]{:S(2)}, u32[]{:S(2)}) collective-permute-start(f32[32,128]{1,0:T(8,128)S(1)} %get-tuple-element.27), channel_id=1, source_target_pairs={{1,2},{2,1},{3,0},{0,3},{5,6},{6,5},{7,4},{4,7},{9,10},{10,9},{11,... | collective-permute-start | bytes 49160 | tf_op jit(solution)/shard_map/ppermute | solution.py:373
  12.9 0.2 collective-permute-start.5
  13.1 0.0 copy-done.1
  13.1 0.5 %deal.1 = (f32[256,384]{1,0:T(8,128)S(1)}, bf16[128,384]{1,0:T(8,128)(2,1)S(1)}, bf16[384,256]{1,0:T(8,128)(2,1)S(1)}, f32[8,128]{1,0:T(8,128)S(1)}) custom-call(f32[4,32,256]{2,1,0:T(8,128)S(1)} %copy-done.1, f32[72,256]{1,0:T(8,128)S(1)} %get-tuple-element.22.up_ref, f32[72,256]{1,0:T(8,128)S(1)} %get-tuple-element.23.down_ref, ...), custom_call_target="tpu_custom_call" | custom-call | flops 300000000 | bytes 1500000 | tf_op jit(solution)/shard_map/deal/pallas_call | solution.py:404
  13.6 0.0 collective-permute-done.6.far_ref
  13.6 3.5 %collective-permute-done.4.next_ref = f32[32,128]{1,0:T(8,128)S(1)} collective-permute-done((f32[32,128]{1,0:T(8,128)S(1)}, f32[32,128]{1,0:T(8,128)S(1)}, u32[]{:S(2)}, u32[]{:S(2)}) %collective-permute-start.4) | collective-permute-done | bytes 16416 | tf_op jit(solution)/shard_map/ppermute | solution.py:373
  17.1 0.0 collective-permute-done.5.swap_ref
  17.1 0.1 join.1.own_ref
  17.2 0.1 collective-permute-start.7
  17.3 1.0 %first.1 = (f32[4,8,3,8,128]{4,3,2,1,0:T(8,128)S(1)}, f32[4,8,3,8,128]{4,3,2,1,0:T(8,128)S(1)}) custom-call(f32[256,384]{1,0:T(8,128)S(1)} %get-tuple-element.25.cells_ref, bf16[128,384]{1,0:T(8,128)(2,1)S(1)} %get-tuple-element.26.select_ref, f32[32,128]{1,0:T(8,128)S(1)} %collective-permute-done.4.next_ref, f32[32,128]{1,0:T(8,128)S(1)} %collective-permute-done.5.swap_ref), custom_call_target="tpu_custom_call" | custom-call | flops 20000000 | bytes 2000000 | tf_op jit(solution)/shard_map/first/pallas_call | solution.py:435
  18.3 0.1 collective-permute-done.7.mate_ref
  18.4 4.7 %steps.1 = f32[4,32,256]{2,1,0:T(8,128)} custom-call(f32[4,8,3,8,128]{4,3,2,1,0:T(8,128)S(1)} %get-tuple-element.29.field_ref, f32[4,8,3,8,128]{4,3,2,1,0:T(8,128)S(1)} %get-tuple-element.30.change_ref, bf16[384,256]{1,0:T(8,128)(2,1)S(1)} %get-tuple-element.31.select_ref, f32[8,128]{1,0:T(8,128)S(1)} %join.1.own_ref, ...), custom_call_target="tpu_custom_call" | custom-call | tf_op jit(solution)/shard_map/steps/pallas_call | solution.py:445
Async XLA Ops:
  0.0 0.9 %copy-start = (f32[4,32,256]{2,1,0:T(8,128)S(1)}, f32[4,32,256]{2,1,0:T(8,128)}, u32[]{:S(2)}) copy-start(f32[4,32,256]{2,1,0:T(8,128)} %state_ref.3) | copy-start | bytes 393220
  1.1 7.7 %collective-permute-start = (f32[72,256]{1,0:T(8,128)S(1)}, f32[72,256]{1,0:T(8,128)S(1)}, u32[]{:S(2)}, u32[]{:S(2)}) collective-permute-start(f32[72,256]{1,0:T(8,128)S(1)} %get-tuple-element.19), channel_id=1, source_target_pairs={{4,8},{8,4},{12,16},{16,12},{20,24},{24,20},{28,0},{0,28},{5,9},{9... | collective-permute-start | bytes 221192 | tf_op jit(solution)/shard_map/ppermute | solution.py:373
  4.5 4.3 %collective-permute-start.3 = (f32[72,256]{1,0:T(8,128)S(1)}, f32[72,256]{1,0:T(8,128)S(1)}, u32[]{:S(2)}, u32[]{:S(2)}) collective-permute-start(f32[72,256]{1,0:T(8,128)S(1)} %get-tuple-element.21), channel_id=1, source_target_pairs={{0,4},{4,0},{8,12},{12,8},{16,20},{20,16},{24,28},{28,24},{1,5},{5... | collective-permute-start | bytes 221192 | tf_op jit(solution)/shard_map/ppermute | solution.py:373
  4.5 8.7 %copy-start.1 = (f32[4,32,256]{2,1,0:T(8,128)S(1)}, f32[4,32,256]{2,1,0:T(8,128)}, u32[]{:S(2)}) copy-start(f32[4,32,256]{2,1,0:T(8,128)} %state_ref.3) | copy-start | bytes 393220
  4.5 3.6 %collective-permute-start.2 = (f32[8,128]{1,0:T(8,128)S(1)}, f32[8,128]{1,0:T(8,128)S(1)}, u32[]{:S(2)}, u32[]{:S(2)}) collective-permute-start(f32[8,128]{1,0:T(8,128)S(1)} %get-tuple-element.20.own_ref), channel_id=1, source_target_pairs={{0,16},{4,20},{8,24},{12,28},{16,0},{20,4},{24,8},{28,12},{1,17},{... | collective-permute-start | bytes 12296 | tf_op jit(solution)/shard_map/ppermute | solution.py:365
  5.7 3.0 %collective-permute-start.1 = (f32[8,128]{1,0:T(8,128)S(1)}, f32[8,128]{1,0:T(8,128)S(1)}, u32[]{:S(2)}, u32[]{:S(2)}) collective-permute-start(f32[8,128]{1,0:T(8,128)S(1)} %get-tuple-element.20.own_ref), channel_id=1, source_target_pairs={{0,12},{4,24},{8,20},{12,0},{16,28},{20,8},{24,4},{28,16},{1,13},{... | collective-permute-start | bytes 12296 | tf_op jit(solution)/shard_map/ppermute | solution.py:377
  8.9 4.7 %collective-permute-start.6 = (f32[8,128]{1,0:T(8,128)S(1)}, f32[8,128]{1,0:T(8,128)S(1)}, u32[]{:S(2)}, u32[]{:S(2)}) collective-permute-start(f32[8,128]{1,0:T(8,128)S(1)} %get-tuple-element.24.own_ref), channel_id=1, source_target_pairs={{0,2},{1,3},{2,0},{3,1},{4,6},{5,7},{6,4},{7,5},{8,10},{9,11},{10,... | collective-permute-start | bytes 12296 | tf_op jit(solution)/shard_map/ppermute | solution.py:365
  11.5 5.5 %collective-permute-start.4 = (f32[32,128]{1,0:T(8,128)S(1)}, f32[32,128]{1,0:T(8,128)S(1)}, u32[]{:S(2)}, u32[]{:S(2)}) collective-permute-start(f32[32,128]{1,0:T(8,128)S(1)} %get-tuple-element.27), channel_id=1, source_target_pairs={{1,2},{2,1},{3,0},{0,3},{5,6},{6,5},{7,4},{4,7},{9,10},{10,9},{11,... | collective-permute-start | bytes 49160 | tf_op jit(solution)/shard_map/ppermute | solution.py:373
  12.9 4.2 %collective-permute-start.5 = (f32[32,128]{1,0:T(8,128)S(1)}, f32[32,128]{1,0:T(8,128)S(1)}, u32[]{:S(2)}, u32[]{:S(2)}) collective-permute-start(f32[32,128]{1,0:T(8,128)S(1)} %get-tuple-element.28), channel_id=1, source_target_pairs={{0,1},{1,0},{2,3},{3,2},{4,5},{5,4},{6,7},{7,6},{8,9},{9,8},{10,11... | collective-permute-start | bytes 49160 | tf_op jit(solution)/shard_map/ppermute | solution.py:373
  17.2 1.2 %collective-permute-start.7 = (f32[8,128]{1,0:T(8,128)S(1)}, f32[8,128]{1,0:T(8,128)S(1)}, u32[]{:S(2)}, u32[]{:S(2)}) collective-permute-start(f32[8,128]{1,0:T(8,128)S(1)} %join.1.own_ref), channel_id=1, source_target_pairs={{0,4},{4,0},{8,12},{12,8},{16,20},{20,16},{24,28},{28,24},{1,5},{5... | collective-permute-start | bytes 12296 | tf_op jit(solution)/shard_map/ppermute | solution.py:365

commit v12 on v11

--- a/solution.py
+++ b/solution.py
@@ -157,7 +157,7 @@
         else:
             first_low = low
         high = next_high
-    faces.append(face(high, rolled(first_low, -1, 1)))
+    faces.append(face(high, known(rolled(first_low[0], -1, 1))))
     return [minus(faces[at], faces[at - 1] if at else rolled(faces[-1], 1, 1)) for at in range(count)]
 
 
@@ -179,7 +179,7 @@
         if self.first_low is None:
             self.first_low = low
         else:
-            flux = face(rolled(self.high, 1, 0) if row == 0 else self.high, low)
+            flux = face(known(rolled(self.high[0], 1, 0)) if row == 0 else self.high, low)
             if self.last_flux is None:
                 self.first_flux = flux
             else:
@@ -244,13 +244,6 @@
     goal = iota((wide, cols), 1)
     back = place_of(source % LANES, source // LANES, groups) == goal + HALO
     back_select_ref[...] = jnp.where(back, 1.0, 0.0).astype(jnp.bfloat16)
-
-
-def join_kernel(next_ref, swap_ref, far_ref, own_ref, top_ref):
-    speeds = jnp.maximum(next_ref[0:8, :], swap_ref[0:8, :])
-    carried = (iota((8, LANES), 0) == 0) & (iota((8, LANES), 1) < LANES // 2)
-    known_here = jnp.maximum(own_ref[...], far_ref[...])
-    top_ref[...] = jnp.full((8, LANES), jnp.max(jnp.where(carried, speeds, known_here)))
 
 
 def first_kernel(cells_ref, select_ref, next_ref, swap_ref, field_ref, change_ref, plain, dealt):
@@ -416,14 +409,8 @@
         cost_estimate=pl.CostEstimate(flops=300_000_000, bytes_accessed=1_500_000, transcendentals=0),
         name="deal",
     )(state, up, down, top)
-    top = pl.pallas_call(
-        join_kernel,
-        out_shape=array(8, LANES),
-        in_specs=[VMEM] * 4,
-        out_specs=VMEM,
-        compiler_params=params(4),
-        name="join",
-    )(second, first, far, top)
+    carried = (iota((8, LANES), 0) == 0) & (iota((8, LANES), 1) < LANES // 2)
+    top = jnp.maximum(jnp.maximum(top, far), jnp.where(carried, jnp.maximum(first[:8], second[:8]), 0.0))
     for axis, covered in (("gy", 4), ("gx", 8)):
         while covered < lax.axis_size(axis):
             top = jnp.maximum(top, sent(top, axis, covered))

time: 23.3 us -> 23.9 us (1.026)
  waiting for transfers between devices: 6.66 us -> 7.32 us
    ppermute x4, starting transfers between devices: 4.98 us -> 2.54 us  [swapped_pairs(): return lax.ppermute(value, axis, pairs)]
    ppermute x3, waiting for transfers between devices: 2.52 us -> 0.14 us  [swapped_bit(): lax.ppermute(value, axis, [(i, i ^ by) for i in range(lax.axis_size(axis))])]
    ppermute x4, waiting for transfers between devices: 3.48 us -> 5.77 us  [swapped_pairs(): return lax.ppermute(value, axis, pairs)]
    ppermute x3, starting transfers between devices: 3.96 us -> 5.7 us  [swapped_bit(): lax.ppermute(value, axis, [(i, i ^ by) for i in range(lax.axis_size(axis))])]
    ppermute x1, waiting for transfers between devices: 0.66 us -> 1.4 us  [swapped_threes(): lax.ppermute(value, axis, [(i, (i + 3 - 6 * (i % 2)) % count) for i in ra...]
    ppermute x1, starting transfers between devices: 0.01 us -> 0.65 us  [swapped_threes(): lax.ppermute(value, axis, [(i, (i + 3 - 6 * (i % 2)) % count) for i in ra...]
where the time goes in v12:
time: 23.9 us; the launch traced here: 23.8 us
  starting transfers between devices  8.88 us (37%)
  waiting for transfers between devices  7.32 us (31%)
  Pallas kernels  6.5 us (27%)
  local copies, waits for them, and re-layouts  0.91 us (4%)
    ppermute x4, waiting for transfers between devices, swapped_pairs(): return lax.ppermute(value, axis, pairs)  5.77 us
    ppermute x3, starting transfers between devices, swapped_bit(): lax.ppermute(value, axis, [(i, i ^ by) for i in range(lax.axis_size(axis))])  5.7 us
    pallas_call x1, Pallas kernels, local(): pl.pallas_call(steps_kernel, out_shape=array(parts, rows, cols), in_specs...  4.74 us
    ppermute x4, starting transfers between devices, swapped_pairs(): return lax.ppermute(value, axis, pairs)  2.54 us
    ppermute x1, waiting for transfers between devices, swapped_threes(): lax.ppermute(value, axis, [(i, (i + 3 - 6 * (i % 2)) % count) for i in ra...  1.4 us
    pallas_call x1, Pallas kernels, local(): pl.pallas_call(first_kernel, out_shape=(dealt_type, dealt_type), in_specs...  1.01 us
    unnamed x4, local copies, waits for them, and re-layouts  0.91 us
    ppermute x1, starting transfers between devices, swapped_threes(): lax.ppermute(value, axis, [(i, (i + 3 - 6 * (i % 2)) % count) for i in ra...  0.65 us
  transfers between devices with their start and end apart: 8, of which 4 were waited for; matrix products, arithmetic and copies ran while one was open for 0% of the time, Pallas kernels for 6%

profile of v12, /device:TPU:0, one launch (start us, length us, event | category | flops | bytes accessed | tf_op | source)
XLA Modules:
  0.0 23.8 jit_solution(9425876666110267830)
XLA Ops:
  0.0 0.0 copy-start
  0.0 0.9 %copy-done = f32[4,32,256]{2,1,0:T(8,128)S(1)} copy-done((f32[4,32,256]{2,1,0:T(8,128)S(1)}, f32[4,32,256]{2,1,0:T(8,128)}, u32[]{:S(2)}) %copy-start) | copy-done | bytes 131096
  0.9 0.0 copy-start.1
  0.9 0.2 edge.1
  1.1 3.0 %collective-permute-start.2 = (f32[8,128]{1,0:T(8,128)S(1)}, f32[8,128]{1,0:T(8,128)S(1)}, u32[]{:S(2)}, u32[]{:S(2)}) collective-permute-start(f32[8,128]{1,0:T(8,128)S(1)} %get-tuple-element.20.own_ref), channel_id=1, source_target_pairs={{0,16},{4,20},{8,24},{12,28},{16,0},{20,4},{24,8},{28,12},{1,17},{... | collective-permute-start | bytes 12296 | tf_op jit(solution)/shard_map/ppermute | solution.py:358
  4.1 0.7 %collective-permute-start.1 = (f32[8,128]{1,0:T(8,128)S(1)}, f32[8,128]{1,0:T(8,128)S(1)}, u32[]{:S(2)}, u32[]{:S(2)}) collective-permute-start(f32[8,128]{1,0:T(8,128)S(1)} %get-tuple-element.20.own_ref), channel_id=1, source_target_pairs={{0,12},{4,24},{8,20},{12,0},{16,28},{20,8},{24,4},{28,16},{1,13},{... | collective-permute-start | bytes 12296 | tf_op jit(solution)/shard_map/ppermute | solution.py:370
  4.8 0.6 %collective-permute-start = (f32[72,256]{1,0:T(8,128)S(1)}, f32[72,256]{1,0:T(8,128)S(1)}, u32[]{:S(2)}, u32[]{:S(2)}) collective-permute-start(f32[72,256]{1,0:T(8,128)S(1)} %get-tuple-element.19), channel_id=1, source_target_pairs={{4,8},{8,4},{12,16},{16,12},{20,24},{24,20},{28,0},{0,28},{5,9},{9... | collective-permute-start | bytes 221192 | tf_op jit(solution)/shard_map/ppermute | solution.py:366
  5.4 0.3 %collective-permute-start.3 = (f32[72,256]{1,0:T(8,128)S(1)}, f32[72,256]{1,0:T(8,128)S(1)}, u32[]{:S(2)}, u32[]{:S(2)}) collective-permute-start(f32[72,256]{1,0:T(8,128)S(1)} %get-tuple-element.21), channel_id=1, source_target_pairs={{0,4},{4,0},{8,12},{12,8},{16,20},{20,16},{24,28},{28,24},{1,5},{5... | collective-permute-start | bytes 221192 | tf_op jit(solution)/shard_map/ppermute | solution.py:366
  5.7 0.0 collective-permute-done.2.four_ref
  5.7 1.4 %collective-permute-done.1.three_ref = f32[8,128]{1,0:T(8,128)S(1)} collective-permute-done((f32[8,128]{1,0:T(8,128)S(1)}, f32[8,128]{1,0:T(8,128)S(1)}, u32[]{:S(2)}, u32[]{:S(2)}) %collective-permute-start.1) | collective-permute-done | bytes 4128 | tf_op jit(solution)/shard_map/ppermute | solution.py:370
  7.1 2.3 %collective-permute-done.next_ref = f32[72,256]{1,0:T(8,128)S(1)} collective-permute-done((f32[72,256]{1,0:T(8,128)S(1)}, f32[72,256]{1,0:T(8,128)S(1)}, u32[]{:S(2)}, u32[]{:S(2)}) %collective-permute-start) | collective-permute-done | bytes 73760 | tf_op jit(solution)/shard_map/ppermute | solution.py:366
  9.4 0.0 collective-permute-done.3.swap_ref
  9.4 0.0 copy-done.1
  9.4 0.1 pack.1
  9.6 2.7 %collective-permute-start.6 = (f32[8,128]{1,0:T(8,128)S(1)}, f32[8,128]{1,0:T(8,128)S(1)}, u32[]{:S(2)}, u32[]{:S(2)}) collective-permute-start(f32[8,128]{1,0:T(8,128)S(1)} %get-tuple-element.24.own_ref), channel_id=1, source_target_pairs={{0,2},{1,3},{2,0},{3,1},{4,6},{5,7},{6,4},{7,5},{8,10},{9,11},{10,... | collective-permute-start | bytes 12296 | tf_op jit(solution)/shard_map/ppermute | solution.py:358
  12.2 1.3 %collective-permute-start.4 = (f32[32,128]{1,0:T(8,128)S(1)}, f32[32,128]{1,0:T(8,128)S(1)}, u32[]{:S(2)}, u32[]{:S(2)}) collective-permute-start(f32[32,128]{1,0:T(8,128)S(1)} %get-tuple-element.27), channel_id=1, source_target_pairs={{1,2},{2,1},{3,0},{0,3},{5,6},{6,5},{7,4},{4,7},{9,10},{10,9},{11,... | collective-permute-start | bytes 49160 | tf_op jit(solution)/shard_map/ppermute | solution.py:366
  13.6 0.2 collective-permute-start.5
  13.8 0.5 %deal.1 = (f32[256,384]{1,0:T(8,128)S(1)}, bf16[128,384]{1,0:T(8,128)(2,1)S(1)}, bf16[384,256]{1,0:T(8,128)(2,1)S(1)}, f32[8,128]{1,0:T(8,128)S(1)}) custom-call(f32[4,32,256]{2,1,0:T(8,128)S(1)} %copy-done.1, f32[72,256]{1,0:T(8,128)S(1)} %get-tuple-element.22.up_ref, f32[72,256]{1,0:T(8,128)S(1)} %get-tuple-element.23.down_ref, ...), custom_call_target="tpu_custom_call" | custom-call | flops 300000000 | bytes 1500000 | tf_op jit(solution)/shard_map/deal/pallas_call | solution.py:397
  14.3 0.0 collective-permute-done.6
  14.3 3.5 %collective-permute-done.4.next_ref = f32[32,128]{1,0:T(8,128)S(1)} collective-permute-done((f32[32,128]{1,0:T(8,128)S(1)}, f32[32,128]{1,0:T(8,128)S(1)}, u32[]{:S(2)}, u32[]{:S(2)}) %collective-permute-start.4) | collective-permute-done | bytes 16416 | tf_op jit(solution)/shard_map/ppermute | solution.py:366
  17.8 0.0 collective-permute-done.5.swap_ref
  17.8 0.1 fusion.1.own_ref
  17.8 0.0 collective-permute-start.7
  17.9 1.0 %first.1 = (f32[4,8,3,8,128]{4,3,2,1,0:T(8,128)S(1)}, f32[4,8,3,8,128]{4,3,2,1,0:T(8,128)S(1)}) custom-call(f32[256,384]{1,0:T(8,128)S(1)} %get-tuple-element.25.cells_ref, bf16[128,384]{1,0:T(8,128)(2,1)S(1)} %get-tuple-element.26.select_ref, f32[32,128]{1,0:T(8,128)S(1)} %collective-permute-done.4.next_ref, f32[32,128]{1,0:T(8,128)S(1)} %collective-permute-done.5.swap_ref), custom_call_target="tpu_custom_call" | custom-call | flops 20000000 | bytes 2000000 | tf_op jit(solution)/shard_map/first/pallas_call | solution.py:422
  18.9 0.1 collective-permute-done.7.mate_ref
  19.0 4.7 %steps.1 = f32[4,32,256]{2,1,0:T(8,128)} custom-call(f32[4,8,3,8,128]{4,3,2,1,0:T(8,128)S(1)} %get-tuple-element.29.field_ref, f32[4,8,3,8,128]{4,3,2,1,0:T(8,128)S(1)} %get-tuple-element.30.change_ref, bf16[384,256]{1,0:T(8,128)(2,1)S(1)} %get-tuple-element.31.select_ref, f32[8,128]{1,0:T(8,128)S(1)} %fusion.1.own_ref, ...), custom_call_target="tpu_custom_call" | custom-call | tf_op jit(solution)/shard_map/steps/pallas_call | solution.py:432
  (2 shorter events, 0.0 us)
Async XLA Ops:
  0.0 0.9 %copy-start = (f32[4,32,256]{2,1,0:T(8,128)S(1)}, f32[4,32,256]{2,1,0:T(8,128)}, u32[]{:S(2)}) copy-start(f32[4,32,256]{2,1,0:T(8,128)} %state_ref.3) | copy-start | bytes 393220
  0.9 8.5 %copy-start.1 = (f32[4,32,256]{2,1,0:T(8,128)S(1)}, f32[4,32,256]{2,1,0:T(8,128)}, u32[]{:S(2)}) copy-start(f32[4,32,256]{2,1,0:T(8,128)} %state_ref.3) | copy-start | bytes 393220
  1.1 4.7 %collective-permute-start.2 = (f32[8,128]{1,0:T(8,128)S(1)}, f32[8,128]{1,0:T(8,128)S(1)}, u32[]{:S(2)}, u32[]{:S(2)}) collective-permute-start(f32[8,128]{1,0:T(8,128)S(1)} %get-tuple-element.20.own_ref), channel_id=1, source_target_pairs={{0,16},{4,20},{8,24},{12,28},{16,0},{20,4},{24,8},{28,12},{1,17},{... | collective-permute-start | bytes 12296 | tf_op jit(solution)/shard_map/ppermute | solution.py:358
  4.1 3.0 %collective-permute-start.1 = (f32[8,128]{1,0:T(8,128)S(1)}, f32[8,128]{1,0:T(8,128)S(1)}, u32[]{:S(2)}, u32[]{:S(2)}) collective-permute-start(f32[8,128]{1,0:T(8,128)S(1)} %get-tuple-element.20.own_ref), channel_id=1, source_target_pairs={{0,12},{4,24},{8,20},{12,0},{16,28},{20,8},{24,4},{28,16},{1,13},{... | collective-permute-start | bytes 12296 | tf_op jit(solution)/shard_map/ppermute | solution.py:370
  4.8 4.7 %collective-permute-start = (f32[72,256]{1,0:T(8,128)S(1)}, f32[72,256]{1,0:T(8,128)S(1)}, u32[]{:S(2)}, u32[]{:S(2)}) collective-permute-start(f32[72,256]{1,0:T(8,128)S(1)} %get-tuple-element.19), channel_id=1, source_target_pairs={{4,8},{8,4},{12,16},{16,12},{20,24},{24,20},{28,0},{0,28},{5,9},{9... | collective-permute-start | bytes 221192 | tf_op jit(solution)/shard_map/ppermute | solution.py:366
  5.4 4.1 %collective-permute-start.3 = (f32[72,256]{1,0:T(8,128)S(1)}, f32[72,256]{1,0:T(8,128)S(1)}, u32[]{:S(2)}, u32[]{:S(2)}) collective-permute-start(f32[72,256]{1,0:T(8,128)S(1)} %get-tuple-element.21), channel_id=1, source_target_pairs={{0,4},{4,0},{8,12},{12,8},{16,20},{20,16},{24,28},{28,24},{1,5},{5... | collective-permute-start | bytes 221192 | tf_op jit(solution)/shard_map/ppermute | solution.py:366
  9.6 4.7 %collective-permute-start.6 = (f32[8,128]{1,0:T(8,128)S(1)}, f32[8,128]{1,0:T(8,128)S(1)}, u32[]{:S(2)}, u32[]{:S(2)}) collective-permute-start(f32[8,128]{1,0:T(8,128)S(1)} %get-tuple-element.24.own_ref), channel_id=1, source_target_pairs={{0,2},{1,3},{2,0},{3,1},{4,6},{5,7},{6,4},{7,5},{8,10},{9,11},{10,... | collective-permute-start | bytes 12296 | tf_op jit(solution)/shard_map/ppermute | solution.py:358
  12.2 5.5 %collective-permute-start.4 = (f32[32,128]{1,0:T(8,128)S(1)}, f32[32,128]{1,0:T(8,128)S(1)}, u32[]{:S(2)}, u32[]{:S(2)}) collective-permute-start(f32[32,128]{1,0:T(8,128)S(1)} %get-tuple-element.27), channel_id=1, source_target_pairs={{1,2},{2,1},{3,0},{0,3},{5,6},{6,5},{7,4},{4,7},{9,10},{10,9},{11,... | collective-permute-start | bytes 49160 | tf_op jit(solution)/shard_map/ppermute | solution.py:366
  13.6 4.2 %collective-permute-start.5 = (f32[32,128]{1,0:T(8,128)S(1)}, f32[32,128]{1,0:T(8,128)S(1)}, u32[]{:S(2)}, u32[]{:S(2)}) collective-permute-start(f32[32,128]{1,0:T(8,128)S(1)} %get-tuple-element.28), channel_id=1, source_target_pairs={{0,1},{1,0},{2,3},{3,2},{4,5},{5,4},{6,7},{7,6},{8,9},{9,8},{10,11... | collective-permute-start | bytes 49160 | tf_op jit(solution)/shard_map/ppermute | solution.py:366
  17.8 1.2 %collective-permute-start.7 = (f32[8,128]{1,0:T(8,128)S(1)}, f32[8,128]{1,0:T(8,128)S(1)}, u32[]{:S(2)}, u32[]{:S(2)}) collective-permute-start(f32[8,128]{1,0:T(8,128)S(1)} %fusion.1.own_ref), channel_id=1, source_target_pairs={{0,4},{4,0},{8,12},{12,8},{16,20},{20,16},{24,28},{28,24},{1,5},{5... | collective-permute-start | bytes 12296 | tf_op jit(solution)/shard_map/ppermute | solution.py:358

commit v13 on v11

--- a/solution.py
+++ b/solution.py
@@ -157,7 +157,7 @@
         else:
             first_low = low
         high = next_high
-    faces.append(face(high, rolled(first_low, -1, 1)))
+    faces.append(face(high, known(rolled(first_low[0], -1, 1))))
     return [minus(faces[at], faces[at - 1] if at else rolled(faces[-1], 1, 1)) for at in range(count)]
 
 
@@ -179,7 +179,7 @@
         if self.first_low is None:
             self.first_low = low
         else:
-            flux = face(rolled(self.high, 1, 0) if row == 0 else self.high, low)
+            flux = face(known(rolled(self.high[0], 1, 0)) if row == 0 else self.high, low)
             if self.last_flux is None:
                 self.first_flux = flux
             else:
@@ -291,7 +291,7 @@
     changes(load, count, groups, 0, store)
 
 
-def steps_kernel(field_ref, change_ref, select_ref, own_ref, mate_ref, out_ref, field, base, mid, dealt, result, sems):
+def steps_kernel(field_ref, change_ref, select_ref, own_ref, mate_ref, out_ref, field, base, mid, dealt, plain, result, sems):
     rows, cols = out_ref.shape[1:]
     tall = rows + 2 * HALO
     groups = field_ref.shape[2]
@@ -309,9 +309,21 @@
                 mid[comp, row, col] = moved - move
 
         def to_field(row, col, parts):
-            for comp in range(4):
-                new = base[comp, row, col] - parts[comp]
-                dealt[comp, col, pl.ds(start + row, 8, stride=count), :] = new
+            new = [base[comp, row, col] - parts[comp] for comp in range(4)]
+            if start + 4 < 4 * STEPS:
+                for comp in range(4):
+                    dealt[comp, col, pl.ds(start + row, 8, stride=count), :] = new[comp]
+                return
+            place = place_of(iota((8, LANES), 1), col, groups)
+            inside = (place >= HALO) & (place < HALO + cols)
+            ready.setdefault(row, {})[col] = [jnp.where(inside, part, 0.0) for part in new]
+            if len(ready[row]) == groups:
+                lines = [jnp.concatenate([ready[row][at][comp] for at in range(groups)], axis=1) for comp in range(4)]
+                found = selected(jnp.concatenate(lines, axis=0), select_ref[...])
+                for comp in range(4):
+                    for tile in range(cols // LANES):
+                        cells = found[comp * 8 : (comp + 1) * 8, tile * LANES : (tile + 1) * LANES]
+                        plain[comp, tile, pl.ds(row, 8, stride=count), :] = cells
 
         def load_from(ref):
             return lambda row, col: [ref[comp, row, col] for comp in range(4)]
@@ -328,24 +340,17 @@
             changes(load_from(old), count, groups, 0, to_mid)
         changes(load_from(mid), count, groups, count // 2, to_field)
 
+    ready = {}
     one_step(0, tall // 8, field_ref, change_ref)
     for index in range(1, STEPS):
         one_step(4 * index, (tall - 8 * index) // 8, field, None)
 
-    wide = groups * LANES
-    lane = iota((rows, LANES), 1)
-    parts = []
+    copies = []
+    skip = HALO - 4 * (STEPS - 1)
     for comp in range(4):
-        line = []
-        for group in range(groups):
-            place = place_of(lane, group, groups)
-            inside = (place >= HALO) & (place < HALO + cols)
-            line.append(jnp.where(inside, dealt[comp, group, HALO : HALO + rows, :], 0.0))
-        parts.append(jnp.concatenate(line, axis=1))
-    found = selected(jnp.concatenate(parts, axis=0), select_ref[...])
-    copies = []
-    for comp in range(4):
-        result[comp] = ((2.0 / SCALES[comp]) / scales[comp]) * found[comp * rows : (comp + 1) * rows, :]
+        for tile in range(cols // LANES):
+            cells = plain[comp, tile, skip : skip + rows, :]
+            result[comp, :, tile * LANES : (tile + 1) * LANES] = ((2.0 / SCALES[comp]) / scales[comp]) * cells
         copies.append(pltpu.make_async_copy(result.at[comp], out_ref.at[comp], sems.at[comp]))
         copies[-1].start()
     for copy in copies:
@@ -448,7 +453,7 @@
         in_specs=[VMEM] * 5,
         out_specs=pl.BlockSpec(memory_space=pl.ANY),
         scratch_shapes=[dealt] * 3
-        + [plain, pltpu.VMEM((parts, rows, cols), jnp.float32), pltpu.SemaphoreType.DMA((parts,))],
+        + [plain, plain, pltpu.VMEM((parts, rows, cols), jnp.float32), pltpu.SemaphoreType.DMA((parts,))],
         compiler_params=params(16),
         name="steps",
     )(field, change, back_select, top, mate)

time: 23.3 us -> 23.5 us (level)
  no operation moved by 1% of the time
where the time goes in v13:
time: 23.5 us; the launch traced here: 23.3 us
  starting transfers between devices  8.95 us (38%)
  Pallas kernels  6.75 us (29%)
  waiting for transfers between devices  6.65 us (28%)
  local copies, waits for them, and re-layouts  0.91 us (4%)
    ppermute x4, starting transfers between devices, swapped_pairs(): return lax.ppermute(value, axis, pairs)  4.98 us
    pallas_call x1, Pallas kernels, local(): pl.pallas_call(steps_kernel, out_shape=array(parts, rows, cols), in_specs...  4.87 us
    ppermute x3, starting transfers between devices, swapped_bit(): lax.ppermute(value, axis, [(i, i ^ by) for i in range(lax.axis_size(axis))])  3.96 us
    ppermute x4, waiting for transfers between devices, swapped_pairs(): return lax.ppermute(value, axis, pairs)  3.48 us
    ppermute x3, waiting for transfers between devices, swapped_bit(): lax.ppermute(value, axis, [(i, i ^ by) for i in range(lax.axis_size(axis))])  2.51 us
    pallas_call x1, Pallas kernels, local(): pl.pallas_call(first_kernel, out_shape=(dealt_type, dealt_type), in_specs...  1.01 us
    unnamed x4, local copies, waits for them, and re-layouts  0.91 us
    ppermute x1, waiting for transfers between devices, swapped_threes(): lax.ppermute(value, axis, [(i, (i + 3 - 6 * (i % 2)) % count) for i in ra...  0.66 us
  transfers between devices with their start and end apart: 8, of which 4 were waited for; matrix products, arithmetic and copies ran while one was open for 0% of the time, Pallas kernels for 6%

profile of v13, /device:TPU:0, one launch (start us, length us, event | category | flops | bytes accessed | tf_op | source)
XLA Modules:
  0.0 23.3 jit_solution(8272486990918316837)
XLA Ops:
  0.0 0.0 copy-start
  0.0 0.9 %copy-done = f32[4,32,256]{2,1,0:T(8,128)S(1)} copy-done((f32[4,32,256]{2,1,0:T(8,128)S(1)}, f32[4,32,256]{2,1,0:T(8,128)}, u32[]{:S(2)}) %copy-start) | copy-done | bytes 131096
  0.9 0.2 edge.1
  1.1 3.4 %collective-permute-start = (f32[72,256]{1,0:T(8,128)S(1)}, f32[72,256]{1,0:T(8,128)S(1)}, u32[]{:S(2)}, u32[]{:S(2)}) collective-permute-start(f32[72,256]{1,0:T(8,128)S(1)} %get-tuple-element.19), channel_id=1, source_target_pairs={{4,8},{8,4},{12,16},{16,12},{20,24},{24,20},{28,0},{0,28},{5,9},{9... | collective-permute-start | bytes 221192 | tf_op jit(solution)/shard_map/ppermute | solution.py:378
  4.5 0.0 collective-permute-start.3
  4.5 0.0 copy-start.1
  4.5 1.2 %collective-permute-start.2 = (f32[8,128]{1,0:T(8,128)S(1)}, f32[8,128]{1,0:T(8,128)S(1)}, u32[]{:S(2)}, u32[]{:S(2)}) collective-permute-start(f32[8,128]{1,0:T(8,128)S(1)} %get-tuple-element.20.own_ref), channel_id=1, source_target_pairs={{0,16},{4,20},{8,24},{12,28},{16,0},{20,4},{24,8},{28,12},{1,17},{... | collective-permute-start | bytes 12296 | tf_op jit(solution)/shard_map/ppermute | solution.py:370
  5.7 0.0 collective-permute-start.1
  5.7 2.4 %collective-permute-done.2.four_ref = f32[8,128]{1,0:T(8,128)S(1)} collective-permute-done((f32[8,128]{1,0:T(8,128)S(1)}, f32[8,128]{1,0:T(8,128)S(1)}, u32[]{:S(2)}, u32[]{:S(2)}) %collective-permute-start.2) | collective-permute-done | bytes 4128 | tf_op jit(solution)/shard_map/ppermute | solution.py:370
  8.1 0.7 %collective-permute-done.1.three_ref = f32[8,128]{1,0:T(8,128)S(1)} collective-permute-done((f32[8,128]{1,0:T(8,128)S(1)}, f32[8,128]{1,0:T(8,128)S(1)}, u32[]{:S(2)}, u32[]{:S(2)}) %collective-permute-start.1) | collective-permute-done | bytes 4128 | tf_op jit(solution)/shard_map/ppermute | solution.py:382
  8.7 0.0 collective-permute-done.next_ref
  8.7 0.0 collective-permute-done.3.swap_ref
  8.8 0.1 pack.1
  8.9 2.7 %collective-permute-start.6 = (f32[8,128]{1,0:T(8,128)S(1)}, f32[8,128]{1,0:T(8,128)S(1)}, u32[]{:S(2)}, u32[]{:S(2)}) collective-permute-start(f32[8,128]{1,0:T(8,128)S(1)} %get-tuple-element.24.own_ref), channel_id=1, source_target_pairs={{0,2},{1,3},{2,0},{3,1},{4,6},{5,7},{6,4},{7,5},{8,10},{9,11},{10,... | collective-permute-start | bytes 12296 | tf_op jit(solution)/shard_map/ppermute | solution.py:370
  11.5 1.4 %collective-permute-start.4 = (f32[32,128]{1,0:T(8,128)S(1)}, f32[32,128]{1,0:T(8,128)S(1)}, u32[]{:S(2)}, u32[]{:S(2)}) collective-permute-start(f32[32,128]{1,0:T(8,128)S(1)} %get-tuple-element.27), channel_id=1, source_target_pairs={{1,2},{2,1},{3,0},{0,3},{5,6},{6,5},{7,4},{4,7},{9,10},{10,9},{11,... | collective-permute-start | bytes 49160 | tf_op jit(solution)/shard_map/ppermute | solution.py:378
  12.9 0.2 collective-permute-start.5
  13.1 0.0 copy-done.1
  13.1 0.5 %deal.1 = (f32[256,384]{1,0:T(8,128)S(1)}, bf16[128,384]{1,0:T(8,128)(2,1)S(1)}, bf16[384,256]{1,0:T(8,128)(2,1)S(1)}, f32[8,128]{1,0:T(8,128)S(1)}) custom-call(f32[4,32,256]{2,1,0:T(8,128)S(1)} %copy-done.1, f32[72,256]{1,0:T(8,128)S(1)} %get-tuple-element.22.up_ref, f32[72,256]{1,0:T(8,128)S(1)} %get-tuple-element.23.down_ref, ...), custom_call_target="tpu_custom_call" | custom-call | flops 300000000 | bytes 1500000 | tf_op jit(solution)/shard_map/deal/pallas_call | solution.py:409
  13.6 0.0 collective-permute-done.6.far_ref
  13.6 3.5 %collective-permute-done.4.next_ref = f32[32,128]{1,0:T(8,128)S(1)} collective-permute-done((f32[32,128]{1,0:T(8,128)S(1)}, f32[32,128]{1,0:T(8,128)S(1)}, u32[]{:S(2)}, u32[]{:S(2)}) %collective-permute-start.4) | collective-permute-done | bytes 16416 | tf_op jit(solution)/shard_map/ppermute | solution.py:378
  17.1 0.0 collective-permute-done.5.swap_ref
  17.1 0.1 join.1.own_ref
  17.2 0.1 collective-permute-start.7
  17.3 1.0 %first.1 = (f32[4,8,3,8,128]{4,3,2,1,0:T(8,128)S(1)}, f32[4,8,3,8,128]{4,3,2,1,0:T(8,128)S(1)}) custom-call(f32[256,384]{1,0:T(8,128)S(1)} %get-tuple-element.25.cells_ref, bf16[128,384]{1,0:T(8,128)(2,1)S(1)} %get-tuple-element.26.select_ref, f32[32,128]{1,0:T(8,128)S(1)} %collective-permute-done.4.next_ref, f32[32,128]{1,0:T(8,128)S(1)} %collective-permute-done.5.swap_ref), custom_call_target="tpu_custom_call" | custom-call | flops 20000000 | bytes 2000000 | tf_op jit(solution)/shard_map/first/pallas_call | solution.py:440
  18.3 0.1 collective-permute-done.7.mate_ref
  18.4 4.9 %steps.1 = f32[4,32,256]{2,1,0:T(8,128)} custom-call(f32[4,8,3,8,128]{4,3,2,1,0:T(8,128)S(1)} %get-tuple-element.29.field_ref, f32[4,8,3,8,128]{4,3,2,1,0:T(8,128)S(1)} %get-tuple-element.30.change_ref, bf16[384,256]{1,0:T(8,128)(2,1)S(1)} %get-tuple-element.31.select_ref, f32[8,128]{1,0:T(8,128)S(1)} %join.1.own_ref, ...), custom_call_target="tpu_custom_call" | custom-call | tf_op jit(solution)/shard_map/steps/pallas_call | solution.py:450
Async XLA Ops:
  0.0 0.9 %copy-start = (f32[4,32,256]{2,1,0:T(8,128)S(1)}, f32[4,32,256]{2,1,0:T(8,128)}, u32[]{:S(2)}) copy-start(f32[4,32,256]{2,1,0:T(8,128)} %state_ref.3) | copy-start | bytes 393220
  1.1 7.7 %collective-permute-start = (f32[72,256]{1,0:T(8,128)S(1)}, f32[72,256]{1,0:T(8,128)S(1)}, u32[]{:S(2)}, u32[]{:S(2)}) collective-permute-start(f32[72,256]{1,0:T(8,128)S(1)} %get-tuple-element.19), channel_id=1, source_target_pairs={{4,8},{8,4},{12,16},{16,12},{20,24},{24,20},{28,0},{0,28},{5,9},{9... | collective-permute-start | bytes 221192 | tf_op jit(solution)/shard_map/ppermute | solution.py:378
  4.5 4.3 %collective-permute-start.3 = (f32[72,256]{1,0:T(8,128)S(1)}, f32[72,256]{1,0:T(8,128)S(1)}, u32[]{:S(2)}, u32[]{:S(2)}) collective-permute-start(f32[72,256]{1,0:T(8,128)S(1)} %get-tuple-element.21), channel_id=1, source_target_pairs={{0,4},{4,0},{8,12},{12,8},{16,20},{20,16},{24,28},{28,24},{1,5},{5... | collective-permute-start | bytes 221192 | tf_op jit(solution)/shard_map/ppermute | solution.py:378
  4.5 8.7 %copy-start.1 = (f32[4,32,256]{2,1,0:T(8,128)S(1)}, f32[4,32,256]{2,1,0:T(8,128)}, u32[]{:S(2)}) copy-start(f32[4,32,256]{2,1,0:T(8,128)} %state_ref.3) | copy-start | bytes 393220
  4.5 3.6 %collective-permute-start.2 = (f32[8,128]{1,0:T(8,128)S(1)}, f32[8,128]{1,0:T(8,128)S(1)}, u32[]{:S(2)}, u32[]{:S(2)}) collective-permute-start(f32[8,128]{1,0:T(8,128)S(1)} %get-tuple-element.20.own_ref), channel_id=1, source_target_pairs={{0,16},{4,20},{8,24},{12,28},{16,0},{20,4},{24,8},{28,12},{1,17},{... | collective-permute-start | bytes 12296 | tf_op jit(solution)/shard_map/ppermute | solution.py:370
  5.7 3.0 %collective-permute-start.1 = (f32[8,128]{1,0:T(8,128)S(1)}, f32[8,128]{1,0:T(8,128)S(1)}, u32[]{:S(2)}, u32[]{:S(2)}) collective-permute-start(f32[8,128]{1,0:T(8,128)S(1)} %get-tuple-element.20.own_ref), channel_id=1, source_target_pairs={{0,12},{4,24},{8,20},{12,0},{16,28},{20,8},{24,4},{28,16},{1,13},{... | collective-permute-start | bytes 12296 | tf_op jit(solution)/shard_map/ppermute | solution.py:382
  8.9 4.7 %collective-permute-start.6 = (f32[8,128]{1,0:T(8,128)S(1)}, f32[8,128]{1,0:T(8,128)S(1)}, u32[]{:S(2)}, u32[]{:S(2)}) collective-permute-start(f32[8,128]{1,0:T(8,128)S(1)} %get-tuple-element.24.own_ref), channel_id=1, source_target_pairs={{0,2},{1,3},{2,0},{3,1},{4,6},{5,7},{6,4},{7,5},{8,10},{9,11},{10,... | collective-permute-start | bytes 12296 | tf_op jit(solution)/shard_map/ppermute | solution.py:370
  11.5 5.5 %collective-permute-start.4 = (f32[32,128]{1,0:T(8,128)S(1)}, f32[32,128]{1,0:T(8,128)S(1)}, u32[]{:S(2)}, u32[]{:S(2)}) collective-permute-start(f32[32,128]{1,0:T(8,128)S(1)} %get-tuple-element.27), channel_id=1, source_target_pairs={{1,2},{2,1},{3,0},{0,3},{5,6},{6,5},{7,4},{4,7},{9,10},{10,9},{11,... | collective-permute-start | bytes 49160 | tf_op jit(solution)/shard_map/ppermute | solution.py:378
  12.9 4.2 %collective-permute-start.5 = (f32[32,128]{1,0:T(8,128)S(1)}, f32[32,128]{1,0:T(8,128)S(1)}, u32[]{:S(2)}, u32[]{:S(2)}) collective-permute-start(f32[32,128]{1,0:T(8,128)S(1)} %get-tuple-element.28), channel_id=1, source_target_pairs={{0,1},{1,0},{2,3},{3,2},{4,5},{5,4},{6,7},{7,6},{8,9},{9,8},{10,11... | collective-permute-start | bytes 49160 | tf_op jit(solution)/shard_map/ppermute | solution.py:378
  17.2 1.2 %collective-permute-start.7 = (f32[8,128]{1,0:T(8,128)S(1)}, f32[8,128]{1,0:T(8,128)S(1)}, u32[]{:S(2)}, u32[]{:S(2)}) collective-permute-start(f32[8,128]{1,0:T(8,128)S(1)} %join.1.own_ref), channel_id=1, source_target_pairs={{0,4},{4,0},{8,12},{12,8},{16,20},{20,16},{24,28},{28,24},{1,5},{5... | collective-permute-start | bytes 12296 | tf_op jit(solution)/shard_map/ppermute | solution.py:370

commit v14 on v11

--- a/solution.py
+++ b/solution.py
@@ -151,13 +151,14 @@
     jumps = [minus(values[at + 1], values[at]) for at in range(count - 1)] + [end_jump]
     faces, first_low, high = [], None, None
     for at in range(count):
-        low, next_high = cell(wholes[at], jumps[at - 1] if at else rolled(end_jump, 1, 1), jumps[at])
+        jump = jumps[at - 1] if at else minus(values[0], rolled(values[-1], 1, 1))
+        low, next_high = cell(wholes[at], jump, jumps[at])
         if at:
             faces.append(face(high, low))
         else:
             first_low = low
         high = next_high
-    faces.append(face(high, rolled(first_low, -1, 1)))
+    faces.append(face(high, known(rolled(first_low[0], -1, 1))))
     return [minus(faces[at], faces[at - 1] if at else rolled(faces[-1], 1, 1)) for at in range(count)]
 
 
@@ -165,6 +166,7 @@
     def __init__(self, count, begin, here, after):
         self.count, self.begin = count, begin
         self.jump = self.first_jump = minus(after, here)
+        self.before = here
         self.first_low = self.first_flux = self.last_flux = self.high = None
 
     def feed(self, row, here, whole, after):
@@ -173,20 +175,20 @@
             next_jump = self.first_jump
         else:
             next_jump = minus(rolled(after, -1, 0) if next_row == 0 else after, here)
-        jump = rolled(self.jump, 1, 0) if row == 0 else self.jump
+        jump = minus(here, rolled(self.before, 1, 0)) if row == 0 else self.jump
         low, high = cell(whole, jump, next_jump)
         done = []
         if self.first_low is None:
             self.first_low = low
         else:
-            flux = face(rolled(self.high, 1, 0) if row == 0 else self.high, low)
+            flux = face(known(rolled(self.high[0], 1, 0)) if row == 0 else self.high, low)
             if self.last_flux is None:
                 self.first_flux = flux
             else:
                 seen = rolled(flux, -1, 0) if row == 0 else flux
                 done.append(((row - 1) % self.count, minus(seen, self.last_flux)))
             self.last_flux = flux
-        self.high, self.jump = high, next_jump
+        self.high, self.jump, self.before = high, next_jump, here
         if after is None:
             flux = face(high, self.first_low)
             done.append((row, minus(flux, self.last_flux)))

time: 23.3 us -> 23.2 us (level)
  transfers between devices with their start and end apart: 8 -> 8, of which waited for: 4 -> 4; matrix products, arithmetic and copies ran while one was open for 0% -> 0% of each run, Pallas kernels for 6% -> 7%
where the time goes in v14:
time: 23.2 us; the launch traced here: 23 us
  starting transfers between devices  8.95 us (39%)
  waiting for transfers between devices  6.62 us (29%)
  Pallas kernels  6.51 us (28%)
  local copies, waits for them, and re-layouts  0.91 us (4%)
    ppermute x4, starting transfers between devices, swapped_pairs(): return lax.ppermute(value, axis, pairs)  4.98 us
    pallas_call x1, Pallas kernels, local(): pl.pallas_call(steps_kernel, out_shape=array(parts, rows, cols), in_specs...  4.59 us
    ppermute x3, starting transfers between devices, swapped_bit(): lax.ppermute(value, axis, [(i, i ^ by) for i in range(lax.axis_size(axis))])  3.96 us
    ppermute x4, waiting for transfers between devices, swapped_pairs(): return lax.ppermute(value, axis, pairs)  3.48 us
    ppermute x3, waiting for transfers between devices, swapped_bit(): lax.ppermute(value, axis, [(i, i ^ by) for i in range(lax.axis_size(axis))])  2.48 us
    pallas_call x1, Pallas kernels, local(): pl.pallas_call(first_kernel, out_shape=(dealt_type, dealt_type), in_specs...  1.04 us
    unnamed x4, local copies, waits for them, and re-layouts  0.91 us
    ppermute x1, waiting for transfers between devices, swapped_threes(): lax.ppermute(value, axis, [(i, (i + 3 - 6 * (i % 2)) % count) for i in ra...  0.66 us
  transfers between devices with their start and end apart: 8, of which 4 were waited for; matrix products, arithmetic and copies ran while one was open for 0% of the time, Pallas kernels for 7%

profile of v14, /device:TPU:0, one launch (start us, length us, event | category | flops | bytes accessed | tf_op | source)
XLA Modules:
  0.0 23.0 jit_solution(16205013886585864228)
XLA Ops:
  0.0 0.0 copy-start
  0.0 0.9 %copy-done = f32[4,32,256]{2,1,0:T(8,128)S(1)} copy-done((f32[4,32,256]{2,1,0:T(8,128)S(1)}, f32[4,32,256]{2,1,0:T(8,128)}, u32[]{:S(2)}) %copy-start) | copy-done | bytes 131096
  0.9 0.2 edge.1
  1.1 3.4 %collective-permute-start = (f32[72,256]{1,0:T(8,128)S(1)}, f32[72,256]{1,0:T(8,128)S(1)}, u32[]{:S(2)}, u32[]{:S(2)}) collective-permute-start(f32[72,256]{1,0:T(8,128)S(1)} %get-tuple-element.19), channel_id=1, source_target_pairs={{4,8},{8,4},{12,16},{16,12},{20,24},{24,20},{28,0},{0,28},{5,9},{9... | collective-permute-start | bytes 221192 | tf_op jit(solution)/shard_map/ppermute | solution.py:375
  4.5 0.0 collective-permute-start.3
  4.5 0.0 copy-start.1
  4.5 1.2 %collective-permute-start.2 = (f32[8,128]{1,0:T(8,128)S(1)}, f32[8,128]{1,0:T(8,128)S(1)}, u32[]{:S(2)}, u32[]{:S(2)}) collective-permute-start(f32[8,128]{1,0:T(8,128)S(1)} %get-tuple-element.20.own_ref), channel_id=1, source_target_pairs={{0,16},{4,20},{8,24},{12,28},{16,0},{20,4},{24,8},{28,12},{1,17},{... | collective-permute-start | bytes 12296 | tf_op jit(solution)/shard_map/ppermute | solution.py:367
  5.7 0.0 collective-permute-start.1
  5.7 2.4 %collective-permute-done.2.four_ref = f32[8,128]{1,0:T(8,128)S(1)} collective-permute-done((f32[8,128]{1,0:T(8,128)S(1)}, f32[8,128]{1,0:T(8,128)S(1)}, u32[]{:S(2)}, u32[]{:S(2)}) %collective-permute-start.2) | collective-permute-done | bytes 4128 | tf_op jit(solution)/shard_map/ppermute | solution.py:367
  8.1 0.7 %collective-permute-done.1.three_ref = f32[8,128]{1,0:T(8,128)S(1)} collective-permute-done((f32[8,128]{1,0:T(8,128)S(1)}, f32[8,128]{1,0:T(8,128)S(1)}, u32[]{:S(2)}, u32[]{:S(2)}) %collective-permute-start.1) | collective-permute-done | bytes 4128 | tf_op jit(solution)/shard_map/ppermute | solution.py:379
  8.7 0.0 collective-permute-done.next_ref
  8.7 0.0 collective-permute-done.3.swap_ref
  8.8 0.1 pack.1
  8.9 2.7 %collective-permute-start.6 = (f32[8,128]{1,0:T(8,128)S(1)}, f32[8,128]{1,0:T(8,128)S(1)}, u32[]{:S(2)}, u32[]{:S(2)}) collective-permute-start(f32[8,128]{1,0:T(8,128)S(1)} %get-tuple-element.24.own_ref), channel_id=1, source_target_pairs={{0,2},{1,3},{2,0},{3,1},{4,6},{5,7},{6,4},{7,5},{8,10},{9,11},{10,... | collective-permute-start | bytes 12296 | tf_op jit(solution)/shard_map/ppermute | solution.py:367
  11.5 1.4 %collective-permute-start.4 = (f32[32,128]{1,0:T(8,128)S(1)}, f32[32,128]{1,0:T(8,128)S(1)}, u32[]{:S(2)}, u32[]{:S(2)}) collective-permute-start(f32[32,128]{1,0:T(8,128)S(1)} %get-tuple-element.27), channel_id=1, source_target_pairs={{1,2},{2,1},{3,0},{0,3},{5,6},{6,5},{7,4},{4,7},{9,10},{10,9},{11,... | collective-permute-start | bytes 49160 | tf_op jit(solution)/shard_map/ppermute | solution.py:375
  12.9 0.2 collective-permute-start.5
  13.1 0.0 copy-done.1
  13.1 0.5 %deal.1 = (f32[256,384]{1,0:T(8,128)S(1)}, bf16[128,384]{1,0:T(8,128)(2,1)S(1)}, bf16[384,256]{1,0:T(8,128)(2,1)S(1)}, f32[8,128]{1,0:T(8,128)S(1)}) custom-call(f32[4,32,256]{2,1,0:T(8,128)S(1)} %copy-done.1, f32[72,256]{1,0:T(8,128)S(1)} %get-tuple-element.22.up_ref, f32[72,256]{1,0:T(8,128)S(1)} %get-tuple-element.23.down_ref, ...), custom_call_target="tpu_custom_call" | custom-call | flops 300000000 | bytes 1500000 | tf_op jit(solution)/shard_map/deal/pallas_call | solution.py:406
  13.6 0.0 collective-permute-done.6.far_ref
  13.6 3.5 %collective-permute-done.4.next_ref = f32[32,128]{1,0:T(8,128)S(1)} collective-permute-done((f32[32,128]{1,0:T(8,128)S(1)}, f32[32,128]{1,0:T(8,128)S(1)}, u32[]{:S(2)}, u32[]{:S(2)}) %collective-permute-start.4) | collective-permute-done | bytes 16416 | tf_op jit(solution)/shard_map/ppermute | solution.py:375
  17.1 0.0 collective-permute-done.5.swap_ref
  17.1 0.1 join.1.own_ref
  17.2 0.1 collective-permute-start.7
  17.3 1.0 %first.1 = (f32[4,8,3,8,128]{4,3,2,1,0:T(8,128)S(1)}, f32[4,8,3,8,128]{4,3,2,1,0:T(8,128)S(1)}) custom-call(f32[256,384]{1,0:T(8,128)S(1)} %get-tuple-element.25.cells_ref, bf16[128,384]{1,0:T(8,128)(2,1)S(1)} %get-tuple-element.26.select_ref, f32[32,128]{1,0:T(8,128)S(1)} %collective-permute-done.4.next_ref, f32[32,128]{1,0:T(8,128)S(1)} %collective-permute-done.5.swap_ref), custom_call_target="tpu_custom_call" | custom-call | flops 20000000 | bytes 2000000 | tf_op jit(solution)/shard_map/first/pallas_call | solution.py:437
  18.3 0.1 collective-permute-done.7.mate_ref
  18.4 4.6 %steps.1 = f32[4,32,256]{2,1,0:T(8,128)} custom-call(f32[4,8,3,8,128]{4,3,2,1,0:T(8,128)S(1)} %get-tuple-element.29.field_ref, f32[4,8,3,8,128]{4,3,2,1,0:T(8,128)S(1)} %get-tuple-element.30.change_ref, bf16[384,256]{1,0:T(8,128)(2,1)S(1)} %get-tuple-element.31.select_ref, f32[8,128]{1,0:T(8,128)S(1)} %join.1.own_ref, ...), custom_call_target="tpu_custom_call" | custom-call | tf_op jit(solution)/shard_map/steps/pallas_call | solution.py:447
Async XLA Ops:
  0.0 0.9 %copy-start = (f32[4,32,256]{2,1,0:T(8,128)S(1)}, f32[4,32,256]{2,1,0:T(8,128)}, u32[]{:S(2)}) copy-start(f32[4,32,256]{2,1,0:T(8,128)} %state_ref.3) | copy-start | bytes 393220
  1.1 7.7 %collective-permute-start = (f32[72,256]{1,0:T(8,128)S(1)}, f32[72,256]{1,0:T(8,128)S(1)}, u32[]{:S(2)}, u32[]{:S(2)}) collective-permute-start(f32[72,256]{1,0:T(8,128)S(1)} %get-tuple-element.19), channel_id=1, source_target_pairs={{4,8},{8,4},{12,16},{16,12},{20,24},{24,20},{28,0},{0,28},{5,9},{9... | collective-permute-start | bytes 221192 | tf_op jit(solution)/shard_map/ppermute | solution.py:375
  4.5 4.3 %collective-permute-start.3 = (f32[72,256]{1,0:T(8,128)S(1)}, f32[72,256]{1,0:T(8,128)S(1)}, u32[]{:S(2)}, u32[]{:S(2)}) collective-permute-start(f32[72,256]{1,0:T(8,128)S(1)} %get-tuple-element.21), channel_id=1, source_target_pairs={{0,4},{4,0},{8,12},{12,8},{16,20},{20,16},{24,28},{28,24},{1,5},{5... | collective-permute-start | bytes 221192 | tf_op jit(solution)/shard_map/ppermute | solution.py:375
  4.5 8.7 %copy-start.1 = (f32[4,32,256]{2,1,0:T(8,128)S(1)}, f32[4,32,256]{2,1,0:T(8,128)}, u32[]{:S(2)}) copy-start(f32[4,32,256]{2,1,0:T(8,128)} %state_ref.3) | copy-start | bytes 393220
  4.5 3.6 %collective-permute-start.2 = (f32[8,128]{1,0:T(8,128)S(1)}, f32[8,128]{1,0:T(8,128)S(1)}, u32[]{:S(2)}, u32[]{:S(2)}) collective-permute-start(f32[8,128]{1,0:T(8,128)S(1)} %get-tuple-element.20.own_ref), channel_id=1, source_target_pairs={{0,16},{4,20},{8,24},{12,28},{16,0},{20,4},{24,8},{28,12},{1,17},{... | collective-permute-start | bytes 12296 | tf_op jit(solution)/shard_map/ppermute | solution.py:367
  5.7 3.0 %collective-permute-start.1 = (f32[8,128]{1,0:T(8,128)S(1)}, f32[8,128]{1,0:T(8,128)S(1)}, u32[]{:S(2)}, u32[]{:S(2)}) collective-permute-start(f32[8,128]{1,0:T(8,128)S(1)} %get-tuple-element.20.own_ref), channel_id=1, source_target_pairs={{0,12},{4,24},{8,20},{12,0},{16,28},{20,8},{24,4},{28,16},{1,13},{... | collective-permute-start | bytes 12296 | tf_op jit(solution)/shard_map/ppermute | solution.py:379
  8.9 4.7 %collective-permute-start.6 = (f32[8,128]{1,0:T(8,128)S(1)}, f32[8,128]{1,0:T(8,128)S(1)}, u32[]{:S(2)}, u32[]{:S(2)}) collective-permute-start(f32[8,128]{1,0:T(8,128)S(1)} %get-tuple-element.24.own_ref), channel_id=1, source_target_pairs={{0,2},{1,3},{2,0},{3,1},{4,6},{5,7},{6,4},{7,5},{8,10},{9,11},{10,... | collective-permute-start | bytes 12296 | tf_op jit(solution)/shard_map/ppermute | solution.py:367
  11.5 5.5 %collective-permute-start.4 = (f32[32,128]{1,0:T(8,128)S(1)}, f32[32,128]{1,0:T(8,128)S(1)}, u32[]{:S(2)}, u32[]{:S(2)}) collective-permute-start(f32[32,128]{1,0:T(8,128)S(1)} %get-tuple-element.27), channel_id=1, source_target_pairs={{1,2},{2,1},{3,0},{0,3},{5,6},{6,5},{7,4},{4,7},{9,10},{10,9},{11,... | collective-permute-start | bytes 49160 | tf_op jit(solution)/shard_map/ppermute | solution.py:375
  12.9 4.2 %collective-permute-start.5 = (f32[32,128]{1,0:T(8,128)S(1)}, f32[32,128]{1,0:T(8,128)S(1)}, u32[]{:S(2)}, u32[]{:S(2)}) collective-permute-start(f32[32,128]{1,0:T(8,128)S(1)} %get-tuple-element.28), channel_id=1, source_target_pairs={{0,1},{1,0},{2,3},{3,2},{4,5},{5,4},{6,7},{7,6},{8,9},{9,8},{10,11... | collective-permute-start | bytes 49160 | tf_op jit(solution)/shard_map/ppermute | solution.py:375
  17.2 1.2 %collective-permute-start.7 = (f32[8,128]{1,0:T(8,128)S(1)}, f32[8,128]{1,0:T(8,128)S(1)}, u32[]{:S(2)}, u32[]{:S(2)}) collective-permute-start(f32[8,128]{1,0:T(8,128)S(1)} %join.1.own_ref), channel_id=1, source_target_pairs={{0,4},{4,0},{8,12},{12,8},{16,20},{20,16},{24,28},{28,24},{1,5},{5... | collective-permute-start | bytes 12296 | tf_op jit(solution)/shard_map/ppermute | solution.py:367

commit v15 on v14

--- a/solution.py
+++ b/solution.py
@@ -300,7 +300,7 @@
     scale = (0.125 * COURANT / MOMENTUM) / jnp.max(jnp.maximum(own_ref[...], mate_ref[...]))
     scales = (1.0, scale, scale, scale * scale)
 
-    def one_step(start, count, old, first_changes):
+    def one_step(start, count, old, first_changes, keep):
         def to_mid(row, col, parts):
             for comp in range(4):
                 cells, move = old[comp, row, col], parts[comp]
@@ -313,7 +313,10 @@
         def to_field(row, col, parts):
             for comp in range(4):
                 new = base[comp, row, col] - parts[comp]
-                dealt[comp, col, pl.ds(start + row, 8, stride=count), :] = new
+                if keep:
+                    field[comp, row, col] = new
+                else:
+                    dealt[comp, col, pl.ds(start + row, 8, stride=count), :] = new
 
         def load_from(ref):
             return lambda row, col: [ref[comp, row, col] for comp in range(4)]
@@ -323,16 +326,19 @@
                 for col in range(groups):
                     to_mid(row, col, [first_changes[comp, row, col] for comp in range(4)])
         else:
+            changes(load_from(old), count, groups, 0, to_mid)
+        changes(load_from(mid), count, groups, count // 2, to_field)
+
+    for index in range(STEPS):
+        start = 8 * (index // 2)
+        count = (tall - 2 * start) // 8
+        if index and index % 2 == 0:
             for comp in range(4):
                 for row in range(count):
                     for col in range(groups):
-                        old[comp, row, col] = dealt[comp, col, pl.ds(start + row, 8, stride=count), :]
-            changes(load_from(old), count, groups, 0, to_mid)
-        changes(load_from(mid), count, groups, count // 2, to_field)
-
-    one_step(0, tall // 8, field_ref, change_ref)
-    for index in range(1, STEPS):
-        one_step(4 * index, (tall - 8 * index) // 8, field, None)
+                        field[comp, row, col] = dealt[comp, col, pl.ds(start + row, 8, stride=count), :]
+        keep = index % 2 == 0 and index + 1 < STEPS
+        one_step(start, count, field if index else field_ref, None if index else change_ref, keep)
 
     wide = groups * LANES
     lane = iota((rows, LANES), 1)

time: 23.2 us -> 23.5 us (1.013)
  Pallas kernels: 6.51 us -> 6.81 us
    pallas_call x1, Pallas kernels: 4.59 us -> 4.89 us  [local(): pl.pallas_call(steps_kernel, out_shape=array(parts, rows, cols), in_specs...]
  transfers between devices with their start and end apart: 8 -> 8, of which waited for: 4 -> 4; matrix products, arithmetic and copies ran while one was open for 0% -> 0% of each run, Pallas kernels for 7% -> 6%
where the time goes in v15:
time: 23.5 us; the launch traced here: 23.3 us
  starting transfers between devices  8.95 us (38%)
  Pallas kernels  6.81 us (29%)
  waiting for transfers between devices  6.62 us (28%)
  local copies, waits for them, and re-layouts  0.91 us (4%)
    ppermute x4, starting transfers between devices, swapped_pairs(): return lax.ppermute(value, axis, pairs)  4.98 us
    pallas_call x1, Pallas kernels, local(): pl.pallas_call(steps_kernel, out_shape=array(parts, rows, cols), in_specs...  4.89 us
    ppermute x3, starting transfers between devices, swapped_bit(): lax.ppermute(value, axis, [(i, i ^ by) for i in range(lax.axis_size(axis))])  3.96 us
    ppermute x4, waiting for transfers between devices, swapped_pairs(): return lax.ppermute(value, axis, pairs)  3.48 us
    ppermute x3, waiting for transfers between devices, swapped_bit(): lax.ppermute(value, axis, [(i, i ^ by) for i in range(lax.axis_size(axis))])  2.48 us
    pallas_call x1, Pallas kernels, local(): pl.pallas_call(first_kernel, out_shape=(dealt_type, dealt_type), in_specs...  1.04 us
    unnamed x4, local copies, waits for them, and re-layouts  0.91 us
    ppermute x1, waiting for transfers between devices, swapped_threes(): lax.ppermute(value, axis, [(i, (i + 3 - 6 * (i % 2)) % count) for i in ra...  0.66 us
  transfers between devices with their start and end apart: 8, of which 4 were waited for; matrix products, arithmetic and copies ran while one was open for 0% of the time, Pallas kernels for 6%

profile of v15, /device:TPU:0, one launch (start us, length us, event | category | flops | bytes accessed | tf_op | source)
XLA Modules:
  0.0 23.3 jit_solution(14567897992000627645)
XLA Ops:
  0.0 0.0 copy-start
  0.0 0.9 %copy-done = f32[4,32,256]{2,1,0:T(8,128)S(1)} copy-done((f32[4,32,256]{2,1,0:T(8,128)S(1)}, f32[4,32,256]{2,1,0:T(8,128)}, u32[]{:S(2)}) %copy-start) | copy-done | bytes 131096
  0.9 0.2 edge.1
  1.1 3.4 %collective-permute-start = (f32[72,256]{1,0:T(8,128)S(1)}, f32[72,256]{1,0:T(8,128)S(1)}, u32[]{:S(2)}, u32[]{:S(2)}) collective-permute-start(f32[72,256]{1,0:T(8,128)S(1)} %get-tuple-element.19), channel_id=1, source_target_pairs={{4,8},{8,4},{12,16},{16,12},{20,24},{24,20},{28,0},{0,28},{5,9},{9... | collective-permute-start | bytes 221192 | tf_op jit(solution)/shard_map/ppermute | solution.py:381
  4.5 0.0 collective-permute-start.3
  4.5 0.0 copy-start.1
  4.5 1.2 %collective-permute-start.2 = (f32[8,128]{1,0:T(8,128)S(1)}, f32[8,128]{1,0:T(8,128)S(1)}, u32[]{:S(2)}, u32[]{:S(2)}) collective-permute-start(f32[8,128]{1,0:T(8,128)S(1)} %get-tuple-element.20.own_ref), channel_id=1, source_target_pairs={{0,16},{4,20},{8,24},{12,28},{16,0},{20,4},{24,8},{28,12},{1,17},{... | collective-permute-start | bytes 12296 | tf_op jit(solution)/shard_map/ppermute | solution.py:373
  5.7 0.0 collective-permute-start.1
  5.7 2.4 %collective-permute-done.2.four_ref = f32[8,128]{1,0:T(8,128)S(1)} collective-permute-done((f32[8,128]{1,0:T(8,128)S(1)}, f32[8,128]{1,0:T(8,128)S(1)}, u32[]{:S(2)}, u32[]{:S(2)}) %collective-permute-start.2) | collective-permute-done | bytes 4128 | tf_op jit(solution)/shard_map/ppermute | solution.py:373
  8.1 0.7 %collective-permute-done.1.three_ref = f32[8,128]{1,0:T(8,128)S(1)} collective-permute-done((f32[8,128]{1,0:T(8,128)S(1)}, f32[8,128]{1,0:T(8,128)S(1)}, u32[]{:S(2)}, u32[]{:S(2)}) %collective-permute-start.1) | collective-permute-done | bytes 4128 | tf_op jit(solution)/shard_map/ppermute | solution.py:385
  8.7 0.0 collective-permute-done.next_ref
  8.7 0.0 collective-permute-done.3.swap_ref
  8.8 0.1 pack.1
  8.9 2.7 %collective-permute-start.6 = (f32[8,128]{1,0:T(8,128)S(1)}, f32[8,128]{1,0:T(8,128)S(1)}, u32[]{:S(2)}, u32[]{:S(2)}) collective-permute-start(f32[8,128]{1,0:T(8,128)S(1)} %get-tuple-element.24.own_ref), channel_id=1, source_target_pairs={{0,2},{1,3},{2,0},{3,1},{4,6},{5,7},{6,4},{7,5},{8,10},{9,11},{10,... | collective-permute-start | bytes 12296 | tf_op jit(solution)/shard_map/ppermute | solution.py:373
  11.5 1.4 %collective-permute-start.4 = (f32[32,128]{1,0:T(8,128)S(1)}, f32[32,128]{1,0:T(8,128)S(1)}, u32[]{:S(2)}, u32[]{:S(2)}) collective-permute-start(f32[32,128]{1,0:T(8,128)S(1)} %get-tuple-element.27), channel_id=1, source_target_pairs={{1,2},{2,1},{3,0},{0,3},{5,6},{6,5},{7,4},{4,7},{9,10},{10,9},{11,... | collective-permute-start | bytes 49160 | tf_op jit(solution)/shard_map/ppermute | solution.py:381
  12.9 0.2 collective-permute-start.5
  13.1 0.0 copy-done.1
  13.1 0.5 %deal.1 = (f32[256,384]{1,0:T(8,128)S(1)}, bf16[128,384]{1,0:T(8,128)(2,1)S(1)}, bf16[384,256]{1,0:T(8,128)(2,1)S(1)}, f32[8,128]{1,0:T(8,128)S(1)}) custom-call(f32[4,32,256]{2,1,0:T(8,128)S(1)} %copy-done.1, f32[72,256]{1,0:T(8,128)S(1)} %get-tuple-element.22.up_ref, f32[72,256]{1,0:T(8,128)S(1)} %get-tuple-element.23.down_ref, ...), custom_call_target="tpu_custom_call" | custom-call | flops 300000000 | bytes 1500000 | tf_op jit(solution)/shard_map/deal/pallas_call | solution.py:412
  13.6 0.0 collective-permute-done.6.far_ref
  13.6 3.5 %collective-permute-done.4.next_ref = f32[32,128]{1,0:T(8,128)S(1)} collective-permute-done((f32[32,128]{1,0:T(8,128)S(1)}, f32[32,128]{1,0:T(8,128)S(1)}, u32[]{:S(2)}, u32[]{:S(2)}) %collective-permute-start.4) | collective-permute-done | bytes 16416 | tf_op jit(solution)/shard_map/ppermute | solution.py:381
  17.1 0.0 collective-permute-done.5.swap_ref
  17.1 0.1 join.1.own_ref
  17.2 0.1 collective-permute-start.7
  17.3 1.0 %first.1 = (f32[4,8,3,8,128]{4,3,2,1,0:T(8,128)S(1)}, f32[4,8,3,8,128]{4,3,2,1,0:T(8,128)S(1)}) custom-call(f32[256,384]{1,0:T(8,128)S(1)} %get-tuple-element.25.cells_ref, bf16[128,384]{1,0:T(8,128)(2,1)S(1)} %get-tuple-element.26.select_ref, f32[32,128]{1,0:T(8,128)S(1)} %collective-permute-done.4.next_ref, f32[32,128]{1,0:T(8,128)S(1)} %collective-permute-done.5.swap_ref), custom_call_target="tpu_custom_call" | custom-call | flops 20000000 | bytes 2000000 | tf_op jit(solution)/shard_map/first/pallas_call | solution.py:443
  18.3 0.1 collective-permute-done.7.mate_ref
  18.4 4.9 %steps.1 = f32[4,32,256]{2,1,0:T(8,128)} custom-call(f32[4,8,3,8,128]{4,3,2,1,0:T(8,128)S(1)} %get-tuple-element.29.field_ref, f32[4,8,3,8,128]{4,3,2,1,0:T(8,128)S(1)} %get-tuple-element.30.change_ref, bf16[384,256]{1,0:T(8,128)(2,1)S(1)} %get-tuple-element.31.select_ref, f32[8,128]{1,0:T(8,128)S(1)} %join.1.own_ref, ...), custom_call_target="tpu_custom_call" | custom-call | tf_op jit(solution)/shard_map/steps/pallas_call | solution.py:453
Async XLA Ops:
  0.0 0.9 %copy-start = (f32[4,32,256]{2,1,0:T(8,128)S(1)}, f32[4,32,256]{2,1,0:T(8,128)}, u32[]{:S(2)}) copy-start(f32[4,32,256]{2,1,0:T(8,128)} %state_ref.3) | copy-start | bytes 393220
  1.1 7.7 %collective-permute-start = (f32[72,256]{1,0:T(8,128)S(1)}, f32[72,256]{1,0:T(8,128)S(1)}, u32[]{:S(2)}, u32[]{:S(2)}) collective-permute-start(f32[72,256]{1,0:T(8,128)S(1)} %get-tuple-element.19), channel_id=1, source_target_pairs={{4,8},{8,4},{12,16},{16,12},{20,24},{24,20},{28,0},{0,28},{5,9},{9... | collective-permute-start | bytes 221192 | tf_op jit(solution)/shard_map/ppermute | solution.py:381
  4.5 4.3 %collective-permute-start.3 = (f32[72,256]{1,0:T(8,128)S(1)}, f32[72,256]{1,0:T(8,128)S(1)}, u32[]{:S(2)}, u32[]{:S(2)}) collective-permute-start(f32[72,256]{1,0:T(8,128)S(1)} %get-tuple-element.21), channel_id=1, source_target_pairs={{0,4},{4,0},{8,12},{12,8},{16,20},{20,16},{24,28},{28,24},{1,5},{5... | collective-permute-start | bytes 221192 | tf_op jit(solution)/shard_map/ppermute | solution.py:381
  4.5 8.7 %copy-start.1 = (f32[4,32,256]{2,1,0:T(8,128)S(1)}, f32[4,32,256]{2,1,0:T(8,128)}, u32[]{:S(2)}) copy-start(f32[4,32,256]{2,1,0:T(8,128)} %state_ref.3) | copy-start | bytes 393220
  4.5 3.6 %collective-permute-start.2 = (f32[8,128]{1,0:T(8,128)S(1)}, f32[8,128]{1,0:T(8,128)S(1)}, u32[]{:S(2)}, u32[]{:S(2)}) collective-permute-start(f32[8,128]{1,0:T(8,128)S(1)} %get-tuple-element.20.own_ref), channel_id=1, source_target_pairs={{0,16},{4,20},{8,24},{12,28},{16,0},{20,4},{24,8},{28,12},{1,17},{... | collective-permute-start | bytes 12296 | tf_op jit(solution)/shard_map/ppermute | solution.py:373
  5.7 3.0 %collective-permute-start.1 = (f32[8,128]{1,0:T(8,128)S(1)}, f32[8,128]{1,0:T(8,128)S(1)}, u32[]{:S(2)}, u32[]{:S(2)}) collective-permute-start(f32[8,128]{1,0:T(8,128)S(1)} %get-tuple-element.20.own_ref), channel_id=1, source_target_pairs={{0,12},{4,24},{8,20},{12,0},{16,28},{20,8},{24,4},{28,16},{1,13},{... | collective-permute-start | bytes 12296 | tf_op jit(solution)/shard_map/ppermute | solution.py:385
  8.9 4.7 %collective-permute-start.6 = (f32[8,128]{1,0:T(8,128)S(1)}, f32[8,128]{1,0:T(8,128)S(1)}, u32[]{:S(2)}, u32[]{:S(2)}) collective-permute-start(f32[8,128]{1,0:T(8,128)S(1)} %get-tuple-element.24.own_ref), channel_id=1, source_target_pairs={{0,2},{1,3},{2,0},{3,1},{4,6},{5,7},{6,4},{7,5},{8,10},{9,11},{10,... | collective-permute-start | bytes 12296 | tf_op jit(solution)/shard_map/ppermute | solution.py:373
  11.5 5.5 %collective-permute-start.4 = (f32[32,128]{1,0:T(8,128)S(1)}, f32[32,128]{1,0:T(8,128)S(1)}, u32[]{:S(2)}, u32[]{:S(2)}) collective-permute-start(f32[32,128]{1,0:T(8,128)S(1)} %get-tuple-element.27), channel_id=1, source_target_pairs={{1,2},{2,1},{3,0},{0,3},{5,6},{6,5},{7,4},{4,7},{9,10},{10,9},{11,... | collective-permute-start | bytes 49160 | tf_op jit(solution)/shard_map/ppermute | solution.py:381
  12.9 4.2 %collective-permute-start.5 = (f32[32,128]{1,0:T(8,128)S(1)}, f32[32,128]{1,0:T(8,128)S(1)}, u32[]{:S(2)}, u32[]{:S(2)}) collective-permute-start(f32[32,128]{1,0:T(8,128)S(1)} %get-tuple-element.28), channel_id=1, source_target_pairs={{0,1},{1,0},{2,3},{3,2},{4,5},{5,4},{6,7},{7,6},{8,9},{9,8},{10,11... | collective-permute-start | bytes 49160 | tf_op jit(solution)/shard_map/ppermute | solution.py:381
  17.2 1.2 %collective-permute-start.7 = (f32[8,128]{1,0:T(8,128)S(1)}, f32[8,128]{1,0:T(8,128)S(1)}, u32[]{:S(2)}, u32[]{:S(2)}) collective-permute-start(f32[8,128]{1,0:T(8,128)S(1)} %join.1.own_ref), channel_id=1, source_target_pairs={{0,4},{4,0},{8,12},{12,8},{16,20},{20,16},{24,28},{28,24},{1,5},{5... | collective-permute-start | bytes 12296 | tf_op jit(solution)/shard_map/ppermute | solution.py:373

commit v16 on v14

--- a/solution.py
+++ b/solution.py
@@ -138,6 +138,26 @@
 
 def rolled(tree, by, axis):
     return jax.tree.map(lambda value: pltpu.roll(value, by % value.shape[axis], axis=axis), tree)
+
+
+class Slots:
+    ROWS = 40
+
+    def __init__(self, ref):
+        self.ref, self.used = ref, 0
+
+    def __call__(self, parts, by):
+        return [self.move(part, by) for part in parts]
+
+    def move(self, value, by):
+        slot = self.used % self.ref.shape[0]
+        self.used += 1
+        self.ref[slot, pl.ds(8, 8, stride=3), :] = value
+        return self.ref[slot, pl.ds(8 - 3 * by, 8, stride=3), :]
+
+
+def turned(parts, by):
+    return rolled(parts, by, 0)
 
 
 def cell(whole, jump_before, jump_after):
@@ -163,8 +183,8 @@
 
 
 class Column:
-    def __init__(self, count, begin, here, after):
-        self.count, self.begin = count, begin
+    def __init__(self, count, here, after, shifted):
+        self.count, self.shifted = count, shifted
         self.jump = self.first_jump = minus(after, here)
         self.before = here
         self.first_low = self.first_flux = self.last_flux = self.high = None
@@ -174,18 +194,18 @@
         if after is None:
             next_jump = self.first_jump
         else:
-            next_jump = minus(rolled(after, -1, 0) if next_row == 0 else after, here)
-        jump = minus(here, rolled(self.before, 1, 0)) if row == 0 else self.jump
+            next_jump = minus(self.shifted(after, -1) if next_row == 0 else after, here)
+        jump = minus(here, self.shifted(self.before, 1)) if row == 0 else self.jump
         low, high = cell(whole, jump, next_jump)
         done = []
         if self.first_low is None:
             self.first_low = low
         else:
-            flux = face(known(rolled(self.high[0], 1, 0)) if row == 0 else self.high, low)
+            flux = face(known(self.shifted(self.high[0], 1)) if row == 0 else self.high, low)
             if self.last_flux is None:
                 self.first_flux = flux
             else:
-                seen = rolled(flux, -1, 0) if row == 0 else flux
+                seen = self.shifted(flux, -1) if row == 0 else flux
                 done.append(((row - 1) % self.count, minus(seen, self.last_flux)))
             self.last_flux = flux
         self.high, self.jump, self.before = high, next_jump, here
@@ -199,10 +219,10 @@
 Y_ORDER = (0, 2, 1, 3)
 
 
-def changes(load, rows, cols, begin, store):
+def changes(load, rows, cols, begin, store, shifted=turned):
     along_y = {}
     values = {at: [load((begin + at) % rows, col) for col in range(cols)] for at in range(2)}
-    columns = [Column(rows, begin, values[0][col], values[1][col]) for col in range(cols)]
+    columns = [Column(rows, values[0][col], values[1][col], shifted) for col in range(cols)]
     for at in range(1, rows + 1):
         row = (begin + at) % rows
         here = values.pop(at)
@@ -293,12 +313,14 @@
     changes(load, count, groups, 0, store)
 
 
-def steps_kernel(field_ref, change_ref, select_ref, own_ref, mate_ref, out_ref, field, base, mid, dealt, result, sems):
+def steps_kernel(field_ref, change_ref, select_ref, own_ref, mate_ref, out_ref, field, base, mid, dealt, result, slots, sems):
     rows, cols = out_ref.shape[1:]
     tall = rows + 2 * HALO
     groups = field_ref.shape[2]
     scale = (0.125 * COURANT / MOMENTUM) / jnp.max(jnp.maximum(own_ref[...], mate_ref[...]))
     scales = (1.0, scale, scale, scale * scale)
+
+    shifted = Slots(slots)
 
     def one_step(start, count, old, first_changes):
         def to_mid(row, col, parts):
@@ -327,8 +349,8 @@
                 for row in range(count):
                     for col in range(groups):
                         old[comp, row, col] = dealt[comp, col, pl.ds(start + row, 8, stride=count), :]
-            changes(load_from(old), count, groups, 0, to_mid)
-        changes(load_from(mid), count, groups, count // 2, to_field)
+            changes(load_from(old), count, groups, 0, to_mid, shifted)
+        changes(load_from(mid), count, groups, count // 2, to_field, shifted)
 
     one_step(0, tall // 8, field_ref, change_ref)
     for index in range(1, STEPS):
@@ -450,7 +472,12 @@
         in_specs=[VMEM] * 5,
         out_specs=pl.BlockSpec(memory_space=pl.ANY),
         scratch_shapes=[dealt] * 3
-        + [plain, pltpu.VMEM((parts, rows, cols), jnp.float32), pltpu.SemaphoreType.DMA((parts,))],
+        + [
+            plain,
+            pltpu.VMEM((parts, rows, cols), jnp.float32),
+            pltpu.VMEM((16 * groups * 2, Slots.ROWS, LANES), jnp.float32),
+            pltpu.SemaphoreType.DMA((parts,)),
+        ],
         compiler_params=params(16),
         name="steps",
     )(field, change, back_select, top, mate)

time: 23.2 us -> 23.4 us (level)
  transfers between devices with their start and end apart: 8 -> 8, of which waited for: 4 -> 4; matrix products, arithmetic and copies ran while one was open for 0% -> 0% of each run, Pallas kernels for 7% -> 6%
where the time goes in v16:
time: 23.4 us; the launch traced here: 23.2 us
  starting transfers between devices  8.95 us (38%)
  Pallas kernels  6.69 us (29%)
  waiting for transfers between devices  6.62 us (28%)
  local copies, waits for them, and re-layouts  0.91 us (4%)
    ppermute x4, starting transfers between devices, swapped_pairs(): return lax.ppermute(value, axis, pairs)  4.98 us
    pallas_call x1, Pallas kernels, local(): pl.pallas_call(steps_kernel, out_shape=array(parts, rows, cols), in_specs...  4.78 us
    ppermute x3, starting transfers between devices, swapped_bit(): lax.ppermute(value, axis, [(i, i ^ by) for i in range(lax.axis_size(axis))])  3.96 us
    ppermute x4, waiting for transfers between devices, swapped_pairs(): return lax.ppermute(value, axis, pairs)  3.48 us
    ppermute x3, waiting for transfers between devices, swapped_bit(): lax.ppermute(value, axis, [(i, i ^ by) for i in range(lax.axis_size(axis))])  2.48 us
    pallas_call x1, Pallas kernels, local(): pl.pallas_call(first_kernel, out_shape=(dealt_type, dealt_type), in_specs...  1.04 us
    unnamed x4, local copies, waits for them, and re-layouts  0.91 us
    ppermute x1, waiting for transfers between devices, swapped_threes(): lax.ppermute(value, axis, [(i, (i + 3 - 6 * (i % 2)) % count) for i in ra...  0.66 us
  transfers between devices with their start and end apart: 8, of which 4 were waited for; matrix products, arithmetic and copies ran while one was open for 0% of the time, Pallas kernels for 6%

profile of v16, /device:TPU:0, one launch (start us, length us, event | category | flops | bytes accessed | tf_op | source)
XLA Modules:
  0.0 23.2 jit_solution(3161912177742798856)
XLA Ops:
  0.0 0.0 copy-start
  0.0 0.9 %copy-done = f32[4,32,256]{2,1,0:T(8,128)S(1)} copy-done((f32[4,32,256]{2,1,0:T(8,128)S(1)}, f32[4,32,256]{2,1,0:T(8,128)}, u32[]{:S(2)}) %copy-start) | copy-done | bytes 131096
  0.9 0.2 edge.1
  1.1 3.4 %collective-permute-start = (f32[72,256]{1,0:T(8,128)S(1)}, f32[72,256]{1,0:T(8,128)S(1)}, u32[]{:S(2)}, u32[]{:S(2)}) collective-permute-start(f32[72,256]{1,0:T(8,128)S(1)} %get-tuple-element.19), channel_id=1, source_target_pairs={{4,8},{8,4},{12,16},{16,12},{20,24},{24,20},{28,0},{0,28},{5,9},{9... | collective-permute-start | bytes 221192 | tf_op jit(solution)/shard_map/ppermute | solution.py:397
  4.5 0.0 collective-permute-start.3
  4.5 0.0 copy-start.1
  4.5 1.2 %collective-permute-start.2 = (f32[8,128]{1,0:T(8,128)S(1)}, f32[8,128]{1,0:T(8,128)S(1)}, u32[]{:S(2)}, u32[]{:S(2)}) collective-permute-start(f32[8,128]{1,0:T(8,128)S(1)} %get-tuple-element.20.own_ref), channel_id=1, source_target_pairs={{0,16},{4,20},{8,24},{12,28},{16,0},{20,4},{24,8},{28,12},{1,17},{... | collective-permute-start | bytes 12296 | tf_op jit(solution)/shard_map/ppermute | solution.py:389
  5.7 0.0 collective-permute-start.1
  5.7 2.4 %collective-permute-done.2.four_ref = f32[8,128]{1,0:T(8,128)S(1)} collective-permute-done((f32[8,128]{1,0:T(8,128)S(1)}, f32[8,128]{1,0:T(8,128)S(1)}, u32[]{:S(2)}, u32[]{:S(2)}) %collective-permute-start.2) | collective-permute-done | bytes 4128 | tf_op jit(solution)/shard_map/ppermute | solution.py:389
  8.1 0.7 %collective-permute-done.1.three_ref = f32[8,128]{1,0:T(8,128)S(1)} collective-permute-done((f32[8,128]{1,0:T(8,128)S(1)}, f32[8,128]{1,0:T(8,128)S(1)}, u32[]{:S(2)}, u32[]{:S(2)}) %collective-permute-start.1) | collective-permute-done | bytes 4128 | tf_op jit(solution)/shard_map/ppermute | solution.py:401
  8.7 0.0 collective-permute-done.next_ref
  8.7 0.0 collective-permute-done.3.swap_ref
  8.8 0.1 pack.1
  8.9 2.7 %collective-permute-start.6 = (f32[8,128]{1,0:T(8,128)S(1)}, f32[8,128]{1,0:T(8,128)S(1)}, u32[]{:S(2)}, u32[]{:S(2)}) collective-permute-start(f32[8,128]{1,0:T(8,128)S(1)} %get-tuple-element.24.own_ref), channel_id=1, source_target_pairs={{0,2},{1,3},{2,0},{3,1},{4,6},{5,7},{6,4},{7,5},{8,10},{9,11},{10,... | collective-permute-start | bytes 12296 | tf_op jit(solution)/shard_map/ppermute | solution.py:389
  11.5 1.4 %collective-permute-start.4 = (f32[32,128]{1,0:T(8,128)S(1)}, f32[32,128]{1,0:T(8,128)S(1)}, u32[]{:S(2)}, u32[]{:S(2)}) collective-permute-start(f32[32,128]{1,0:T(8,128)S(1)} %get-tuple-element.27), channel_id=1, source_target_pairs={{1,2},{2,1},{3,0},{0,3},{5,6},{6,5},{7,4},{4,7},{9,10},{10,9},{11,... | collective-permute-start | bytes 49160 | tf_op jit(solution)/shard_map/ppermute | solution.py:397
  12.9 0.2 collective-permute-start.5
  13.1 0.0 copy-done.1
  13.1 0.5 %deal.1 = (f32[256,384]{1,0:T(8,128)S(1)}, bf16[128,384]{1,0:T(8,128)(2,1)S(1)}, bf16[384,256]{1,0:T(8,128)(2,1)S(1)}, f32[8,128]{1,0:T(8,128)S(1)}) custom-call(f32[4,32,256]{2,1,0:T(8,128)S(1)} %copy-done.1, f32[72,256]{1,0:T(8,128)S(1)} %get-tuple-element.22.up_ref, f32[72,256]{1,0:T(8,128)S(1)} %get-tuple-element.23.down_ref, ...), custom_call_target="tpu_custom_call" | custom-call | flops 300000000 | bytes 1500000 | tf_op jit(solution)/shard_map/deal/pallas_call | solution.py:428
  13.6 0.0 collective-permute-done.6.far_ref
  13.6 3.5 %collective-permute-done.4.next_ref = f32[32,128]{1,0:T(8,128)S(1)} collective-permute-done((f32[32,128]{1,0:T(8,128)S(1)}, f32[32,128]{1,0:T(8,128)S(1)}, u32[]{:S(2)}, u32[]{:S(2)}) %collective-permute-start.4) | collective-permute-done | bytes 16416 | tf_op jit(solution)/shard_map/ppermute | solution.py:397
  17.1 0.0 collective-permute-done.5.swap_ref
  17.1 0.1 join.1.own_ref
  17.2 0.1 collective-permute-start.7
  17.3 1.0 %first.1 = (f32[4,8,3,8,128]{4,3,2,1,0:T(8,128)S(1)}, f32[4,8,3,8,128]{4,3,2,1,0:T(8,128)S(1)}) custom-call(f32[256,384]{1,0:T(8,128)S(1)} %get-tuple-element.25.cells_ref, bf16[128,384]{1,0:T(8,128)(2,1)S(1)} %get-tuple-element.26.select_ref, f32[32,128]{1,0:T(8,128)S(1)} %collective-permute-done.4.next_ref, f32[32,128]{1,0:T(8,128)S(1)} %collective-permute-done.5.swap_ref), custom_call_target="tpu_custom_call" | custom-call | flops 20000000 | bytes 2000000 | tf_op jit(solution)/shard_map/first/pallas_call | solution.py:459
  18.3 0.1 collective-permute-done.7.mate_ref
  18.4 4.8 %steps.1 = f32[4,32,256]{2,1,0:T(8,128)} custom-call(f32[4,8,3,8,128]{4,3,2,1,0:T(8,128)S(1)} %get-tuple-element.29.field_ref, f32[4,8,3,8,128]{4,3,2,1,0:T(8,128)S(1)} %get-tuple-element.30.change_ref, bf16[384,256]{1,0:T(8,128)(2,1)S(1)} %get-tuple-element.31.select_ref, f32[8,128]{1,0:T(8,128)S(1)} %join.1.own_ref, ...), custom_call_target="tpu_custom_call" | custom-call | tf_op jit(solution)/shard_map/steps/pallas_call | solution.py:469
Async XLA Ops:
  0.0 0.9 %copy-start = (f32[4,32,256]{2,1,0:T(8,128)S(1)}, f32[4,32,256]{2,1,0:T(8,128)}, u32[]{:S(2)}) copy-start(f32[4,32,256]{2,1,0:T(8,128)} %state_ref.3) | copy-start | bytes 393220
  1.1 7.7 %collective-permute-start = (f32[72,256]{1,0:T(8,128)S(1)}, f32[72,256]{1,0:T(8,128)S(1)}, u32[]{:S(2)}, u32[]{:S(2)}) collective-permute-start(f32[72,256]{1,0:T(8,128)S(1)} %get-tuple-element.19), channel_id=1, source_target_pairs={{4,8},{8,4},{12,16},{16,12},{20,24},{24,20},{28,0},{0,28},{5,9},{9... | collective-permute-start | bytes 221192 | tf_op jit(solution)/shard_map/ppermute | solution.py:397
  4.5 4.3 %collective-permute-start.3 = (f32[72,256]{1,0:T(8,128)S(1)}, f32[72,256]{1,0:T(8,128)S(1)}, u32[]{:S(2)}, u32[]{:S(2)}) collective-permute-start(f32[72,256]{1,0:T(8,128)S(1)} %get-tuple-element.21), channel_id=1, source_target_pairs={{0,4},{4,0},{8,12},{12,8},{16,20},{20,16},{24,28},{28,24},{1,5},{5... | collective-permute-start | bytes 221192 | tf_op jit(solution)/shard_map/ppermute | solution.py:397
  4.5 8.7 %copy-start.1 = (f32[4,32,256]{2,1,0:T(8,128)S(1)}, f32[4,32,256]{2,1,0:T(8,128)}, u32[]{:S(2)}) copy-start(f32[4,32,256]{2,1,0:T(8,128)} %state_ref.3) | copy-start | bytes 393220
  4.5 3.6 %collective-permute-start.2 = (f32[8,128]{1,0:T(8,128)S(1)}, f32[8,128]{1,0:T(8,128)S(1)}, u32[]{:S(2)}, u32[]{:S(2)}) collective-permute-start(f32[8,128]{1,0:T(8,128)S(1)} %get-tuple-element.20.own_ref), channel_id=1, source_target_pairs={{0,16},{4,20},{8,24},{12,28},{16,0},{20,4},{24,8},{28,12},{1,17},{... | collective-permute-start | bytes 12296 | tf_op jit(solution)/shard_map/ppermute | solution.py:389
  5.7 3.0 %collective-permute-start.1 = (f32[8,128]{1,0:T(8,128)S(1)}, f32[8,128]{1,0:T(8,128)S(1)}, u32[]{:S(2)}, u32[]{:S(2)}) collective-permute-start(f32[8,128]{1,0:T(8,128)S(1)} %get-tuple-element.20.own_ref), channel_id=1, source_target_pairs={{0,12},{4,24},{8,20},{12,0},{16,28},{20,8},{24,4},{28,16},{1,13},{... | collective-permute-start | bytes 12296 | tf_op jit(solution)/shard_map/ppermute | solution.py:401
  8.9 4.7 %collective-permute-start.6 = (f32[8,128]{1,0:T(8,128)S(1)}, f32[8,128]{1,0:T(8,128)S(1)}, u32[]{:S(2)}, u32[]{:S(2)}) collective-permute-start(f32[8,128]{1,0:T(8,128)S(1)} %get-tuple-element.24.own_ref), channel_id=1, source_target_pairs={{0,2},{1,3},{2,0},{3,1},{4,6},{5,7},{6,4},{7,5},{8,10},{9,11},{10,... | collective-permute-start | bytes 12296 | tf_op jit(solution)/shard_map/ppermute | solution.py:389
  11.5 5.5 %collective-permute-start.4 = (f32[32,128]{1,0:T(8,128)S(1)}, f32[32,128]{1,0:T(8,128)S(1)}, u32[]{:S(2)}, u32[]{:S(2)}) collective-permute-start(f32[32,128]{1,0:T(8,128)S(1)} %get-tuple-element.27), channel_id=1, source_target_pairs={{1,2},{2,1},{3,0},{0,3},{5,6},{6,5},{7,4},{4,7},{9,10},{10,9},{11,... | collective-permute-start | bytes 49160 | tf_op jit(solution)/shard_map/ppermute | solution.py:397
  12.9 4.2 %collective-permute-start.5 = (f32[32,128]{1,0:T(8,128)S(1)}, f32[32,128]{1,0:T(8,128)S(1)}, u32[]{:S(2)}, u32[]{:S(2)}) collective-permute-start(f32[32,128]{1,0:T(8,128)S(1)} %get-tuple-element.28), channel_id=1, source_target_pairs={{0,1},{1,0},{2,3},{3,2},{4,5},{5,4},{6,7},{7,6},{8,9},{9,8},{10,11... | collective-permute-start | bytes 49160 | tf_op jit(solution)/shard_map/ppermute | solution.py:397
  17.2 1.2 %collective-permute-start.7 = (f32[8,128]{1,0:T(8,128)S(1)}, f32[8,128]{1,0:T(8,128)S(1)}, u32[]{:S(2)}, u32[]{:S(2)}) collective-permute-start(f32[8,128]{1,0:T(8,128)S(1)} %join.1.own_ref), channel_id=1, source_target_pairs={{0,4},{4,0},{8,12},{12,8},{16,20},{20,16},{24,28},{28,24},{1,5},{5... | collective-permute-start | bytes 12296 | tf_op jit(solution)/shard_map/ppermute | solution.py:389

commit v17 on v14

--- a/solution.py
+++ b/solution.py
@@ -293,7 +293,7 @@
     changes(load, count, groups, 0, store)
 
 
-def steps_kernel(field_ref, change_ref, select_ref, own_ref, mate_ref, out_ref, field, base, mid, dealt, result, sems):
+def steps_kernel(field_ref, change_ref, select_ref, own_ref, mate_ref, out_ref, mid, dealt, result, sems):
     rows, cols = out_ref.shape[1:]
     tall = rows + 2 * HALO
     groups = field_ref.shape[2]
@@ -302,37 +302,39 @@
 
     def one_step(start, count, old, first_changes):
         def to_mid(row, col, parts):
+            here = old(row, col)
             for comp in range(4):
-                cells, move = old[comp, row, col], parts[comp]
-                if first_changes is not None:
-                    cells, move = scales[comp] * cells, (scales[comp] * scale) * move
-                moved = cells - move
-                base[comp, row, col] = moved
-                mid[comp, row, col] = moved - move
-
-        def to_field(row, col, parts):
+                mid[comp, row, col] = (here[comp] - parts[comp]) - parts[comp]
+
+        def to_dealt(row, col, parts):
+            here = old(row, col)
             for comp in range(4):
-                new = base[comp, row, col] - parts[comp]
+                new = 0.5 * (here[comp] + mid[comp, row, col]) - parts[comp]
                 dealt[comp, col, pl.ds(start + row, 8, stride=count), :] = new
-
-        def load_from(ref):
-            return lambda row, col: [ref[comp, row, col] for comp in range(4)]
 
         if first_changes is not None:
             for row in range(count):
                 for col in range(groups):
-                    to_mid(row, col, [first_changes[comp, row, col] for comp in range(4)])
+                    to_mid(row, col, first_changes(row, col))
         else:
-            for comp in range(4):
-                for row in range(count):
-                    for col in range(groups):
-                        old[comp, row, col] = dealt[comp, col, pl.ds(start + row, 8, stride=count), :]
-            changes(load_from(old), count, groups, 0, to_mid)
-        changes(load_from(mid), count, groups, count // 2, to_field)
-
-    one_step(0, tall // 8, field_ref, change_ref)
+            changes(old, count, groups, 0, to_mid)
+        changes(lambda row, col: [mid[comp, row, col] for comp in range(4)], count, groups, count // 2, to_dealt)
+
+    def scaled_field(row, col):
+        return [scales[comp] * field_ref[comp, row, col] for comp in range(4)]
+
+    def scaled_change(row, col):
+        return [(scales[comp] * scale) * change_ref[comp, row, col] for comp in range(4)]
+
+    one_step(0, tall // 8, scaled_field, scaled_change)
     for index in range(1, STEPS):
-        one_step(4 * index, (tall - 8 * index) // 8, field, None)
+        start = 4 * index
+        count = (tall - 8 * index) // 8
+
+        def from_dealt(row, col, start=start, count=count):
+            return [dealt[comp, col, pl.ds(start + row, 8, stride=count), :] for comp in range(4)]
+
+        one_step(start, count, from_dealt, None)
 
     wide = groups * LANES
     lane = iota((rows, LANES), 1)
@@ -449,7 +451,7 @@
         out_shape=array(parts, rows, cols),
         in_specs=[VMEM] * 5,
         out_specs=pl.BlockSpec(memory_space=pl.ANY),
-        scratch_shapes=[dealt] * 3
+        scratch_shapes=[dealt]
         + [plain, pltpu.VMEM((parts, rows, cols), jnp.float32), pltpu.SemaphoreType.DMA((parts,))],
         compiler_params=params(16),
         name="steps",

time: 23.2 us -> 23.3 us (level)
  no operation moved by 1% of the time
where the time goes in v17:
time: 23.3 us; the launch traced here: 23.1 us
  starting transfers between devices  8.95 us (38%)
  waiting for transfers between devices  6.62 us (28%)
  Pallas kernels  6.61 us (28%)
  local copies, waits for them, and re-layouts  0.91 us (4%)
    ppermute x4, starting transfers between devices, swapped_pairs(): return lax.ppermute(value, axis, pairs)  4.98 us
    pallas_call x1, Pallas kernels, local(): pl.pallas_call(steps_kernel, out_shape=array(parts, rows, cols), in_specs...  4.69 us
    ppermute x3, starting transfers between devices, swapped_bit(): lax.ppermute(value, axis, [(i, i ^ by) for i in range(lax.axis_size(axis))])  3.96 us
    ppermute x4, waiting for transfers between devices, swapped_pairs(): return lax.ppermute(value, axis, pairs)  3.48 us
    ppermute x3, waiting for transfers between devices, swapped_bit(): lax.ppermute(value, axis, [(i, i ^ by) for i in range(lax.axis_size(axis))])  2.48 us
    pallas_call x1, Pallas kernels, local(): pl.pallas_call(first_kernel, out_shape=(dealt_type, dealt_type), in_specs...  1.04 us
    unnamed x4, local copies, waits for them, and re-layouts  0.91 us
    ppermute x1, waiting for transfers between devices, swapped_threes(): lax.ppermute(value, axis, [(i, (i + 3 - 6 * (i % 2)) % count) for i in ra...  0.66 us
  transfers between devices with their start and end apart: 8, of which 4 were waited for; matrix products, arithmetic and copies ran while one was open for 0% of the time, Pallas kernels for 7%

profile of v17, /device:TPU:0, one launch (start us, length us, event | category | flops | bytes accessed | tf_op | source)
XLA Modules:
  0.0 23.1 jit_solution(14055653049240393914)
XLA Ops:
  0.0 0.0 copy-start
  0.0 0.9 %copy-done = f32[4,32,256]{2,1,0:T(8,128)S(1)} copy-done((f32[4,32,256]{2,1,0:T(8,128)S(1)}, f32[4,32,256]{2,1,0:T(8,128)}, u32[]{:S(2)}) %copy-start) | copy-done | bytes 131096
  0.9 0.2 edge.1
  1.1 3.4 %collective-permute-start = (f32[72,256]{1,0:T(8,128)S(1)}, f32[72,256]{1,0:T(8,128)S(1)}, u32[]{:S(2)}, u32[]{:S(2)}) collective-permute-start(f32[72,256]{1,0:T(8,128)S(1)} %get-tuple-element.19), channel_id=1, source_target_pairs={{4,8},{8,4},{12,16},{16,12},{20,24},{24,20},{28,0},{0,28},{5,9},{9... | collective-permute-start | bytes 221192 | tf_op jit(solution)/shard_map/ppermute | solution.py:377
  4.5 0.0 collective-permute-start.3
  4.5 0.0 copy-start.1
  4.5 1.2 %collective-permute-start.2 = (f32[8,128]{1,0:T(8,128)S(1)}, f32[8,128]{1,0:T(8,128)S(1)}, u32[]{:S(2)}, u32[]{:S(2)}) collective-permute-start(f32[8,128]{1,0:T(8,128)S(1)} %get-tuple-element.20.own_ref), channel_id=1, source_target_pairs={{0,16},{4,20},{8,24},{12,28},{16,0},{20,4},{24,8},{28,12},{1,17},{... | collective-permute-start | bytes 12296 | tf_op jit(solution)/shard_map/ppermute | solution.py:369
  5.7 0.0 collective-permute-start.1
  5.7 2.4 %collective-permute-done.2.four_ref = f32[8,128]{1,0:T(8,128)S(1)} collective-permute-done((f32[8,128]{1,0:T(8,128)S(1)}, f32[8,128]{1,0:T(8,128)S(1)}, u32[]{:S(2)}, u32[]{:S(2)}) %collective-permute-start.2) | collective-permute-done | bytes 4128 | tf_op jit(solution)/shard_map/ppermute | solution.py:369
  8.1 0.7 %collective-permute-done.1.three_ref = f32[8,128]{1,0:T(8,128)S(1)} collective-permute-done((f32[8,128]{1,0:T(8,128)S(1)}, f32[8,128]{1,0:T(8,128)S(1)}, u32[]{:S(2)}, u32[]{:S(2)}) %collective-permute-start.1) | collective-permute-done | bytes 4128 | tf_op jit(solution)/shard_map/ppermute | solution.py:381
  8.7 0.0 collective-permute-done.next_ref
  8.7 0.0 collective-permute-done.3.swap_ref
  8.8 0.1 pack.1
  8.9 2.7 %collective-permute-start.6 = (f32[8,128]{1,0:T(8,128)S(1)}, f32[8,128]{1,0:T(8,128)S(1)}, u32[]{:S(2)}, u32[]{:S(2)}) collective-permute-start(f32[8,128]{1,0:T(8,128)S(1)} %get-tuple-element.24.own_ref), channel_id=1, source_target_pairs={{0,2},{1,3},{2,0},{3,1},{4,6},{5,7},{6,4},{7,5},{8,10},{9,11},{10,... | collective-permute-start | bytes 12296 | tf_op jit(solution)/shard_map/ppermute | solution.py:369
  11.5 1.4 %collective-permute-start.4 = (f32[32,128]{1,0:T(8,128)S(1)}, f32[32,128]{1,0:T(8,128)S(1)}, u32[]{:S(2)}, u32[]{:S(2)}) collective-permute-start(f32[32,128]{1,0:T(8,128)S(1)} %get-tuple-element.27), channel_id=1, source_target_pairs={{1,2},{2,1},{3,0},{0,3},{5,6},{6,5},{7,4},{4,7},{9,10},{10,9},{11,... | collective-permute-start | bytes 49160 | tf_op jit(solution)/shard_map/ppermute | solution.py:377
  12.9 0.2 collective-permute-start.5
  13.1 0.0 copy-done.1
  13.1 0.5 %deal.1 = (f32[256,384]{1,0:T(8,128)S(1)}, bf16[128,384]{1,0:T(8,128)(2,1)S(1)}, bf16[384,256]{1,0:T(8,128)(2,1)S(1)}, f32[8,128]{1,0:T(8,128)S(1)}) custom-call(f32[4,32,256]{2,1,0:T(8,128)S(1)} %copy-done.1, f32[72,256]{1,0:T(8,128)S(1)} %get-tuple-element.22.up_ref, f32[72,256]{1,0:T(8,128)S(1)} %get-tuple-element.23.down_ref, ...), custom_call_target="tpu_custom_call" | custom-call | flops 300000000 | bytes 1500000 | tf_op jit(solution)/shard_map/deal/pallas_call | solution.py:408
  13.6 0.0 collective-permute-done.6.far_ref
  13.6 3.5 %collective-permute-done.4.next_ref = f32[32,128]{1,0:T(8,128)S(1)} collective-permute-done((f32[32,128]{1,0:T(8,128)S(1)}, f32[32,128]{1,0:T(8,128)S(1)}, u32[]{:S(2)}, u32[]{:S(2)}) %collective-permute-start.4) | collective-permute-done | bytes 16416 | tf_op jit(solution)/shard_map/ppermute | solution.py:377
  17.1 0.0 collective-permute-done.5.swap_ref
  17.1 0.1 join.1.own_ref
  17.2 0.1 collective-permute-start.7
  17.3 1.0 %first.1 = (f32[4,8,3,8,128]{4,3,2,1,0:T(8,128)S(1)}, f32[4,8,3,8,128]{4,3,2,1,0:T(8,128)S(1)}) custom-call(f32[256,384]{1,0:T(8,128)S(1)} %get-tuple-element.25.cells_ref, bf16[128,384]{1,0:T(8,128)(2,1)S(1)} %get-tuple-element.26.select_ref, f32[32,128]{1,0:T(8,128)S(1)} %collective-permute-done.4.next_ref, f32[32,128]{1,0:T(8,128)S(1)} %collective-permute-done.5.swap_ref), custom_call_target="tpu_custom_call" | custom-call | flops 20000000 | bytes 2000000 | tf_op jit(solution)/shard_map/first/pallas_call | solution.py:439
  18.3 0.1 collective-permute-done.7.mate_ref
  18.4 4.7 %steps.1 = f32[4,32,256]{2,1,0:T(8,128)} custom-call(f32[4,8,3,8,128]{4,3,2,1,0:T(8,128)S(1)} %get-tuple-element.29.field_ref, f32[4,8,3,8,128]{4,3,2,1,0:T(8,128)S(1)} %get-tuple-element.30.change_ref, bf16[384,256]{1,0:T(8,128)(2,1)S(1)} %get-tuple-element.31.select_ref, f32[8,128]{1,0:T(8,128)S(1)} %join.1.own_ref, ...), custom_call_target="tpu_custom_call" | custom-call | tf_op jit(solution)/shard_map/steps/pallas_call | solution.py:449
Async XLA Ops:
  0.0 0.9 %copy-start = (f32[4,32,256]{2,1,0:T(8,128)S(1)}, f32[4,32,256]{2,1,0:T(8,128)}, u32[]{:S(2)}) copy-start(f32[4,32,256]{2,1,0:T(8,128)} %state_ref.3) | copy-start | bytes 393220
  1.1 7.7 %collective-permute-start = (f32[72,256]{1,0:T(8,128)S(1)}, f32[72,256]{1,0:T(8,128)S(1)}, u32[]{:S(2)}, u32[]{:S(2)}) collective-permute-start(f32[72,256]{1,0:T(8,128)S(1)} %get-tuple-element.19), channel_id=1, source_target_pairs={{4,8},{8,4},{12,16},{16,12},{20,24},{24,20},{28,0},{0,28},{5,9},{9... | collective-permute-start | bytes 221192 | tf_op jit(solution)/shard_map/ppermute | solution.py:377
  4.5 4.3 %collective-permute-start.3 = (f32[72,256]{1,0:T(8,128)S(1)}, f32[72,256]{1,0:T(8,128)S(1)}, u32[]{:S(2)}, u32[]{:S(2)}) collective-permute-start(f32[72,256]{1,0:T(8,128)S(1)} %get-tuple-element.21), channel_id=1, source_target_pairs={{0,4},{4,0},{8,12},{12,8},{16,20},{20,16},{24,28},{28,24},{1,5},{5... | collective-permute-start | bytes 221192 | tf_op jit(solution)/shard_map/ppermute | solution.py:377
  4.5 8.7 %copy-start.1 = (f32[4,32,256]{2,1,0:T(8,128)S(1)}, f32[4,32,256]{2,1,0:T(8,128)}, u32[]{:S(2)}) copy-start(f32[4,32,256]{2,1,0:T(8,128)} %state_ref.3) | copy-start | bytes 393220
  4.5 3.6 %collective-permute-start.2 = (f32[8,128]{1,0:T(8,128)S(1)}, f32[8,128]{1,0:T(8,128)S(1)}, u32[]{:S(2)}, u32[]{:S(2)}) collective-permute-start(f32[8,128]{1,0:T(8,128)S(1)} %get-tuple-element.20.own_ref), channel_id=1, source_target_pairs={{0,16},{4,20},{8,24},{12,28},{16,0},{20,4},{24,8},{28,12},{1,17},{... | collective-permute-start | bytes 12296 | tf_op jit(solution)/shard_map/ppermute | solution.py:369
  5.7 3.0 %collective-permute-start.1 = (f32[8,128]{1,0:T(8,128)S(1)}, f32[8,128]{1,0:T(8,128)S(1)}, u32[]{:S(2)}, u32[]{:S(2)}) collective-permute-start(f32[8,128]{1,0:T(8,128)S(1)} %get-tuple-element.20.own_ref), channel_id=1, source_target_pairs={{0,12},{4,24},{8,20},{12,0},{16,28},{20,8},{24,4},{28,16},{1,13},{... | collective-permute-start | bytes 12296 | tf_op jit(solution)/shard_map/ppermute | solution.py:381
  8.9 4.7 %collective-permute-start.6 = (f32[8,128]{1,0:T(8,128)S(1)}, f32[8,128]{1,0:T(8,128)S(1)}, u32[]{:S(2)}, u32[]{:S(2)}) collective-permute-start(f32[8,128]{1,0:T(8,128)S(1)} %get-tuple-element.24.own_ref), channel_id=1, source_target_pairs={{0,2},{1,3},{2,0},{3,1},{4,6},{5,7},{6,4},{7,5},{8,10},{9,11},{10,... | collective-permute-start | bytes 12296 | tf_op jit(solution)/shard_map/ppermute | solution.py:369
  11.5 5.5 %collective-permute-start.4 = (f32[32,128]{1,0:T(8,128)S(1)}, f32[32,128]{1,0:T(8,128)S(1)}, u32[]{:S(2)}, u32[]{:S(2)}) collective-permute-start(f32[32,128]{1,0:T(8,128)S(1)} %get-tuple-element.27), channel_id=1, source_target_pairs={{1,2},{2,1},{3,0},{0,3},{5,6},{6,5},{7,4},{4,7},{9,10},{10,9},{11,... | collective-permute-start | bytes 49160 | tf_op jit(solution)/shard_map/ppermute | solution.py:377
  12.9 4.2 %collective-permute-start.5 = (f32[32,128]{1,0:T(8,128)S(1)}, f32[32,128]{1,0:T(8,128)S(1)}, u32[]{:S(2)}, u32[]{:S(2)}) collective-permute-start(f32[32,128]{1,0:T(8,128)S(1)} %get-tuple-element.28), channel_id=1, source_target_pairs={{0,1},{1,0},{2,3},{3,2},{4,5},{5,4},{6,7},{7,6},{8,9},{9,8},{10,11... | collective-permute-start | bytes 49160 | tf_op jit(solution)/shard_map/ppermute | solution.py:377
  17.2 1.2 %collective-permute-start.7 = (f32[8,128]{1,0:T(8,128)S(1)}, f32[8,128]{1,0:T(8,128)S(1)}, u32[]{:S(2)}, u32[]{:S(2)}) collective-permute-start(f32[8,128]{1,0:T(8,128)S(1)} %join.1.own_ref), channel_id=1, source_target_pairs={{0,4},{4,0},{8,12},{12,8},{16,20},{20,16},{24,28},{28,24},{1,5},{5... | collective-permute-start | bytes 12296 | tf_op jit(solution)/shard_map/ppermute | solution.py:369

commit v18 on v14

--- a/solution.py
+++ b/solution.py
@@ -34,7 +34,7 @@
     return lax.rem(lax.axis_index(axis), 2) == 1
 
 
-def edge_kernel(block_ref, first_ref, second_ref, top_ref):
+def edge_kernel(block_ref, rows_ref, top_ref):
     rows = block_ref.shape[1]
     density, mom_x, mom_y, energy = (block_ref[comp] for comp in range(4))
     inv = 1.0 / density
@@ -43,26 +43,24 @@
     top = jnp.max(speed)
     is_odd = odd("gx")
     for comp in range(4):
-        span = slice(comp * HALO, (comp + 1) * HALO)
         head = block_ref[comp, 0:HALO, :]
         tail = block_ref[comp, rows - HALO : rows, :]
-        first_ref[span, :] = jnp.where(is_odd, head, tail)
-        second_ref[span, :] = jnp.where(is_odd, tail, head)
-    first_ref[4 * HALO :, :] = jnp.full((8, first_ref.shape[1]), top)
-    second_ref[4 * HALO :, :] = jnp.full((8, second_ref.shape[1]), top)
+        rows_ref[comp * HALO : (comp + 1) * HALO, :] = jnp.where(is_odd, tail, head)
+    rows_ref[4 * HALO :, :] = jnp.full((8, rows_ref.shape[1]), top)
     top_ref[...] = jnp.full(top_ref.shape, top)
 
 
-def pack_kernel(state_ref, next_ref, three_ref, four_ref, swap_ref, own_ref, up_ref, down_ref, first_ref, second_ref, top_ref):
+def pack_kernel(state_ref, next_ref, three_ref, four_ref, mate_ref, own_ref, up_ref, down_ref, first_ref, second_ref, top_ref):
     rows = state_ref.shape[1]
     cols = state_ref.shape[2]
     half = rows // 2 + HALO
     lane = iota((half, LANES), 1)
     is_odd = odd("gx")
-    up_ref[...] = jnp.where(is_odd, swap_ref[...], next_ref[...])
-    down_ref[...] = jnp.where(is_odd, next_ref[...], swap_ref[...])
-    top = jnp.maximum(jnp.maximum(own_ref[...], jnp.maximum(three_ref[...], four_ref[...])),
-                      jnp.maximum(up_ref[4 * HALO :, 0:LANES], down_ref[4 * HALO :, 0:LANES]))
+    for comp in range(4):
+        span = slice(comp * HALO, (comp + 1) * HALO)
+        up_ref[span, :] = jnp.where(is_odd, mate_ref[comp, rows - HALO : rows, :], next_ref[span, :])
+        down_ref[span, :] = jnp.where(is_odd, next_ref[span, :], mate_ref[comp, 0:HALO, :])
+    top = jnp.maximum(jnp.maximum(own_ref[...], next_ref[4 * HALO :, 0:LANES]), jnp.maximum(three_ref[...], four_ref[...]))
 
     def edge(low, at):
         lanes = slice(low, low + LANES)
@@ -378,17 +376,17 @@
         count = lax.axis_size(axis)
         return lax.ppermute(value, axis, [(i, (i + 3 - 6 * (i % 2)) % count) for i in range(count)])
 
-    edge_type = array(parts * HALO + 8, cols)
-    first, second, top = pl.pallas_call(
+    edge_type = array(parts * HALO, cols)
+    mate = swapped_pairs(state, "gx", 0)
+    second, top = pl.pallas_call(
         edge_kernel,
-        out_shape=(edge_type, edge_type, array(8, LANES)),
+        out_shape=(array(parts * HALO + 8, cols), array(8, LANES)),
         in_specs=[VMEM],
-        out_specs=(VMEM,) * 3,
+        out_specs=(VMEM,) * 2,
         compiler_params=params(4),
         name="edge",
     )(state)
     second = swapped_pairs(second, "gx", 1)
-    first = swapped_pairs(first, "gx", 0)
     far = swapped_threes(top, "gx"), swapped_bit(top, "gx", 4)
     side_type = array(tall // 2, LANES)
     up, down, first, second, top = pl.pallas_call(
@@ -398,7 +396,7 @@
         out_specs=(VMEM,) * 5,
         compiler_params=params(4),
         name="pack",
-    )(state, second, *far, first, top)
+    )(state, second, *far, mate, top)
     second = swapped_pairs(second, "gy", 1)
     first = swapped_pairs(first, "gy", 0)
     far = swapped_bit(top, "gy", 2)
@@ -430,7 +428,7 @@
         while covered < lax.axis_size(axis):
             top = jnp.maximum(top, sent(top, axis, covered))
             covered *= 2
-    mate = swapped_bit(top, "gx", 1)
+    top_of_mate = swapped_bit(top, "gx", 1)
     dealt_type = array(parts, tall // 8, groups, 8, LANES)
     dealt = pltpu.VMEM(dealt_type.shape, jnp.float32)
     plain = pltpu.VMEM((parts, groups, tall, LANES), jnp.float32)
@@ -453,7 +451,7 @@
         + [plain, pltpu.VMEM((parts, rows, cols), jnp.float32), pltpu.SemaphoreType.DMA((parts,))],
         compiler_params=params(16),
         name="steps",
-    )(field, change, back_select, top, mate)
+    )(field, change, back_select, top, top_of_mate)
 
 
 def solution(mesh):

time: 23.2 us -> 23.2 us (level)
    ppermute x3, starting transfers between devices: 3.96 us -> 3.23 us  [swapped_bit(): lax.ppermute(value, axis, [(i, i ^ by) for i in range(lax.axis_size(axis))])]
    ppermute x3, waiting for transfers between devices: 2.48 us -> 3.21 us  [swapped_bit(): lax.ppermute(value, axis, [(i, i ^ by) for i in range(lax.axis_size(axis))])]
    ppermute x4, starting transfers between devices: 4.98 us -> 5.65 us  [swapped_pairs(): return lax.ppermute(value, axis, pairs)]
    ppermute x1, waiting for transfers between devices: 0.66 us -> 0.01 us  [swapped_threes(): lax.ppermute(value, axis, [(i, (i + 3 - 6 * (i % 2)) % count) for i in ra...]
  transfers between devices with their start and end apart: 8 -> 8, of which waited for: 4 -> 3; matrix products, arithmetic and copies ran while one was open for 0% -> 0% of each run, Pallas kernels for 7% -> 7%
where the time goes in v18:
time: 23.2 us; the launch traced here: 23.1 us
  starting transfers between devices  8.89 us (38%)
  waiting for transfers between devices  6.69 us (29%)
  Pallas kernels  6.49 us (28%)
  local copies, waits for them, and re-layouts  0.91 us (4%)
    ppermute x4, starting transfers between devices, swapped_pairs(): return lax.ppermute(value, axis, pairs)  5.65 us
    pallas_call x1, Pallas kernels, local(): pl.pallas_call(steps_kernel, out_shape=array(parts, rows, cols), in_specs...  4.58 us
    ppermute x4, waiting for transfers between devices, swapped_pairs(): return lax.ppermute(value, axis, pairs)  3.49 us
    ppermute x3, starting transfers between devices, swapped_bit(): lax.ppermute(value, axis, [(i, i ^ by) for i in range(lax.axis_size(axis))])  3.23 us
    ppermute x3, waiting for transfers between devices, swapped_bit(): lax.ppermute(value, axis, [(i, i ^ by) for i in range(lax.axis_size(axis))])  3.21 us
    pallas_call x1, Pallas kernels, local(): pl.pallas_call(first_kernel, out_shape=(dealt_type, dealt_type), in_specs...  1.04 us
    unnamed x4, local copies, waits for them, and re-layouts  0.91 us
  transfers between devices with their start and end apart: 8, of which 3 were waited for; matrix products, arithmetic and copies ran while one was open for 0% of the time, Pallas kernels for 7%

profile of v18, /device:TPU:0, one launch (start us, length us, event | category | flops | bytes accessed | tf_op | source)
XLA Modules:
  0.0 23.1 jit_solution(5503626581057403988)
XLA Ops:
  0.0 0.5 %collective-permute-start.3 = (f32[4,32,256]{2,1,0:T(8,128)}, f32[4,32,256]{2,1,0:T(8,128)S(1)}, u32[]{:S(2)}, u32[]{:S(2)}) collective-permute-start(f32[4,32,256]{2,1,0:T(8,128)} %state_ref.3), channel_id=1, source_target_pairs={{0,4},{4,0},{8,12},{12,8},{16,20},{20,16},{24,28},{28,24},{1,5},{5... | collective-permute-start | bytes 393224 | tf_op jit(solution)/shard_map/ppermute | solution.py:373
  0.5 0.0 copy-start
  0.5 0.9 %copy-done = f32[4,32,256]{2,1,0:T(8,128)S(1)} copy-done((f32[4,32,256]{2,1,0:T(8,128)S(1)}, f32[4,32,256]{2,1,0:T(8,128)}, u32[]{:S(2)}) %copy-start) | copy-done | bytes 131096
  1.4 0.0 copy-start.1
  1.4 0.2 edge.1
  1.5 3.6 %collective-permute-start = (f32[72,256]{1,0:T(8,128)S(1)}, f32[72,256]{1,0:T(8,128)S(1)}, u32[]{:S(2)}, u32[]{:S(2)}) collective-permute-start(f32[72,256]{1,0:T(8,128)S(1)} %get-tuple-element.18), channel_id=1, source_target_pairs={{4,8},{8,4},{12,16},{16,12},{20,24},{24,20},{28,0},{0,28},{5,9},{9... | collective-permute-start | bytes 221192 | tf_op jit(solution)/shard_map/ppermute | solution.py:373
  5.1 0.5 %collective-permute-start.2 = (f32[8,128]{1,0:T(8,128)S(1)}, f32[8,128]{1,0:T(8,128)S(1)}, u32[]{:S(2)}, u32[]{:S(2)}) collective-permute-start(f32[8,128]{1,0:T(8,128)S(1)} %get-tuple-element.19.own_ref), channel_id=1, source_target_pairs={{0,16},{4,20},{8,24},{12,28},{16,0},{20,4},{24,8},{28,12},{1,17},{... | collective-permute-start | bytes 12296 | tf_op jit(solution)/shard_map/ppermute | solution.py:365
  5.6 0.0 collective-permute-start.1
  5.7 3.1 %collective-permute-done.2.four_ref = f32[8,128]{1,0:T(8,128)S(1)} collective-permute-done((f32[8,128]{1,0:T(8,128)S(1)}, f32[8,128]{1,0:T(8,128)S(1)}, u32[]{:S(2)}, u32[]{:S(2)}) %collective-permute-start.2) | collective-permute-done | bytes 4128 | tf_op jit(solution)/shard_map/ppermute | solution.py:365
  8.8 0.0 collective-permute-done.1.three_ref
  8.8 0.0 collective-permute-done.next_ref
  8.8 0.0 collective-permute-done.3.mate_ref
  8.8 0.0 copy-done.1
  8.8 0.1 pack.1
  8.9 2.7 %collective-permute-start.6 = (f32[8,128]{1,0:T(8,128)S(1)}, f32[8,128]{1,0:T(8,128)S(1)}, u32[]{:S(2)}, u32[]{:S(2)}) collective-permute-start(f32[8,128]{1,0:T(8,128)S(1)} %get-tuple-element.22.own_ref), channel_id=1, source_target_pairs={{0,2},{1,3},{2,0},{3,1},{4,6},{5,7},{6,4},{7,5},{8,10},{9,11},{10,... | collective-permute-start | bytes 12296 | tf_op jit(solution)/shard_map/ppermute | solution.py:365
  11.6 1.3 %collective-permute-start.4 = (f32[32,128]{1,0:T(8,128)S(1)}, f32[32,128]{1,0:T(8,128)S(1)}, u32[]{:S(2)}, u32[]{:S(2)}) collective-permute-start(f32[32,128]{1,0:T(8,128)S(1)} %get-tuple-element.25), channel_id=1, source_target_pairs={{1,2},{2,1},{3,0},{0,3},{5,6},{6,5},{7,4},{4,7},{9,10},{10,9},{11,... | collective-permute-start | bytes 49160 | tf_op jit(solution)/shard_map/ppermute | solution.py:373
  12.9 0.2 collective-permute-start.5
  13.1 0.5 %deal.1 = (f32[256,384]{1,0:T(8,128)S(1)}, bf16[128,384]{1,0:T(8,128)(2,1)S(1)}, bf16[384,256]{1,0:T(8,128)(2,1)S(1)}, f32[8,128]{1,0:T(8,128)S(1)}) custom-call(f32[4,32,256]{2,1,0:T(8,128)S(1)} %copy-done.1, f32[64,256]{1,0:T(8,128)S(1)} %get-tuple-element.20.up_ref, f32[64,256]{1,0:T(8,128)S(1)} %get-tuple-element.21.down_ref, ...), custom_call_target="tpu_custom_call" | custom-call | flops 300000000 | bytes 1500000 | tf_op jit(solution)/shard_map/deal/pallas_call | solution.py:404
  13.6 0.0 collective-permute-done.6.far_ref
  13.6 3.5 %collective-permute-done.4.next_ref = f32[32,128]{1,0:T(8,128)S(1)} collective-permute-done((f32[32,128]{1,0:T(8,128)S(1)}, f32[32,128]{1,0:T(8,128)S(1)}, u32[]{:S(2)}, u32[]{:S(2)}) %collective-permute-start.4) | collective-permute-done | bytes 16416 | tf_op jit(solution)/shard_map/ppermute | solution.py:373
  17.1 0.0 collective-permute-done.5.swap_ref
  17.1 0.1 join.1.own_ref
  17.2 0.1 collective-permute-start.7
  17.3 1.0 %first.1 = (f32[4,8,3,8,128]{4,3,2,1,0:T(8,128)S(1)}, f32[4,8,3,8,128]{4,3,2,1,0:T(8,128)S(1)}) custom-call(f32[256,384]{1,0:T(8,128)S(1)} %get-tuple-element.23.cells_ref, bf16[128,384]{1,0:T(8,128)(2,1)S(1)} %get-tuple-element.24.select_ref, f32[32,128]{1,0:T(8,128)S(1)} %collective-permute-done.4.next_ref, f32[32,128]{1,0:T(8,128)S(1)} %collective-permute-done.5.swap_ref), custom_call_target="tpu_custom_call" | custom-call | flops 20000000 | bytes 2000000 | tf_op jit(solution)/shard_map/first/pallas_call | solution.py:435
  18.4 0.1 collective-permute-done.7.mate_ref
  18.5 4.6 %steps.1 = f32[4,32,256]{2,1,0:T(8,128)} custom-call(f32[4,8,3,8,128]{4,3,2,1,0:T(8,128)S(1)} %get-tuple-element.27.field_ref, f32[4,8,3,8,128]{4,3,2,1,0:T(8,128)S(1)} %get-tuple-element.28.change_ref, bf16[384,256]{1,0:T(8,128)(2,1)S(1)} %get-tuple-element.29.select_ref, f32[8,128]{1,0:T(8,128)S(1)} %join.1.own_ref, ...), custom_call_target="tpu_custom_call" | custom-call | tf_op jit(solution)/shard_map/steps/pallas_call | solution.py:445
Async XLA Ops:
  0.0 8.8 %collective-permute-start.3 = (f32[4,32,256]{2,1,0:T(8,128)}, f32[4,32,256]{2,1,0:T(8,128)S(1)}, u32[]{:S(2)}, u32[]{:S(2)}) collective-permute-start(f32[4,32,256]{2,1,0:T(8,128)} %state_ref.3), channel_id=1, source_target_pairs={{0,4},{4,0},{8,12},{12,8},{16,20},{20,16},{24,28},{28,24},{1,5},{5... | collective-permute-start | bytes 393224 | tf_op jit(solution)/shard_map/ppermute | solution.py:373
  0.5 0.9 %copy-start = (f32[4,32,256]{2,1,0:T(8,128)S(1)}, f32[4,32,256]{2,1,0:T(8,128)}, u32[]{:S(2)}) copy-start(f32[4,32,256]{2,1,0:T(8,128)} %state_ref.3) | copy-start | bytes 393220
  1.4 7.4 %copy-start.1 = (f32[4,32,256]{2,1,0:T(8,128)S(1)}, f32[4,32,256]{2,1,0:T(8,128)}, u32[]{:S(2)}) copy-start(f32[4,32,256]{2,1,0:T(8,128)} %state_ref.3) | copy-start | bytes 393220
  1.5 7.2 %collective-permute-start = (f32[72,256]{1,0:T(8,128)S(1)}, f32[72,256]{1,0:T(8,128)S(1)}, u32[]{:S(2)}, u32[]{:S(2)}) collective-permute-start(f32[72,256]{1,0:T(8,128)S(1)} %get-tuple-element.18), channel_id=1, source_target_pairs={{4,8},{8,4},{12,16},{16,12},{20,24},{24,20},{28,0},{0,28},{5,9},{9... | collective-permute-start | bytes 221192 | tf_op jit(solution)/shard_map/ppermute | solution.py:373
  5.1 3.6 %collective-permute-start.2 = (f32[8,128]{1,0:T(8,128)S(1)}, f32[8,128]{1,0:T(8,128)S(1)}, u32[]{:S(2)}, u32[]{:S(2)}) collective-permute-start(f32[8,128]{1,0:T(8,128)S(1)} %get-tuple-element.19.own_ref), channel_id=1, source_target_pairs={{0,16},{4,20},{8,24},{12,28},{16,0},{20,4},{24,8},{28,12},{1,17},{... | collective-permute-start | bytes 12296 | tf_op jit(solution)/shard_map/ppermute | solution.py:365
  5.6 3.1 %collective-permute-start.1 = (f32[8,128]{1,0:T(8,128)S(1)}, f32[8,128]{1,0:T(8,128)S(1)}, u32[]{:S(2)}, u32[]{:S(2)}) collective-permute-start(f32[8,128]{1,0:T(8,128)S(1)} %get-tuple-element.19.own_ref), channel_id=1, source_target_pairs={{0,12},{4,24},{8,20},{12,0},{16,28},{20,8},{24,4},{28,16},{1,13},{... | collective-permute-start | bytes 12296 | tf_op jit(solution)/shard_map/ppermute | solution.py:377
  8.9 4.7 %collective-permute-start.6 = (f32[8,128]{1,0:T(8,128)S(1)}, f32[8,128]{1,0:T(8,128)S(1)}, u32[]{:S(2)}, u32[]{:S(2)}) collective-permute-start(f32[8,128]{1,0:T(8,128)S(1)} %get-tuple-element.22.own_ref), channel_id=1, source_target_pairs={{0,2},{1,3},{2,0},{3,1},{4,6},{5,7},{6,4},{7,5},{8,10},{9,11},{10,... | collective-permute-start | bytes 12296 | tf_op jit(solution)/shard_map/ppermute | solution.py:365
  11.6 5.5 %collective-permute-start.4 = (f32[32,128]{1,0:T(8,128)S(1)}, f32[32,128]{1,0:T(8,128)S(1)}, u32[]{:S(2)}, u32[]{:S(2)}) collective-permute-start(f32[32,128]{1,0:T(8,128)S(1)} %get-tuple-element.25), channel_id=1, source_target_pairs={{1,2},{2,1},{3,0},{0,3},{5,6},{6,5},{7,4},{4,7},{9,10},{10,9},{11,... | collective-permute-start | bytes 49160 | tf_op jit(solution)/shard_map/ppermute | solution.py:373
  12.9 4.2 %collective-permute-start.5 = (f32[32,128]{1,0:T(8,128)S(1)}, f32[32,128]{1,0:T(8,128)S(1)}, u32[]{:S(2)}, u32[]{:S(2)}) collective-permute-start(f32[32,128]{1,0:T(8,128)S(1)} %get-tuple-element.26), channel_id=1, source_target_pairs={{0,1},{1,0},{2,3},{3,2},{4,5},{5,4},{6,7},{7,6},{8,9},{9,8},{10,11... | collective-permute-start | bytes 49160 | tf_op jit(solution)/shard_map/ppermute | solution.py:373
  17.2 1.2 %collective-permute-start.7 = (f32[8,128]{1,0:T(8,128)S(1)}, f32[8,128]{1,0:T(8,128)S(1)}, u32[]{:S(2)}, u32[]{:S(2)}) collective-permute-start(f32[8,128]{1,0:T(8,128)S(1)} %join.1.own_ref), channel_id=1, source_target_pairs={{0,4},{4,0},{8,12},{12,8},{16,20},{20,16},{24,28},{28,24},{1,5},{5... | collective-permute-start | bytes 12296 | tf_op jit(solution)/shard_map/ppermute | solution.py:365

commit v19 on v14

--- a/solution.py
+++ b/solution.py
@@ -14,6 +14,7 @@
 GAMMA = 1.4
 COURANT = 0.35
 TINY = 1e-30
+MARGIN = 8
 
 VMEM = pl.BlockSpec(memory_space=pltpu.VMEM)
 
@@ -163,60 +164,44 @@
 
 
 class Column:
-    def __init__(self, count, begin, here, after):
-        self.count, self.begin = count, begin
-        self.jump = self.first_jump = minus(after, here)
-        self.before = here
-        self.first_low = self.first_flux = self.last_flux = self.high = None
-
-    def feed(self, row, here, whole, after):
-        next_row = (row + 1) % self.count
-        if after is None:
-            next_jump = self.first_jump
-        else:
-            next_jump = minus(rolled(after, -1, 0) if next_row == 0 else after, here)
-        jump = minus(here, rolled(self.before, 1, 0)) if row == 0 else self.jump
-        low, high = cell(whole, jump, next_jump)
-        done = []
-        if self.first_low is None:
-            self.first_low = low
-        else:
-            flux = face(known(rolled(self.high[0], 1, 0)) if row == 0 else self.high, low)
-            if self.last_flux is None:
-                self.first_flux = flux
-            else:
-                seen = rolled(flux, -1, 0) if row == 0 else flux
-                done.append(((row - 1) % self.count, minus(seen, self.last_flux)))
-            self.last_flux = flux
-        self.high, self.jump, self.before = high, next_jump, here
-        if after is None:
-            flux = face(high, self.first_low)
-            done.append((row, minus(flux, self.last_flux)))
-            done.append(((row + 1) % self.count, minus(self.first_flux, flux)))
+    def __init__(self, count, jump):
+        self.count, self.jump, self.high, self.flux = count, jump, None, None
+
+    def feed(self, row, whole, next_jump):
+        slope = [minmod(self.jump[comp], next_jump[comp]) for comp in range(4)]
+        done = None
+        if row >= 0:
+            flux = face(self.high, known(minus(whole, slope)))
+            done = minus(flux, self.flux) if row else None
+            self.flux = flux
+        if row < self.count:
+            self.high = known([whole[comp] + slope[comp] for comp in range(4)])
+        self.jump = next_jump
         return done
 
 
 Y_ORDER = (0, 2, 1, 3)
 
 
-def changes(load, rows, cols, begin, store):
+def changes(load, rows, cols, store):
     along_y = {}
-    values = {at: [load((begin + at) % rows, col) for col in range(cols)] for at in range(2)}
-    columns = [Column(rows, begin, values[0][col], values[1][col]) for col in range(cols)]
-    for at in range(1, rows + 1):
-        row = (begin + at) % rows
-        here = values.pop(at)
-        if at < rows:
-            values[at + 1] = [load((row + 1) % rows, col) for col in range(cols)]
+    here = [load(-1, col) for col in range(cols)]
+    columns = [Column(rows, minus(here[col], load(-2, col))) for col in range(cols)]
+    for row in range(-1, rows + 1):
+        after = [load(row + 1, col) for col in range(cols)]
         whole = [[part + part for part in value] for value in here]
-        ready = []
-        for col in range(cols):
-            after = values[at + 1][col] if at < rows else None
-            ready += [(col, *item) for item in columns[col].feed(row, here[col], whole[col], after)]
-        along_y[row] = row_changes(*([[part[comp] for comp in Y_ORDER] for part in value] for value in (here, whole)))
-        for col, done, parts in ready:
-            other = along_y[done][col]
-            store(done, col, [parts[comp] + other[Y_ORDER[comp]] for comp in range(4)])
+        ready = [columns[col].feed(row, whole[col], minus(after[col], here[col])) for col in range(cols)]
+        if row > 0:
+            for col in range(cols):
+                other = along_y[row - 1][col]
+                store(row - 1, col, [ready[col][comp] + other[Y_ORDER[comp]] for comp in range(4)])
+        if 0 <= row < rows:
+            along_y[row] = row_changes(*([[part[comp] for comp in Y_ORDER] for part in value] for value in (here, whole)))
+        here = after
+
+
+def strips(start, count, row):
+    return pl.ds(MARGIN + start + row, 8, stride=count)
 
 
 def place_of(lane, group, groups):
@@ -255,7 +240,7 @@
     top_ref[...] = jnp.full((8, LANES), jnp.max(jnp.where(carried, speeds, known_here)))
 
 
-def first_kernel(cells_ref, select_ref, next_ref, swap_ref, field_ref, change_ref, plain, dealt):
+def first_kernel(cells_ref, select_ref, next_ref, swap_ref, field_ref, change_ref, plain):
     half = next_ref.shape[0]
     tall = 2 * half
     groups = cells_ref.shape[1] // LANES
@@ -276,63 +261,58 @@
     for comp in range(4):
         for group in range(groups):
             cells = found[comp * tall : (comp + 1) * tall, group * LANES : (group + 1) * LANES]
-            dealt[comp, group] = (0.5 * SCALES[comp]) * cells
+            field_ref[comp, group, MARGIN : MARGIN + tall, :] = (0.5 * SCALES[comp]) * cells
     count = tall // 8
-    for comp in range(4):
-        for row in range(count):
-            for group in range(groups):
-                field_ref[comp, row, group] = dealt[comp, group, pl.ds(row, 8, stride=count), :]
 
     def store(row, col, parts):
         for comp in range(4):
             change_ref[comp, row, col] = parts[comp]
 
     def load(row, col):
-        return [field_ref[comp, row, col] for comp in range(4)]
-
-    changes(load, count, groups, 0, store)
-
-
-def steps_kernel(field_ref, change_ref, select_ref, own_ref, mate_ref, out_ref, field, base, mid, dealt, result, sems):
+        return [field_ref[comp, col, strips(0, count, row), :] for comp in range(4)]
+
+    changes(load, count, groups, store)
+
+
+def steps_kernel(field_ref, change_ref, select_ref, own_ref, mate_ref, out_ref, field, base, mid, result, sems):
     rows, cols = out_ref.shape[1:]
     tall = rows + 2 * HALO
-    groups = field_ref.shape[2]
+    groups = field_ref.shape[1]
     scale = (0.125 * COURANT / MOMENTUM) / jnp.max(jnp.maximum(own_ref[...], mate_ref[...]))
     scales = (1.0, scale, scale, scale * scale)
 
-    def one_step(start, count, old, first_changes):
+    for index in range(STEPS):
+        start = 4 * index
+        count = (tall - 2 * start) // 8
+
         def to_mid(row, col, parts):
+            rows_of = strips(start, count, row)
             for comp in range(4):
-                cells, move = old[comp, row, col], parts[comp]
-                if first_changes is not None:
+                cells, move = field[comp, col, rows_of, :] if index else field_ref[comp, col, rows_of, :], parts[comp]
+                if index == 0:
                     cells, move = scales[comp] * cells, (scales[comp] * scale) * move
                 moved = cells - move
-                base[comp, row, col] = moved
-                mid[comp, row, col] = moved - move
+                base[comp, col, rows_of, :] = moved
+                mid[comp, col, rows_of, :] = moved - move
 
         def to_field(row, col, parts):
+            rows_of = strips(start + 4, count - 1, row)
             for comp in range(4):
-                new = base[comp, row, col] - parts[comp]
-                dealt[comp, col, pl.ds(start + row, 8, stride=count), :] = new
-
-        def load_from(ref):
-            return lambda row, col: [ref[comp, row, col] for comp in range(4)]
-
-        if first_changes is not None:
+                field[comp, col, rows_of, :] = base[comp, col, rows_of, :] - parts[comp]
+
+        def from_field(row, col):
+            return [field[comp, col, strips(start, count, row), :] for comp in range(4)]
+
+        def from_mid(row, col):
+            return [mid[comp, col, strips(start + 4, count - 1, row), :] for comp in range(4)]
+
+        if index == 0:
             for row in range(count):
                 for col in range(groups):
-                    to_mid(row, col, [first_changes[comp, row, col] for comp in range(4)])
+                    to_mid(row, col, [change_ref[comp, row, col] for comp in range(4)])
         else:
-            for comp in range(4):
-                for row in range(count):
-                    for col in range(groups):
-                        old[comp, row, col] = dealt[comp, col, pl.ds(start + row, 8, stride=count), :]
-            changes(load_from(old), count, groups, 0, to_mid)
-        changes(load_from(mid), count, groups, count // 2, to_field)
-
-    one_step(0, tall // 8, field_ref, change_ref)
-    for index in range(1, STEPS):
-        one_step(4 * index, (tall - 8 * index) // 8, field, None)
+            changes(from_field, count, groups, to_mid)
+        changes(from_mid, count - 1, groups, to_field)
 
     wide = groups * LANES
     lane = iota((rows, LANES), 1)
@@ -342,7 +322,7 @@
         for group in range(groups):
             place = place_of(lane, group, groups)
             inside = (place >= HALO) & (place < HALO + cols)
-            line.append(jnp.where(inside, dealt[comp, group, HALO : HALO + rows, :], 0.0))
+            line.append(jnp.where(inside, field[comp, group, MARGIN + HALO : MARGIN + HALO + rows, :], 0.0))
         parts.append(jnp.concatenate(line, axis=1))
     found = selected(jnp.concatenate(parts, axis=0), select_ref[...])
     copies = []
@@ -431,15 +411,15 @@
             top = jnp.maximum(top, sent(top, axis, covered))
             covered *= 2
     mate = swapped_bit(top, "gx", 1)
-    dealt_type = array(parts, tall // 8, groups, 8, LANES)
-    dealt = pltpu.VMEM(dealt_type.shape, jnp.float32)
-    plain = pltpu.VMEM((parts, groups, tall, LANES), jnp.float32)
+    change_type = array(parts, tall // 8, groups, 8, LANES)
+    field_type = array(parts, groups, tall + 2 * MARGIN, LANES)
+    stage_array = pltpu.VMEM(field_type.shape, jnp.float32)
     field, change = pl.pallas_call(
         first_kernel,
-        out_shape=(dealt_type, dealt_type),
+        out_shape=(field_type, change_type),
         in_specs=[VMEM] * 4,
         out_specs=(VMEM,) * 2,
-        scratch_shapes=[pltpu.VMEM((parts * tall, LANES), jnp.float32), plain],
+        scratch_shapes=[pltpu.VMEM((parts * tall, LANES), jnp.float32)],
         compiler_params=params(16),
         cost_estimate=pl.CostEstimate(flops=20_000_000, bytes_accessed=2_000_000, transcendentals=400_000),
         name="first",
@@ -449,8 +429,8 @@
         out_shape=array(parts, rows, cols),
         in_specs=[VMEM] * 5,
         out_specs=pl.BlockSpec(memory_space=pl.ANY),
-        scratch_shapes=[dealt] * 3
-        + [plain, pltpu.VMEM((parts, rows, cols), jnp.float32), pltpu.SemaphoreType.DMA((parts,))],
+        scratch_shapes=[stage_array] * 3
+        + [pltpu.VMEM((parts, rows, cols), jnp.float32), pltpu.SemaphoreType.DMA((parts,))],
         compiler_params=params(16),
         name="steps",
     )(field, change, back_select, top, mate)

time: 23.2 us -> 23.3 us (level)
  no operation moved by 1% of the time
where the time goes in v19:
time: 23.3 us; the launch traced here: 23.2 us
  starting transfers between devices  8.95 us (38%)
  Pallas kernels  6.66 us (29%)
  waiting for transfers between devices  6.58 us (28%)
  local copies, waits for them, and re-layouts  0.91 us (4%)
    ppermute x4, starting transfers between devices, swapped_pairs(): return lax.ppermute(value, axis, pairs)  4.98 us
    pallas_call x1, Pallas kernels, local(): pl.pallas_call(steps_kernel, out_shape=array(parts, rows, cols), in_specs...  4.71 us
    ppermute x3, starting transfers between devices, swapped_bit(): lax.ppermute(value, axis, [(i, i ^ by) for i in range(lax.axis_size(axis))])  3.96 us
    ppermute x4, waiting for transfers between devices, swapped_pairs(): return lax.ppermute(value, axis, pairs)  3.48 us
    ppermute x3, waiting for transfers between devices, swapped_bit(): lax.ppermute(value, axis, [(i, i ^ by) for i in range(lax.axis_size(axis))])  2.44 us
    pallas_call x1, Pallas kernels, local(): pl.pallas_call(first_kernel, out_shape=(field_type, change_type), in_spec...  1.08 us
    unnamed x4, local copies, waits for them, and re-layouts  0.91 us
    ppermute x1, waiting for transfers between devices, swapped_threes(): lax.ppermute(value, axis, [(i, (i + 3 - 6 * (i % 2)) % count) for i in ra...  0.66 us
  transfers between devices with their start and end apart: 8, of which 4 were waited for; matrix products, arithmetic and copies ran while one was open for 0% of the time, Pallas kernels for 7%

profile of v19, /device:TPU:0, one launch (start us, length us, event | category | flops | bytes accessed | tf_op | source)
XLA Modules:
  0.0 23.2 jit_solution(13592397821249639699)
XLA Ops:
  0.0 0.0 copy-start
  0.0 0.9 %copy-done = f32[4,32,256]{2,1,0:T(8,128)S(1)} copy-done((f32[4,32,256]{2,1,0:T(8,128)S(1)}, f32[4,32,256]{2,1,0:T(8,128)}, u32[]{:S(2)}) %copy-start) | copy-done | bytes 131096
  0.9 0.2 edge.1
  1.1 3.4 %collective-permute-start = (f32[72,256]{1,0:T(8,128)S(1)}, f32[72,256]{1,0:T(8,128)S(1)}, u32[]{:S(2)}, u32[]{:S(2)}) collective-permute-start(f32[72,256]{1,0:T(8,128)S(1)} %get-tuple-element.19), channel_id=1, source_target_pairs={{4,8},{8,4},{12,16},{16,12},{20,24},{24,20},{28,0},{0,28},{5,9},{9... | collective-permute-start | bytes 221192 | tf_op jit(solution)/shard_map/ppermute | solution.py:355
  4.5 0.0 collective-permute-start.3
  4.5 0.0 copy-start.1
  4.5 1.2 %collective-permute-start.2 = (f32[8,128]{1,0:T(8,128)S(1)}, f32[8,128]{1,0:T(8,128)S(1)}, u32[]{:S(2)}, u32[]{:S(2)}) collective-permute-start(f32[8,128]{1,0:T(8,128)S(1)} %get-tuple-element.20.own_ref), channel_id=1, source_target_pairs={{0,16},{4,20},{8,24},{12,28},{16,0},{20,4},{24,8},{28,12},{1,17},{... | collective-permute-start | bytes 12296 | tf_op jit(solution)/shard_map/ppermute | solution.py:347
  5.7 0.0 collective-permute-start.1
  5.7 2.4 %collective-permute-done.2.four_ref = f32[8,128]{1,0:T(8,128)S(1)} collective-permute-done((f32[8,128]{1,0:T(8,128)S(1)}, f32[8,128]{1,0:T(8,128)S(1)}, u32[]{:S(2)}, u32[]{:S(2)}) %collective-permute-start.2) | collective-permute-done | bytes 4128 | tf_op jit(solution)/shard_map/ppermute | solution.py:347
  8.1 0.7 %collective-permute-done.1.three_ref = f32[8,128]{1,0:T(8,128)S(1)} collective-permute-done((f32[8,128]{1,0:T(8,128)S(1)}, f32[8,128]{1,0:T(8,128)S(1)}, u32[]{:S(2)}, u32[]{:S(2)}) %collective-permute-start.1) | collective-permute-done | bytes 4128 | tf_op jit(solution)/shard_map/ppermute | solution.py:359
  8.7 0.0 collective-permute-done.next_ref
  8.7 0.0 collective-permute-done.3.swap_ref
  8.8 0.1 pack.1
  8.9 2.7 %collective-permute-start.6 = (f32[8,128]{1,0:T(8,128)S(1)}, f32[8,128]{1,0:T(8,128)S(1)}, u32[]{:S(2)}, u32[]{:S(2)}) collective-permute-start(f32[8,128]{1,0:T(8,128)S(1)} %get-tuple-element.24.own_ref), channel_id=1, source_target_pairs={{0,2},{1,3},{2,0},{3,1},{4,6},{5,7},{6,4},{7,5},{8,10},{9,11},{10,... | collective-permute-start | bytes 12296 | tf_op jit(solution)/shard_map/ppermute | solution.py:347
  11.5 1.4 %collective-permute-start.4 = (f32[32,128]{1,0:T(8,128)S(1)}, f32[32,128]{1,0:T(8,128)S(1)}, u32[]{:S(2)}, u32[]{:S(2)}) collective-permute-start(f32[32,128]{1,0:T(8,128)S(1)} %get-tuple-element.27), channel_id=1, source_target_pairs={{1,2},{2,1},{3,0},{0,3},{5,6},{6,5},{7,4},{4,7},{9,10},{10,9},{11,... | collective-permute-start | bytes 49160 | tf_op jit(solution)/shard_map/ppermute | solution.py:355
  12.9 0.2 collective-permute-start.5
  13.1 0.0 copy-done.1
  13.1 0.5 %deal.1 = (f32[256,384]{1,0:T(8,128)S(1)}, bf16[128,384]{1,0:T(8,128)(2,1)S(1)}, bf16[384,256]{1,0:T(8,128)(2,1)S(1)}, f32[8,128]{1,0:T(8,128)S(1)}) custom-call(f32[4,32,256]{2,1,0:T(8,128)S(1)} %copy-done.1, f32[72,256]{1,0:T(8,128)S(1)} %get-tuple-element.22.up_ref, f32[72,256]{1,0:T(8,128)S(1)} %get-tuple-element.23.down_ref, ...), custom_call_target="tpu_custom_call" | custom-call | flops 300000000 | bytes 1500000 | tf_op jit(solution)/shard_map/deal/pallas_call | solution.py:386
  13.6 0.0 collective-permute-done.6.far_ref
  13.6 3.5 %collective-permute-done.4.next_ref = f32[32,128]{1,0:T(8,128)S(1)} collective-permute-done((f32[32,128]{1,0:T(8,128)S(1)}, f32[32,128]{1,0:T(8,128)S(1)}, u32[]{:S(2)}, u32[]{:S(2)}) %collective-permute-start.4) | collective-permute-done | bytes 16416 | tf_op jit(solution)/shard_map/ppermute | solution.py:355
  17.1 0.0 collective-permute-done.5.swap_ref
  17.1 0.1 join.1.own_ref
  17.2 0.1 collective-permute-start.7
  17.3 1.1 %first.1 = (f32[4,3,80,128]{3,2,1,0:T(8,128)S(1)}, f32[4,8,3,8,128]{4,3,2,1,0:T(8,128)S(1)}) custom-call(f32[256,384]{1,0:T(8,128)S(1)} %get-tuple-element.25.cells_ref, bf16[128,384]{1,0:T(8,128)(2,1)S(1)} %get-tuple-element.26.select_ref, f32[32,128]{1,0:T(8,128)S(1)} %collective-permute-done.4.next_ref, f32[32,128]{1,0:T(8,128)S(1)} %collective-permute-done.5.swap_ref), custom_call_target="tpu_custom_call" | custom-call | flops 20000000 | bytes 2000000 | tf_op jit(solution)/shard_map/first/pallas_call | solution.py:417
  18.4 0.1 collective-permute-done.7.mate_ref
  18.4 4.7 %steps.1 = f32[4,32,256]{2,1,0:T(8,128)} custom-call(f32[4,3,80,128]{3,2,1,0:T(8,128)S(1)} %get-tuple-element.29.field_ref, f32[4,8,3,8,128]{4,3,2,1,0:T(8,128)S(1)} %get-tuple-element.30.change_ref, bf16[384,256]{1,0:T(8,128)(2,1)S(1)} %get-tuple-element.31.select_ref, f32[8,128]{1,0:T(8,128)S(1)} %join.1.own_ref, f32[8,128]{1,0:T(8,128)S(1)} %collective-permute-done.7.mate_ref), custom_call_target="tpu_custom_call" | custom-call | tf_op jit(solution)/shard_map/steps/pallas_call | solution.py:427
Async XLA Ops:
  0.0 0.9 %copy-start = (f32[4,32,256]{2,1,0:T(8,128)S(1)}, f32[4,32,256]{2,1,0:T(8,128)}, u32[]{:S(2)}) copy-start(f32[4,32,256]{2,1,0:T(8,128)} %state_ref.3) | copy-start | bytes 393220
  1.1 7.7 %collective-permute-start = (f32[72,256]{1,0:T(8,128)S(1)}, f32[72,256]{1,0:T(8,128)S(1)}, u32[]{:S(2)}, u32[]{:S(2)}) collective-permute-start(f32[72,256]{1,0:T(8,128)S(1)} %get-tuple-element.19), channel_id=1, source_target_pairs={{4,8},{8,4},{12,16},{16,12},{20,24},{24,20},{28,0},{0,28},{5,9},{9... | collective-permute-start | bytes 221192 | tf_op jit(solution)/shard_map/ppermute | solution.py:355
  4.5 4.3 %collective-permute-start.3 = (f32[72,256]{1,0:T(8,128)S(1)}, f32[72,256]{1,0:T(8,128)S(1)}, u32[]{:S(2)}, u32[]{:S(2)}) collective-permute-start(f32[72,256]{1,0:T(8,128)S(1)} %get-tuple-element.21), channel_id=1, source_target_pairs={{0,4},{4,0},{8,12},{12,8},{16,20},{20,16},{24,28},{28,24},{1,5},{5... | collective-permute-start | bytes 221192 | tf_op jit(solution)/shard_map/ppermute | solution.py:355
  4.5 8.7 %copy-start.1 = (f32[4,32,256]{2,1,0:T(8,128)S(1)}, f32[4,32,256]{2,1,0:T(8,128)}, u32[]{:S(2)}) copy-start(f32[4,32,256]{2,1,0:T(8,128)} %state_ref.3) | copy-start | bytes 393220
  4.5 3.6 %collective-permute-start.2 = (f32[8,128]{1,0:T(8,128)S(1)}, f32[8,128]{1,0:T(8,128)S(1)}, u32[]{:S(2)}, u32[]{:S(2)}) collective-permute-start(f32[8,128]{1,0:T(8,128)S(1)} %get-tuple-element.20.own_ref), channel_id=1, source_target_pairs={{0,16},{4,20},{8,24},{12,28},{16,0},{20,4},{24,8},{28,12},{1,17},{... | collective-permute-start | bytes 12296 | tf_op jit(solution)/shard_map/ppermute | solution.py:347
  5.7 3.0 %collective-permute-start.1 = (f32[8,128]{1,0:T(8,128)S(1)}, f32[8,128]{1,0:T(8,128)S(1)}, u32[]{:S(2)}, u32[]{:S(2)}) collective-permute-start(f32[8,128]{1,0:T(8,128)S(1)} %get-tuple-element.20.own_ref), channel_id=1, source_target_pairs={{0,12},{4,24},{8,20},{12,0},{16,28},{20,8},{24,4},{28,16},{1,13},{... | collective-permute-start | bytes 12296 | tf_op jit(solution)/shard_map/ppermute | solution.py:359
  8.9 4.7 %collective-permute-start.6 = (f32[8,128]{1,0:T(8,128)S(1)}, f32[8,128]{1,0:T(8,128)S(1)}, u32[]{:S(2)}, u32[]{:S(2)}) collective-permute-start(f32[8,128]{1,0:T(8,128)S(1)} %get-tuple-element.24.own_ref), channel_id=1, source_target_pairs={{0,2},{1,3},{2,0},{3,1},{4,6},{5,7},{6,4},{7,5},{8,10},{9,11},{10,... | collective-permute-start | bytes 12296 | tf_op jit(solution)/shard_map/ppermute | solution.py:347
  11.5 5.5 %collective-permute-start.4 = (f32[32,128]{1,0:T(8,128)S(1)}, f32[32,128]{1,0:T(8,128)S(1)}, u32[]{:S(2)}, u32[]{:S(2)}) collective-permute-start(f32[32,128]{1,0:T(8,128)S(1)} %get-tuple-element.27), channel_id=1, source_target_pairs={{1,2},{2,1},{3,0},{0,3},{5,6},{6,5},{7,4},{4,7},{9,10},{10,9},{11,... | collective-permute-start | bytes 49160 | tf_op jit(solution)/shard_map/ppermute | solution.py:355
  12.9 4.2 %collective-permute-start.5 = (f32[32,128]{1,0:T(8,128)S(1)}, f32[32,128]{1,0:T(8,128)S(1)}, u32[]{:S(2)}, u32[]{:S(2)}) collective-permute-start(f32[32,128]{1,0:T(8,128)S(1)} %get-tuple-element.28), channel_id=1, source_target_pairs={{0,1},{1,0},{2,3},{3,2},{4,5},{5,4},{6,7},{7,6},{8,9},{9,8},{10,11... | collective-permute-start | bytes 49160 | tf_op jit(solution)/shard_map/ppermute | solution.py:355
  17.2 1.2 %collective-permute-start.7 = (f32[8,128]{1,0:T(8,128)S(1)}, f32[8,128]{1,0:T(8,128)S(1)}, u32[]{:S(2)}, u32[]{:S(2)}) collective-permute-start(f32[8,128]{1,0:T(8,128)S(1)} %join.1.own_ref), channel_id=1, source_target_pairs={{0,4},{4,0},{8,12},{12,8},{16,20},{20,16},{24,28},{28,24},{1,5},{5... | collective-permute-start | bytes 12296 | tf_op jit(solution)/shard_map/ppermute | solution.py:347

commit v20 on v14

--- a/solution.py
+++ b/solution.py
@@ -91,14 +91,16 @@
     top_ref[...] = top
 
 
-def selected(values, select):
-    rows = values.shape[0]
+def selected(lists, select):
+    rows = lists[0].shape[0]
     parts = []
-    for _ in range(3):
-        parts.append(values.astype(jnp.bfloat16))
-        values = values - parts[-1].astype(jnp.float32)
+    for values in lists:
+        for _ in range(3):
+            parts.append(values.astype(jnp.bfloat16))
+            values = values - parts[-1].astype(jnp.float32)
     found = jnp.dot(jnp.concatenate(parts, axis=0), select, preferred_element_type=jnp.float32)
-    return (found[0:rows] + found[rows : 2 * rows]) + found[2 * rows :]
+    thirds = [found[at * rows : (at + 1) * rows] for at in range(len(parts))]
+    return [(thirds[at] + thirds[at + 1]) + thirds[at + 2] for at in range(0, len(parts), 3)]
 
 
 def minmod(first, second):
@@ -240,7 +242,7 @@
     place = place_of(goal % LANES, goal // LANES, groups)
     place = jnp.where(place < cols + 2 * HALO, (place + wide - HALO) % wide, 0)
     select = jnp.where(source == place, 1.0, 0.0).astype(jnp.bfloat16)
-    dealt_ref[...] = selected(plain[...], select[0:cols])
+    dealt_ref[...] = selected([plain[...]], select[0:cols])[0]
     halo_select_ref[...] = select[cols:]
     source = iota((wide, cols), 0)
     goal = iota((wide, cols), 1)
@@ -272,7 +274,7 @@
             right = pltpu.roll(from_after, (-at) % LANES, axis=1)
             low = comp * tall + side * half
             plain[low : low + half, :] = jnp.where(lane < LANES // 2, right, left)
-    found = cells_ref[...] + selected(plain[...], select_ref[...])
+    found = cells_ref[...] + selected([plain[...]], select_ref[...])[0]
     for comp in range(4):
         for group in range(groups):
             cells = found[comp * tall : (comp + 1) * tall, group * LANES : (group + 1) * LANES]
@@ -344,10 +346,10 @@
             inside = (place >= HALO) & (place < HALO + cols)
             line.append(jnp.where(inside, dealt[comp, group, HALO : HALO + rows, :], 0.0))
         parts.append(jnp.concatenate(line, axis=1))
-    found = selected(jnp.concatenate(parts, axis=0), select_ref[...])
+    found = selected(parts, select_ref[...])
     copies = []
     for comp in range(4):
-        result[comp] = ((2.0 / SCALES[comp]) / scales[comp]) * found[comp * rows : (comp + 1) * rows, :]
+        result[comp] = ((2.0 / SCALES[comp]) / scales[comp]) * found[comp]
         copies.append(pltpu.make_async_copy(result.at[comp], out_ref.at[comp], sems.at[comp]))
         copies[-1].start()
     for copy in copies:

time: 23.2 us -> 23.2 us (level)
  no operation moved by 1% of the time
where the time goes in v20:
time: 23.2 us; the launch traced here: 23 us
  starting transfers between devices  8.95 us (39%)
  waiting for transfers between devices  6.62 us (29%)
  Pallas kernels  6.52 us (28%)
  local copies, waits for them, and re-layouts  0.91 us (4%)
    ppermute x4, starting transfers between devices, swapped_pairs(): return lax.ppermute(value, axis, pairs)  4.98 us
    pallas_call x1, Pallas kernels, local(): pl.pallas_call(steps_kernel, out_shape=array(parts, rows, cols), in_specs...  4.6 us
    ppermute x3, starting transfers between devices, swapped_bit(): lax.ppermute(value, axis, [(i, i ^ by) for i in range(lax.axis_size(axis))])  3.96 us
    ppermute x4, waiting for transfers between devices, swapped_pairs(): return lax.ppermute(value, axis, pairs)  3.48 us
    ppermute x3, waiting for transfers between devices, swapped_bit(): lax.ppermute(value, axis, [(i, i ^ by) for i in range(lax.axis_size(axis))])  2.48 us
    pallas_call x1, Pallas kernels, local(): pl.pallas_call(first_kernel, out_shape=(dealt_type, dealt_type), in_specs...  1.04 us
    unnamed x4, local copies, waits for them, and re-layouts  0.91 us
    ppermute x1, waiting for transfers between devices, swapped_threes(): lax.ppermute(value, axis, [(i, (i + 3 - 6 * (i % 2)) % count) for i in ra...  0.66 us
  transfers between devices with their start and end apart: 8, of which 4 were waited for; matrix products, arithmetic and copies ran while one was open for 0% of the time, Pallas kernels for 7%

profile of v20, /device:TPU:0, one launch (start us, length us, event | category | flops | bytes accessed | tf_op | source)
XLA Modules:
  0.0 23.0 jit_solution(15462936096985662208)
XLA Ops:
  0.0 0.0 copy-start
  0.0 0.9 %copy-done = f32[4,32,256]{2,1,0:T(8,128)S(1)} copy-done((f32[4,32,256]{2,1,0:T(8,128)S(1)}, f32[4,32,256]{2,1,0:T(8,128)}, u32[]{:S(2)}) %copy-start) | copy-done | bytes 131096
  0.9 0.2 edge.1
  1.1 3.4 %collective-permute-start = (f32[72,256]{1,0:T(8,128)S(1)}, f32[72,256]{1,0:T(8,128)S(1)}, u32[]{:S(2)}, u32[]{:S(2)}) collective-permute-start(f32[72,256]{1,0:T(8,128)S(1)} %get-tuple-element.19), channel_id=1, source_target_pairs={{4,8},{8,4},{12,16},{16,12},{20,24},{24,20},{28,0},{0,28},{5,9},{9... | collective-permute-start | bytes 221192 | tf_op jit(solution)/shard_map/ppermute | solution.py:377
  4.5 0.0 collective-permute-start.3
  4.5 0.0 copy-start.1
  4.5 1.2 %collective-permute-start.2 = (f32[8,128]{1,0:T(8,128)S(1)}, f32[8,128]{1,0:T(8,128)S(1)}, u32[]{:S(2)}, u32[]{:S(2)}) collective-permute-start(f32[8,128]{1,0:T(8,128)S(1)} %get-tuple-element.20.own_ref), channel_id=1, source_target_pairs={{0,16},{4,20},{8,24},{12,28},{16,0},{20,4},{24,8},{28,12},{1,17},{... | collective-permute-start | bytes 12296 | tf_op jit(solution)/shard_map/ppermute | solution.py:369
  5.7 0.0 collective-permute-start.1
  5.7 2.4 %collective-permute-done.2.four_ref = f32[8,128]{1,0:T(8,128)S(1)} collective-permute-done((f32[8,128]{1,0:T(8,128)S(1)}, f32[8,128]{1,0:T(8,128)S(1)}, u32[]{:S(2)}, u32[]{:S(2)}) %collective-permute-start.2) | collective-permute-done | bytes 4128 | tf_op jit(solution)/shard_map/ppermute | solution.py:369
  8.1 0.7 %collective-permute-done.1.three_ref = f32[8,128]{1,0:T(8,128)S(1)} collective-permute-done((f32[8,128]{1,0:T(8,128)S(1)}, f32[8,128]{1,0:T(8,128)S(1)}, u32[]{:S(2)}, u32[]{:S(2)}) %collective-permute-start.1) | collective-permute-done | bytes 4128 | tf_op jit(solution)/shard_map/ppermute | solution.py:381
  8.7 0.0 collective-permute-done.next_ref
  8.7 0.0 collective-permute-done.3.swap_ref
  8.8 0.1 pack.1
  8.9 2.7 %collective-permute-start.6 = (f32[8,128]{1,0:T(8,128)S(1)}, f32[8,128]{1,0:T(8,128)S(1)}, u32[]{:S(2)}, u32[]{:S(2)}) collective-permute-start(f32[8,128]{1,0:T(8,128)S(1)} %get-tuple-element.24.own_ref), channel_id=1, source_target_pairs={{0,2},{1,3},{2,0},{3,1},{4,6},{5,7},{6,4},{7,5},{8,10},{9,11},{10,... | collective-permute-start | bytes 12296 | tf_op jit(solution)/shard_map/ppermute | solution.py:369
  11.5 1.4 %collective-permute-start.4 = (f32[32,128]{1,0:T(8,128)S(1)}, f32[32,128]{1,0:T(8,128)S(1)}, u32[]{:S(2)}, u32[]{:S(2)}) collective-permute-start(f32[32,128]{1,0:T(8,128)S(1)} %get-tuple-element.27), channel_id=1, source_target_pairs={{1,2},{2,1},{3,0},{0,3},{5,6},{6,5},{7,4},{4,7},{9,10},{10,9},{11,... | collective-permute-start | bytes 49160 | tf_op jit(solution)/shard_map/ppermute | solution.py:377
  12.9 0.2 collective-permute-start.5
  13.1 0.0 copy-done.1
  13.1 0.5 %deal.1 = (f32[256,384]{1,0:T(8,128)S(1)}, bf16[128,384]{1,0:T(8,128)(2,1)S(1)}, bf16[384,256]{1,0:T(8,128)(2,1)S(1)}, f32[8,128]{1,0:T(8,128)S(1)}) custom-call(f32[4,32,256]{2,1,0:T(8,128)S(1)} %copy-done.1, f32[72,256]{1,0:T(8,128)S(1)} %get-tuple-element.22.up_ref, f32[72,256]{1,0:T(8,128)S(1)} %get-tuple-element.23.down_ref, ...), custom_call_target="tpu_custom_call" | custom-call | flops 300000000 | bytes 1500000 | tf_op jit(solution)/shard_map/deal/pallas_call | solution.py:408
  13.6 0.0 collective-permute-done.6.far_ref
  13.6 3.5 %collective-permute-done.4.next_ref = f32[32,128]{1,0:T(8,128)S(1)} collective-permute-done((f32[32,128]{1,0:T(8,128)S(1)}, f32[32,128]{1,0:T(8,128)S(1)}, u32[]{:S(2)}, u32[]{:S(2)}) %collective-permute-start.4) | collective-permute-done | bytes 16416 | tf_op jit(solution)/shard_map/ppermute | solution.py:377
  17.1 0.0 collective-permute-done.5.swap_ref
  17.1 0.1 join.1.own_ref
  17.2 0.1 collective-permute-start.7
  17.3 1.0 %first.1 = (f32[4,8,3,8,128]{4,3,2,1,0:T(8,128)S(1)}, f32[4,8,3,8,128]{4,3,2,1,0:T(8,128)S(1)}) custom-call(f32[256,384]{1,0:T(8,128)S(1)} %get-tuple-element.25.cells_ref, bf16[128,384]{1,0:T(8,128)(2,1)S(1)} %get-tuple-element.26.select_ref, f32[32,128]{1,0:T(8,128)S(1)} %collective-permute-done.4.next_ref, f32[32,128]{1,0:T(8,128)S(1)} %collective-permute-done.5.swap_ref), custom_call_target="tpu_custom_call" | custom-call | flops 20000000 | bytes 2000000 | tf_op jit(solution)/shard_map/first/pallas_call | solution.py:439
  18.3 0.1 collective-permute-done.7.mate_ref
  18.4 4.6 %steps.1 = f32[4,32,256]{2,1,0:T(8,128)} custom-call(f32[4,8,3,8,128]{4,3,2,1,0:T(8,128)S(1)} %get-tuple-element.29.field_ref, f32[4,8,3,8,128]{4,3,2,1,0:T(8,128)S(1)} %get-tuple-element.30.change_ref, bf16[384,256]{1,0:T(8,128)(2,1)S(1)} %get-tuple-element.31.select_ref, f32[8,128]{1,0:T(8,128)S(1)} %join.1.own_ref, ...), custom_call_target="tpu_custom_call" | custom-call | tf_op jit(solution)/shard_map/steps/pallas_call | solution.py:449
Async XLA Ops:
  0.0 0.9 %copy-start = (f32[4,32,256]{2,1,0:T(8,128)S(1)}, f32[4,32,256]{2,1,0:T(8,128)}, u32[]{:S(2)}) copy-start(f32[4,32,256]{2,1,0:T(8,128)} %state_ref.3) | copy-start | bytes 393220
  1.1 7.7 %collective-permute-start = (f32[72,256]{1,0:T(8,128)S(1)}, f32[72,256]{1,0:T(8,128)S(1)}, u32[]{:S(2)}, u32[]{:S(2)}) collective-permute-start(f32[72,256]{1,0:T(8,128)S(1)} %get-tuple-element.19), channel_id=1, source_target_pairs={{4,8},{8,4},{12,16},{16,12},{20,24},{24,20},{28,0},{0,28},{5,9},{9... | collective-permute-start | bytes 221192 | tf_op jit(solution)/shard_map/ppermute | solution.py:377
  4.5 4.3 %collective-permute-start.3 = (f32[72,256]{1,0:T(8,128)S(1)}, f32[72,256]{1,0:T(8,128)S(1)}, u32[]{:S(2)}, u32[]{:S(2)}) collective-permute-start(f32[72,256]{1,0:T(8,128)S(1)} %get-tuple-element.21), channel_id=1, source_target_pairs={{0,4},{4,0},{8,12},{12,8},{16,20},{20,16},{24,28},{28,24},{1,5},{5... | collective-permute-start | bytes 221192 | tf_op jit(solution)/shard_map/ppermute | solution.py:377
  4.5 8.7 %copy-start.1 = (f32[4,32,256]{2,1,0:T(8,128)S(1)}, f32[4,32,256]{2,1,0:T(8,128)}, u32[]{:S(2)}) copy-start(f32[4,32,256]{2,1,0:T(8,128)} %state_ref.3) | copy-start | bytes 393220
  4.5 3.6 %collective-permute-start.2 = (f32[8,128]{1,0:T(8,128)S(1)}, f32[8,128]{1,0:T(8,128)S(1)}, u32[]{:S(2)}, u32[]{:S(2)}) collective-permute-start(f32[8,128]{1,0:T(8,128)S(1)} %get-tuple-element.20.own_ref), channel_id=1, source_target_pairs={{0,16},{4,20},{8,24},{12,28},{16,0},{20,4},{24,8},{28,12},{1,17},{... | collective-permute-start | bytes 12296 | tf_op jit(solution)/shard_map/ppermute | solution.py:369
  5.7 3.0 %collective-permute-start.1 = (f32[8,128]{1,0:T(8,128)S(1)}, f32[8,128]{1,0:T(8,128)S(1)}, u32[]{:S(2)}, u32[]{:S(2)}) collective-permute-start(f32[8,128]{1,0:T(8,128)S(1)} %get-tuple-element.20.own_ref), channel_id=1, source_target_pairs={{0,12},{4,24},{8,20},{12,0},{16,28},{20,8},{24,4},{28,16},{1,13},{... | collective-permute-start | bytes 12296 | tf_op jit(solution)/shard_map/ppermute | solution.py:381
  8.9 4.7 %collective-permute-start.6 = (f32[8,128]{1,0:T(8,128)S(1)}, f32[8,128]{1,0:T(8,128)S(1)}, u32[]{:S(2)}, u32[]{:S(2)}) collective-permute-start(f32[8,128]{1,0:T(8,128)S(1)} %get-tuple-element.24.own_ref), channel_id=1, source_target_pairs={{0,2},{1,3},{2,0},{3,1},{4,6},{5,7},{6,4},{7,5},{8,10},{9,11},{10,... | collective-permute-start | bytes 12296 | tf_op jit(solution)/shard_map/ppermute | solution.py:369
  11.5 5.5 %collective-permute-start.4 = (f32[32,128]{1,0:T(8,128)S(1)}, f32[32,128]{1,0:T(8,128)S(1)}, u32[]{:S(2)}, u32[]{:S(2)}) collective-permute-start(f32[32,128]{1,0:T(8,128)S(1)} %get-tuple-element.27), channel_id=1, source_target_pairs={{1,2},{2,1},{3,0},{0,3},{5,6},{6,5},{7,4},{4,7},{9,10},{10,9},{11,... | collective-permute-start | bytes 49160 | tf_op jit(solution)/shard_map/ppermute | solution.py:377
  12.9 4.2 %collective-permute-start.5 = (f32[32,128]{1,0:T(8,128)S(1)}, f32[32,128]{1,0:T(8,128)S(1)}, u32[]{:S(2)}, u32[]{:S(2)}) collective-permute-start(f32[32,128]{1,0:T(8,128)S(1)} %get-tuple-element.28), channel_id=1, source_target_pairs={{0,1},{1,0},{2,3},{3,2},{4,5},{5,4},{6,7},{7,6},{8,9},{9,8},{10,11... | collective-permute-start | bytes 49160 | tf_op jit(solution)/shard_map/ppermute | solution.py:377
  17.2 1.2 %collective-permute-start.7 = (f32[8,128]{1,0:T(8,128)S(1)}, f32[8,128]{1,0:T(8,128)S(1)}, u32[]{:S(2)}, u32[]{:S(2)}) collective-permute-start(f32[8,128]{1,0:T(8,128)S(1)} %join.1.own_ref), channel_id=1, source_target_pairs={{0,4},{4,0},{8,12},{12,8},{16,20},{20,16},{24,28},{28,24},{1,5},{5... | collective-permute-start | bytes 12296 | tf_op jit(solution)/shard_map/ppermute | solution.py:369

commit v21 on v12

--- a/solution.py
+++ b/solution.py
@@ -151,7 +151,8 @@
     jumps = [minus(values[at + 1], values[at]) for at in range(count - 1)] + [end_jump]
     faces, first_low, high = [], None, None
     for at in range(count):
-        low, next_high = cell(wholes[at], jumps[at - 1] if at else rolled(end_jump, 1, 1), jumps[at])
+        jump = jumps[at - 1] if at else minus(values[0], rolled(values[-1], 1, 1))
+        low, next_high = cell(wholes[at], jump, jumps[at])
         if at:
             faces.append(face(high, low))
         else:
@@ -165,6 +166,7 @@
     def __init__(self, count, begin, here, after):
         self.count, self.begin = count, begin
         self.jump = self.first_jump = minus(after, here)
+        self.before = here
         self.first_low = self.first_flux = self.last_flux = self.high = None
 
     def feed(self, row, here, whole, after):
@@ -173,7 +175,7 @@
             next_jump = self.first_jump
         else:
             next_jump = minus(rolled(after, -1, 0) if next_row == 0 else after, here)
-        jump = rolled(self.jump, 1, 0) if row == 0 else self.jump
+        jump = minus(here, rolled(self.before, 1, 0)) if row == 0 else self.jump
         low, high = cell(whole, jump, next_jump)
         done = []
         if self.first_low is None:
@@ -186,7 +188,7 @@
                 seen = rolled(flux, -1, 0) if row == 0 else flux
                 done.append(((row - 1) % self.count, minus(seen, self.last_flux)))
             self.last_flux = flux
-        self.high, self.jump = high, next_jump
+        self.high, self.jump, self.before = high, next_jump, here
         if after is None:
             flux = face(high, self.first_low)
             done.append((row, minus(flux, self.last_flux)))
@@ -221,8 +223,10 @@
     return groups * lane + group
 
 
-def deal_kernel(state_ref, up_ref, down_ref, own_ref, dealt_ref, halo_select_ref, back_select_ref, top_ref, plain):
+def deal_kernel(state_ref, up_ref, down_ref, own_ref, dealt_ref, halo_select_ref, back_select_ref, top_ref, carried_ref, plain):
     top_ref[...] = own_ref[...]
+    carried = (iota((8, LANES), 0) == 0) & (iota((8, LANES), 1) < LANES // 2)
+    carried_ref[...] = jnp.where(carried, 1.0, 0.0)
     rows, cols = state_ref.shape[1:]
     tall = rows + 2 * HALO
     wide = dealt_ref.shape[1]
@@ -394,23 +398,23 @@
     first = swapped_pairs(first, "gy", 0)
     far = swapped_bit(top, "gy", 2)
     wide = groups * LANES
-    cells, halo_select, back_select, top = pl.pallas_call(
+    cells, halo_select, back_select, top, carried = pl.pallas_call(
         deal_kernel,
         out_shape=(
             array(parts * tall, wide),
             jax.ShapeDtypeStruct((wide - cols, wide), jnp.bfloat16),
             jax.ShapeDtypeStruct((wide, cols), jnp.bfloat16),
             array(8, LANES),
+            array(8, LANES),
         ),
         in_specs=[VMEM] * 4,
-        out_specs=(VMEM,) * 4,
+        out_specs=(VMEM,) * 5,
         scratch_shapes=[pltpu.VMEM((parts * tall, cols), jnp.float32)],
         compiler_params=params(8),
         cost_estimate=pl.CostEstimate(flops=300_000_000, bytes_accessed=1_500_000, transcendentals=0),
         name="deal",
     )(state, up, down, top)
-    carried = (iota((8, LANES), 0) == 0) & (iota((8, LANES), 1) < LANES // 2)
-    top = jnp.maximum(jnp.maximum(top, far), jnp.where(carried, jnp.maximum(first[:8], second[:8]), 0.0))
+    top = jnp.maximum(jnp.maximum(top, far), carried * jnp.maximum(first[:8], second[:8]))
     for axis, covered in (("gy", 4), ("gx", 8)):
         while covered < lax.axis_size(axis):
             top = jnp.maximum(top, sent(top, axis, covered))

time: 23.9 us -> 23.1 us (0.967)
  waiting for transfers between devices: 7.32 us -> 6.62 us
    ppermute x4, starting transfers between devices: 2.54 us -> 4.98 us  [swapped_pairs(): return lax.ppermute(value, axis, pairs)]
    ppermute x3, waiting for transfers between devices: 0.14 us -> 2.48 us  [swapped_bit(): lax.ppermute(value, axis, [(i, i ^ by) for i in range(lax.axis_size(axis))])]
    ppermute x4, waiting for transfers between devices: 5.77 us -> 3.48 us  [swapped_pairs(): return lax.ppermute(value, axis, pairs)]
    ppermute x3, starting transfers between devices: 5.7 us -> 3.96 us  [swapped_bit(): lax.ppermute(value, axis, [(i, i ^ by) for i in range(lax.axis_size(axis))])]
    ppermute x1, waiting for transfers between devices: 1.4 us -> 0.66 us  [swapped_threes(): lax.ppermute(value, axis, [(i, (i + 3 - 6 * (i % 2)) % count) for i in ra...]
    ppermute x1, starting transfers between devices: 0.65 us -> 0.01 us  [swapped_threes(): lax.ppermute(value, axis, [(i, (i + 3 - 6 * (i % 2)) % count) for i in ra...]
  transfers between devices with their start and end apart: 8 -> 8, of which waited for: 4 -> 4; matrix products, arithmetic and copies ran while one was open for 0% -> 0% of each run, Pallas kernels for 6% -> 7%
where the time goes in v21:
time: 23.1 us; the launch traced here: 22.9 us
  starting transfers between devices  8.95 us (39%)
  waiting for transfers between devices  6.62 us (29%)
  Pallas kernels  6.39 us (28%)
  local copies, waits for them, and re-layouts  0.91 us (4%)
    ppermute x4, starting transfers between devices, swapped_pairs(): return lax.ppermute(value, axis, pairs)  4.98 us
    pallas_call x1, Pallas kernels, local(): pl.pallas_call(steps_kernel, out_shape=array(parts, rows, cols), in_specs...  4.59 us
    ppermute x3, starting transfers between devices, swapped_bit(): lax.ppermute(value, axis, [(i, i ^ by) for i in range(lax.axis_size(axis))])  3.96 us
    ppermute x4, waiting for transfers between devices, swapped_pairs(): return lax.ppermute(value, axis, pairs)  3.48 us
    ppermute x3, waiting for transfers between devices, swapped_bit(): lax.ppermute(value, axis, [(i, i ^ by) for i in range(lax.axis_size(axis))])  2.48 us
    pallas_call x1, Pallas kernels, local(): pl.pallas_call(first_kernel, out_shape=(dealt_type, dealt_type), in_specs...  1.04 us
    unnamed x4, local copies, waits for them, and re-layouts  0.91 us
    ppermute x1, waiting for transfers between devices, swapped_threes(): lax.ppermute(value, axis, [(i, (i + 3 - 6 * (i % 2)) % count) for i in ra...  0.66 us
  transfers between devices with their start and end apart: 8, of which 4 were waited for; matrix products, arithmetic and copies ran while one was open for 0% of the time, Pallas kernels for 7%

profile of v21, /device:TPU:0, one launch (start us, length us, event | category | flops | bytes accessed | tf_op | source)
XLA Modules:
  0.0 22.9 jit_solution(8895021990024725060)
XLA Ops:
  0.0 0.0 copy-start
  0.0 0.9 %copy-done = f32[4,32,256]{2,1,0:T(8,128)S(1)} copy-done((f32[4,32,256]{2,1,0:T(8,128)S(1)}, f32[4,32,256]{2,1,0:T(8,128)}, u32[]{:S(2)}) %copy-start) | copy-done | bytes 131096
  0.9 0.2 edge.1
  1.1 3.4 %collective-permute-start = (f32[72,256]{1,0:T(8,128)S(1)}, f32[72,256]{1,0:T(8,128)S(1)}, u32[]{:S(2)}, u32[]{:S(2)}) collective-permute-start(f32[72,256]{1,0:T(8,128)S(1)} %get-tuple-element.20), channel_id=1, source_target_pairs={{4,8},{8,4},{12,16},{16,12},{20,24},{24,20},{28,0},{0,28},{5,9},{9... | collective-permute-start | bytes 221192 | tf_op jit(solution)/shard_map/ppermute | solution.py:370
  4.5 0.0 collective-permute-start.3
  4.5 0.0 copy-start.1
  4.5 1.2 %collective-permute-start.2 = (f32[8,128]{1,0:T(8,128)S(1)}, f32[8,128]{1,0:T(8,128)S(1)}, u32[]{:S(2)}, u32[]{:S(2)}) collective-permute-start(f32[8,128]{1,0:T(8,128)S(1)} %get-tuple-element.21.own_ref), channel_id=1, source_target_pairs={{0,16},{4,20},{8,24},{12,28},{16,0},{20,4},{24,8},{28,12},{1,17},{... | collective-permute-start | bytes 12296 | tf_op jit(solution)/shard_map/ppermute | solution.py:362
  5.7 0.0 collective-permute-start.1
  5.7 2.4 %collective-permute-done.2.four_ref = f32[8,128]{1,0:T(8,128)S(1)} collective-permute-done((f32[8,128]{1,0:T(8,128)S(1)}, f32[8,128]{1,0:T(8,128)S(1)}, u32[]{:S(2)}, u32[]{:S(2)}) %collective-permute-start.2) | collective-permute-done | bytes 4128 | tf_op jit(solution)/shard_map/ppermute | solution.py:362
  8.1 0.7 %collective-permute-done.1.three_ref = f32[8,128]{1,0:T(8,128)S(1)} collective-permute-done((f32[8,128]{1,0:T(8,128)S(1)}, f32[8,128]{1,0:T(8,128)S(1)}, u32[]{:S(2)}, u32[]{:S(2)}) %collective-permute-start.1) | collective-permute-done | bytes 4128 | tf_op jit(solution)/shard_map/ppermute | solution.py:374
  8.7 0.0 collective-permute-done.next_ref
  8.7 0.0 collective-permute-done.3.swap_ref
  8.8 0.1 pack.1
  8.9 2.7 %collective-permute-start.6 = (f32[8,128]{1,0:T(8,128)S(1)}, f32[8,128]{1,0:T(8,128)S(1)}, u32[]{:S(2)}, u32[]{:S(2)}) collective-permute-start(f32[8,128]{1,0:T(8,128)S(1)} %get-tuple-element.25.own_ref), channel_id=1, source_target_pairs={{0,2},{1,3},{2,0},{3,1},{4,6},{5,7},{6,4},{7,5},{8,10},{9,11},{10,... | collective-permute-start | bytes 12296 | tf_op jit(solution)/shard_map/ppermute | solution.py:362
  11.5 1.4 %collective-permute-start.4 = (f32[32,128]{1,0:T(8,128)S(1)}, f32[32,128]{1,0:T(8,128)S(1)}, u32[]{:S(2)}, u32[]{:S(2)}) collective-permute-start(f32[32,128]{1,0:T(8,128)S(1)} %get-tuple-element.28), channel_id=1, source_target_pairs={{1,2},{2,1},{3,0},{0,3},{5,6},{6,5},{7,4},{4,7},{9,10},{10,9},{11,... | collective-permute-start | bytes 49160 | tf_op jit(solution)/shard_map/ppermute | solution.py:370
  12.9 0.2 collective-permute-start.5
  13.1 0.0 copy-done.1
  13.1 0.5 %deal.1 = (f32[256,384]{1,0:T(8,128)S(1)}, bf16[128,384]{1,0:T(8,128)(2,1)S(1)}, bf16[384,256]{1,0:T(8,128)(2,1)S(1)}, f32[8,128]{1,0:T(8,128)S(1)}, f32[8,128]{1,0:T(8,128)S(1)}) custom-call(f32[4,32,256]{2,1,0:T(8,128)S(1)} %copy-done.1, f32[72,256]{1,0:T(8,128)S(1)} %get-tuple-element.23.up_ref, f32[72,256]{1,0:T(8,128)S(1)} %get-tuple-element.24.down_ref, ...), custom_call_target="tpu_custom_call" | custom-call | flops 300000000 | bytes 1500000 | tf_op jit(solution)/shard_map/deal/pallas_call | solution.py:401
  13.6 0.0 collective-permute-done.6
  13.6 3.5 %collective-permute-done.4.next_ref = f32[32,128]{1,0:T(8,128)S(1)} collective-permute-done((f32[32,128]{1,0:T(8,128)S(1)}, f32[32,128]{1,0:T(8,128)S(1)}, u32[]{:S(2)}, u32[]{:S(2)}) %collective-permute-start.4) | collective-permute-done | bytes 16416 | tf_op jit(solution)/shard_map/ppermute | solution.py:370
  17.1 0.0 collective-permute-done.5.swap_ref
  17.1 0.1 collective-permute-start.7
  17.2 1.0 %first.1 = (f32[4,8,3,8,128]{4,3,2,1,0:T(8,128)S(1)}, f32[4,8,3,8,128]{4,3,2,1,0:T(8,128)S(1)}) custom-call(f32[256,384]{1,0:T(8,128)S(1)} %get-tuple-element.26.cells_ref, bf16[128,384]{1,0:T(8,128)(2,1)S(1)} %get-tuple-element.27.select_ref, f32[32,128]{1,0:T(8,128)S(1)} %collective-permute-done.4.next_ref, f32[32,128]{1,0:T(8,128)S(1)} %collective-permute-done.5.swap_ref), custom_call_target="tpu_custom_call" | custom-call | flops 20000000 | bytes 2000000 | tf_op jit(solution)/shard_map/first/pallas_call | solution.py:426
  18.2 0.1 collective-permute-done.7.mate_ref
  18.3 4.6 %steps.1 = f32[4,32,256]{2,1,0:T(8,128)} custom-call(f32[4,8,3,8,128]{4,3,2,1,0:T(8,128)S(1)} %get-tuple-element.30.field_ref, f32[4,8,3,8,128]{4,3,2,1,0:T(8,128)S(1)} %get-tuple-element.31.change_ref, bf16[384,256]{1,0:T(8,128)(2,1)S(1)} %get-tuple-element.32.select_ref, f32[8,128]{1,0:T(8,128)S(1)} %fusion.1.own_ref, ...), custom_call_target="tpu_custom_call" | custom-call | tf_op jit(solution)/shard_map/steps/pallas_call | solution.py:436
  (1 shorter events, 0.0 us)
Async XLA Ops:
  0.0 0.9 %copy-start = (f32[4,32,256]{2,1,0:T(8,128)S(1)}, f32[4,32,256]{2,1,0:T(8,128)}, u32[]{:S(2)}) copy-start(f32[4,32,256]{2,1,0:T(8,128)} %state_ref.3) | copy-start | bytes 393220
  1.1 7.7 %collective-permute-start = (f32[72,256]{1,0:T(8,128)S(1)}, f32[72,256]{1,0:T(8,128)S(1)}, u32[]{:S(2)}, u32[]{:S(2)}) collective-permute-start(f32[72,256]{1,0:T(8,128)S(1)} %get-tuple-element.20), channel_id=1, source_target_pairs={{4,8},{8,4},{12,16},{16,12},{20,24},{24,20},{28,0},{0,28},{5,9},{9... | collective-permute-start | bytes 221192 | tf_op jit(solution)/shard_map/ppermute | solution.py:370
  4.5 4.3 %collective-permute-start.3 = (f32[72,256]{1,0:T(8,128)S(1)}, f32[72,256]{1,0:T(8,128)S(1)}, u32[]{:S(2)}, u32[]{:S(2)}) collective-permute-start(f32[72,256]{1,0:T(8,128)S(1)} %get-tuple-element.22), channel_id=1, source_target_pairs={{0,4},{4,0},{8,12},{12,8},{16,20},{20,16},{24,28},{28,24},{1,5},{5... | collective-permute-start | bytes 221192 | tf_op jit(solution)/shard_map/ppermute | solution.py:370
  4.5 8.7 %copy-start.1 = (f32[4,32,256]{2,1,0:T(8,128)S(1)}, f32[4,32,256]{2,1,0:T(8,128)}, u32[]{:S(2)}) copy-start(f32[4,32,256]{2,1,0:T(8,128)} %state_ref.3) | copy-start | bytes 393220
  4.5 3.6 %collective-permute-start.2 = (f32[8,128]{1,0:T(8,128)S(1)}, f32[8,128]{1,0:T(8,128)S(1)}, u32[]{:S(2)}, u32[]{:S(2)}) collective-permute-start(f32[8,128]{1,0:T(8,128)S(1)} %get-tuple-element.21.own_ref), channel_id=1, source_target_pairs={{0,16},{4,20},{8,24},{12,28},{16,0},{20,4},{24,8},{28,12},{1,17},{... | collective-permute-start | bytes 12296 | tf_op jit(solution)/shard_map/ppermute | solution.py:362
  5.7 3.0 %collective-permute-start.1 = (f32[8,128]{1,0:T(8,128)S(1)}, f32[8,128]{1,0:T(8,128)S(1)}, u32[]{:S(2)}, u32[]{:S(2)}) collective-permute-start(f32[8,128]{1,0:T(8,128)S(1)} %get-tuple-element.21.own_ref), channel_id=1, source_target_pairs={{0,12},{4,24},{8,20},{12,0},{16,28},{20,8},{24,4},{28,16},{1,13},{... | collective-permute-start | bytes 12296 | tf_op jit(solution)/shard_map/ppermute | solution.py:374
  8.9 4.7 %collective-permute-start.6 = (f32[8,128]{1,0:T(8,128)S(1)}, f32[8,128]{1,0:T(8,128)S(1)}, u32[]{:S(2)}, u32[]{:S(2)}) collective-permute-start(f32[8,128]{1,0:T(8,128)S(1)} %get-tuple-element.25.own_ref), channel_id=1, source_target_pairs={{0,2},{1,3},{2,0},{3,1},{4,6},{5,7},{6,4},{7,5},{8,10},{9,11},{10,... | collective-permute-start | bytes 12296 | tf_op jit(solution)/shard_map/ppermute | solution.py:362
  11.5 5.5 %collective-permute-start.4 = (f32[32,128]{1,0:T(8,128)S(1)}, f32[32,128]{1,0:T(8,128)S(1)}, u32[]{:S(2)}, u32[]{:S(2)}) collective-permute-start(f32[32,128]{1,0:T(8,128)S(1)} %get-tuple-element.28), channel_id=1, source_target_pairs={{1,2},{2,1},{3,0},{0,3},{5,6},{6,5},{7,4},{4,7},{9,10},{10,9},{11,... | collective-permute-start | bytes 49160 | tf_op jit(solution)/shard_map/ppermute | solution.py:370
  12.9 4.2 %collective-permute-start.5 = (f32[32,128]{1,0:T(8,128)S(1)}, f32[32,128]{1,0:T(8,128)S(1)}, u32[]{:S(2)}, u32[]{:S(2)}) collective-permute-start(f32[32,128]{1,0:T(8,128)S(1)} %get-tuple-element.29), channel_id=1, source_target_pairs={{0,1},{1,0},{2,3},{3,2},{4,5},{5,4},{6,7},{7,6},{8,9},{9,8},{10,11... | collective-permute-start | bytes 49160 | tf_op jit(solution)/shard_map/ppermute | solution.py:370
  17.1 1.2 %collective-permute-start.7 = (f32[8,128]{1,0:T(8,128)S(1)}, f32[8,128]{1,0:T(8,128)S(1)}, u32[]{:S(2)}, u32[]{:S(2)}) collective-permute-start(f32[8,128]{1,0:T(8,128)S(1)} %fusion.1.own_ref), channel_id=1, source_target_pairs={{0,4},{4,0},{8,12},{12,8},{16,20},{20,16},{24,28},{28,24},{1,5},{5... | collective-permute-start | bytes 12296 | tf_op jit(solution)/shard_map/ppermute | solution.py:362

commit v22 on v21

--- a/solution.py
+++ b/solution.py
@@ -53,16 +53,16 @@
     top_ref[...] = jnp.full(top_ref.shape, top)
 
 
-def pack_kernel(state_ref, next_ref, three_ref, four_ref, swap_ref, own_ref, up_ref, down_ref, first_ref, second_ref, top_ref):
+def pack_kernel(state_ref, next_ref, three_ref, four_ref, swap_ref, own_ref, first_ref, second_ref, top_ref):
     rows = state_ref.shape[1]
     cols = state_ref.shape[2]
     half = rows // 2 + HALO
     lane = iota((half, LANES), 1)
     is_odd = odd("gx")
-    up_ref[...] = jnp.where(is_odd, swap_ref[...], next_ref[...])
-    down_ref[...] = jnp.where(is_odd, next_ref[...], swap_ref[...])
+    up = jnp.where(is_odd, swap_ref[...], next_ref[...])
+    down = jnp.where(is_odd, next_ref[...], swap_ref[...])
     top = jnp.maximum(jnp.maximum(own_ref[...], jnp.maximum(three_ref[...], four_ref[...])),
-                      jnp.maximum(up_ref[4 * HALO :, 0:LANES], down_ref[4 * HALO :, 0:LANES]))
+                      jnp.maximum(up[4 * HALO :, 0:LANES], down[4 * HALO :, 0:LANES]))
 
     def edge(low, at):
         lanes = slice(low, low + LANES)
@@ -71,9 +71,9 @@
             for comp in range(4):
                 span = slice(comp * HALO, (comp + 1) * HALO)
                 if side == 0:
-                    cells = jnp.concatenate([up_ref[span, lanes], state_ref[comp, 0 : rows // 2, lanes]], axis=0)
+                    cells = jnp.concatenate([up[span, lanes], state_ref[comp, 0 : rows // 2, lanes]], axis=0)
                 else:
-                    cells = jnp.concatenate([state_ref[comp, rows // 2 : rows, lanes], down_ref[span, lanes]], axis=0)
+                    cells = jnp.concatenate([state_ref[comp, rows // 2 : rows, lanes], down[span, lanes]], axis=0)
                 goal = side * (LANES // 2) + comp * HALO
                 moved = pltpu.roll(cells, (goal - at) % LANES, axis=1)
                 total = jnp.where((lane >= goal) & (lane < goal + HALO), moved, total)
@@ -223,7 +223,7 @@
     return groups * lane + group
 
 
-def deal_kernel(state_ref, up_ref, down_ref, own_ref, dealt_ref, halo_select_ref, back_select_ref, top_ref, carried_ref, plain):
+def deal_kernel(state_ref, next_ref, swap_ref, own_ref, dealt_ref, halo_select_ref, back_select_ref, top_ref, carried_ref, plain):
     top_ref[...] = own_ref[...]
     carried = (iota((8, LANES), 0) == 0) & (iota((8, LANES), 1) < LANES // 2)
     carried_ref[...] = jnp.where(carried, 1.0, 0.0)
@@ -234,9 +234,9 @@
     for comp in range(4):
         span = slice(comp * HALO, (comp + 1) * HALO)
         low = comp * tall
-        plain[low : low + HALO, :] = up_ref[span, :]
+        plain[low : low + HALO, :] = jnp.where(odd("gx"), swap_ref[span, :], next_ref[span, :])
         plain[low + HALO : low + HALO + rows, :] = state_ref[comp]
-        plain[low + HALO + rows : low + tall, :] = down_ref[span, :]
+        plain[low + HALO + rows : low + tall, :] = jnp.where(odd("gx"), next_ref[span, :], swap_ref[span, :])
     source = iota((wide, wide), 0)
     goal = iota((wide, wide), 1)
     place = place_of(goal % LANES, goal // LANES, groups)
@@ -386,11 +386,12 @@
     first = swapped_pairs(first, "gx", 0)
     far = swapped_threes(top, "gx"), swapped_bit(top, "gx", 4)
     side_type = array(tall // 2, LANES)
-    up, down, first, second, top = pl.pallas_call(
+    row_halos = second, first
+    first, second, top = pl.pallas_call(
         pack_kernel,
-        out_shape=(edge_type, edge_type, side_type, side_type, array(8, LANES)),
+        out_shape=(side_type, side_type, array(8, LANES)),
         in_specs=[VMEM] * 6,
-        out_specs=(VMEM,) * 5,
+        out_specs=(VMEM,) * 3,
         compiler_params=params(4),
         name="pack",
     )(state, second, *far, first, top)
@@ -413,7 +414,7 @@
         compiler_params=params(8),
         cost_estimate=pl.CostEstimate(flops=300_000_000, bytes_accessed=1_500_000, transcendentals=0),
         name="deal",
-    )(state, up, down, top)
+    )(state, *row_halos, top)
     top = jnp.maximum(jnp.maximum(top, far), carried * jnp.maximum(first[:8], second[:8]))
     for axis, covered in (("gy", 4), ("gx", 8)):
         while covered < lax.axis_size(axis):

time: 23.1 us -> 23.1 us (level)
  no operation moved by 1% of the time
where the time goes in v22:
time: 23.1 us; the launch traced here: 22.9 us
  starting transfers between devices  8.95 us (39%)
  waiting for transfers between devices  6.61 us (29%)
  Pallas kernels  6.39 us (28%)
  local copies, waits for them, and re-layouts  0.91 us (4%)
    ppermute x4, starting transfers between devices, swapped_pairs(): return lax.ppermute(value, axis, pairs)  4.98 us
    pallas_call x1, Pallas kernels, local(): pl.pallas_call(steps_kernel, out_shape=array(parts, rows, cols), in_specs...  4.59 us
    ppermute x3, starting transfers between devices, swapped_bit(): lax.ppermute(value, axis, [(i, i ^ by) for i in range(lax.axis_size(axis))])  3.96 us
    ppermute x4, waiting for transfers between devices, swapped_pairs(): return lax.ppermute(value, axis, pairs)  3.48 us
    ppermute x3, waiting for transfers between devices, swapped_bit(): lax.ppermute(value, axis, [(i, i ^ by) for i in range(lax.axis_size(axis))])  2.48 us
    pallas_call x1, Pallas kernels, local(): pl.pallas_call(first_kernel, out_shape=(dealt_type, dealt_type), in_specs...  1.04 us
    unnamed x4, local copies, waits for them, and re-layouts  0.91 us
    ppermute x1, waiting for transfers between devices, swapped_threes(): lax.ppermute(value, axis, [(i, (i + 3 - 6 * (i % 2)) % count) for i in ra...  0.66 us
  transfers between devices with their start and end apart: 8, of which 4 were waited for; matrix products, arithmetic and copies ran while one was open for 0% of the time, Pallas kernels for 7%

profile of v22, /device:TPU:0, one launch (start us, length us, event | category | flops | bytes accessed | tf_op | source)
XLA Modules:
  0.0 22.9 jit_solution(16622587966543471714)
XLA Ops:
  0.0 0.0 copy-start
  0.0 0.9 %copy-done = f32[4,32,256]{2,1,0:T(8,128)S(1)} copy-done((f32[4,32,256]{2,1,0:T(8,128)S(1)}, f32[4,32,256]{2,1,0:T(8,128)}, u32[]{:S(2)}) %copy-start) | copy-done | bytes 131096
  0.9 0.2 edge.1
  1.1 3.4 %collective-permute-start = (f32[72,256]{1,0:T(8,128)S(1)}, f32[72,256]{1,0:T(8,128)S(1)}, u32[]{:S(2)}, u32[]{:S(2)}) collective-permute-start(f32[72,256]{1,0:T(8,128)S(1)} %get-tuple-element.18), channel_id=1, source_target_pairs={{4,8},{8,4},{12,16},{16,12},{20,24},{24,20},{28,0},{0,28},{5,9},{9... | collective-permute-start | bytes 221192 | tf_op jit(solution)/shard_map/ppermute | solution.py:370
  4.5 0.0 collective-permute-start.1
  4.5 0.0 copy-start.1
  4.5 1.2 %collective-permute-start.3 = (f32[8,128]{1,0:T(8,128)S(1)}, f32[8,128]{1,0:T(8,128)S(1)}, u32[]{:S(2)}, u32[]{:S(2)}) collective-permute-start(f32[8,128]{1,0:T(8,128)S(1)} %get-tuple-element.20.own_ref), channel_id=1, source_target_pairs={{0,16},{4,20},{8,24},{12,28},{16,0},{20,4},{24,8},{28,12},{1,17},{... | collective-permute-start | bytes 12296 | tf_op jit(solution)/shard_map/ppermute | solution.py:362
  5.7 0.0 collective-permute-start.2
  5.7 2.4 %collective-permute-done.3.four_ref = f32[8,128]{1,0:T(8,128)S(1)} collective-permute-done((f32[8,128]{1,0:T(8,128)S(1)}, f32[8,128]{1,0:T(8,128)S(1)}, u32[]{:S(2)}, u32[]{:S(2)}) %collective-permute-start.3) | collective-permute-done | bytes 4128 | tf_op jit(solution)/shard_map/ppermute | solution.py:362
  8.1 0.7 %collective-permute-done.2.three_ref = f32[8,128]{1,0:T(8,128)S(1)} collective-permute-done((f32[8,128]{1,0:T(8,128)S(1)}, f32[8,128]{1,0:T(8,128)S(1)}, u32[]{:S(2)}, u32[]{:S(2)}) %collective-permute-start.2) | collective-permute-done | bytes 4128 | tf_op jit(solution)/shard_map/ppermute | solution.py:374
  8.7 0.0 collective-permute-done.next_ref
  8.7 0.0 collective-permute-done.1.swap_ref
  8.8 0.1 pack.1
  8.9 2.7 %collective-permute-start.6 = (f32[8,128]{1,0:T(8,128)S(1)}, f32[8,128]{1,0:T(8,128)S(1)}, u32[]{:S(2)}, u32[]{:S(2)}) collective-permute-start(f32[8,128]{1,0:T(8,128)S(1)} %get-tuple-element.21.own_ref), channel_id=1, source_target_pairs={{0,2},{1,3},{2,0},{3,1},{4,6},{5,7},{6,4},{7,5},{8,10},{9,11},{10,... | collective-permute-start | bytes 12296 | tf_op jit(solution)/shard_map/ppermute | solution.py:362
  11.5 1.4 %collective-permute-start.4 = (f32[32,128]{1,0:T(8,128)S(1)}, f32[32,128]{1,0:T(8,128)S(1)}, u32[]{:S(2)}, u32[]{:S(2)}) collective-permute-start(f32[32,128]{1,0:T(8,128)S(1)} %get-tuple-element.24), channel_id=1, source_target_pairs={{1,2},{2,1},{3,0},{0,3},{5,6},{6,5},{7,4},{4,7},{9,10},{10,9},{11,... | collective-permute-start | bytes 49160 | tf_op jit(solution)/shard_map/ppermute | solution.py:370
  12.9 0.2 collective-permute-start.5
  13.1 0.0 copy-done.1
  13.1 0.5 %deal.1 = (f32[256,384]{1,0:T(8,128)S(1)}, bf16[128,384]{1,0:T(8,128)(2,1)S(1)}, bf16[384,256]{1,0:T(8,128)(2,1)S(1)}, f32[8,128]{1,0:T(8,128)S(1)}, f32[8,128]{1,0:T(8,128)S(1)}) custom-call(f32[4,32,256]{2,1,0:T(8,128)S(1)} %copy-done.1, f32[72,256]{1,0:T(8,128)S(1)} %collective-permute-done.next_ref, f32[72,256]{1,0:T(8,128)S(1)} %collective-permute-done.1.swap_ref, ...), custom_call_target="tpu_custom_call" | custom-call | flops 300000000 | bytes 1500000 | tf_op jit(solution)/shard_map/deal/pallas_call | solution.py:402
  13.6 0.0 collective-permute-done.6
  13.6 3.5 %collective-permute-done.4.next_ref = f32[32,128]{1,0:T(8,128)S(1)} collective-permute-done((f32[32,128]{1,0:T(8,128)S(1)}, f32[32,128]{1,0:T(8,128)S(1)}, u32[]{:S(2)}, u32[]{:S(2)}) %collective-permute-start.4) | collective-permute-done | bytes 16416 | tf_op jit(solution)/shard_map/ppermute | solution.py:370
  17.1 0.0 collective-permute-done.5.swap_ref
  17.1 0.1 collective-permute-start.7
  17.2 1.0 %first.1 = (f32[4,8,3,8,128]{4,3,2,1,0:T(8,128)S(1)}, f32[4,8,3,8,128]{4,3,2,1,0:T(8,128)S(1)}) custom-call(f32[256,384]{1,0:T(8,128)S(1)} %get-tuple-element.22.cells_ref, bf16[128,384]{1,0:T(8,128)(2,1)S(1)} %get-tuple-element.23.select_ref, f32[32,128]{1,0:T(8,128)S(1)} %collective-permute-done.4.next_ref, f32[32,128]{1,0:T(8,128)S(1)} %collective-permute-done.5.swap_ref), custom_call_target="tpu_custom_call" | custom-call | flops 20000000 | bytes 2000000 | tf_op jit(solution)/shard_map/first/pallas_call | solution.py:427
  18.2 0.1 collective-permute-done.7.mate_ref
  18.3 4.6 %steps.1 = f32[4,32,256]{2,1,0:T(8,128)} custom-call(f32[4,8,3,8,128]{4,3,2,1,0:T(8,128)S(1)} %get-tuple-element.26.field_ref, f32[4,8,3,8,128]{4,3,2,1,0:T(8,128)S(1)} %get-tuple-element.27.change_ref, bf16[384,256]{1,0:T(8,128)(2,1)S(1)} %get-tuple-element.28.select_ref, f32[8,128]{1,0:T(8,128)S(1)} %fusion.1.own_ref, ...), custom_call_target="tpu_custom_call" | custom-call | tf_op jit(solution)/shard_map/steps/pallas_call | solution.py:437
  (1 shorter events, 0.0 us)
Async XLA Ops:
  0.0 0.9 %copy-start = (f32[4,32,256]{2,1,0:T(8,128)S(1)}, f32[4,32,256]{2,1,0:T(8,128)}, u32[]{:S(2)}) copy-start(f32[4,32,256]{2,1,0:T(8,128)} %state_ref.3) | copy-start | bytes 393220
  1.1 7.7 %collective-permute-start = (f32[72,256]{1,0:T(8,128)S(1)}, f32[72,256]{1,0:T(8,128)S(1)}, u32[]{:S(2)}, u32[]{:S(2)}) collective-permute-start(f32[72,256]{1,0:T(8,128)S(1)} %get-tuple-element.18), channel_id=1, source_target_pairs={{4,8},{8,4},{12,16},{16,12},{20,24},{24,20},{28,0},{0,28},{5,9},{9... | collective-permute-start | bytes 221192 | tf_op jit(solution)/shard_map/ppermute | solution.py:370
  4.5 4.3 %collective-permute-start.1 = (f32[72,256]{1,0:T(8,128)S(1)}, f32[72,256]{1,0:T(8,128)S(1)}, u32[]{:S(2)}, u32[]{:S(2)}) collective-permute-start(f32[72,256]{1,0:T(8,128)S(1)} %get-tuple-element.19), channel_id=1, source_target_pairs={{0,4},{4,0},{8,12},{12,8},{16,20},{20,16},{24,28},{28,24},{1,5},{5... | collective-permute-start | bytes 221192 | tf_op jit(solution)/shard_map/ppermute | solution.py:370
  4.5 8.7 %copy-start.1 = (f32[4,32,256]{2,1,0:T(8,128)S(1)}, f32[4,32,256]{2,1,0:T(8,128)}, u32[]{:S(2)}) copy-start(f32[4,32,256]{2,1,0:T(8,128)} %state_ref.3) | copy-start | bytes 393220
  4.5 3.6 %collective-permute-start.3 = (f32[8,128]{1,0:T(8,128)S(1)}, f32[8,128]{1,0:T(8,128)S(1)}, u32[]{:S(2)}, u32[]{:S(2)}) collective-permute-start(f32[8,128]{1,0:T(8,128)S(1)} %get-tuple-element.20.own_ref), channel_id=1, source_target_pairs={{0,16},{4,20},{8,24},{12,28},{16,0},{20,4},{24,8},{28,12},{1,17},{... | collective-permute-start | bytes 12296 | tf_op jit(solution)/shard_map/ppermute | solution.py:362
  5.7 3.0 %collective-permute-start.2 = (f32[8,128]{1,0:T(8,128)S(1)}, f32[8,128]{1,0:T(8,128)S(1)}, u32[]{:S(2)}, u32[]{:S(2)}) collective-permute-start(f32[8,128]{1,0:T(8,128)S(1)} %get-tuple-element.20.own_ref), channel_id=1, source_target_pairs={{0,12},{4,24},{8,20},{12,0},{16,28},{20,8},{24,4},{28,16},{1,13},{... | collective-permute-start | bytes 12296 | tf_op jit(solution)/shard_map/ppermute | solution.py:374
  8.9 4.7 %collective-permute-start.6 = (f32[8,128]{1,0:T(8,128)S(1)}, f32[8,128]{1,0:T(8,128)S(1)}, u32[]{:S(2)}, u32[]{:S(2)}) collective-permute-start(f32[8,128]{1,0:T(8,128)S(1)} %get-tuple-element.21.own_ref), channel_id=1, source_target_pairs={{0,2},{1,3},{2,0},{3,1},{4,6},{5,7},{6,4},{7,5},{8,10},{9,11},{10,... | collective-permute-start | bytes 12296 | tf_op jit(solution)/shard_map/ppermute | solution.py:362
  11.5 5.5 %collective-permute-start.4 = (f32[32,128]{1,0:T(8,128)S(1)}, f32[32,128]{1,0:T(8,128)S(1)}, u32[]{:S(2)}, u32[]{:S(2)}) collective-permute-start(f32[32,128]{1,0:T(8,128)S(1)} %get-tuple-element.24), channel_id=1, source_target_pairs={{1,2},{2,1},{3,0},{0,3},{5,6},{6,5},{7,4},{4,7},{9,10},{10,9},{11,... | collective-permute-start | bytes 49160 | tf_op jit(solution)/shard_map/ppermute | solution.py:370
  12.9 4.2 %collective-permute-start.5 = (f32[32,128]{1,0:T(8,128)S(1)}, f32[32,128]{1,0:T(8,128)S(1)}, u32[]{:S(2)}, u32[]{:S(2)}) collective-permute-start(f32[32,128]{1,0:T(8,128)S(1)} %get-tuple-element.25), channel_id=1, source_target_pairs={{0,1},{1,0},{2,3},{3,2},{4,5},{5,4},{6,7},{7,6},{8,9},{9,8},{10,11... | collective-permute-start | bytes 49160 | tf_op jit(solution)/shard_map/ppermute | solution.py:370
  17.1 1.2 %collective-permute-start.7 = (f32[8,128]{1,0:T(8,128)S(1)}, f32[8,128]{1,0:T(8,128)S(1)}, u32[]{:S(2)}, u32[]{:S(2)}) collective-permute-start(f32[8,128]{1,0:T(8,128)S(1)} %fusion.1.own_ref), channel_id=1, source_target_pairs={{0,4},{4,0},{8,12},{12,8},{16,20},{20,16},{24,28},{28,24},{1,5},{5... | collective-permute-start | bytes 12296 | tf_op jit(solution)/shard_map/ppermute | solution.py:362

commit v23 on v22

--- a/solution.py
+++ b/solution.py
@@ -343,8 +343,10 @@
     copies = []
     for comp in range(4):
         result[comp] = ((2.0 / SCALES[comp]) / scales[comp]) * found[comp * rows : (comp + 1) * rows, :]
-        copies.append(pltpu.make_async_copy(result.at[comp], out_ref.at[comp], sems.at[comp]))
-        copies[-1].start()
+        for side in range(2):
+            part = (comp, pl.ds(side * (rows // 2), rows // 2))
+            copies.append(pltpu.make_async_copy(result.at[part], out_ref.at[part], sems.at[comp, side]))
+            copies[-1].start()
     for copy in copies:
         copy.wait()
 
@@ -440,7 +442,7 @@
         in_specs=[VMEM] * 5,
         out_specs=pl.BlockSpec(memory_space=pl.ANY),
         scratch_shapes=[dealt] * 3
-        + [plain, pltpu.VMEM((parts, rows, cols), jnp.float32), pltpu.SemaphoreType.DMA((parts,))],
+        + [plain, pltpu.VMEM((parts, rows, cols), jnp.float32), pltpu.SemaphoreType.DMA((parts, 2))],
         compiler_params=params(16),
         name="steps",
     )(field, change, back_select, top, mate)

time: 23.1 us -> 23.1 us (level)
  no operation moved by 1% of the time
where the time goes in v23:
time: 23.1 us; the launch traced here: 22.9 us
  starting transfers between devices  8.95 us (39%)
  waiting for transfers between devices  6.61 us (29%)
  Pallas kernels  6.42 us (28%)
  local copies, waits for them, and re-layouts  0.91 us (4%)
    ppermute x4, starting transfers between devices, swapped_pairs(): return lax.ppermute(value, axis, pairs)  4.98 us
    pallas_call x1, Pallas kernels, local(): pl.pallas_call(steps_kernel, out_shape=array(parts, rows, cols), in_specs...  4.62 us
    ppermute x3, starting transfers between devices, swapped_bit(): lax.ppermute(value, axis, [(i, i ^ by) for i in range(lax.axis_size(axis))])  3.96 us
    ppermute x4, waiting for transfers between devices, swapped_pairs(): return lax.ppermute(value, axis, pairs)  3.48 us
    ppermute x3, waiting for transfers between devices, swapped_bit(): lax.ppermute(value, axis, [(i, i ^ by) for i in range(lax.axis_size(axis))])  2.48 us
    pallas_call x1, Pallas kernels, local(): pl.pallas_call(first_kernel, out_shape=(dealt_type, dealt_type), in_specs...  1.04 us
    unnamed x4, local copies, waits for them, and re-layouts  0.91 us
    ppermute x1, waiting for transfers between devices, swapped_threes(): lax.ppermute(value, axis, [(i, (i + 3 - 6 * (i % 2)) % count) for i in ra...  0.66 us
  transfers between devices with their start and end apart: 8, of which 4 were waited for; matrix products, arithmetic and copies ran while one was open for 0% of the time, Pallas kernels for 7%

profile of v23, /device:TPU:0, one launch (start us, length us, event | category | flops | bytes accessed | tf_op | source)
XLA Modules:
  0.0 22.9 jit_solution(4274768750145778002)
XLA Ops:
  0.0 0.0 copy-start
  0.0 0.9 %copy-done = f32[4,32,256]{2,1,0:T(8,128)S(1)} copy-done((f32[4,32,256]{2,1,0:T(8,128)S(1)}, f32[4,32,256]{2,1,0:T(8,128)}, u32[]{:S(2)}) %copy-start) | copy-done | bytes 131096
  0.9 0.2 edge.1
  1.1 3.4 %collective-permute-start = (f32[72,256]{1,0:T(8,128)S(1)}, f32[72,256]{1,0:T(8,128)S(1)}, u32[]{:S(2)}, u32[]{:S(2)}) collective-permute-start(f32[72,256]{1,0:T(8,128)S(1)} %get-tuple-element.18), channel_id=1, source_target_pairs={{4,8},{8,4},{12,16},{16,12},{20,24},{24,20},{28,0},{0,28},{5,9},{9... | collective-permute-start | bytes 221192 | tf_op jit(solution)/shard_map/ppermute | solution.py:372
  4.5 0.0 collective-permute-start.1
  4.5 0.0 copy-start.1
  4.5 1.2 %collective-permute-start.3 = (f32[8,128]{1,0:T(8,128)S(1)}, f32[8,128]{1,0:T(8,128)S(1)}, u32[]{:S(2)}, u32[]{:S(2)}) collective-permute-start(f32[8,128]{1,0:T(8,128)S(1)} %get-tuple-element.20.own_ref), channel_id=1, source_target_pairs={{0,16},{4,20},{8,24},{12,28},{16,0},{20,4},{24,8},{28,12},{1,17},{... | collective-permute-start | bytes 12296 | tf_op jit(solution)/shard_map/ppermute | solution.py:364
  5.7 0.0 collective-permute-start.2
  5.7 2.4 %collective-permute-done.3.four_ref = f32[8,128]{1,0:T(8,128)S(1)} collective-permute-done((f32[8,128]{1,0:T(8,128)S(1)}, f32[8,128]{1,0:T(8,128)S(1)}, u32[]{:S(2)}, u32[]{:S(2)}) %collective-permute-start.3) | collective-permute-done | bytes 4128 | tf_op jit(solution)/shard_map/ppermute | solution.py:364
  8.1 0.7 %collective-permute-done.2.three_ref = f32[8,128]{1,0:T(8,128)S(1)} collective-permute-done((f32[8,128]{1,0:T(8,128)S(1)}, f32[8,128]{1,0:T(8,128)S(1)}, u32[]{:S(2)}, u32[]{:S(2)}) %collective-permute-start.2) | collective-permute-done | bytes 4128 | tf_op jit(solution)/shard_map/ppermute | solution.py:376
  8.7 0.0 collective-permute-done.next_ref
  8.7 0.0 collective-permute-done.1.swap_ref
  8.8 0.1 pack.1
  8.9 2.7 %collective-permute-start.6 = (f32[8,128]{1,0:T(8,128)S(1)}, f32[8,128]{1,0:T(8,128)S(1)}, u32[]{:S(2)}, u32[]{:S(2)}) collective-permute-start(f32[8,128]{1,0:T(8,128)S(1)} %get-tuple-element.21.own_ref), channel_id=1, source_target_pairs={{0,2},{1,3},{2,0},{3,1},{4,6},{5,7},{6,4},{7,5},{8,10},{9,11},{10,... | collective-permute-start | bytes 12296 | tf_op jit(solution)/shard_map/ppermute | solution.py:364
  11.5 1.4 %collective-permute-start.4 = (f32[32,128]{1,0:T(8,128)S(1)}, f32[32,128]{1,0:T(8,128)S(1)}, u32[]{:S(2)}, u32[]{:S(2)}) collective-permute-start(f32[32,128]{1,0:T(8,128)S(1)} %get-tuple-element.24), channel_id=1, source_target_pairs={{1,2},{2,1},{3,0},{0,3},{5,6},{6,5},{7,4},{4,7},{9,10},{10,9},{11,... | collective-permute-start | bytes 49160 | tf_op jit(solution)/shard_map/ppermute | solution.py:372
  12.9 0.2 collective-permute-start.5
  13.1 0.0 copy-done.1
  13.1 0.5 %deal.1 = (f32[256,384]{1,0:T(8,128)S(1)}, bf16[128,384]{1,0:T(8,128)(2,1)S(1)}, bf16[384,256]{1,0:T(8,128)(2,1)S(1)}, f32[8,128]{1,0:T(8,128)S(1)}, f32[8,128]{1,0:T(8,128)S(1)}) custom-call(f32[4,32,256]{2,1,0:T(8,128)S(1)} %copy-done.1, f32[72,256]{1,0:T(8,128)S(1)} %collective-permute-done.next_ref, f32[72,256]{1,0:T(8,128)S(1)} %collective-permute-done.1.swap_ref, ...), custom_call_target="tpu_custom_call" | custom-call | flops 300000000 | bytes 1500000 | tf_op jit(solution)/shard_map/deal/pallas_call | solution.py:404
  13.6 0.0 collective-permute-done.6
  13.6 3.5 %collective-permute-done.4.next_ref = f32[32,128]{1,0:T(8,128)S(1)} collective-permute-done((f32[32,128]{1,0:T(8,128)S(1)}, f32[32,128]{1,0:T(8,128)S(1)}, u32[]{:S(2)}, u32[]{:S(2)}) %collective-permute-start.4) | collective-permute-done | bytes 16416 | tf_op jit(solution)/shard_map/ppermute | solution.py:372
  17.1 0.0 collective-permute-done.5.swap_ref
  17.1 0.1 collective-permute-start.7
  17.2 1.0 %first.1 = (f32[4,8,3,8,128]{4,3,2,1,0:T(8,128)S(1)}, f32[4,8,3,8,128]{4,3,2,1,0:T(8,128)S(1)}) custom-call(f32[256,384]{1,0:T(8,128)S(1)} %get-tuple-element.22.cells_ref, bf16[128,384]{1,0:T(8,128)(2,1)S(1)} %get-tuple-element.23.select_ref, f32[32,128]{1,0:T(8,128)S(1)} %collective-permute-done.4.next_ref, f32[32,128]{1,0:T(8,128)S(1)} %collective-permute-done.5.swap_ref), custom_call_target="tpu_custom_call" | custom-call | flops 20000000 | bytes 2000000 | tf_op jit(solution)/shard_map/first/pallas_call | solution.py:429
  18.2 0.1 collective-permute-done.7.mate_ref
  18.3 4.6 %steps.1 = f32[4,32,256]{2,1,0:T(8,128)} custom-call(f32[4,8,3,8,128]{4,3,2,1,0:T(8,128)S(1)} %get-tuple-element.26.field_ref, f32[4,8,3,8,128]{4,3,2,1,0:T(8,128)S(1)} %get-tuple-element.27.change_ref, bf16[384,256]{1,0:T(8,128)(2,1)S(1)} %get-tuple-element.28.select_ref, f32[8,128]{1,0:T(8,128)S(1)} %fusion.1.own_ref, ...), custom_call_target="tpu_custom_call" | custom-call | tf_op jit(solution)/shard_map/steps/pallas_call | solution.py:439
  (1 shorter events, 0.0 us)
Async XLA Ops:
  0.0 0.9 %copy-start = (f32[4,32,256]{2,1,0:T(8,128)S(1)}, f32[4,32,256]{2,1,0:T(8,128)}, u32[]{:S(2)}) copy-start(f32[4,32,256]{2,1,0:T(8,128)} %state_ref.3) | copy-start | bytes 393220
  1.1 7.7 %collective-permute-start = (f32[72,256]{1,0:T(8,128)S(1)}, f32[72,256]{1,0:T(8,128)S(1)}, u32[]{:S(2)}, u32[]{:S(2)}) collective-permute-start(f32[72,256]{1,0:T(8,128)S(1)} %get-tuple-element.18), channel_id=1, source_target_pairs={{4,8},{8,4},{12,16},{16,12},{20,24},{24,20},{28,0},{0,28},{5,9},{9... | collective-permute-start | bytes 221192 | tf_op jit(solution)/shard_map/ppermute | solution.py:372
  4.5 4.3 %collective-permute-start.1 = (f32[72,256]{1,0:T(8,128)S(1)}, f32[72,256]{1,0:T(8,128)S(1)}, u32[]{:S(2)}, u32[]{:S(2)}) collective-permute-start(f32[72,256]{1,0:T(8,128)S(1)} %get-tuple-element.19), channel_id=1, source_target_pairs={{0,4},{4,0},{8,12},{12,8},{16,20},{20,16},{24,28},{28,24},{1,5},{5... | collective-permute-start | bytes 221192 | tf_op jit(solution)/shard_map/ppermute | solution.py:372
  4.5 8.7 %copy-start.1 = (f32[4,32,256]{2,1,0:T(8,128)S(1)}, f32[4,32,256]{2,1,0:T(8,128)}, u32[]{:S(2)}) copy-start(f32[4,32,256]{2,1,0:T(8,128)} %state_ref.3) | copy-start | bytes 393220
  4.5 3.6 %collective-permute-start.3 = (f32[8,128]{1,0:T(8,128)S(1)}, f32[8,128]{1,0:T(8,128)S(1)}, u32[]{:S(2)}, u32[]{:S(2)}) collective-permute-start(f32[8,128]{1,0:T(8,128)S(1)} %get-tuple-element.20.own_ref), channel_id=1, source_target_pairs={{0,16},{4,20},{8,24},{12,28},{16,0},{20,4},{24,8},{28,12},{1,17},{... | collective-permute-start | bytes 12296 | tf_op jit(solution)/shard_map/ppermute | solution.py:364
  5.7 3.0 %collective-permute-start.2 = (f32[8,128]{1,0:T(8,128)S(1)}, f32[8,128]{1,0:T(8,128)S(1)}, u32[]{:S(2)}, u32[]{:S(2)}) collective-permute-start(f32[8,128]{1,0:T(8,128)S(1)} %get-tuple-element.20.own_ref), channel_id=1, source_target_pairs={{0,12},{4,24},{8,20},{12,0},{16,28},{20,8},{24,4},{28,16},{1,13},{... | collective-permute-start | bytes 12296 | tf_op jit(solution)/shard_map/ppermute | solution.py:376
  8.9 4.7 %collective-permute-start.6 = (f32[8,128]{1,0:T(8,128)S(1)}, f32[8,128]{1,0:T(8,128)S(1)}, u32[]{:S(2)}, u32[]{:S(2)}) collective-permute-start(f32[8,128]{1,0:T(8,128)S(1)} %get-tuple-element.21.own_ref), channel_id=1, source_target_pairs={{0,2},{1,3},{2,0},{3,1},{4,6},{5,7},{6,4},{7,5},{8,10},{9,11},{10,... | collective-permute-start | bytes 12296 | tf_op jit(solution)/shard_map/ppermute | solution.py:364
  11.5 5.5 %collective-permute-start.4 = (f32[32,128]{1,0:T(8,128)S(1)}, f32[32,128]{1,0:T(8,128)S(1)}, u32[]{:S(2)}, u32[]{:S(2)}) collective-permute-start(f32[32,128]{1,0:T(8,128)S(1)} %get-tuple-element.24), channel_id=1, source_target_pairs={{1,2},{2,1},{3,0},{0,3},{5,6},{6,5},{7,4},{4,7},{9,10},{10,9},{11,... | collective-permute-start | bytes 49160 | tf_op jit(solution)/shard_map/ppermute | solution.py:372
  12.9 4.2 %collective-permute-start.5 = (f32[32,128]{1,0:T(8,128)S(1)}, f32[32,128]{1,0:T(8,128)S(1)}, u32[]{:S(2)}, u32[]{:S(2)}) collective-permute-start(f32[32,128]{1,0:T(8,128)S(1)} %get-tuple-element.25), channel_id=1, source_target_pairs={{0,1},{1,0},{2,3},{3,2},{4,5},{5,4},{6,7},{7,6},{8,9},{9,8},{10,11... | collective-permute-start | bytes 49160 | tf_op jit(solution)/shard_map/ppermute | solution.py:372
  17.1 1.2 %collective-permute-start.7 = (f32[8,128]{1,0:T(8,128)S(1)}, f32[8,128]{1,0:T(8,128)S(1)}, u32[]{:S(2)}, u32[]{:S(2)}) collective-permute-start(f32[8,128]{1,0:T(8,128)S(1)} %fusion.1.own_ref), channel_id=1, source_target_pairs={{0,4},{4,0},{8,12},{12,8},{16,20},{20,16},{24,28},{28,24},{1,5},{5... | collective-permute-start | bytes 12296 | tf_op jit(solution)/shard_map/ppermute | solution.py:364
